TPU v7x, 32 devices: a whole 2x2x4 slice. The times are simulated.
32 devices in a mesh: dp: 16 (over z, y, x), col: 2 (over core).
Axes of the slice: x: 2, y: 2, z: 4, core: 2. Of those that a mesh axis runs over, the one named last changes fastest.
Arguments:
- embeddings: bfloat16 [8192, 4096], P('dp'), may hold values from -16 to 16
- rotation: bfloat16 [4096, 4096], P(None, 'col'), may hold values from -0.09375 to 0.09375
- codes: int32 [8192, 512], P('dp', 'col'), may hold values from 0 to 255
- codebooks: bfloat16 [512, 256, 8], P('col'), may hold values from -16 to 16
Outputs:
- new_rotation: float32 [4096, 4096], P('dp', 'col')
All inputs are finite; a program needn't handle non-finite values.
Results may differ from a plain program's by a relative error of at most 0.015.
Values may be sent and summed in bfloat16 or wider, within the bound.
No kernel may reach another device: no remote copies, remote signals or barrier semaphores. Data moves between devices by JAX's collectives and lax.ppermute only.
A program may use at most 128 MiB of HBM per device.

v0:
```python
import math

import jax
import jax.numpy as jnp
from jax import lax
from jax.sharding import PartitionSpec as P

STEPS = 2


def rebuild_rows(codes, codebooks):
    tok_rows, sub_count = codes.shape
    centroids = codebooks.shape[1]
    sub_width = codebooks.shape[2]
    group_size = min(16, sub_count)
    centroid_ids = jnp.arange(centroids, dtype=jnp.int32)
    diag_eye = jnp.eye(group_size, dtype=jnp.bfloat16)
    pieces = []
    for first_sub in range(0, sub_count, group_size):
        sub_ids = codes[:, first_sub : first_sub + group_size]
        onehot = (sub_ids[:, :, None] == centroid_ids[None, None, :]).astype(jnp.bfloat16)
        onehot = onehot.reshape(tok_rows, group_size * centroids)
        block_table = (
            codebooks[first_sub : first_sub + group_size][:, :, None, :]
            * diag_eye[:, None, :, None]
        )
        block_table = block_table.reshape(group_size * centroids, group_size * sub_width)
        pieces.append(
            jnp.dot(onehot, block_table, preferred_element_type=jnp.float32).astype(jnp.bfloat16)
        )
    return jnp.concatenate(pieces, axis=1)


def contract_rows(left_rows, right_rows):
    return lax.dot_general(
        left_rows, right_rows, (((0,), (0,)), ((), ())), preferred_element_type=jnp.float32
    )


def shards(embeddings, rotation, codes, codebooks):
    tok_rows, model_width = embeddings.shape
    rows_total = tok_rows * lax.axis_size("dp")
    block_rows = model_width // lax.axis_size("dp")
    rotated = jnp.dot(embeddings, rotation, preferred_element_type=jnp.float32)
    rebuilt = rebuild_rows(codes, codebooks)
    rebuilt_wide = rebuilt.astype(jnp.float32)
    residue = rotated - rebuilt_wide
    partial_value = jnp.sum(residue * residue, axis=1)
    row_error = lax.psum(partial_value, "col")
    weights = 1.0 / (1.0 + row_error / (2.0 * model_width))
    weighted = (weights[:, None] * rebuilt_wide).astype(jnp.bfloat16)
    cross_block = lax.psum_scatter(
        contract_rows(embeddings, weighted), "dp", scatter_dimension=0, tiled=True
    )
    start_row = lax.axis_index("dp") * block_rows
    prior_block = lax.dynamic_slice_in_dim(rotation, start_row, block_rows, 0).astype(jnp.float32)
    cross_block = cross_block + 0.2 * rows_total * prior_block
    frob_total = lax.psum(jnp.sum(cross_block * cross_block), ("dp", "col"))
    norm_scale = 1.4 * jnp.sqrt(frob_total / model_width)
    iterate = cross_block / norm_scale
    for step_index in range(STEPS):
        half_iter = iterate.astype(jnp.bfloat16)
        row_panel = lax.all_gather(half_iter, "col", axis=1, tiled=True)
        gram_term = contract_rows(row_panel, half_iter)
        gram_panel = lax.psum(gram_term.astype(jnp.bfloat16), "dp")
        product = jnp.dot(row_panel, gram_panel, preferred_element_type=jnp.float32)
        iterate = 1.5 * iterate - 0.5 * product
    return math.sqrt(model_width) * iterate


def solution(mesh):
    placed = (P("dp", None), P(None, "col"), P("dp", "col"), P("col", None, None))
    return jax.shard_map(
        shards, mesh=mesh, in_specs=placed, out_specs=P("dp", "col"), check_vma=False
    )
```

profile of v0, /device:TPU:0, one launch (start us, length us, event | category | flops | bytes accessed | tf_op | source)
XLA Modules:
  0.0 1884.9 jit_solution(12807766196460391845)
XLA Ops:
  12.7 2.8 iota_compare_fusion.14
  20.6 2.8 iota_compare_fusion.12
  29.5 3.3 iota_compare_fusion.10
  38.8 2.8 iota_compare_fusion.8
  47.6 3.0 iota_compare_fusion.6
  56.8 2.8 iota_compare_fusion.4
  65.7 2.8 iota_compare_fusion.2
  74.6 3.0 iota_compare_fusion
  97.5 2.6 fusion.17
  117.6 14.2 fusion.1
  131.8 2.6 psum.28
  134.4 17.8 convolution_bitcast_fusion
  154.1 684.3 %reduce-scatter.2.cloned.1.call-done = f32[256,2048]{0,1:T(8,128)} async-done(((f32[4096,2048]{0,1:T(8,128)}), f32[256,2048]{0,1:T(8,128)}) %reduce-scatter.2.cloned.1.call-update) | async-done | bytes 2097168 | tf_op jit(solution)/shard_map/reduce_scatter | solution.py:52
  838.4 2.9 multiply_reduce_fusion
  841.3 44.6 %psum.29 = f32[]{:T(128)} all-reduce(f32[]{:T(128)} %multiply_reduce_fusion), channel_id=1, replica_groups=mesh['dp'=16,'col'=2] {'dp','col'}, use_global_device_ids=true, to_apply=%region_4.0 | all-reduce | flops 1 | bytes 8 | tf_op jit(solution)/shard_map/psum | solution.py:58
  888.2 11.8 all-gather.3.cloned.1.call-done
  900.0 12.2 convolution_convert_fusion.1
  912.3 456.9 %all-reduce.3.cloned.1.call-done = bf16[4096,2048]{1,0:T(8,128)(2,1)} async-done(((bf16[4096,2048]{1,0:T(8,128)(2,1)}), bf16[4096,2048]{1,0:T(8,128)(2,1)}) %all-reduce.3.cloned.1.call-update) | async-done | bytes 16777232 | tf_op jit(solution)/shard_map/psum | solution.py:65
  1369.1 14.8 fusion.29
  1384.3 9.4 all-gather.5.cloned.1.call-done
  1393.7 12.2 convolution_convert_fusion
  1405.8 456.9 %all-reduce.5.cloned.1.call-done = bf16[4096,2048]{1,0:T(8,128)(2,1)} async-done(((bf16[4096,2048]{1,0:T(8,128)(2,1)}), bf16[4096,2048]{1,0:T(8,128)(2,1)}) %all-reduce.5.cloned.1.call-update) | async-done | bytes 16777232 | tf_op jit(solution)/shard_map/psum | solution.py:65
  1862.8 12.3 fusion.5
  1875.1 2.9 copy.44
  (115 shorter events, 88.5 us)
Async XLA Ops:
  6.5 831.8 %reduce-scatter.2.cloned.1.call-start = ((), (), s32[]{:S(2)}) async-start(), calls=%async_computation.1 | async-start | bytes 35651584 | tf_op jit(solution)/shard_map/reduce_scatter | solution.py:52
  10.6 1.0 copy-start
  84.5 2.2 copy-start.3
  86.6 2.2 copy-start.4
  88.8 2.2 copy-start.5
  91.0 2.2 copy-start.6
  93.2 2.2 copy-start.7
  95.4 2.2 copy-start.8
  97.5 2.6 copy-start.9
  100.1 2.2 copy-start.10
  102.3 2.2 copy-start.11
  104.5 2.2 copy-start.12
  106.7 2.2 copy-start.13
  108.8 2.2 copy-start.14
  111.0 2.2 copy-start.15
  113.2 2.2 copy-start.16
  152.2 747.8 %all-gather.3.cloned.1.call-start = ((), (), s32[]{:S(2)}) async-start(), calls=%async_computation.2 | async-start | bytes 3145728 | tf_op jit(solution)/shard_map/all_gather | solution.py:63
  838.4 48.2 %copy-start.1 = (f32[256,2048]{0,1:T(8,128)S(1)}, f32[256,2048]{0,1:T(8,128)}, u32[]{:S(2)}) copy-start(f32[256,2048]{0,1:T(8,128)} %reduce-scatter.2.cloned.1.call-done) | copy-start | bytes 6291460
  887.9 481.2 %all-reduce.3.cloned.1.call-start = ((), (), s32[]{:S(2)}) async-start(), calls=%async_computation.3 | async-start | bytes 33554432 | tf_op jit(solution)/shard_map/psum | solution.py:65
  912.2 481.4 %all-gather.5.cloned.1.call-start = ((), (), s32[]{:S(2)}) async-start(), calls=%async_computation.4 | async-start | bytes 3145728 | tf_op jit(solution)/shard_map/all_gather | solution.py:63
  1384.0 478.8 %all-reduce.5.cloned.1.call-start = ((), (), s32[]{:S(2)}) async-start(), calls=%async_computation.5 | async-start | bytes 33554432 | tf_op jit(solution)/shard_map/psum | solution.py:65
  1405.8 457.0 %copy-start.2 = (bf16[256,4096]{0,1:T(8,128)(2,1)S(1)}, bf16[256,4096]{0,1:T(8,128)(2,1)}, u32[]{:S(2)}) copy-start(bf16[256,4096]{0,1:T(8,128)(2,1)} %all-gather.5.cloned.1.call-done) | copy-start | bytes 6291460
Sparse Core Ops, SparseCore 0:
  152.3 686.0 reduce-scatter.1
  888.0 11.9 all-gather.2
  912.3 456.7 all-reduce.2
  1384.1 9.5 all-gather.4
  1406.0 456.7 all-reduce.4
where the time goes:
time: 1890 us; the launch traced here: 1880 us
  waiting for transfers between devices  1620 us (86%)
  matrix products  119 us (6%)
  local copies, waits for them, and re-layouts  54.4 us (3%)
  blocking collectives  47.2 us (2%)
  other arithmetic  30 us (2%)
    psum x2, waiting for transfers between devices, shards(): gram_panel = lax.psum(gram_term.astype(jnp.bfloat16), 'dp')  914 us
    reduce_scatter x1, waiting for transfers between devices, shards(): lax.psum_scatter(contract_rows(embeddings, weighted), 'dp', scatter_dimen...  684 us
    unnamed x67, local copies, waits for them, and re-layouts  47.6 us
    psum x1, blocking collectives, shards(): frob_total = lax.psum(jnp.sum(cross_block * cross_block), ('dp', 'col'))  44.6 us
    dot_general x3, matrix products, contract_rows(): lax.dot_general(left_rows, right_rows, (((0,), (0,)), ((), ())), preferre...  42.1 us
  transfers between devices with their start and end apart: 5, of which 5 were waited for; matrix products, arithmetic and copies ran while one was open for 0% of the time, Pallas kernels for 0%

commit v1 on v0

v1 whole, which is shorter than its diff:
```python
import functools
import math

import jax
import jax.numpy as jnp
from jax import lax
from jax.experimental import pallas as pl
from jax.experimental.pallas import tpu as pltpu
from jax.sharding import PartitionSpec as P

LANES = 128


def lookup_kernel(group, codes_ref, table_ref, out_ref, ids_ref):
    subs, rows = codes_ref.shape[1:]
    width = table_ref.shape[1]
    halves = table_ref.shape[2] // LANES
    ids_ref[...] = codes_ref[0].astype(jnp.float32).astype(jnp.int32)

    def body(step, carry):
        base = pl.multiple_of(step * group, group)
        for first in range(0, rows, LANES):
            ids_all = ids_ref[pl.ds(base, group), first : first + LANES]
            for pair in range(0, group, 2):
                both = []
                for sub in (pair, pair + 1):
                    ids = jnp.broadcast_to(ids_all[sub : sub + 1], (width, LANES))
                    lane = jnp.bitwise_and(ids, LANES - 1)
                    picked = None
                    for half in range(halves):
                        entries = table_ref[base + sub, :, half * LANES : (half + 1) * LANES]
                        got = jnp.take_along_axis(
                            entries, lane, axis=1, mode="promise_in_bounds"
                        )
                        picked = got if half == 0 else jnp.where(ids >= half * LANES, got, picked)
                    both.append(picked)
                out_ref[
                    pl.ds(pl.multiple_of((base + pair) * width, 2 * width), 2 * width),
                    first : first + LANES,
                ] = jnp.concatenate(both, axis=0).astype(out_ref.dtype)
        return carry

    lax.fori_loop(0, subs // group, body, 0)


def rebuild_rows(codes, table):
    blocks, subs, rows = codes.shape
    width, centroids = table.shape[1:]
    tile = min(32, subs)
    return pl.pallas_call(
        functools.partial(lookup_kernel, 8),
        grid=(subs // tile, blocks),
        in_specs=[
            pl.BlockSpec((1, tile, rows), lambda m, b: (b, m, 0)),
            pl.BlockSpec((tile, width, centroids), lambda m, b: (m, 0, 0)),
        ],
        out_specs=pl.BlockSpec((tile * width, rows), lambda m, b: (m, b)),
        out_shape=jax.ShapeDtypeStruct((subs * width, blocks * rows), jnp.bfloat16),
        scratch_shapes=[pltpu.VMEM((tile, rows), jnp.int32)],
        compiler_params=pltpu.CompilerParams(vmem_limit_bytes=32 * 1024 * 1024),
        name="lookup",
    )(codes, table)


def sum_over_col(value):
    if lax.axis_size("col") == 2:
        return value + lax.ppermute(
            value.astype(jnp.bfloat16), "col", [(0, 1), (1, 0)]
        ).astype(jnp.float32)
    return lax.psum(value, "col")


def shards(embeddings, rotation, codes, codebooks):
    tok_rows, model_width = embeddings.shape
    dp, col = lax.axis_size("dp"), lax.axis_size("col")
    rows_total = tok_rows * dp
    block_rows = model_width // dp
    part_rows = tok_rows // col

    table = jnp.transpose(codebooks, (0, 2, 1)).astype(jnp.float32)
    codes_t = codes.T.astype(jnp.bfloat16)
    all_codes = lax.all_gather(codes_t, "dp")

    own = rebuild_rows(codes_t[None], table)
    rotated = lax.dot_general(
        rotation, embeddings, (((0,), (1,)), ((), ())), preferred_element_type=jnp.float32
    )
    residue = rotated - own.astype(jnp.float32)
    row_error = lax.psum(jnp.sum(residue * residue, axis=0), "col")
    weights = 1.0 / (1.0 + row_error / (2.0 * model_width))
    scaled = (weights[:, None] * embeddings.astype(jnp.float32)).astype(jnp.bfloat16)

    mine = lax.dynamic_slice_in_dim(scaled, lax.axis_index("col") * part_rows, part_rows, 0)
    sent = lax.all_to_all(mine, "dp", split_axis=1, concat_axis=0, tiled=True)
    sent = sent.reshape(dp, part_rows, block_rows)
    columns = lax.all_gather(sent, "col", axis=1, tiled=True).reshape(rows_total, block_rows)

    rebuilt = rebuild_rows(all_codes, table)
    cross = lax.dot_general(
        columns, rebuilt, (((0,), (1,)), ((), ())), preferred_element_type=jnp.float32
    )
    start_row = lax.axis_index("dp") * block_rows
    prior = lax.dynamic_slice_in_dim(rotation, start_row, block_rows, 0).astype(jnp.float32)
    cross = cross + 0.2 * rows_total * prior

    panel = lax.all_gather(cross.astype(jnp.bfloat16), "dp", axis=0, tiled=True)
    wide = panel.astype(jnp.float32)
    frob_total = lax.psum(jnp.sum(wide * wide), "col")
    inv_square = model_width / (1.96 * frob_total)

    def times_gram(value):
        inner = lax.dot_general(
            value.astype(jnp.bfloat16), panel, (((1,), (1,)), ((), ())),
            preferred_element_type=jnp.float32,
        )
        inner = sum_over_col(inner * inv_square)
        return jnp.dot(inner.astype(jnp.bfloat16), panel, preferred_element_type=jnp.float32)

    start = cross * jnp.sqrt(inv_square)
    first = 1.5 * start - 0.5 * times_gram(start)
    inner = 1.5 * first - 0.5 * times_gram(first)
    inner = times_gram(inner)
    inner = 1.5 * inner - 0.5 * times_gram(inner)
    return math.sqrt(model_width) * (1.5 * first - 0.5 * inner)


def solution(mesh):
    placed = (P("dp", None), P(None, "col"), P("dp", "col"), P("col", None, None))
    return jax.shard_map(
        shards, mesh=mesh, in_specs=placed, out_specs=P("dp", "col"), check_vma=False
    )
```

time: 1890 us -> 596 us (0.32)
  waiting for transfers between devices: 1620 us -> 207 us
  Pallas kernels: 0 us -> 95.3 us
  blocking collectives: 47.2 us -> 89.2 us
  local copies, waits for them, and re-layouts: 54.4 us -> 17.1 us
  matrix products: 119 us -> 147 us
    psum x2 -> x0, waiting for transfers between devices: 914 us -> none  [shards(): gram_panel = lax.psum(gram_term.astype(jnp.bfloat16), 'dp')]
    reduce_scatter x1 -> x0, waiting for transfers between devices: 684 us -> none  [shards(): lax.psum_scatter(contract_rows(embeddings, weighted), 'dp', scatter_dimen...]
    all_gather x2 -> x3, waiting for transfers between devices: 21.2 us -> 191 us  [the longest x1 191 us: shards(): panel = lax.all_gather(cross.astype(jnp.bfloat16), 'dp', axis=0, tiled=True)]
    pallas_call x0 -> x2, Pallas kernels: none -> 95.3 us  [rebuild_rows(): pl.pallas_call(functools.partial(lookup_kernel, 8), grid=(subs // tile, b...]
    all_to_all x0 -> x1, blocking collectives: none -> 83.2 us  [shards(): sent = lax.all_to_all(mine, 'dp', split_axis=1, concat_axis=0, tiled=True)]
    psum x2, blocking collectives: 47.2 us -> 5.98 us  [the longest x1 3.39 us: shards(): frob_total = lax.psum(jnp.sum(wide * wide), 'col')]
    unnamed x67 -> x8, local copies, waits for them, and re-layouts: 47.6 us -> 7.5 us
    dot_general x22 -> x9, matrix products: 119 us -> 147 us  [the longest x4 76.6 us: times_gram(): lax.dot_general(value.astype(jnp.bfloat16), panel, (((1,), (1,)), ((), ()...]
  transfers between devices with their start and end apart: 5 -> 7, of which waited for: 5 -> 5; matrix products, arithmetic and copies ran while one was open for 0% -> 4% of each run, Pallas kernels for 0% -> 16%
where the time goes in v1:
time: 596 us; the launch traced here: 586 us
  waiting for transfers between devices  207 us (35%)
  matrix products  147 us (25%)
  Pallas kernels  95.3 us (16%)
  blocking collectives  89.2 us (15%)
  local copies, waits for them, and re-layouts  17.1 us (3%)
  other arithmetic  15.1 us (3%)
  between operations  14.1 us (2%)
    all_gather x1, waiting for transfers between devices, shards(): panel = lax.all_gather(cross.astype(jnp.bfloat16), 'dp', axis=0, tiled=True)  191 us
    pallas_call x2, Pallas kernels, rebuild_rows(): pl.pallas_call(functools.partial(lookup_kernel, 8), grid=(subs // tile, b...  95.3 us
    all_to_all x1, blocking collectives, shards(): sent = lax.all_to_all(mine, 'dp', split_axis=1, concat_axis=0, tiled=True)  83.2 us
    dot_general x4, matrix products, times_gram(): lax.dot_general(value.astype(jnp.bfloat16), panel, (((1,), (1,)), ((), ()...  76.6 us
    dot_general x3, matrix products, times_gram(): jnp.dot(inner.astype(jnp.bfloat16), panel, preferred_element_type=jnp.flo...  39.5 us
    dot_general x1, matrix products, shards(): lax.dot_general(columns, rebuilt, (((0,), (1,)), ((), ())), preferred_ele...  17.9 us
    ppermute x4, waiting for transfers between devices, sum_over_col(): lax.ppermute(value.astype(jnp.bfloat16), 'col', [(0, 1), (1, 0)])  16.4 us
    dot_general x1, matrix products, shards(): lax.dot_general(rotation, embeddings, (((0,), (1,)), ((), ())), preferred...  12.6 us
  transfers between devices with their start and end apart: 7, of which 5 were waited for; matrix products, arithmetic and copies ran while one was open for 4% of the time, Pallas kernels for 16%

profile of v1, /device:TPU:0, one launch (start us, length us, event | category | flops | bytes accessed | tf_op | source)
XLA Modules:
  0.0 585.6 jit_solution(76774051523704390)
XLA Ops:
  10.0 5.3 lookup.2
  15.3 12.6 %multiply_reduce_fusion.1 = f32[512]{0:T(512)S(1)} fusion(bf16[2048,512]{1,0:T(8,128)(2,1)S(1)} %lookup.2, bf16[4096,2048]{1,0:T(8,128)(2,1)} %param.5, bf16[512,4096]{1,0:T(8,128)(2,1)S(1)} %copy-done.1), kind=kOutput, calls=%fused_computation.10 | convolution fusion | flops 8594128896 | bytes 23070720 | tf_op jit(solution)/shard_map/dot_general | solution.py:85
  28.0 2.6 psum.14
  30.6 3.1 constant_dynamic-slice_fusion
  33.8 4.1 copy.10
  39.9 83.2 %all_to_all.16 = bf16[256,16,256]{0,2,1:T(8,128)(2,1)} all-to-all(bf16[256,16,256]{0,2,1:T(8,128)(2,1)S(1)} %bitcast.24), channel_id=1, replica_groups=mesh['dp'=16,'col'=2] {'dp'}, dimensions={1} | all-to-all | bytes 4194304 | tf_op jit(solution)/shard_map/all_to_all | solution.py:94
  123.2 2.2 copy-done
  125.3 90.0 %lookup.3 = bf16[2048,8192]{1,0:T(8,128)(2,1)} custom-call(bf16[16,256,512]{2,1,0:T(8,128)(2,1)S(1)} %bitcast.23, f32[256,8,256]{2,1,0:T(8,128)S(1)} %convert_bitcast_fusion.table_ref), custom_call_target="tpu_custom_call" | custom-call | tf_op jit(solution)/shard_map/lookup/pallas_call | solution.py:50
  215.3 6.4 %copy.9 = bf16[16,512,256]{2,1,0:T(8,128)(2,1)} copy(bf16[16,512,256]{1,2,0:T(8,128)(2,1)} %all-gather.5.cloned.1.call-done) | data formatting | bytes 8388608 | tf_op jit(solution)/shard_map/all_gather | solution.py:96
  221.7 17.9 %fusion.11 = (bf16[256,2048]{1,0:T(8,128)(2,1)}, f32[256,2048]{1,0:T(8,128)}) fusion(bf16[4096,2048]{1,0:T(8,128)(2,1)} %param.5, s32[]{:T(128)S(6)} %select_n.7, bf16[8192,256]{1,0:T(8,128)(2,1)} %bitcast.26, bf16[2048,8192]{1,0:T(8,128)(2,1)} %lookup.3), kind=kOutput, calls=%fused_computation.33 | convolution fusion | flops 8592031744 | bytes 41943044 | tf_op jit(solution)/shard_map/dot_general | solution.py:99
  239.6 191.0 %all-gather.7.cloned.1.call-done = bf16[4096,2048]{1,0:T(8,128)(2,1)} async-done(((bf16[256,2048]{1,0:T(8,128)(2,1)}), bf16[4096,2048]{1,0:T(8,128)(2,1)}) %all-gather.7.cloned.1.call-update) | async-done | bytes 16777232 | tf_op jit(solution)/shard_map/all_gather | solution.py:106
  430.6 11.0 %multiply_reduce_fusion = f32[]{:T(128)} fusion(bf16[4096,2048]{1,0:T(8,128)(2,1)} %all-gather.7.cloned.1.call-done), kind=kLoop, calls=%fused_computation | loop fusion | flops 25165824 | bytes 16777220 | tf_op jit(solution)/shard_map/reduce_sum | solution.py:108
  441.5 3.4 psum.15
  445.6 12.9 %fusion.12 = (bf16[256,4096]{1,0:T(8,128)(2,1)S(1)}, f32[256,4096]{1,0:T(8,128)}) fusion(f32[]{:T(128)S(6)} %div.15, bf16[4096,2048]{1,0:T(8,128)(2,1)} %all-gather.7.cloned.1.call-done, f32[256,2048]{1,0:T(8,128)} %get-tuple-element.8, f32[]{:T(128)S(6)} %sqrt.3), kind=kOutput, calls=%fused_computation.34 | convolution fusion | flops 4298113024 | bytes 25165832 | tf_op jit(solution)/shard_map/dot_general | solution.py:112
  458.7 4.0 collective-permute-done
  462.7 12.2 %fusion = f32[256,2048]{1,0:T(8,128)S(1)} fusion(bf16[4096,2048]{1,0:T(8,128)(2,1)} %all-gather.7.cloned.1.call-done, f32[256,4096]{1,0:T(8,128)} %get-tuple-element.10, bf16[256,4096]{1,0:T(8,128)(2,1)S(1)} %collective-permute-done, f32[256,2048]{1,0:T(8,128)} %get-tuple-element.8, f32[]{:T(128)S(6)} %sqrt.3), kind=kOutput, calls=%fused_computation.15 | convolution fusion | flops 4300210176 | bytes 27262980 | tf_op jit(solution)/shard_map/dot_general | solution.py:117
  474.9 19.5 %fusion.13 = (bf16[256,4096]{1,0:T(8,128)(2,1)}, f32[256,4096]{1,0:T(8,128)}) fusion(f32[]{:T(128)S(6)} %div.15, bf16[4096,2048]{1,0:T(8,128)(2,1)} %all-gather.7.cloned.1.call-done, f32[256,2048]{1,0:T(8,128)S(1)} %fusion), kind=kOutput, calls=%fused_computation.35 | convolution fusion | flops 4297588736 | bytes 25165828 | tf_op jit(solution)/shard_map/dot_general | solution.py:112
  494.6 4.2 collective-permute-done.1
  498.8 31.4 %fusion.14 = (bf16[256,4096]{1,0:T(8,128)(2,1)}, f32[256,4096]{1,0:T(8,128)}) fusion(f32[]{:T(128)S(6)} %div.15, bf16[4096,2048]{1,0:T(8,128)(2,1)} %all-gather.7.cloned.1.call-done, f32[256,4096]{1,0:T(8,128)} %get-tuple-element.12, bf16[256,4096]{1,0:T(8,128)(2,1)S(1)} %collective-permute-done.1, f32[256,2048]{1,0:T(8,128)} %copy-done.2), kind=kOutput, calls=%fused_computation.36 | convolution fusion | flops 8597274624 | bytes 31457284 | tf_op jit(solution)/shard_map/dot_general | solution.py:112
  530.4 4.2 collective-permute-done.2
  534.6 12.9 %fusion.3 = f32[256,2048]{1,0:T(8,128)} fusion(bf16[4096,2048]{1,0:T(8,128)(2,1)} %all-gather.7.cloned.1.call-done, f32[256,4096]{1,0:T(8,128)} %get-tuple-element.14, bf16[256,4096]{1,0:T(8,128)(2,1)S(1)} %collective-permute-done.2), kind=kOutput, calls=%fused_computation.18 | convolution fusion | flops 4298113024 | bytes 25165824 | tf_op jit(solution)/shard_map/dot_general | solution.py:117
  547.5 12.9 %fusion.15 = (bf16[256,4096]{1,0:T(8,128)(2,1)S(1)}, f32[256,4096]{1,0:T(8,128)}) fusion(f32[]{:T(128)S(6)} %div.15, bf16[4096,2048]{1,0:T(8,128)(2,1)} %all-gather.7.cloned.1.call-done, f32[256,2048]{1,0:T(8,128)} %fusion.3), kind=kOutput, calls=%fused_computation.37 | convolution fusion | flops 4297588736 | bytes 25165828 | tf_op jit(solution)/shard_map/dot_general | solution.py:112
  560.5 4.0 collective-permute-done.3
  564.5 14.4 %subtract_multiply_fusion = f32[256,2048]{1,0:T(8,128)} fusion(f32[256,2048]{1,0:T(8,128)} %fusion.3, f32[256,2048]{1,0:T(8,128)} %copy-done.2, bf16[4096,2048]{1,0:T(8,128)(2,1)} %all-gather.7.cloned.1.call-done, f32[256,4096]{1,0:T(8,128)} %get-tuple-element.16, bf16[256,4096]{1,0:T(8,128)(2,1)S(1)} %collective-permute-done.3), kind=kOutput, calls=%fused_computation.20 | convolution fusion | flops 4301783040 | bytes 29360128 | tf_op jit(solution)/shard_map/dot_general | solution.py:117
  (23 shorter events, 6.3 us)
Async XLA Ops:
  6.5 116.6 %all-gather.9.cloned.1.call-start = ((), (), s32[]{:S(2)}) async-start(), calls=%async_computation.3 | async-start | bytes 4456448 | tf_op jit(solution)/shard_map/all_gather | solution.py:82
  8.6 206.8 %all-gather.5.cloned.1.call-start = ((), (), s32[]{:S(2)}) async-start(), calls=%async_computation.1 | async-start | bytes 6291456 | tf_op jit(solution)/shard_map/all_gather | solution.py:96
  10.0 5.3 copy-start.1
  123.1 307.5 %all-gather.7.cloned.1.call-start = ((), (), s32[]{:S(2)}) async-start(), calls=%async_computation.2 | async-start | bytes 17825792 | tf_op jit(solution)/shard_map/all_gather | solution.py:106
  123.2 2.2 copy-start
  458.5 4.2 collective-permute-start
  474.9 19.5 %copy-start.2 = (f32[256,2048]{1,0:T(8,128)}, f32[256,2048]{1,0:T(8,128)S(1)}, u32[]{:S(2)}) copy-start(f32[256,2048]{1,0:T(8,128)S(1)} %fusion) | copy-start | bytes 6291460
  494.4 4.4 collective-permute-start.1
  530.2 4.4 collective-permute-start.2
  560.3 4.2 collective-permute-start.3
Sparse Core Ops, SparseCore 0:
  10.1 107.6 all-gather.8
  123.2 12.1 all-gather.4
  239.7 190.8 all-gather.6

commit v2 on v1

v2 whole, which is shorter than its diff:
```python
import functools
import math

import jax
import jax.numpy as jnp
from jax import lax
from jax.experimental import pallas as pl
from jax.experimental.pallas import tpu as pltpu
from jax.sharding import PartitionSpec as P

LANES = 128
GROUP = 8
CHUNKS = 4
VMEM_BYTES = 56 * 1024 * 1024
ANY = pl.BlockSpec(memory_space=pl.ANY)
VMEM = pl.BlockSpec(memory_space=pltpu.VMEM)


def split_kernel(place_ref, rows_ref, *refs):
    blocks, sems = refs[:-1], refs[-1]
    part_rows, block_cols = blocks[0].shape
    first_row = pl.multiple_of(place_ref[1] * part_rows, part_rows)
    copies = []
    for shift, block in enumerate(blocks):
        owner = lax.rem(place_ref[0] + shift, len(blocks))
        first_col = pl.multiple_of(owner * block_cols, block_cols)
        copies.append(
            pltpu.make_async_copy(
                rows_ref.at[pl.ds(first_row, part_rows), pl.ds(first_col, block_cols)],
                block,
                sems.at[shift],
            )
        )
    for copy in copies:
        copy.start()
    for copy in copies:
        copy.wait()


def split_blocks(place, embeddings, dp, col):
    rows, width = embeddings.shape
    block = jax.ShapeDtypeStruct((rows // col, width // dp), embeddings.dtype)
    return pl.pallas_call(
        split_kernel,
        grid_spec=pltpu.PrefetchScalarGridSpec(
            num_scalar_prefetch=1,
            grid=(),
            in_specs=[ANY],
            out_specs=[ANY] * dp,
            scratch_shapes=[pltpu.SemaphoreType.DMA((dp,))],
        ),
        out_shape=[block] * dp,
        name="split",
    )(place, embeddings)


def lookup_kernel(place_ref, codes_ref, table_ref, out_ref, ids_ref):
    subs, rows = codes_ref.shape[1:]
    width = table_ref.shape[1]
    halves = table_ref.shape[2] // LANES
    ids_ref[...] = codes_ref[0].astype(jnp.float32).astype(jnp.int32)

    def body(step, carry):
        base = pl.multiple_of(step * GROUP, GROUP)
        for first in range(0, rows, LANES):
            ids_all = ids_ref[pl.ds(base, GROUP), first : first + LANES]
            for pair in range(0, GROUP, 2):
                both = []
                for sub in (pair, pair + 1):
                    ids = jnp.broadcast_to(ids_all[sub : sub + 1], (width, LANES))
                    lane = jnp.bitwise_and(ids, LANES - 1)
                    picked = None
                    for half in range(halves):
                        entries = table_ref[base + sub, :, half * LANES : (half + 1) * LANES]
                        got = jnp.take_along_axis(
                            entries, lane, axis=1, mode="promise_in_bounds"
                        )
                        picked = got if half == 0 else jnp.where(ids >= half * LANES, got, picked)
                    both.append(picked)
                out_ref[
                    pl.ds(pl.multiple_of((base + pair) * width, 2 * width), 2 * width),
                    first : first + LANES,
                ] = jnp.concatenate(both, axis=0).astype(out_ref.dtype)
        return carry

    lax.fori_loop(0, subs // GROUP, body, 0)


def rebuild_rows(place, codes, table):
    blocks, subs, rows = codes.shape
    width, centroids = table.shape[1:]
    tile = min(64, subs)
    return pl.pallas_call(
        lookup_kernel,
        grid_spec=pltpu.PrefetchScalarGridSpec(
            num_scalar_prefetch=1,
            grid=(subs // tile, blocks),
            in_specs=[
                pl.BlockSpec(
                    (1, tile, rows), lambda m, s, place: (lax.rem(place[0] + blocks - s, blocks), m, 0)
                ),
                pl.BlockSpec((tile, width, centroids), lambda m, s, place: (m, 0, 0)),
            ],
            out_specs=pl.BlockSpec((tile * width, rows), lambda m, s, place: (m, s)),
            scratch_shapes=[pltpu.VMEM((tile, rows), jnp.int32)],
        ),
        out_shape=jax.ShapeDtypeStruct((subs * width, blocks * rows), jnp.bfloat16),
        compiler_params=pltpu.CompilerParams(vmem_limit_bytes=VMEM_BYTES),
        name="lookup",
    )(place, codes, table)


def load_panel(pieces, panel_ref, sems):
    dp, chunk, block = pieces[0].shape

    def copy(index, piece, owner):
        return pltpu.make_async_copy(
            piece.at[owner],
            panel_ref.at[
                pl.ds(pl.multiple_of(index * chunk, chunk), chunk),
                pl.ds(pl.multiple_of(owner * block, block), block),
            ],
            sems.at[index, owner],
        )

    for index, piece in enumerate(pieces):
        for owner in range(dp):
            copy(index, piece, owner).start()

    def wait(index):
        for owner in range(dp):
            copy(index, pieces[0], owner).wait()

    return chunk, wait


def times_panel(value_ref, panel_ref, out_ref):
    wide = min(512, panel_ref.shape[1])

    def body(step, carry):
        span = pl.ds(pl.multiple_of(step * wide, wide), wide)
        out_ref[:, span] = jnp.dot(
            value_ref[...], panel_ref[:, span], preferred_element_type=jnp.float32
        ).astype(out_ref.dtype)
        return carry

    lax.fori_loop(0, panel_ref.shape[1] // wide, body, 0)


def first_kernel(own_ref, *refs):
    count = len(refs) - 4
    pieces, (inner_ref, square_ref, panel_ref, sems) = refs[:count], refs[count:]
    chunk, wait = load_panel(pieces, panel_ref, sems)
    square_ref[...] = jnp.zeros_like(square_ref)
    wide = 512

    def body(index, carry):
        wait(index)
        span = pl.ds(pl.multiple_of(index * chunk, chunk), chunk)
        total = jnp.zeros(square_ref.shape, jnp.float32)
        for first in range(0, panel_ref.shape[1], wide):
            values = panel_ref[span, first : first + wide].astype(jnp.float32)
            total += jnp.sum((values * values).reshape(chunk // 8, 8, wide), axis=0)
        square_ref[...] += total
        return carry

    lax.fori_loop(0, len(pieces), body, 0)
    times_panel(own_ref, panel_ref, inner_ref)


def scale_of(model_width, mine_ref, other_ref):
    total = jnp.sum(mine_ref[...] + other_ref[...], axis=(0, 1), keepdims=True)
    return model_width / (1.96 * total)


def next_kernel(step, mine_ref, other_ref, mine_square_ref, other_square_ref, *refs):
    last = step == 3
    states = 2 if last else 1
    held, refs = refs[:states], refs[states:]
    count = len(refs) - (4 if last else 6)
    pieces, refs = refs[:count], refs[count:]
    if last:
        out_ref, panel_ref, sum_ref, sems = refs
    else:
        state_ref, inner_ref, panel_ref, sum_ref, value_ref, sems = refs
    chunk, wait = load_panel(pieces, panel_ref, sems)
    model_width = panel_ref.shape[1]
    scale = scale_of(model_width, mine_square_ref, other_square_ref)
    sum_ref[...] = (
        (mine_ref[...].astype(jnp.float32) + other_ref[...].astype(jnp.float32)) * scale
    ).astype(sum_ref.dtype)

    def body(index, carry):
        wait(index)
        span = pl.ds(pl.multiple_of(index * chunk, chunk), chunk)
        product = lax.dot_general(
            panel_ref[span, :], sum_ref[...], (((1,), (1,)), ((), ())),
            preferred_element_type=jnp.float32,
        )
        if step == 2:
            made = product
        else:
            made = 1.5 * held[0][span, :] - 0.5 * product
        if last:
            made = (1.5 * held[1][span, :] - 0.5 * made) * (math.sqrt(model_width) * jnp.sqrt(scale))
            out_ref[:, span] = made.T
        else:
            state_ref[span, :] = made
            value_ref[:, span] = made.T.astype(value_ref.dtype)
        return carry

    lax.fori_loop(0, len(pieces), body, 0)
    if not last:
        times_panel(value_ref, panel_ref, inner_ref)


def apply_first(own, pieces):
    dp, chunk, block = pieces[0].shape
    cols = chunk * len(pieces)
    return pl.pallas_call(
        first_kernel,
        in_specs=[VMEM] + [ANY] * len(pieces),
        out_specs=[VMEM, VMEM],
        out_shape=[
            jax.ShapeDtypeStruct((block, dp * block), jnp.bfloat16),
            jax.ShapeDtypeStruct((8, 512), jnp.float32),
        ],
        scratch_shapes=[
            pltpu.VMEM((cols, dp * block), jnp.bfloat16),
            pltpu.SemaphoreType.DMA((len(pieces), dp)),
        ],
        compiler_params=pltpu.CompilerParams(vmem_limit_bytes=VMEM_BYTES),
        name="first",
    )(own, *pieces)


def apply_next(step, inner, squares, held, pieces):
    dp, chunk, block = pieces[0].shape
    cols = chunk * len(pieces)
    last = step == 3
    if last:
        out_shape = jax.ShapeDtypeStruct((block, cols), jnp.float32)
        value = []
    else:
        out_shape = [
            jax.ShapeDtypeStruct((cols, block), jnp.float32),
            jax.ShapeDtypeStruct((block, dp * block), jnp.bfloat16),
        ]
        value = [pltpu.VMEM((block, cols), jnp.bfloat16)]
    return pl.pallas_call(
        functools.partial(next_kernel, step),
        in_specs=[VMEM] * (4 + len(held)) + [ANY] * len(pieces),
        out_specs=VMEM if last else [VMEM, VMEM],
        out_shape=out_shape,
        scratch_shapes=[
            pltpu.VMEM((cols, dp * block), jnp.bfloat16),
            pltpu.VMEM((block, dp * block), jnp.bfloat16),
        ]
        + value
        + [pltpu.SemaphoreType.DMA((len(pieces), dp))],
        compiler_params=pltpu.CompilerParams(vmem_limit_bytes=VMEM_BYTES),
        name="apply%d" % step,
    )(*inner, *squares, *held, *pieces)


def both_cores(value):
    if lax.axis_size("col") == 2:
        return value, lax.ppermute(value, "col", [(0, 1), (1, 0)])
    total = lax.psum(value.astype(jnp.float32), "col").astype(value.dtype)
    return total, jnp.zeros_like(total)


def columns_of_all(place, embeddings, dp, col):
    mine = split_blocks(place, embeddings, dp, col)
    parts = [mine[0]] + [
        lax.ppermute(mine[shift], "dp", [(i, (i + shift) % dp) for i in range(dp)])
        for shift in range(1, dp)
    ]
    share = jnp.stack(parts)
    if col == 2:
        other = lax.ppermute(share, "col", [(0, 1), (1, 0)])
        at_zero = place[1] == 0
        return jnp.concatenate(
            [jnp.where(at_zero, share, other), jnp.where(at_zero, other, share)], axis=1
        )
    return lax.all_gather(share, "col", axis=1, tiled=True)


def shards(embeddings, rotation, codes, codebooks):
    tok_rows, model_width = embeddings.shape
    sub_count = codes.shape[1]
    sub_width = codebooks.shape[2]
    dp, col = lax.axis_size("dp"), lax.axis_size("col")
    rows_total = tok_rows * dp
    block_rows = model_width // dp
    sub_chunk = sub_count // CHUNKS
    chunk = sub_chunk * sub_width
    place = jnp.stack([lax.axis_index("dp"), lax.axis_index("col")]).astype(jnp.int32)

    columns = columns_of_all(place, embeddings, dp, col)
    codes_t = codes.T.astype(jnp.bfloat16)
    all_codes = [
        lax.all_gather(codes_t[first : first + sub_chunk], "dp")
        for first in range(0, sub_count, sub_chunk)
    ]

    table = jnp.transpose(codebooks, (0, 2, 1)).astype(jnp.float32)
    own = rebuild_rows(place, codes_t[None], table)
    rotated = lax.dot_general(
        rotation, embeddings, (((0,), (1,)), ((), ())), preferred_element_type=jnp.float32
    )
    residue = rotated - own.astype(jnp.float32)
    row_error = lax.psum(jnp.sum(residue * residue, axis=0), "col")
    weights = lax.all_gather(1.0 / (1.0 + row_error / (2.0 * model_width)), "dp")
    order = lax.rem(place[0] + dp - jnp.arange(dp, dtype=jnp.int32), dp)
    weights = jnp.take(weights, order, axis=0, mode="clip")
    scaled = (weights[:, :, None] * columns.astype(jnp.float32)).astype(jnp.bfloat16)
    scaled = scaled.reshape(rows_total, block_rows)

    start_row = lax.axis_index("dp") * block_rows
    prior = lax.dynamic_slice_in_dim(rotation, start_row, block_rows, 0).T
    blocks, pieces = [], []
    for index in range(CHUNKS):
        table_part = table[index * sub_chunk : (index + 1) * sub_chunk]
        rebuilt = rebuild_rows(place, all_codes[index], table_part)
        cross = jnp.dot(rebuilt, scaled, preferred_element_type=jnp.float32)
        prior_part = prior[index * chunk : (index + 1) * chunk].astype(jnp.float32)
        blocks.append(cross + 0.2 * rows_total * prior_part)
        pieces.append(lax.all_gather(blocks[-1].astype(jnp.bfloat16), "dp"))

    start = jnp.concatenate(blocks, axis=0)
    inner, square = apply_first(start.T.astype(jnp.bfloat16), pieces)
    squares = both_cores(square)
    first, inner = apply_next(0, both_cores(inner), squares, [start], pieces)
    state, inner = apply_next(1, both_cores(inner), squares, [first], pieces)
    state, inner = apply_next(2, both_cores(inner), squares, [state], pieces)
    return apply_next(3, both_cores(inner), squares, [state, first], pieces)


def solution(mesh):
    placed = (P("dp", None), P(None, "col"), P("dp", "col"), P("col", None, None))
    return jax.shard_map(
        shards, mesh=mesh, in_specs=placed, out_specs=P("dp", "col"), check_vma=False
    )
```

time: 596 us -> 694 us (1.16); the launches traced: 586 us -> 693 us
  Pallas kernels: 95.3 us -> 253 us
  matrix products: 147 us -> 35.4 us
  waiting for transfers between devices: 207 us -> 269 us
  blocking collectives: 89.2 us -> 46.4 us
  starting transfers between devices: 0.81 us -> 37.3 us
  local copies, waits for them, and re-layouts: 17.1 us -> 29.5 us
    pallas_call x2 -> x11, Pallas kernels: 95.3 us -> 253 us  [the longest x5 105 us: rebuild_rows(): pl.pallas_call(lookup_kernel, grid_spec=pltpu.PrefetchScalarGridSpec(num_...]
    dot_general x8 -> x4, matrix products: 134 us -> 22.4 us  [shards(): cross = jnp.dot(rebuilt, scaled, preferred_element_type=jnp.float32)]
    all_to_all x1 -> x0, blocking collectives: 83.2 us -> none  [shards(): sent = lax.all_to_all(mine, 'dp', split_axis=1, concat_axis=0, tiled=True)]
    all_gather x3 -> x8, waiting for transfers between devices: 191 us -> 243 us  [the longest x4 243 us: shards(): pieces.append(lax.all_gather(blocks[-1].astype(jnp.bfloat16), 'dp'))]
    all_gather x0 -> x1, blocking collectives: none -> 43.9 us  [shards(): lax.all_gather(1.0 / (1.0 + row_error / (2.0 * model_width)), 'dp')]
    ppermute x4 -> x21, starting transfers between devices: 0.72 us -> 36.8 us  [the longest x15 35.6 us: columns_of_all(): lax.ppermute(mine[shift], 'dp', [(i, (i + shift) % dp) for i in range(dp)])]
    unnamed x8 -> x73, local copies, waits for them, and re-layouts: 7.5 us -> 23.4 us
    reduce_sum x1 -> x0, other arithmetic: 11 us -> none  [shards(): frob_total = lax.psum(jnp.sum(wide * wide), 'col')]
  transfers between devices with their start and end apart: 7 -> 29, of which waited for: 5 -> 11; matrix products, arithmetic and copies ran while one was open for 4% -> 9% of each run, Pallas kernels for 16% -> 25%
where the time goes in v2:
time: 694 us; the launch traced here: 693 us
  waiting for transfers between devices  269 us (39%)
  Pallas kernels  253 us (36%)
  blocking collectives  46.4 us (7%)
  starting transfers between devices  37.3 us (5%)
  matrix products  35.4 us (5%)
  local copies, waits for them, and re-layouts  29.5 us (4%)
  between operations  13.9 us (2%)
  other arithmetic  8.97 us (1%)
    all_gather x4, waiting for transfers between devices, shards(): pieces.append(lax.all_gather(blocks[-1].astype(jnp.bfloat16), 'dp'))  243 us
    pallas_call x5, Pallas kernels, rebuild_rows(): pl.pallas_call(lookup_kernel, grid_spec=pltpu.PrefetchScalarGridSpec(num_...  105 us
    pallas_call x4, Pallas kernels, apply_next(): pl.pallas_call(functools.partial(next_kernel, step), in_specs=[VMEM] * (4...  67.6 us
    pallas_call x1, Pallas kernels, split_blocks(): pl.pallas_call(split_kernel, grid_spec=pltpu.PrefetchScalarGridSpec(num_s...  65.4 us
    all_gather x1, blocking collectives, shards(): lax.all_gather(1.0 / (1.0 + row_error / (2.0 * model_width)), 'dp')  43.9 us
    ppermute x15, starting transfers between devices, columns_of_all(): lax.ppermute(mine[shift], 'dp', [(i, (i + shift) % dp) for i in range(dp)])  35.6 us
    unnamed x73, local copies, waits for them, and re-layouts  23.4 us
    dot_general x4, matrix products, shards(): cross = jnp.dot(rebuilt, scaled, preferred_element_type=jnp.float32)  22.4 us
  transfers between devices with their start and end apart: 29, of which 11 were waited for; matrix products, arithmetic and copies ran while one was open for 9% of the time, Pallas kernels for 25%

profile of v2, /device:TPU:0, one launch (start us, length us, event | category | flops | bytes accessed | tf_op | source)
XLA Modules:
  0.0 693.2 jit_solution(1461042619110728251)
XLA Ops:
  11.4 65.4 %split.1 = (bf16[256,256]{1,0:T(8,128)(2,1)}, bf16[256,256]{1,0:T(8,128)(2,1)}, bf16[256,256]{1,0:T(8,128)(2,1)}, bf16[256,256]{1,0:T(8,128)(2,1)}, bf16[256,256...) custom-call(s32[2]{0:T(128)} %pad_add_fusion.place_ref, ...), custom_call_target="tpu_custom_call" | custom-call | tf_op jit(solution)/shard_map/split/pallas_call | solution.py:43
  90.7 8.0 %lookup.6 = bf16[2048,512]{1,0:T(8,128)(2,1)} custom-call(s32[2]{0:T(128)} %pad_add_fusion.place_ref, bf16[1,256,512]{2,1,0:T(8,128)(2,1)} %get-tuple-element.59.codes_ref, f32[256,8,256]{2,1,0:T(8,128)} %convert_bitcast_fusion.table_ref), custom_call_target="tpu_custom_call" | custom-call | tf_op jit(solution)/shard_map/lookup/pallas_call | solution.py:93
  102.1 4.4 collective-permute-start.6
  114.3 5.2 collective-permute-done.5
  119.5 4.9 collective-permute-start.10
  125.1 7.3 %collective-permute-start.11 = (bf16[256,256]{1,0:T(8,128)(2,1)S(1)}, bf16[256,256]{1,0:T(8,128)(2,1)S(1)}, u32[]{:S(2)}, u32[]{:S(2)}) collective-permute-start(bf16[256,256]{1,0:T(8,128)(2,1)S(1)} %copy-done.18), channel_id=1, source_target_pairs={{0,24},{2,26},{4,28},{6,30},{8,0},{10,2},{12,4},{14,6},{16,8},{18,... | collective-permute-start | bytes 393224 | tf_op jit(solution)/shard_map/ppermute | solution.py:276
  146.4 13.0 %multiply_reduce_fusion = f32[512]{0:T(512)S(1)} fusion(bf16[2048,512]{1,0:T(8,128)(2,1)} %lookup.6, bf16[4096,2048]{1,0:T(8,128)(2,1)} %param.5, bf16[512,4096]{1,0:T(8,128)(2,1)S(1)} %copy-done.1), kind=kOutput, calls=%fused_computation.4 | convolution fusion | flops 8594128896 | bytes 23070720 | tf_op jit(solution)/shard_map/dot_general | solution.py:309
  162.0 43.9 %all-gather.9 = f32[16,1,512]{2,1,0:T(1,128)S(1)} all-gather(f32[1,1,512]{2,1,0:T(1,128)S(1)} %bitcast.106), channel_id=3, replica_groups=mesh['dp'=16,'col'=2] {'dp'}, dimensions={0}, use_global_device_ids=true | all-gather | bytes 34816 | tf_op jit(solution)/shard_map/all_gather | solution.py:314
  207.8 24.0 %lookup.5 = bf16[512,8192]{1,0:T(8,128)(2,1)} custom-call(s32[2]{0:T(128)} %pad_add_fusion.place_ref, bf16[16,64,512]{2,1,0:T(8,128)(2,1)} %bitcast.98, f32[64,8,256]{2,1,0:T(8,128)} %get-tuple-element.55.table_ref), custom_call_target="tpu_custom_call" | custom-call | tf_op jit(solution)/shard_map/lookup/pallas_call | solution.py:93
  242.3 24.5 %lookup.9 = bf16[512,8192]{1,0:T(8,128)(2,1)} custom-call(s32[2]{0:T(128)} %pad_add_fusion.place_ref, bf16[16,64,512]{2,1,0:T(8,128)(2,1)} %bitcast.97, f32[64,8,256]{2,1,0:T(8,128)} %get-tuple-element.56.table_ref), custom_call_target="tpu_custom_call" | custom-call | tf_op jit(solution)/shard_map/lookup/pallas_call | solution.py:93
  266.8 6.4 fusion.8
  273.3 24.5 %lookup.8 = bf16[512,8192]{1,0:T(8,128)(2,1)} custom-call(s32[2]{0:T(128)} %pad_add_fusion.place_ref, bf16[16,64,512]{2,1,0:T(8,128)(2,1)} %bitcast.96, f32[64,8,256]{2,1,0:T(8,128)} %get-tuple-element.57.table_ref), custom_call_target="tpu_custom_call" | custom-call | tf_op jit(solution)/shard_map/lookup/pallas_call | solution.py:93
  297.9 6.5 fusion.7
  304.7 24.5 %lookup.7 = bf16[512,8192]{1,0:T(8,128)(2,1)} custom-call(s32[2]{0:T(128)} %pad_add_fusion.place_ref, bf16[16,64,512]{2,1,0:T(8,128)(2,1)} %bitcast.99, f32[64,8,256]{2,1,0:T(8,128)} %get-tuple-element.58.table_ref), custom_call_target="tpu_custom_call" | custom-call | tf_op jit(solution)/shard_map/lookup/pallas_call | solution.py:93
  329.2 6.5 fusion.6
  337.2 10.6 %all-gather.27.cloned.1.call-done = bf16[8192,256]{1,0:T(8,128)(2,1)} async-done(((bf16[512,256]{1,0:T(8,128)(2,1)}), bf16[8192,256]{1,0:T(8,128)(2,1)}) %all-gather.27.cloned.1.call-update) | async-done | bytes 4194320 | tf_op jit(solution)/shard_map/all_gather | solution.py:329
  347.9 77.3 %all-gather.33.cloned.1.call-done = bf16[8192,256]{1,0:T(8,128)(2,1)} async-done(((bf16[512,256]{1,0:T(8,128)(2,1)}), bf16[8192,256]{1,0:T(8,128)(2,1)}) %all-gather.33.cloned.1.call-update) | async-done | bytes 4194320 | tf_op jit(solution)/shard_map/all_gather | solution.py:329
  425.2 77.5 %all-gather.31.cloned.1.call-done = bf16[8192,256]{1,0:T(8,128)(2,1)} async-done(((bf16[512,256]{1,0:T(8,128)(2,1)}), bf16[8192,256]{1,0:T(8,128)(2,1)}) %all-gather.31.cloned.1.call-update) | async-done | bytes 4194320 | tf_op jit(solution)/shard_map/all_gather | solution.py:329
  502.7 77.5 %all-gather.29.cloned.1.call-done = bf16[8192,256]{1,0:T(8,128)(2,1)} async-done(((bf16[512,256]{1,0:T(8,128)(2,1)}), bf16[8192,256]{1,0:T(8,128)(2,1)}) %all-gather.29.cloned.1.call-update) | async-done | bytes 4194320 | tf_op jit(solution)/shard_map/all_gather | solution.py:329
  580.2 14.8 %first.1 = (bf16[256,4096]{1,0:T(8,128)(2,1)}, f32[8,512]{1,0:T(8,128)}) custom-call(bf16[256,2048]{1,0:T(8,128)(2,1)} %copy.10.own_ref, bf16[16,512,256]{2,1,0:T(8,128)(2,1)} %bitcast.73, bf16[16,512,256]{2,1,0:T(8,128)(2,1)} %bitcast.88, bf16[16,512,256]{2,1,0:T(8,128)(2,1)} %bitcast.83, bf16[16,512,256]{2,1,0:T(8,128)(2,1)} %bitcast.78), custom_call_target="tpu_custom_call" | custom-call | tf_op jit(solution)/shard_map/first/pallas_call | solution.py:220
  601.4 18.2 %apply0.1 = (f32[2048,256]{1,0:T(8,128)}, bf16[256,4096]{1,0:T(8,128)(2,1)}) custom-call(bf16[256,4096]{1,0:T(8,128)(2,1)} %get-tuple-element.45.mine_ref, bf16[256,4096]{1,0:T(8,128)(2,1)} %copy-done.6, f32[8,512]{1,0:T(8,128)} %get-tuple-element.46.mine_square_ref, f32[8,512]{1,0:T(8,128)} %copy-done.13, f32[2048,256]{1,0:T(8,128)} %pad_maximum_fusion.1.refs_0_, ...), custom_call_target="tpu_custom_call" | custom-call | tf_op jit(solution)/shard_map/apply0/pallas_call | solution.py:250
  625.4 18.2 %apply1.1 = (f32[2048,256]{1,0:T(8,128)}, bf16[256,4096]{1,0:T(8,128)(2,1)}) custom-call(bf16[256,4096]{1,0:T(8,128)(2,1)} %get-tuple-element.47.mine_ref, bf16[256,4096]{1,0:T(8,128)(2,1)} %copy-done.9, f32[8,512]{1,0:T(8,128)} %get-tuple-element.46.mine_square_ref, f32[8,512]{1,0:T(8,128)} %copy-done.13, f32[2048,256]{1,0:T(8,128)} %get-tuple-element.48.refs_0_.refs_1_, ...), custom_call_target="tpu_custom_call" | custom-call | tf_op jit(solution)/shard_map/apply1/pallas_call | solution.py:250
  649.3 18.2 %apply2.1 = (f32[2048,256]{1,0:T(8,128)}, bf16[256,4096]{1,0:T(8,128)(2,1)}) custom-call(bf16[256,4096]{1,0:T(8,128)(2,1)} %get-tuple-element.49.mine_ref, bf16[256,4096]{1,0:T(8,128)(2,1)} %copy-done.8, f32[8,512]{1,0:T(8,128)} %get-tuple-element.46.mine_square_ref, f32[8,512]{1,0:T(8,128)} %copy-done.13, f32[2048,256]{1,0:T(8,128)} %get-tuple-element.50.refs_0_, ...), custom_call_target="tpu_custom_call" | custom-call | tf_op jit(solution)/shard_map/apply2/pallas_call | solution.py:250
  673.3 13.0 %apply3.1 = f32[256,2048]{1,0:T(8,128)} custom-call(bf16[256,4096]{1,0:T(8,128)(2,1)} %get-tuple-element.51.mine_ref, bf16[256,4096]{1,0:T(8,128)(2,1)} %copy-done.7, f32[8,512]{1,0:T(8,128)} %get-tuple-element.46.mine_square_ref, f32[8,512]{1,0:T(8,128)} %copy-done.13, f32[2048,256]{1,0:T(8,128)} %get-tuple-element.52.refs_0_, ...), custom_call_target="tpu_custom_call" | custom-call | tf_op jit(solution)/shard_map/apply3/pallas_call | solution.py:250
  (151 shorter events, 85.1 us)
Async XLA Ops:
  6.5 201.3 %all-gather.19.cloned.1.call-start = ((), (), s32[]{:S(2)}) async-start(), calls=%async_computation | async-start | bytes 1114112 | tf_op jit(solution)/shard_map/all_gather | solution.py:303
  9.3 233.0 %all-gather.25.cloned.1.call-start = ((), (), s32[]{:S(2)}) async-start(), calls=%async_computation.3 | async-start | bytes 1114112 | tf_op jit(solution)/shard_map/all_gather | solution.py:303
  10.0 263.3 %all-gather.23.cloned.1.call-start = ((), (), s32[]{:S(2)}) async-start(), calls=%async_computation.2 | async-start | bytes 1114112 | tf_op jit(solution)/shard_map/all_gather | solution.py:303
  10.8 293.9 %all-gather.21.cloned.1.call-start = ((), (), s32[]{:S(2)}) async-start(), calls=%async_computation.1 | async-start | bytes 1114112 | tf_op jit(solution)/shard_map/all_gather | solution.py:303
  76.8 22.5 %collective-permute-start = (bf16[256,256]{1,0:T(8,128)(2,1)}, bf16[256,256]{1,0:T(8,128)(2,1)}, u32[]{:S(2)}, u32[]{:S(2)}) collective-permute-start(bf16[256,256]{1,0:T(8,128)(2,1)} %get-tuple-element.30), channel_id=1, source_target_pairs={{0,2},{2,4},{4,6},{6,8},{8,10},{10,12},{12,14},{14,16},{16,18},{18... | collective-permute-start | bytes 393224 | tf_op jit(solution)/shard_map/ppermute | solution.py:276
  79.8 22.3 %collective-permute-start.1 = (bf16[256,256]{1,0:T(8,128)(2,1)}, bf16[256,256]{1,0:T(8,128)(2,1)}, u32[]{:S(2)}, u32[]{:S(2)}) collective-permute-start(bf16[256,256]{1,0:T(8,128)(2,1)} %get-tuple-element.31), channel_id=1, source_target_pairs={{0,4},{2,6},{4,8},{6,10},{8,12},{10,14},{12,16},{14,18},{16,20},{1... | collective-permute-start | bytes 393224 | tf_op jit(solution)/shard_map/ppermute | solution.py:276
  81.4 26.7 %collective-permute-start.2 = (bf16[256,256]{1,0:T(8,128)(2,1)}, bf16[256,256]{1,0:T(8,128)(2,1)}, u32[]{:S(2)}, u32[]{:S(2)}) collective-permute-start(bf16[256,256]{1,0:T(8,128)(2,1)} %get-tuple-element.32), channel_id=1, source_target_pairs={{0,6},{2,8},{4,10},{6,12},{8,14},{10,16},{12,18},{14,20},{16,22},{... | collective-permute-start | bytes 393224 | tf_op jit(solution)/shard_map/ppermute | solution.py:276
  83.8 26.1 %collective-permute-start.3 = (bf16[256,256]{1,0:T(8,128)(2,1)}, bf16[256,256]{1,0:T(8,128)(2,1)S(1)}, u32[]{:S(2)}, u32[]{:S(2)}) collective-permute-start(bf16[256,256]{1,0:T(8,128)(2,1)} %get-tuple-element.33), channel_id=1, source_target_pairs={{0,8},{2,10},{4,12},{6,14},{8,16},{10,18},{12,20},{14,22},{16,24},... | collective-permute-start | bytes 393224 | tf_op jit(solution)/shard_map/ppermute | solution.py:276
  85.4 26.9 %collective-permute-start.4 = (bf16[256,256]{1,0:T(8,128)(2,1)}, bf16[256,256]{1,0:T(8,128)(2,1)S(1)}, u32[]{:S(2)}, u32[]{:S(2)}) collective-permute-start(bf16[256,256]{1,0:T(8,128)(2,1)} %get-tuple-element.34), channel_id=1, source_target_pairs={{0,10},{2,12},{4,14},{6,16},{8,18},{10,20},{12,22},{14,24},{16,26}... | collective-permute-start | bytes 393224 | tf_op jit(solution)/shard_map/ppermute | solution.py:276
  87.0 260.9 %all-gather.27.cloned.1.call-start = ((), (), s32[]{:S(2)}) async-start(), calls=%async_computation.4 | async-start | bytes 4456448 | tf_op jit(solution)/shard_map/all_gather | solution.py:329
  99.4 20.1 %collective-permute-start.5 = (bf16[256,256]{1,0:T(8,128)(2,1)S(1)}, bf16[256,256]{1,0:T(8,128)(2,1)S(1)}, u32[]{:S(2)}, u32[]{:S(2)}) collective-permute-start(bf16[256,256]{1,0:T(8,128)(2,1)S(1)} %copy-done.24), channel_id=1, source_target_pairs={{0,12},{2,14},{4,16},{6,18},{8,20},{10,22},{12,24},{14,26},{16,28}... | collective-permute-start | bytes 393224 | tf_op jit(solution)/shard_map/ppermute | solution.py:276
  102.1 23.0 %collective-permute-start.6 = (bf16[256,256]{1,0:T(8,128)(2,1)S(1)}, bf16[256,256]{1,0:T(8,128)(2,1)S(1)}, u32[]{:S(2)}, u32[]{:S(2)}) collective-permute-start(bf16[256,256]{1,0:T(8,128)(2,1)S(1)} %copy-done.23), channel_id=1, source_target_pairs={{0,14},{2,16},{4,18},{6,20},{8,22},{10,24},{12,26},{14,28},{16,30}... | collective-permute-start | bytes 393224 | tf_op jit(solution)/shard_map/ppermute | solution.py:276
  108.0 25.0 %collective-permute-start.7 = (bf16[256,256]{1,0:T(8,128)(2,1)S(1)}, bf16[256,256]{1,0:T(8,128)(2,1)S(1)}, u32[]{:S(2)}, u32[]{:S(2)}) collective-permute-start(bf16[256,256]{1,0:T(8,128)(2,1)S(1)} %copy-done.22), channel_id=1, source_target_pairs={{0,16},{2,18},{4,20},{6,22},{8,24},{10,26},{12,28},{14,30},{16,0},... | collective-permute-start | bytes 393224 | tf_op jit(solution)/shard_map/ppermute | solution.py:276
  109.9 24.3 %collective-permute-start.8 = (bf16[256,256]{1,0:T(8,128)(2,1)S(1)}, bf16[256,256]{1,0:T(8,128)(2,1)S(1)}, u32[]{:S(2)}, u32[]{:S(2)}) collective-permute-start(bf16[256,256]{1,0:T(8,128)(2,1)S(1)} %copy-done.21), channel_id=1, source_target_pairs={{0,18},{2,20},{4,22},{6,24},{8,26},{10,28},{12,30},{14,0},{16,2},{... | collective-permute-start | bytes 393224 | tf_op jit(solution)/shard_map/ppermute | solution.py:276
  112.3 24.8 %collective-permute-start.9 = (bf16[256,256]{1,0:T(8,128)(2,1)S(1)}, bf16[256,256]{1,0:T(8,128)(2,1)S(1)}, u32[]{:S(2)}, u32[]{:S(2)}) collective-permute-start(bf16[256,256]{1,0:T(8,128)(2,1)S(1)} %copy-done.20), channel_id=1, source_target_pairs={{0,20},{2,22},{4,24},{6,26},{8,28},{10,30},{12,0},{14,2},{16,4},{1... | collective-permute-start | bytes 393224 | tf_op jit(solution)/shard_map/ppermute | solution.py:276
  119.5 19.9 %collective-permute-start.10 = (bf16[256,256]{1,0:T(8,128)(2,1)S(1)}, bf16[256,256]{1,0:T(8,128)(2,1)S(1)}, u32[]{:S(2)}, u32[]{:S(2)}) collective-permute-start(bf16[256,256]{1,0:T(8,128)(2,1)S(1)} %copy-done.19), channel_id=1, source_target_pairs={{0,22},{2,24},{4,26},{6,28},{8,30},{10,0},{12,2},{14,4},{16,6},{18... | collective-permute-start | bytes 393224 | tf_op jit(solution)/shard_map/ppermute | solution.py:276
  125.1 15.0 %collective-permute-start.11 = (bf16[256,256]{1,0:T(8,128)(2,1)S(1)}, bf16[256,256]{1,0:T(8,128)(2,1)S(1)}, u32[]{:S(2)}, u32[]{:S(2)}) collective-permute-start(bf16[256,256]{1,0:T(8,128)(2,1)S(1)} %copy-done.18), channel_id=1, source_target_pairs={{0,24},{2,26},{4,28},{6,30},{8,0},{10,2},{12,4},{14,6},{16,8},{18,... | collective-permute-start | bytes 393224 | tf_op jit(solution)/shard_map/ppermute | solution.py:276
  133.1 7.7 %collective-permute-start.12 = (bf16[256,256]{1,0:T(8,128)(2,1)S(1)}, bf16[256,256]{1,0:T(8,128)(2,1)S(1)}, u32[]{:S(2)}, u32[]{:S(2)}) collective-permute-start(bf16[256,256]{1,0:T(8,128)(2,1)S(1)} %copy-done.17), channel_id=1, source_target_pairs={{0,26},{2,28},{4,30},{6,0},{8,2},{10,4},{12,6},{14,8},{16,10},{18,... | collective-permute-start | bytes 393224 | tf_op jit(solution)/shard_map/ppermute | solution.py:276
  134.3 8.7 %collective-permute-start.13 = (bf16[256,256]{1,0:T(8,128)(2,1)S(1)}, bf16[256,256]{1,0:T(8,128)(2,1)S(1)}, u32[]{:S(2)}, u32[]{:S(2)}) collective-permute-start(bf16[256,256]{1,0:T(8,128)(2,1)S(1)} %copy-done.16), channel_id=1, source_target_pairs={{0,28},{2,30},{4,0},{6,2},{8,4},{10,6},{12,8},{14,10},{16,12},{18,... | collective-permute-start | bytes 393224 | tf_op jit(solution)/shard_map/ppermute | solution.py:276
  137.1 8.6 %collective-permute-start.14 = (bf16[256,256]{1,0:T(8,128)(2,1)S(1)}, bf16[256,256]{1,0:T(8,128)(2,1)S(1)}, u32[]{:S(2)}, u32[]{:S(2)}) collective-permute-start(bf16[256,256]{1,0:T(8,128)(2,1)S(1)} %copy-done.15), channel_id=1, source_target_pairs={{0,30},{2,0},{4,2},{6,4},{8,6},{10,8},{12,10},{14,12},{16,14},{18,... | collective-permute-start | bytes 393224 | tf_op jit(solution)/shard_map/ppermute | solution.py:276
  146.4 85.4 %collective-permute-start.15 = (bf16[16,256,256]{2,1,0:T(8,128)(2,1)}, bf16[16,256,256]{2,1,0:T(8,128)(2,1)}, u32[]{:S(2)}, u32[]{:S(2)}) collective-permute-start(bf16[16,256,256]{2,1,0:T(8,128)(2,1)} %bitcast_dynamic-update-slice_fusion), channel_id=1, source_target_pairs={{0,1},{1,0},{2,3},{3,2},{4,5},{5,4},{6,7},{7,6},{8,9},{9,8},{10,11... | collective-permute-start | bytes 6291464 | tf_op jit(solution)/shard_map/ppermute | solution.py:281
  242.2 183.0 %all-gather.33.cloned.1.call-start = ((), (), s32[]{:S(2)}) async-start(), calls=%async_computation.7 | async-start | bytes 4456448 | tf_op jit(solution)/shard_map/all_gather | solution.py:329
  273.2 229.5 %all-gather.31.cloned.1.call-start = ((), (), s32[]{:S(2)}) async-start(), calls=%async_computation.6 | async-start | bytes 4456448 | tf_op jit(solution)/shard_map/all_gather | solution.py:329
  304.4 275.8 %all-gather.29.cloned.1.call-start = ((), (), s32[]{:S(2)}) async-start(), calls=%async_computation.5 | async-start | bytes 4456448 | tf_op jit(solution)/shard_map/all_gather | solution.py:329
  (32 other events, 708.6 us)
Sparse Core Ops, SparseCore 0:
  10.1 57.9 all-gather.18
  70.9 83.4 all-gather.24
  157.2 56.4 all-gather.22
  216.2 54.0 all-gather.20
  273.0 74.8 all-gather.26
  350.5 74.6 all-gather.32
  428.0 74.6 all-gather.30
  505.5 74.6 all-gather.28

commit v3 on v1

v3 whole, which is shorter than its diff:
```python
import functools
import math

import jax
import jax.numpy as jnp
from jax import lax
from jax.experimental import pallas as pl
from jax.experimental.pallas import tpu as pltpu
from jax.sharding import PartitionSpec as P

LANES = 128
GROUP = 8
CHUNKS = 4
INNER = 4
VMEM_BYTES = 52 * 1024 * 1024
ANY = pl.BlockSpec(memory_space=pl.ANY)
VMEM = pl.BlockSpec(memory_space=pltpu.VMEM)


def lookup_kernel(codes_ref, table_ref, out_ref, ids_ref):
    subs, rows = codes_ref.shape[1:]
    width = table_ref.shape[1]
    halves = table_ref.shape[2] // LANES
    ids_ref[...] = codes_ref[0].astype(jnp.float32).astype(jnp.int32)

    def body(step, carry):
        base = pl.multiple_of(step * GROUP, GROUP)
        for first in range(0, rows, LANES):
            ids_all = ids_ref[pl.ds(base, GROUP), first : first + LANES]
            for pair in range(0, GROUP, 2):
                both = []
                for sub in (pair, pair + 1):
                    ids = jnp.broadcast_to(ids_all[sub : sub + 1], (width, LANES))
                    lane = jnp.bitwise_and(ids, LANES - 1)
                    picked = None
                    for half in range(halves):
                        entries = table_ref[base + sub, :, half * LANES : (half + 1) * LANES]
                        got = jnp.take_along_axis(
                            entries, lane, axis=1, mode="promise_in_bounds"
                        )
                        picked = got if half == 0 else jnp.where(ids >= half * LANES, got, picked)
                    both.append(picked)
                out_ref[
                    pl.ds(pl.multiple_of((base + pair) * width, 2 * width), 2 * width),
                    first : first + LANES,
                ] = jnp.concatenate(both, axis=0).astype(out_ref.dtype)
        return carry

    lax.fori_loop(0, subs // GROUP, body, 0)


def rebuild_rows(codes, table):
    blocks, subs, rows = codes.shape
    width, centroids = table.shape[1:]
    tile = min(64, subs)
    return pl.pallas_call(
        lookup_kernel,
        grid=(subs // tile, blocks),
        in_specs=[
            pl.BlockSpec((1, tile, rows), lambda m, s: (s, m, 0)),
            pl.BlockSpec((tile, width, centroids), lambda m, s: (m, 0, 0)),
        ],
        out_specs=pl.BlockSpec((tile * width, rows), lambda m, s: (m, s)),
        scratch_shapes=[pltpu.VMEM((tile, rows), jnp.int32)],
        out_shape=jax.ShapeDtypeStruct((subs * width, blocks * rows), jnp.bfloat16),
        compiler_params=pltpu.CompilerParams(vmem_limit_bytes=VMEM_BYTES),
        name="lookup",
    )(codes, table)


def load_panel(gathered, panel_ref, sems):
    dp, cols, block = gathered.shape
    chunk = cols // CHUNKS

    def copy(index, owner):
        span = pl.ds(pl.multiple_of(index * chunk, chunk), chunk)
        return pltpu.make_async_copy(
            gathered.at[owner, span],
            panel_ref.at[span, pl.ds(pl.multiple_of(owner * block, block), block)],
            sems.at[index, owner],
        )

    def start(index, carry):
        for owner in range(dp):
            copy(index, owner).start()
        return carry

    def wait(index):
        for owner in range(dp):
            copy(index, owner).wait()

    lax.fori_loop(0, CHUNKS, start, 0)
    return chunk, wait


def first_kernel(own_ref, gathered_ref, inner_ref, square_ref, panel_ref, total_ref, sems):
    chunk, wait = load_panel(gathered_ref, panel_ref, sems)
    square_ref[...] = jnp.zeros_like(square_ref)
    total_ref[...] = jnp.zeros_like(total_ref)
    wide = square_ref.shape[1]

    def body(index, carry):
        wait(index)
        rows = pl.ds(pl.multiple_of(index * chunk, chunk), chunk)

        def part(step, carry):
            span = pl.ds(pl.multiple_of(step * wide, wide), wide)
            values = panel_ref[rows, span]
            total_ref[:, span] += jnp.dot(
                own_ref[:, rows], values, preferred_element_type=jnp.float32
            )
            values = values.astype(jnp.float32)
            square_ref[...] += jnp.sum((values * values).reshape(chunk // 8, 8, wide), axis=0)
            return carry

        return lax.fori_loop(0, panel_ref.shape[1] // wide, part, carry)

    lax.fori_loop(0, CHUNKS, body, 0)
    inner_ref[...] = total_ref[...].astype(inner_ref.dtype)


def next_kernel(step, mine_square_ref, other_square_ref, mine_any, other_any, *refs):
    last = step == 3
    states = 2 if last else 1
    held, refs = refs[:states], refs[states:]
    if last:
        gathered_ref, out_ref, panel_ref, mine_ref, other_ref, sum_ref, panel_sems, sems = refs
    else:
        (gathered_ref, state_ref, inner_ref, panel_ref, mine_ref, other_ref, sum_ref, value_ref,
         panel_sems, sems) = refs
    copies = [
        pltpu.make_async_copy(mine_any, mine_ref, sems.at[0]),
        pltpu.make_async_copy(other_any, other_ref, sems.at[1]),
    ]
    for copy in copies:
        copy.start()
    chunk, wait = load_panel(gathered_ref, panel_ref, panel_sems)
    model_width = panel_ref.shape[1]
    wide = 512
    total = jnp.sum(mine_square_ref[...] + other_square_ref[...], axis=(0, 1), keepdims=True)
    scale = model_width / (1.96 * total)
    for copy in copies:
        copy.wait()

    def turn(index, carry):
        span = pl.ds(pl.multiple_of(index * wide, wide), wide)
        both = mine_ref[:, span].astype(jnp.float32) + other_ref[:, span].astype(jnp.float32)
        sum_ref[span, :] = (both * scale).T.astype(sum_ref.dtype)
        return carry

    lax.fori_loop(0, model_width // wide, turn, 0)

    def body(index, carry):
        wait(index)
        span = pl.ds(pl.multiple_of(index * chunk, chunk), chunk)
        made = jnp.dot(panel_ref[span, :], sum_ref[...], preferred_element_type=jnp.float32)
        if step != 2:
            made = 1.5 * held[0][span, :] - 0.5 * made
        if last:
            made = (1.5 * held[1][span, :] - 0.5 * made) * (math.sqrt(model_width) * jnp.sqrt(scale))
            out_ref[:, span] = made.T
        else:
            state_ref[span, :] = made
            value_ref[:, span] = made.T.astype(value_ref.dtype)
        return carry

    lax.fori_loop(0, CHUNKS, body, 0)
    if last:
        return

    def product(index, carry):
        span = pl.ds(pl.multiple_of(index * wide, wide), wide)
        inner_ref[:, span] = jnp.dot(
            value_ref[...], panel_ref[:, span], preferred_element_type=jnp.float32
        ).astype(inner_ref.dtype)
        return carry

    lax.fori_loop(0, model_width // wide, product, 0)


def apply_first(own, gathered):
    dp, cols, block = gathered.shape
    return pl.pallas_call(
        first_kernel,
        in_specs=[VMEM, ANY],
        out_specs=[VMEM, VMEM],
        out_shape=[
            jax.ShapeDtypeStruct((block, dp * block), jnp.bfloat16),
            jax.ShapeDtypeStruct((8, 512), jnp.float32),
        ],
        scratch_shapes=[
            pltpu.VMEM((cols, dp * block), jnp.bfloat16),
            pltpu.VMEM((block, dp * block), jnp.float32),
            pltpu.SemaphoreType.DMA((CHUNKS, dp)),
        ],
        compiler_params=pltpu.CompilerParams(vmem_limit_bytes=VMEM_BYTES),
        name="first",
    )(own, gathered)


def apply_next(step, inner, squares, held, gathered):
    dp, cols, block = gathered.shape
    last = step == 3
    if last:
        out_shape = jax.ShapeDtypeStruct((block, cols), jnp.float32)
        value = []
    else:
        out_shape = [
            jax.ShapeDtypeStruct((cols, block), jnp.float32),
            jax.ShapeDtypeStruct((block, dp * block), jnp.bfloat16),
        ]
        value = [pltpu.VMEM((block, cols), jnp.bfloat16)]
    return pl.pallas_call(
        functools.partial(next_kernel, step),
        in_specs=[VMEM, VMEM, ANY, ANY] + [VMEM] * len(held) + [ANY],
        out_specs=VMEM if last else [VMEM, VMEM],
        out_shape=out_shape,
        scratch_shapes=[
            pltpu.VMEM((cols, dp * block), jnp.bfloat16),
            pltpu.VMEM((block, dp * block), jnp.bfloat16),
            pltpu.VMEM((block, dp * block), jnp.bfloat16),
            pltpu.VMEM((dp * block, block), jnp.bfloat16),
        ]
        + value
        + [pltpu.SemaphoreType.DMA((CHUNKS, dp)), pltpu.SemaphoreType.DMA((2,))],
        compiler_params=pltpu.CompilerParams(vmem_limit_bytes=VMEM_BYTES),
        name="apply%d" % step,
    )(*squares, *inner, *held, gathered)


def swap_cores(value):
    return lax.ppermute(value, "col", [(0, 1), (1, 0)])


def both_cores(value):
    if lax.axis_size("col") == 2:
        return value, swap_cores(value)
    total = lax.psum(value.astype(jnp.float32), "col").astype(value.dtype)
    return total, jnp.zeros_like(total)


def shards(embeddings, rotation, codes, codebooks):
    tok_rows, model_width = embeddings.shape
    dp, col = lax.axis_size("dp"), lax.axis_size("col")
    rows_total = tok_rows * dp
    block = model_width // dp
    inner_size = math.gcd(dp, INNER)
    outer_size = dp // inner_size
    wide = model_width // outer_size
    part_rows = tok_rows // col
    outer, inner = lax.axis_index("dp") // inner_size, lax.axis_index("dp") % inner_size
    core = lax.axis_index("col")

    def from_outer(value, step):
        pairs = [(i, (i // inner_size ^ step) * inner_size + i % inner_size) for i in range(dp)]
        return lax.ppermute(value, "dp", pairs)

    def from_inner(value, step):
        pairs = [(i, i // inner_size * inner_size + (i % inner_size ^ step)) for i in range(dp)]
        return lax.ppermute(value, "dp", pairs)

    steps = list(range(1, outer_size))
    shares = []
    for step in steps:
        send = lax.dynamic_slice(
            embeddings, (core * part_rows, (outer ^ step) * wide), (part_rows, wide)
        )
        shares.append(from_outer(send, step))
    codes_t = codes.T.astype(jnp.bfloat16)
    group_codes = jnp.stack([codes_t] + [from_outer(codes_t, step) for step in steps])
    columns = [lax.dynamic_slice_in_dim(embeddings, outer * wide, wide, 1)]
    for share in shares:
        if col == 2:
            other = swap_cores(share)
            pair = [jnp.where(core == 0, share, other), jnp.where(core == 0, other, share)]
            columns.append(jnp.concatenate(pair, axis=0))
        else:
            columns.append(lax.all_gather(share, "col", axis=0, tiled=True))

    table = jnp.transpose(codebooks, (0, 2, 1)).astype(jnp.float32)
    own = rebuild_rows(codes_t[None], table)
    rotated = lax.dot_general(
        rotation, embeddings, (((0,), (1,)), ((), ())), preferred_element_type=jnp.float32
    )
    residue = rotated - own.astype(jnp.float32)
    row_error = lax.psum(jnp.sum(residue * residue, axis=0), "col")
    weights = 1.0 / (1.0 + row_error / (2.0 * model_width))
    group_weights = [weights] + [from_outer(weights, step) for step in steps]
    scaled = jnp.concatenate(
        [
            (weight[:, None] * part.astype(jnp.float32)).astype(jnp.bfloat16)
            for weight, part in zip(group_weights, columns)
        ],
        axis=0,
    )

    rebuilt = rebuild_rows(group_codes, table)

    def group_block(step):
        part = lax.dynamic_slice_in_dim(scaled, (inner ^ step) * block, block, 1)
        return jnp.dot(rebuilt, part, preferred_element_type=jnp.float32)

    parts = [
        from_inner(group_block(step).astype(jnp.bfloat16), step)
        for step in reversed(range(1, inner_size))
    ]
    start_row = lax.axis_index("dp") * block
    prior = lax.dynamic_slice_in_dim(rotation, start_row, block, 0).T
    start = group_block(0) + 0.2 * rows_total * prior.astype(jnp.float32)
    for part in parts:
        start = start + part.astype(jnp.float32)
    narrow = start.astype(jnp.bfloat16)
    gathered = lax.all_gather(narrow, "dp")

    inner, square = apply_first(narrow.T, gathered)
    squares = both_cores(square)
    first, inner = apply_next(0, both_cores(inner), squares, [start], gathered)
    state, inner = apply_next(1, both_cores(inner), squares, [first], gathered)
    state, inner = apply_next(2, both_cores(inner), squares, [state], gathered)
    return apply_next(3, both_cores(inner), squares, [state, first], gathered)


def solution(mesh):
    placed = (P("dp", None), P(None, "col"), P("dp", "col"), P("col", None, None))
    return jax.shard_map(
        shards, mesh=mesh, in_specs=placed, out_specs=P("dp", "col"), check_vma=False
    )
```

time: 596 us -> 475 us (0.80); the launches traced: 586 us -> 475 us
  matrix products: 147 us -> 30.8 us
  blocking collectives: 89.2 us -> 2.47 us
  waiting for transfers between devices: 207 us -> 262 us
  starting transfers between devices: 0.81 us -> 32.6 us
  Pallas kernels: 95.3 us -> 112 us
  other arithmetic: 15.1 us -> 7.43 us
    dot_general x8 -> x4, matrix products: 134 us -> 18.1 us  [group_block(): return jnp.dot(rebuilt, part, preferred_element_type=jnp.float32)]
    all_to_all x1 -> x0, blocking collectives: 83.2 us -> none  [shards(): sent = lax.all_to_all(mine, 'dp', split_axis=1, concat_axis=0, tiled=True)]
    ppermute x4 -> x20, waiting for transfers between devices: 16.4 us -> 71.8 us  [the longest x3 43.6 us: from_inner(): return lax.ppermute(value, 'dp', pairs)]
    ppermute x4 -> x20, starting transfers between devices: 0.72 us -> 32.6 us  [the longest x9 28 us: from_outer(): return lax.ppermute(value, 'dp', pairs)]
    pallas_call x2 -> x7, Pallas kernels: 95.3 us -> 112 us  [the longest x4 67.1 us: apply_next(): pl.pallas_call(functools.partial(next_kernel, step), in_specs=[VMEM, VMEM...]
    reduce_sum x1 -> x0, other arithmetic: 11 us -> none  [shards(): frob_total = lax.psum(jnp.sum(wide * wide), 'col')]
    all_gather x1 -> x0, local copies, waits for them, and re-layouts: 6.39 us -> none  [shards(): lax.all_gather(sent, 'col', axis=1, tiled=True)]
    all_gather x3 -> x1, waiting for transfers between devices: 191 us -> 190 us  [shards(): gathered = lax.all_gather(narrow, 'dp')]
  transfers between devices with their start and end apart: 7 -> 21, of which waited for: 5 -> 12; matrix products, arithmetic and copies ran while one was open for 4% -> 5% of each run, Pallas kernels for 16% -> 6%
where the time goes in v3:
time: 475 us
  waiting for transfers between devices  262 us (55%)
  Pallas kernels  112 us (24%)
  starting transfers between devices  32.6 us (7%)
  matrix products  30.8 us (6%)
  local copies, waits for them, and re-layouts  14.2 us (3%)
  between operations  13.7 us (3%)
  other arithmetic  7.43 us (2%)
    all_gather x1, waiting for transfers between devices, shards(): gathered = lax.all_gather(narrow, 'dp')  190 us
    pallas_call x4, Pallas kernels, apply_next(): pl.pallas_call(functools.partial(next_kernel, step), in_specs=[VMEM, VMEM...  67.1 us
    ppermute x3, waiting for transfers between devices, from_inner(): return lax.ppermute(value, 'dp', pairs)  43.6 us
    pallas_call x2, Pallas kernels, rebuild_rows(): pl.pallas_call(lookup_kernel, grid=(subs // tile, blocks), in_specs=[pl.B...  30.8 us
    ppermute x9, starting transfers between devices, from_outer(): return lax.ppermute(value, 'dp', pairs)  28 us
    dot_general x4, matrix products, group_block(): return jnp.dot(rebuilt, part, preferred_element_type=jnp.float32)  18.1 us
    ppermute x8, waiting for transfers between devices, swap_cores(): return lax.ppermute(value, 'col', [(0, 1), (1, 0)])  17.3 us
    pallas_call x1, Pallas kernels, apply_first(): pl.pallas_call(first_kernel, in_specs=[VMEM, ANY], out_specs=[VMEM, VMEM]...  14.1 us
  transfers between devices with their start and end apart: 21, of which 12 were waited for; matrix products, arithmetic and copies ran while one was open for 5% of the time, Pallas kernels for 6%

profile of v3, /device:TPU:0, one launch (start us, length us, event | category | flops | bytes accessed | tf_op | source)
XLA Modules:
  0.0 474.9 jit_solution(3078429345931472908)
XLA Ops:
  8.5 4.0 collective-permute-start.1
  17.4 2.9 collective-permute-start.10
  21.8 7.3 %lookup.3 = bf16[2048,512]{1,0:T(8,128)(2,1)} custom-call(bf16[1,256,512]{2,1,0:T(8,128)(2,1)S(1)} %get-tuple-element.30.codes_ref, f32[256,8,256]{2,1,0:T(8,128)} %convert_bitcast_fusion.table_ref), custom_call_target="tpu_custom_call" | custom-call | tf_op jit(solution)/shard_map/lookup/pallas_call | solution.py:56
  29.1 12.7 %multiply_reduce_fusion = f32[512]{0:T(512)S(1)} fusion(bf16[2048,512]{1,0:T(8,128)(2,1)} %lookup.3, bf16[4096,2048]{1,0:T(8,128)(2,1)} %param.5, bf16[512,4096]{1,0:T(8,128)(2,1)S(1)} %copy-done.5), kind=kOutput, calls=%fused_computation.1 | convolution fusion | flops 8594128896 | bytes 23070720 | tf_op jit(solution)/shard_map/dot_general | solution.py:282
  44.9 10.2 %collective-permute-done.10 = bf16[256,1024]{1,0:T(8,128)(2,1)S(1)} collective-permute-done((bf16[256,1024]{1,0:T(8,128)(2,1)S(1)}, bf16[256,1024]{1,0:T(8,128)(2,1)S(1)}, u32[]{:S(2)}, u32[]{:S(2)}) %collective-permute-start.10) | collective-permute-done | bytes 524320 | tf_op jit(solution)/shard_map/ppermute | solution.py:256
  56.7 2.6 collective-permute-start.9
  59.2 14.9 %collective-permute-start.6 = (f32[512]{0:T(512)S(1)}, f32[512]{0:T(512)S(1)}, u32[]{:S(2)}, u32[]{:S(2)}) collective-permute-start(f32[512]{0:T(512)S(1)} %add_divide_fusion), channel_id=1, source_target_pairs={{0,16},{2,18},{4,20},{6,22},{8,24},{10,26},{12,28},{14,30},{16,0},... | collective-permute-start | bytes 6152 | tf_op jit(solution)/shard_map/ppermute | solution.py:256
  75.4 23.5 %lookup.2 = bf16[2048,2048]{1,0:T(8,128)(2,1)} custom-call(bf16[4,256,512]{2,1,0:T(8,128)(2,1)S(1)} %pad_maximum_fusion.1.codes_ref, f32[256,8,256]{2,1,0:T(8,128)} %convert_bitcast_fusion.table_ref), custom_call_target="tpu_custom_call" | custom-call | tf_op jit(solution)/shard_map/lookup/pallas_call | solution.py:56
  107.3 3.3 convolution_convert_fusion.1
  110.7 3.3 convolution_convert_fusion.2
  114.0 2.7 collective-permute-start.12
  119.3 22.0 %collective-permute-done.12 = bf16[2048,256]{1,0:T(8,128)(2,1)} collective-permute-done((bf16[2048,256]{1,0:T(8,128)(2,1)}, bf16[2048,256]{1,0:T(8,128)(2,1)}, u32[]{:S(2)}, u32[]{:S(2)}) %collective-permute-start.12) | collective-permute-done | bytes 1048608 | tf_op jit(solution)/shard_map/ppermute | solution.py:260
  141.3 21.5 %collective-permute-done.13 = bf16[2048,256]{1,0:T(8,128)(2,1)} collective-permute-done((bf16[2048,256]{1,0:T(8,128)(2,1)}, bf16[2048,256]{1,0:T(8,128)(2,1)}, u32[]{:S(2)}, u32[]{:S(2)}) %collective-permute-start.13) | collective-permute-done | bytes 1048608 | tf_op jit(solution)/shard_map/ppermute | solution.py:260
  162.9 9.0 %fusion.12 = (bf16[2048,256]{1,0:T(8,128)(2,1)}, f32[2048,256]{1,0:T(8,128)}) fusion(bf16[2048,256]{1,0:T(8,128)(2,1)} %collective-permute-done.14, bf16[2048,256]{1,0:T(8,128)(2,1)} %collective-permute-done.13, bf16[2048,256]{1,0:T(8,128)(2,1)} %collective-permute-done.12, bf16[256,2048]{0,1:T(8,128)(2,1)S(1)} %copy.8, bf16[2048,2048]{1,0:T(8,128)(2,1)} %lookup.2, ...), kind=kOutput, calls=%fused_computation.34 | convolution fusion | flops 2152726528 | bytes 16777220 | tf_op jit(solution)/shard_map/dot_general | solution.py:301
  173.7 189.8 %all-gather.3.cloned.1.call-done = bf16[32768,256]{1,0:T(8,128)(2,1)} async-done(((bf16[2048,256]{1,0:T(8,128)(2,1)}), bf16[32768,256]{1,0:T(8,128)(2,1)}) %all-gather.3.cloned.1.call-update) | async-done | bytes 16777232 | tf_op jit(solution)/shard_map/all_gather | solution.py:313
  363.6 14.1 %first.1 = (bf16[256,4096]{1,0:T(8,128)(2,1)}, f32[8,512]{1,0:T(8,128)S(1)}) custom-call(bf16[256,2048]{1,0:T(8,128)(2,1)S(1)} %copy.7.own_ref, bf16[16,2048,256]{2,1,0:T(8,128)(2,1)} %bitcast.20), custom_call_target="tpu_custom_call" | custom-call | tf_op jit(solution)/shard_map/first/pallas_call | solution.py:183
  378.3 3.3 collective-permute-done.15.other_square_ref
  383.5 18.0 %apply0.1 = (f32[2048,256]{1,0:T(8,128)}, bf16[256,4096]{1,0:T(8,128)(2,1)}) custom-call(f32[8,512]{1,0:T(8,128)S(1)} %get-tuple-element.13.mine_square_ref, f32[8,512]{1,0:T(8,128)S(1)} %collective-permute-done.15.other_square_ref, bf16[256,4096]{1,0:T(8,128)(2,1)} %get-tuple-element.14.mine_any, bf16[256,4096]{1,0:T(8,128)(2,1)} %copy-done.1, ...), custom_call_target="tpu_custom_call" | custom-call | tf_op jit(solution)/shard_map/apply0/pallas_call | solution.py:213
  401.8 4.2 collective-permute-done.17.other_any
  407.3 18.1 %apply1.1 = (f32[2048,256]{1,0:T(8,128)}, bf16[256,4096]{1,0:T(8,128)(2,1)}) custom-call(f32[8,512]{1,0:T(8,128)S(1)} %get-tuple-element.13.mine_square_ref, f32[8,512]{1,0:T(8,128)S(1)} %collective-permute-done.15.other_square_ref, bf16[256,4096]{1,0:T(8,128)(2,1)} %get-tuple-element.15.mine_any, bf16[256,4096]{1,0:T(8,128)(2,1)} %copy-done.4, ...), custom_call_target="tpu_custom_call" | custom-call | tf_op jit(solution)/shard_map/apply1/pallas_call | solution.py:213
  425.6 4.2 collective-permute-done.18.other_any
  431.2 18.1 %apply2.1 = (f32[2048,256]{1,0:T(8,128)}, bf16[256,4096]{1,0:T(8,128)(2,1)}) custom-call(f32[8,512]{1,0:T(8,128)S(1)} %get-tuple-element.13.mine_square_ref, f32[8,512]{1,0:T(8,128)S(1)} %collective-permute-done.15.other_square_ref, bf16[256,4096]{1,0:T(8,128)(2,1)} %get-tuple-element.17.mine_any, bf16[256,4096]{1,0:T(8,128)(2,1)} %copy-done.3, ...), custom_call_target="tpu_custom_call" | custom-call | tf_op jit(solution)/shard_map/apply2/pallas_call | solution.py:213
  449.5 4.2 collective-permute-done.19.other_any
  455.1 12.9 %apply3.1 = f32[256,2048]{1,0:T(8,128)} custom-call(f32[8,512]{1,0:T(8,128)S(1)} %get-tuple-element.13.mine_square_ref, f32[8,512]{1,0:T(8,128)S(1)} %collective-permute-done.15.other_square_ref, bf16[256,4096]{1,0:T(8,128)(2,1)} %get-tuple-element.19.mine_any, bf16[256,4096]{1,0:T(8,128)(2,1)} %copy-done.2, f32[2048,256]{1,0:T(8,128)} %get-tuple-element.20.refs_0_, ...), custom_call_target="tpu_custom_call" | custom-call | tf_op jit(solution)/shard_map/apply3/pallas_call | solution.py:213
  (68 shorter events, 34.0 us)
Async XLA Ops:
  6.5 357.0 %all-gather.3.cloned.1.call-start = ((), (), s32[]{:S(2)}) async-start(), calls=%async_computation | async-start | bytes 17825792 | tf_op jit(solution)/shard_map/all_gather | solution.py:313
  7.8 12.5 %copy-start.6 = (bf16[256,256,8]{1,2,0:T(8,128)(2,1)S(1)}, bf16[256,256,8]{1,2,0:T(8,128)(2,1)}, u32[]{:S(2)}) copy-start(bf16[256,256,8]{1,2,0:T(8,128)(2,1)} %param.7) | copy-start | bytes 3145732
  8.5 35.8 %collective-permute-start.1 = (bf16[256,512]{1,0:T(8,128)(2,1)}, bf16[256,512]{1,0:T(8,128)(2,1)}, u32[]{:S(2)}, u32[]{:S(2)}) collective-permute-start(bf16[256,512]{1,0:T(8,128)(2,1)} %get-tuple-element.31), channel_id=1, source_target_pairs={{0,16},{2,18},{4,20},{6,22},{8,24},{10,26},{12,28},{14,30},{16,0},... | collective-permute-start | bytes 786440 | tf_op jit(solution)/shard_map/ppermute | solution.py:256
  12.6 44.1 %collective-permute-start = (bf16[256,512]{1,0:T(8,128)(2,1)}, bf16[256,512]{1,0:T(8,128)(2,1)}, u32[]{:S(2)}, u32[]{:S(2)}) collective-permute-start(bf16[256,512]{1,0:T(8,128)(2,1)} %get-tuple-element.31), channel_id=1, source_target_pairs={{0,8},{2,10},{4,12},{6,14},{8,0},{10,2},{12,4},{14,6},{16,24},{18,... | collective-permute-start | bytes 786440 | tf_op jit(solution)/shard_map/ppermute | solution.py:256
  14.1 45.1 %collective-permute-start.2 = (bf16[256,512]{1,0:T(8,128)(2,1)}, bf16[256,512]{1,0:T(8,128)(2,1)}, u32[]{:S(2)}, u32[]{:S(2)}) collective-permute-start(bf16[256,512]{1,0:T(8,128)(2,1)} %get-tuple-element.31), channel_id=1, source_target_pairs={{0,24},{2,26},{4,28},{6,30},{8,16},{10,18},{12,20},{14,22},{16,8},... | collective-permute-start | bytes 786440 | tf_op jit(solution)/shard_map/ppermute | solution.py:256
  16.5 28.4 %collective-permute-start.4 = (bf16[256,1024]{1,0:T(8,128)(2,1)S(1)}, bf16[256,1024]{1,0:T(8,128)(2,1)S(1)}, u32[]{:S(2)}, u32[]{:S(2)}) collective-permute-start(bf16[256,1024]{1,0:T(8,128)(2,1)S(1)} %get-tuple-element.21), channel_id=1, source_target_pairs={{0,8},{2,10},{4,12},{6,14},{8,0},{10,2},{12,4},{14,6},{16,24},{18,... | collective-permute-start | bytes 1572872 | tf_op jit(solution)/shard_map/ppermute | solution.py:256
  17.4 37.8 %collective-permute-start.10 = (bf16[256,1024]{1,0:T(8,128)(2,1)S(1)}, bf16[256,1024]{1,0:T(8,128)(2,1)S(1)}, u32[]{:S(2)}, u32[]{:S(2)}) collective-permute-start(bf16[256,1024]{1,0:T(8,128)(2,1)S(1)} %get-tuple-element.22), channel_id=1, source_target_pairs={{0,24},{2,26},{4,28},{6,30},{8,16},{10,18},{12,20},{14,22},{16,8},... | collective-permute-start | bytes 1572872 | tf_op jit(solution)/shard_map/ppermute | solution.py:256
  21.8 7.3 %copy-start.5 = (bf16[512,4096]{1,0:T(8,128)(2,1)S(1)}, bf16[512,4096]{1,0:T(8,128)(2,1)}, u32[]{:S(2)}) copy-start(bf16[512,4096]{1,0:T(8,128)(2,1)} %param.4) | copy-start | bytes 12582916
  44.3 54.6 %collective-permute-start.7 = (bf16[256,1024]{1,0:T(8,128)(2,1)}, bf16[256,1024]{1,0:T(8,128)(2,1)S(1)}, u32[]{:S(2)}, u32[]{:S(2)}) collective-permute-start(bf16[256,1024]{1,0:T(8,128)(2,1)} %get-tuple-element.23), channel_id=1, source_target_pairs={{0,16},{2,18},{4,20},{6,22},{8,24},{10,26},{12,28},{14,30},{16,0},... | collective-permute-start | bytes 1572872 | tf_op jit(solution)/shard_map/ppermute | solution.py:256
  44.9 54.5 %collective-permute-start.5 = (bf16[256,1024]{1,0:T(8,128)(2,1)S(1)}, bf16[256,1024]{1,0:T(8,128)(2,1)S(1)}, u32[]{:S(2)}, u32[]{:S(2)}) collective-permute-start(bf16[256,1024]{1,0:T(8,128)(2,1)S(1)} %collective-permute-done.4), channel_id=1, source_target_pairs={{0,1},{1,0},{2,3},{3,2},{4,5},{5,4},{6,7},{7,6},{8,9},{9,8},{10,11... | collective-permute-start | bytes 1572872 | tf_op jit(solution)/shard_map/ppermute | solution.py:232
  55.2 44.3 %collective-permute-start.11 = (bf16[256,1024]{1,0:T(8,128)(2,1)S(1)}, bf16[256,1024]{1,0:T(8,128)(2,1)}, u32[]{:S(2)}, u32[]{:S(2)}) collective-permute-start(bf16[256,1024]{1,0:T(8,128)(2,1)S(1)} %collective-permute-done.10), channel_id=1, source_target_pairs={{0,1},{1,0},{2,3},{3,2},{4,5},{5,4},{6,7},{7,6},{8,9},{9,8},{10,11... | collective-permute-start | bytes 1572872 | tf_op jit(solution)/shard_map/ppermute | solution.py:232
  56.7 44.7 %collective-permute-start.9 = (f32[512]{0:T(512)S(1)}, f32[512]{0:T(512)S(1)}, u32[]{:S(2)}, u32[]{:S(2)}) collective-permute-start(f32[512]{0:T(512)S(1)} %add_divide_fusion), channel_id=1, source_target_pairs={{0,24},{2,26},{4,28},{6,30},{8,16},{10,18},{12,20},{14,22},{16,8},... | collective-permute-start | bytes 6152 | tf_op jit(solution)/shard_map/ppermute | solution.py:256
  59.2 42.4 %collective-permute-start.6 = (f32[512]{0:T(512)S(1)}, f32[512]{0:T(512)S(1)}, u32[]{:S(2)}, u32[]{:S(2)}) collective-permute-start(f32[512]{0:T(512)S(1)} %add_divide_fusion), channel_id=1, source_target_pairs={{0,16},{2,18},{4,20},{6,22},{8,24},{10,26},{12,28},{14,30},{16,0},... | collective-permute-start | bytes 6152 | tf_op jit(solution)/shard_map/ppermute | solution.py:256
  98.9 3.6 collective-permute-start.3
  99.4 1.9 collective-permute-start.8
  105.0 5.7 %copy-start = (bf16[2048,1024]{1,0:T(8,128)(2,1)}, bf16[2048,1024]{1,0:T(8,128)(2,1)S(1)}, u32[]{:S(2)}) copy-start(bf16[2048,1024]{1,0:T(8,128)(2,1)S(1)} %pad_maximum_fusion) | copy-start | bytes 12582916
  114.0 27.3 %collective-permute-start.12 = (bf16[2048,256]{1,0:T(8,128)(2,1)}, bf16[2048,256]{1,0:T(8,128)(2,1)}, u32[]{:S(2)}, u32[]{:S(2)}) collective-permute-start(bf16[2048,256]{1,0:T(8,128)(2,1)} %convolution_convert_fusion.2), channel_id=1, source_target_pairs={{0,6},{2,4},{4,2},{6,0},{8,14},{10,12},{12,10},{14,8},{16,22},{18,... | collective-permute-start | bytes 3145736 | tf_op jit(solution)/shard_map/ppermute | solution.py:260
  116.7 46.1 %collective-permute-start.13 = (bf16[2048,256]{1,0:T(8,128)(2,1)}, bf16[2048,256]{1,0:T(8,128)(2,1)}, u32[]{:S(2)}, u32[]{:S(2)}) collective-permute-start(bf16[2048,256]{1,0:T(8,128)(2,1)} %convolution_convert_fusion.1), channel_id=1, source_target_pairs={{0,4},{2,6},{4,0},{6,2},{8,12},{10,14},{12,8},{14,10},{16,20},{18,... | collective-permute-start | bytes 3145736 | tf_op jit(solution)/shard_map/ppermute | solution.py:260
  117.2 45.7 %collective-permute-start.14 = (bf16[2048,256]{1,0:T(8,128)(2,1)S(1)}, bf16[2048,256]{1,0:T(8,128)(2,1)}, u32[]{:S(2)}, u32[]{:S(2)}) collective-permute-start(bf16[2048,256]{1,0:T(8,128)(2,1)S(1)} %convolution_convert_fusion), channel_id=1, source_target_pairs={{0,2},{2,0},{4,6},{6,4},{8,10},{10,8},{12,14},{14,12},{16,18},{18,... | collective-permute-start | bytes 3145736 | tf_op jit(solution)/shard_map/ppermute | solution.py:260
  377.7 4.5 collective-permute-start.16
  377.8 3.8 collective-permute-start.15
  401.6 4.4 collective-permute-start.17
  425.4 4.4 collective-permute-start.18
  449.3 4.4 collective-permute-start.19
  (6 other events, 10.1 us)
Sparse Core Ops, SparseCore 0:
  172.1 191.3 all-gather.2

commit v4 on v3

--- a/solution.py
+++ b/solution.py
@@ -12,7 +12,7 @@
 GROUP = 8
 CHUNKS = 4
 INNER = 4
-VMEM_BYTES = 52 * 1024 * 1024
+VMEM_BYTES = 24 * 1024 * 1024
 ANY = pl.BlockSpec(memory_space=pl.ANY)
 VMEM = pl.BlockSpec(memory_space=pltpu.VMEM)
 
@@ -68,92 +68,51 @@
     )(codes, table)
 
 
-def load_panel(gathered, panel_ref, sems):
-    dp, cols, block = gathered.shape
-    chunk = cols // CHUNKS
-
-    def copy(index, owner):
-        span = pl.ds(pl.multiple_of(index * chunk, chunk), chunk)
-        return pltpu.make_async_copy(
-            gathered.at[owner, span],
-            panel_ref.at[span, pl.ds(pl.multiple_of(owner * block, block), block)],
-            sems.at[index, owner],
-        )
-
-    def start(index, carry):
-        for owner in range(dp):
-            copy(index, owner).start()
-        return carry
-
-    def wait(index):
-        for owner in range(dp):
-            copy(index, owner).wait()
-
-    lax.fori_loop(0, CHUNKS, start, 0)
-    return chunk, wait
-
-
-def first_kernel(own_ref, gathered_ref, inner_ref, square_ref, panel_ref, total_ref, sems):
-    chunk, wait = load_panel(gathered_ref, panel_ref, sems)
+def first_kernel(panel_ref, own_ref, inner_ref, square_ref):
+    dp, cols, block = panel_ref.shape
     square_ref[...] = jnp.zeros_like(square_ref)
-    total_ref[...] = jnp.zeros_like(total_ref)
-    wide = square_ref.shape[1]
-
-    def body(index, carry):
-        wait(index)
-        rows = pl.ds(pl.multiple_of(index * chunk, chunk), chunk)
-
-        def part(step, carry):
-            span = pl.ds(pl.multiple_of(step * wide, wide), wide)
-            values = panel_ref[rows, span]
-            total_ref[:, span] += jnp.dot(
-                own_ref[:, rows], values, preferred_element_type=jnp.float32
-            )
-            values = values.astype(jnp.float32)
-            square_ref[...] += jnp.sum((values * values).reshape(chunk // 8, 8, wide), axis=0)
-            return carry
-
-        return lax.fori_loop(0, panel_ref.shape[1] // wide, part, carry)
-
-    lax.fori_loop(0, CHUNKS, body, 0)
-    inner_ref[...] = total_ref[...].astype(inner_ref.dtype)
-
-
-def next_kernel(step, mine_square_ref, other_square_ref, mine_any, other_any, *refs):
+
+    def body(owner, carry):
+        values = panel_ref[owner]
+        inner_ref[:, pl.ds(pl.multiple_of(owner * block, block), block)] = jnp.dot(
+            own_ref[...], values, preferred_element_type=jnp.float32
+        ).astype(inner_ref.dtype)
+        values = values.astype(jnp.float32)
+        square_ref[...] += jnp.sum((values * values).reshape(cols // 8, 8, block), axis=0)
+        return carry
+
+    lax.fori_loop(0, dp, body, 0)
+
+
+def next_kernel(step, panel_ref, mine_square_ref, other_square_ref, mine_ref, other_ref, *refs):
     last = step == 3
     states = 2 if last else 1
     held, refs = refs[:states], refs[states:]
     if last:
-        gathered_ref, out_ref, panel_ref, mine_ref, other_ref, sum_ref, panel_sems, sems = refs
+        out_ref, sum_ref = refs
     else:
-        (gathered_ref, state_ref, inner_ref, panel_ref, mine_ref, other_ref, sum_ref, value_ref,
-         panel_sems, sems) = refs
-    copies = [
-        pltpu.make_async_copy(mine_any, mine_ref, sems.at[0]),
-        pltpu.make_async_copy(other_any, other_ref, sems.at[1]),
-    ]
-    for copy in copies:
-        copy.start()
-    chunk, wait = load_panel(gathered_ref, panel_ref, panel_sems)
-    model_width = panel_ref.shape[1]
-    wide = 512
+        state_ref, inner_ref, sum_ref, value_ref = refs
+    dp, cols, block = panel_ref.shape
+    model_width = dp * block
+    chunk = cols // CHUNKS
     total = jnp.sum(mine_square_ref[...] + other_square_ref[...], axis=(0, 1), keepdims=True)
     scale = model_width / (1.96 * total)
-    for copy in copies:
-        copy.wait()
-
-    def turn(index, carry):
-        span = pl.ds(pl.multiple_of(index * wide, wide), wide)
+
+    def turn(owner, carry):
+        span = pl.ds(pl.multiple_of(owner * block, block), block)
         both = mine_ref[:, span].astype(jnp.float32) + other_ref[:, span].astype(jnp.float32)
-        sum_ref[span, :] = (both * scale).T.astype(sum_ref.dtype)
-        return carry
-
-    lax.fori_loop(0, model_width // wide, turn, 0)
+        sum_ref[owner] = (both * scale).T.astype(sum_ref.dtype)
+        return carry
+
+    lax.fori_loop(0, dp, turn, 0)
 
     def body(index, carry):
-        wait(index)
         span = pl.ds(pl.multiple_of(index * chunk, chunk), chunk)
-        made = jnp.dot(panel_ref[span, :], sum_ref[...], preferred_element_type=jnp.float32)
+        made = jnp.zeros((chunk, block), jnp.float32)
+        for owner in range(dp):
+            made += jnp.dot(
+                panel_ref[owner, span, :], sum_ref[owner], preferred_element_type=jnp.float32
+            )
         if step != 2:
             made = 1.5 * held[0][span, :] - 0.5 * made
         if last:
@@ -168,64 +127,55 @@
     if last:
         return
 
-    def product(index, carry):
-        span = pl.ds(pl.multiple_of(index * wide, wide), wide)
-        inner_ref[:, span] = jnp.dot(
-            value_ref[...], panel_ref[:, span], preferred_element_type=jnp.float32
+    def product(owner, carry):
+        inner_ref[:, pl.ds(pl.multiple_of(owner * block, block), block)] = jnp.dot(
+            value_ref[...], panel_ref[owner], preferred_element_type=jnp.float32
         ).astype(inner_ref.dtype)
         return carry
 
-    lax.fori_loop(0, model_width // wide, product, 0)
-
-
-def apply_first(own, gathered):
-    dp, cols, block = gathered.shape
+    lax.fori_loop(0, dp, product, 0)
+
+
+def in_vmem(*values):
+    return [pltpu.with_memory_space_constraint(value, pltpu.VMEM) for value in values]
+
+
+def apply_first(panel, own):
+    dp, cols, block = panel.shape
     return pl.pallas_call(
         first_kernel,
-        in_specs=[VMEM, ANY],
+        in_specs=[VMEM, VMEM],
         out_specs=[VMEM, VMEM],
         out_shape=[
-            jax.ShapeDtypeStruct((block, dp * block), jnp.bfloat16),
-            jax.ShapeDtypeStruct((8, 512), jnp.float32),
-        ],
-        scratch_shapes=[
-            pltpu.VMEM((cols, dp * block), jnp.bfloat16),
-            pltpu.VMEM((block, dp * block), jnp.float32),
-            pltpu.SemaphoreType.DMA((CHUNKS, dp)),
+            pltpu.VMEM((block, dp * block), jnp.bfloat16),
+            pltpu.VMEM((8, block), jnp.float32),
         ],
         compiler_params=pltpu.CompilerParams(vmem_limit_bytes=VMEM_BYTES),
         name="first",
-    )(own, gathered)
-
-
-def apply_next(step, inner, squares, held, gathered):
-    dp, cols, block = gathered.shape
+    )(*in_vmem(panel, own))
+
+
+def apply_next(step, panel, inner, squares, held):
+    dp, cols, block = panel.shape
     last = step == 3
     if last:
         out_shape = jax.ShapeDtypeStruct((block, cols), jnp.float32)
         value = []
     else:
         out_shape = [
-            jax.ShapeDtypeStruct((cols, block), jnp.float32),
-            jax.ShapeDtypeStruct((block, dp * block), jnp.bfloat16),
+            pltpu.VMEM((cols, block), jnp.float32),
+            pltpu.VMEM((block, dp * block), jnp.bfloat16),
         ]
         value = [pltpu.VMEM((block, cols), jnp.bfloat16)]
     return pl.pallas_call(
         functools.partial(next_kernel, step),
-        in_specs=[VMEM, VMEM, ANY, ANY] + [VMEM] * len(held) + [ANY],
+        in_specs=[VMEM] * (5 + len(held)),
         out_specs=VMEM if last else [VMEM, VMEM],
         out_shape=out_shape,
-        scratch_shapes=[
-            pltpu.VMEM((cols, dp * block), jnp.bfloat16),
-            pltpu.VMEM((block, dp * block), jnp.bfloat16),
-            pltpu.VMEM((block, dp * block), jnp.bfloat16),
-            pltpu.VMEM((dp * block, block), jnp.bfloat16),
-        ]
-        + value
-        + [pltpu.SemaphoreType.DMA((CHUNKS, dp)), pltpu.SemaphoreType.DMA((2,))],
+        scratch_shapes=[pltpu.VMEM((dp, block, block), jnp.bfloat16)] + value,
         compiler_params=pltpu.CompilerParams(vmem_limit_bytes=VMEM_BYTES),
         name="apply%d" % step,
-    )(*squares, *inner, *held, gathered)
+    )(*in_vmem(panel, *squares, *inner, *held))
 
 
 def swap_cores(value):
@@ -306,18 +256,18 @@
     ]
     start_row = lax.axis_index("dp") * block
     prior = lax.dynamic_slice_in_dim(rotation, start_row, block, 0).T
-    start = group_block(0) + 0.2 * rows_total * prior.astype(jnp.float32)
+    start = lax.optimization_barrier(group_block(0)) + 0.2 * rows_total * prior.astype(jnp.float32)
     for part in parts:
         start = start + part.astype(jnp.float32)
     narrow = start.astype(jnp.bfloat16)
-    gathered = lax.all_gather(narrow, "dp")
-
-    inner, square = apply_first(narrow.T, gathered)
+    panel = lax.all_gather(narrow, "dp")
+
+    inner, square = apply_first(panel, narrow.T)
     squares = both_cores(square)
-    first, inner = apply_next(0, both_cores(inner), squares, [start], gathered)
-    state, inner = apply_next(1, both_cores(inner), squares, [first], gathered)
-    state, inner = apply_next(2, both_cores(inner), squares, [state], gathered)
-    return apply_next(3, both_cores(inner), squares, [state, first], gathered)
+    first, inner = apply_next(0, panel, both_cores(inner), squares, [start])
+    state, inner = apply_next(1, panel, both_cores(inner), squares, [first])
+    state, inner = apply_next(2, panel, both_cores(inner), squares, [state])
+    return apply_next(3, panel, both_cores(inner), squares, [state, first])
 
 
 def solution(mesh):

time: 475 us -> 447 us (0.941)
  Pallas kernels: 112 us -> 85.6 us
  waiting for transfers between devices: 262 us -> 256 us
  other arithmetic: 7.43 us -> 13.3 us
    pallas_call x5, Pallas kernels: 81.3 us -> 58.4 us  [the longest x4 51.3 us: apply_next(): pl.pallas_call(functools.partial(next_kernel, step), in_specs=[VMEM] * (5...]
    ppermute x3, waiting for transfers between devices: 43.6 us -> 37.6 us  [from_inner(): return lax.ppermute(value, 'dp', pairs)]
  transfers between devices with their start and end apart: 21 -> 21, of which waited for: 12 -> 10; matrix products, arithmetic and copies ran while one was open for 5% -> 7% of each run, Pallas kernels for 6% -> 6%
where the time goes in v4:
time: 447 us; the launch traced here: 446 us
  waiting for transfers between devices  256 us (57%)
  Pallas kernels  85.6 us (19%)
  starting transfers between devices  32.7 us (7%)
  matrix products  28.6 us (6%)
  between operations  13.7 us (3%)
  other arithmetic  13.3 us (3%)
  local copies, waits for them, and re-layouts  13.1 us (3%)
    all_gather x1, waiting for transfers between devices, shards(): panel = lax.all_gather(narrow, 'dp')  190 us
    pallas_call x4, Pallas kernels, apply_next(): pl.pallas_call(functools.partial(next_kernel, step), in_specs=[VMEM] * (5...  51.3 us
    ppermute x3, waiting for transfers between devices, from_inner(): return lax.ppermute(value, 'dp', pairs)  37.6 us
    ppermute x9, starting transfers between devices, from_outer(): return lax.ppermute(value, 'dp', pairs)  28 us
    pallas_call x2, Pallas kernels, rebuild_rows(): pl.pallas_call(lookup_kernel, grid=(subs // tile, blocks), in_specs=[pl.B...  27.2 us
    dot_general x4, matrix products, group_block(): return jnp.dot(rebuilt, part, preferred_element_type=jnp.float32)  16 us
    ppermute x8, waiting for transfers between devices, swap_cores(): return lax.ppermute(value, 'col', [(0, 1), (1, 0)])  15.7 us
    ppermute x9, waiting for transfers between devices, from_outer(): return lax.ppermute(value, 'dp', pairs)  13.4 us
  transfers between devices with their start and end apart: 21, of which 10 were waited for; matrix products, arithmetic and copies ran while one was open for 7% of the time, Pallas kernels for 6%

profile of v4, /device:TPU:0, one launch (start us, length us, event | category | flops | bytes accessed | tf_op | source)
XLA Modules:
  0.0 446.1 jit_solution(15414487021681619846)
XLA Ops:
  8.5 4.0 collective-permute-start.1
  20.7 5.3 %lookup.3 = bf16[2048,512]{1,0:T(8,128)(2,1)S(1)} custom-call(bf16[1,256,512]{2,1,0:T(8,128)(2,1)S(1)} %get-tuple-element.32.codes_ref, f32[256,8,256]{2,1,0:T(8,128)S(1)} %convert_bitcast_fusion.table_ref), custom_call_target="tpu_custom_call" | custom-call | tf_op jit(solution)/shard_map/lookup/pallas_call | solution.py:56
  26.0 12.6 %multiply_reduce_fusion = f32[512]{0:T(512)S(1)} fusion(bf16[2048,512]{1,0:T(8,128)(2,1)S(1)} %lookup.3, bf16[4096,2048]{1,0:T(8,128)(2,1)} %param.5, bf16[512,4096]{1,0:T(8,128)(2,1)S(1)} %copy-done.3), kind=kOutput, calls=%fused_computation.1 | convolution fusion | flops 8594128896 | bytes 23070720 | tf_op jit(solution)/shard_map/dot_general | solution.py:232
  42.2 13.1 %collective-permute-done.10 = bf16[256,1024]{1,0:T(8,128)(2,1)} collective-permute-done((bf16[256,1024]{1,0:T(8,128)(2,1)}, bf16[256,1024]{1,0:T(8,128)(2,1)}, u32[]{:S(2)}, u32[]{:S(2)}) %collective-permute-start.10) | collective-permute-done | bytes 524320 | tf_op jit(solution)/shard_map/ppermute | solution.py:206
  59.3 14.9 %collective-permute-start.6 = (f32[512]{0:T(512)S(1)}, f32[512]{0:T(512)S(1)}, u32[]{:S(2)}, u32[]{:S(2)}) collective-permute-start(f32[512]{0:T(512)S(1)} %add_divide_fusion), channel_id=1, source_target_pairs={{0,16},{2,18},{4,20},{6,22},{8,24},{10,26},{12,28},{14,30},{16,0},... | collective-permute-start | bytes 6152 | tf_op jit(solution)/shard_map/ppermute | solution.py:206
  75.5 21.9 %lookup.2 = bf16[2048,2048]{1,0:T(8,128)(2,1)S(1)} custom-call(bf16[4,256,512]{2,1,0:T(8,128)(2,1)S(1)} %pad_maximum_fusion.1.codes_ref, f32[256,8,256]{2,1,0:T(8,128)S(1)} %convert_bitcast_fusion.table_ref), custom_call_target="tpu_custom_call" | custom-call | tf_op jit(solution)/shard_map/lookup/pallas_call | solution.py:56
  104.3 3.3 convolution_convert_fusion
  107.7 3.4 convolution_convert_fusion.1
  111.0 3.3 convolution_convert_fusion.2
  119.9 6.0 %fusion.6 = f32[2048,256]{1,0:T(8,128)S(1)} fusion(bf16[2048,2048]{1,0:T(8,128)(2,1)} %copy-done.1, bf16[2048,1024]{1,0:T(8,128)(2,1)} %copy-done.2, s32[]{:T(128)S(6)} %select_n.85), kind=kOutput, calls=%fused_computation.18 | convolution fusion | flops 2147483648 | bytes 11534340 | tf_op jit(solution)/shard_map/dot_general | solution.py:251
  125.9 15.6 %collective-permute-done.12 = bf16[2048,256]{1,0:T(8,128)(2,1)S(1)} collective-permute-done((bf16[2048,256]{1,0:T(8,128)(2,1)}, bf16[2048,256]{1,0:T(8,128)(2,1)S(1)}, u32[]{:S(2)}, u32[]{:S(2)}) %collective-permute-start.12) | collective-permute-done | bytes 1048608 | tf_op jit(solution)/shard_map/ppermute | solution.py:210
  141.5 21.7 %collective-permute-done.13 = bf16[2048,256]{1,0:T(8,128)(2,1)} collective-permute-done((bf16[2048,256]{1,0:T(8,128)(2,1)}, bf16[2048,256]{1,0:T(8,128)(2,1)}, u32[]{:S(2)}, u32[]{:S(2)}) %collective-permute-start.13) | collective-permute-done | bytes 1048608 | tf_op jit(solution)/shard_map/ppermute | solution.py:210
  163.5 3.5 fusion.12
  168.5 189.6 %all-gather.3.cloned.1.call-done = bf16[32768,256]{1,0:T(8,128)(2,1)} async-done(((bf16[2048,256]{1,0:T(8,128)(2,1)}), bf16[32768,256]{1,0:T(8,128)(2,1)}) %all-gather.3.cloned.1.call-update) | async-done | bytes 16777232 | tf_op jit(solution)/shard_map/all_gather | solution.py:263
  358.1 5.8 %copy-done = bf16[32768,256]{1,0:T(8,128)(2,1)S(1)} copy-done((bf16[32768,256]{1,0:T(8,128)(2,1)S(1)}, bf16[32768,256]{1,0:T(8,128)(2,1)}, u32[]{:S(2)}) %copy-start) | copy-done | bytes 16777240
  363.9 7.1 %first.1 = (bf16[256,4096]{1,0:T(8,128)(2,1)S(1)}, f32[8,256]{1,0:T(8,128)S(1)}) custom-call(bf16[16,2048,256]{2,1,0:T(8,128)(2,1)S(1)} %bitcast.27, bf16[256,2048]{1,0:T(8,128)(2,1)S(1)} %copy.7.own_ref), custom_call_target="tpu_custom_call" | custom-call | tf_op jit(solution)/shard_map/first/pallas_call | solution.py:145
  371.5 3.7 collective-permute-done.15.other_square_ref
  375.2 14.3 %apply0.1 = (f32[2048,256]{1,0:T(8,128)S(1)}, bf16[256,4096]{1,0:T(8,128)(2,1)S(1)}) custom-call(bf16[16,2048,256]{2,1,0:T(8,128)(2,1)S(1)} %bitcast.28, f32[8,256]{1,0:T(8,128)S(1)} %get-tuple-element.13.mine_square_ref, f32[8,256]{1,0:T(8,128)S(1)} %collective-permute-done.15.other_square_ref, bf16[256,4096]{1,0:T(8,128)(2,1)S(1)} %get-tuple-element.14.mine_ref, ...), custom_call_target="tpu_custom_call" | custom-call | tf_op jit(solution)/shard_map/apply0/pallas_call | solution.py:170
  389.7 4.0 collective-permute-done.17.other_ref
  393.7 14.3 %apply1.1 = (f32[2048,256]{1,0:T(8,128)S(1)}, bf16[256,4096]{1,0:T(8,128)(2,1)S(1)}) custom-call(bf16[16,2048,256]{2,1,0:T(8,128)(2,1)S(1)} %bitcast.29, f32[8,256]{1,0:T(8,128)S(1)} %get-tuple-element.13.mine_square_ref, f32[8,256]{1,0:T(8,128)S(1)} %collective-permute-done.15.other_square_ref, bf16[256,4096]{1,0:T(8,128)(2,1)S(1)} %get-tuple-element.15.mine_ref, ...), custom_call_target="tpu_custom_call" | custom-call | tf_op jit(solution)/shard_map/apply1/pallas_call | solution.py:170
  408.2 4.0 collective-permute-done.18.other_ref
  412.2 14.3 %apply2.1 = (f32[2048,256]{1,0:T(8,128)S(1)}, bf16[256,4096]{1,0:T(8,128)(2,1)S(1)}) custom-call(bf16[16,2048,256]{2,1,0:T(8,128)(2,1)S(1)} %bitcast.30, f32[8,256]{1,0:T(8,128)S(1)} %get-tuple-element.13.mine_square_ref, f32[8,256]{1,0:T(8,128)S(1)} %collective-permute-done.15.other_square_ref, bf16[256,4096]{1,0:T(8,128)(2,1)S(1)} %get-tuple-element.17.mine_ref, ...), custom_call_target="tpu_custom_call" | custom-call | tf_op jit(solution)/shard_map/apply2/pallas_call | solution.py:170
  426.7 4.0 collective-permute-done.19.other_ref
  430.7 8.5 %apply3.1 = f32[256,2048]{1,0:T(8,128)} custom-call(bf16[16,2048,256]{2,1,0:T(8,128)(2,1)S(1)} %bitcast.31, f32[8,256]{1,0:T(8,128)S(1)} %get-tuple-element.13.mine_square_ref, f32[8,256]{1,0:T(8,128)S(1)} %collective-permute-done.15.other_square_ref, bf16[256,4096]{1,0:T(8,128)(2,1)S(1)} %get-tuple-element.19.mine_ref, ...), custom_call_target="tpu_custom_call" | custom-call | tf_op jit(solution)/shard_map/apply3/pallas_call | solution.py:170
  (62 shorter events, 34.2 us)
Async XLA Ops:
  6.5 351.5 %all-gather.3.cloned.1.call-start = ((), (), s32[]{:S(2)}) async-start(), calls=%async_computation | async-start | bytes 17825792 | tf_op jit(solution)/shard_map/all_gather | solution.py:263
  8.5 12.0 %copy-start.4 = (bf16[256,256,8]{1,2,0:T(8,128)(2,1)S(1)}, bf16[256,256,8]{1,2,0:T(8,128)(2,1)}, u32[]{:S(2)}) copy-start(bf16[256,256,8]{1,2,0:T(8,128)(2,1)} %param.7) | copy-start | bytes 3145732
  8.5 32.7 %collective-permute-start.1 = (bf16[256,512]{1,0:T(8,128)(2,1)}, bf16[256,512]{1,0:T(8,128)(2,1)}, u32[]{:S(2)}, u32[]{:S(2)}) collective-permute-start(bf16[256,512]{1,0:T(8,128)(2,1)} %get-tuple-element.33), channel_id=1, source_target_pairs={{0,16},{2,18},{4,20},{6,22},{8,24},{10,26},{12,28},{14,30},{16,0},... | collective-permute-start | bytes 786440 | tf_op jit(solution)/shard_map/ppermute | solution.py:206
  12.5 44.2 %collective-permute-start = (bf16[256,512]{1,0:T(8,128)(2,1)}, bf16[256,512]{1,0:T(8,128)(2,1)}, u32[]{:S(2)}, u32[]{:S(2)}) collective-permute-start(bf16[256,512]{1,0:T(8,128)(2,1)} %get-tuple-element.33), channel_id=1, source_target_pairs={{0,8},{2,10},{4,12},{6,14},{8,0},{10,2},{12,4},{14,6},{16,24},{18,... | collective-permute-start | bytes 786440 | tf_op jit(solution)/shard_map/ppermute | solution.py:206
  14.1 45.2 %collective-permute-start.2 = (bf16[256,512]{1,0:T(8,128)(2,1)}, bf16[256,512]{1,0:T(8,128)(2,1)}, u32[]{:S(2)}, u32[]{:S(2)}) collective-permute-start(bf16[256,512]{1,0:T(8,128)(2,1)} %get-tuple-element.33), channel_id=1, source_target_pairs={{0,24},{2,26},{4,28},{6,30},{8,16},{10,18},{12,20},{14,22},{16,8},... | collective-permute-start | bytes 786440 | tf_op jit(solution)/shard_map/ppermute | solution.py:206
  16.6 25.5 %collective-permute-start.4 = (bf16[256,1024]{1,0:T(8,128)(2,1)}, bf16[256,1024]{1,0:T(8,128)(2,1)}, u32[]{:S(2)}, u32[]{:S(2)}) collective-permute-start(bf16[256,1024]{1,0:T(8,128)(2,1)} %get-tuple-element.23), channel_id=1, source_target_pairs={{0,8},{2,10},{4,12},{6,14},{8,0},{10,2},{12,4},{14,6},{16,24},{18,... | collective-permute-start | bytes 1572872 | tf_op jit(solution)/shard_map/ppermute | solution.py:206
  17.5 37.7 %collective-permute-start.10 = (bf16[256,1024]{1,0:T(8,128)(2,1)}, bf16[256,1024]{1,0:T(8,128)(2,1)}, u32[]{:S(2)}, u32[]{:S(2)}) collective-permute-start(bf16[256,1024]{1,0:T(8,128)(2,1)} %get-tuple-element.24), channel_id=1, source_target_pairs={{0,24},{2,26},{4,28},{6,30},{8,16},{10,18},{12,20},{14,22},{16,8},... | collective-permute-start | bytes 1572872 | tf_op jit(solution)/shard_map/ppermute | solution.py:206
  41.2 56.2 %collective-permute-start.7 = (bf16[256,1024]{1,0:T(8,128)(2,1)}, bf16[256,1024]{1,0:T(8,128)(2,1)}, u32[]{:S(2)}, u32[]{:S(2)}) collective-permute-start(bf16[256,1024]{1,0:T(8,128)(2,1)} %get-tuple-element.25), channel_id=1, source_target_pairs={{0,16},{2,18},{4,20},{6,22},{8,24},{10,26},{12,28},{14,30},{16,0},... | collective-permute-start | bytes 1572872 | tf_op jit(solution)/shard_map/ppermute | solution.py:206
  42.2 55.8 %collective-permute-start.5 = (bf16[256,1024]{1,0:T(8,128)(2,1)}, bf16[256,1024]{1,0:T(8,128)(2,1)}, u32[]{:S(2)}, u32[]{:S(2)}) collective-permute-start(bf16[256,1024]{1,0:T(8,128)(2,1)} %collective-permute-done.4), channel_id=1, source_target_pairs={{0,1},{1,0},{2,3},{3,2},{4,5},{5,4},{6,7},{7,6},{8,9},{9,8},{10,11... | collective-permute-start | bytes 1572872 | tf_op jit(solution)/shard_map/ppermute | solution.py:182
  55.2 44.8 %collective-permute-start.11 = (bf16[256,1024]{1,0:T(8,128)(2,1)}, bf16[256,1024]{1,0:T(8,128)(2,1)}, u32[]{:S(2)}, u32[]{:S(2)}) collective-permute-start(bf16[256,1024]{1,0:T(8,128)(2,1)} %collective-permute-done.10), channel_id=1, source_target_pairs={{0,1},{1,0},{2,3},{3,2},{4,5},{5,4},{6,7},{7,6},{8,9},{9,8},{10,11... | collective-permute-start | bytes 1572872 | tf_op jit(solution)/shard_map/ppermute | solution.py:182
  56.8 46.3 %collective-permute-start.9 = (f32[512]{0:T(512)S(1)}, f32[512]{0:T(512)S(1)}, u32[]{:S(2)}, u32[]{:S(2)}) collective-permute-start(f32[512]{0:T(512)S(1)} %add_divide_fusion), channel_id=1, source_target_pairs={{0,24},{2,26},{4,28},{6,30},{8,16},{10,18},{12,20},{14,22},{16,8},... | collective-permute-start | bytes 6152 | tf_op jit(solution)/shard_map/ppermute | solution.py:206
  59.3 43.9 %collective-permute-start.6 = (f32[512]{0:T(512)S(1)}, f32[512]{0:T(512)S(1)}, u32[]{:S(2)}, u32[]{:S(2)}) collective-permute-start(f32[512]{0:T(512)S(1)} %add_divide_fusion), channel_id=1, source_target_pairs={{0,16},{2,18},{4,20},{6,22},{8,24},{10,26},{12,28},{14,30},{16,0},... | collective-permute-start | bytes 6152 | tf_op jit(solution)/shard_map/ppermute | solution.py:206
  97.4 13.6 %copy-start.1 = (bf16[2048,2048]{1,0:T(8,128)(2,1)}, bf16[2048,2048]{1,0:T(8,128)(2,1)S(1)}, u32[]{:S(2)}) copy-start(bf16[2048,2048]{1,0:T(8,128)(2,1)S(1)} %lookup.2) | copy-start | bytes 25165828
  97.4 6.1 %collective-permute-start.3 = (f32[512]{0:T(512)S(1)}, f32[512]{0:T(512)S(1)}, u32[]{:S(2)}, u32[]{:S(2)}) collective-permute-start(f32[512]{0:T(512)S(1)} %add_divide_fusion), channel_id=1, source_target_pairs={{0,8},{2,10},{4,12},{6,14},{8,0},{10,2},{12,4},{14,6},{16,24},{18,... | collective-permute-start | bytes 6152 | tf_op jit(solution)/shard_map/ppermute | solution.py:206
  97.9 4.0 collective-permute-start.8
  114.4 27.2 %collective-permute-start.12 = (bf16[2048,256]{1,0:T(8,128)(2,1)}, bf16[2048,256]{1,0:T(8,128)(2,1)S(1)}, u32[]{:S(2)}, u32[]{:S(2)}) collective-permute-start(bf16[2048,256]{1,0:T(8,128)(2,1)} %convolution_convert_fusion.2), channel_id=1, source_target_pairs={{0,6},{2,4},{4,2},{6,0},{8,14},{10,12},{12,10},{14,8},{16,22},{18,... | collective-permute-start | bytes 3145736 | tf_op jit(solution)/shard_map/ppermute | solution.py:210
  117.0 46.3 %collective-permute-start.13 = (bf16[2048,256]{1,0:T(8,128)(2,1)}, bf16[2048,256]{1,0:T(8,128)(2,1)}, u32[]{:S(2)}, u32[]{:S(2)}) collective-permute-start(bf16[2048,256]{1,0:T(8,128)(2,1)} %convolution_convert_fusion.1), channel_id=1, source_target_pairs={{0,4},{2,6},{4,0},{6,2},{8,12},{10,14},{12,8},{14,10},{16,20},{18,... | collective-permute-start | bytes 3145736 | tf_op jit(solution)/shard_map/ppermute | solution.py:210
  117.5 46.0 %collective-permute-start.14 = (bf16[2048,256]{1,0:T(8,128)(2,1)}, bf16[2048,256]{1,0:T(8,128)(2,1)}, u32[]{:S(2)}, u32[]{:S(2)}) collective-permute-start(bf16[2048,256]{1,0:T(8,128)(2,1)} %convolution_convert_fusion), channel_id=1, source_target_pairs={{0,2},{2,0},{4,6},{6,4},{8,10},{10,8},{12,14},{14,12},{16,18},{18,... | collective-permute-start | bytes 3145736 | tf_op jit(solution)/shard_map/ppermute | solution.py:210
  141.5 21.7 %copy-start.5 = (bf16[2048,256]{1,0:T(8,128)(2,1)}, bf16[2048,256]{1,0:T(8,128)(2,1)S(1)}, u32[]{:S(2)}) copy-start(bf16[2048,256]{1,0:T(8,128)(2,1)S(1)} %collective-permute-done.12) | copy-start | bytes 3145732
  371.0 4.2 collective-permute-start.16
  371.0 4.2 collective-permute-start.15
  389.5 4.2 collective-permute-start.17
  408.0 4.2 collective-permute-start.18
  426.5 4.2 collective-permute-start.19
  (3 other events, 17.8 us)
Sparse Core Ops, SparseCore 0:
  167.1 190.9 all-gather.2

commit v5 on v4

--- a/solution.py
+++ b/solution.py
@@ -68,50 +68,49 @@
     )(codes, table)
 
 
-def first_kernel(panel_ref, own_ref, inner_ref, square_ref):
-    dp, cols, block = panel_ref.shape
-    square_ref[...] = jnp.zeros_like(square_ref)
-
-    def body(owner, carry):
-        values = panel_ref[owner]
-        inner_ref[:, pl.ds(pl.multiple_of(owner * block, block), block)] = jnp.dot(
+def first_kernel(own_ref, before_ref, *refs):
+    panel, (inner_ref, square_ref) = refs[:-2], refs[-2:]
+    cols, block = panel[0].shape
+    square = before_ref[...]
+    for index, block_ref in enumerate(panel):
+        values = block_ref[...]
+        inner_ref[:, index * block : (index + 1) * block] = jnp.dot(
             own_ref[...], values, preferred_element_type=jnp.float32
         ).astype(inner_ref.dtype)
         values = values.astype(jnp.float32)
-        square_ref[...] += jnp.sum((values * values).reshape(cols // 8, 8, block), axis=0)
-        return carry
-
-    lax.fori_loop(0, dp, body, 0)
-
-
-def next_kernel(step, panel_ref, mine_square_ref, other_square_ref, mine_ref, other_ref, *refs):
+        square += jnp.sum((values * values).reshape(cols // 8, 8, block), axis=0)
+    square_ref[...] = square
+
+
+def next_kernel(step, blocks, parts, mine_square_ref, other_square_ref, *refs):
     last = step == 3
     states = 2 if last else 1
+    panel, refs = refs[:blocks], refs[blocks:]
+    mine, other, refs = refs[:parts], refs[parts : 2 * parts], refs[2 * parts :]
     held, refs = refs[:states], refs[states:]
     if last:
         out_ref, sum_ref = refs
     else:
         state_ref, inner_ref, sum_ref, value_ref = refs
-    dp, cols, block = panel_ref.shape
-    model_width = dp * block
+    cols, block = panel[0].shape
+    model_width = blocks * block
     chunk = cols // CHUNKS
     total = jnp.sum(mine_square_ref[...] + other_square_ref[...], axis=(0, 1), keepdims=True)
     scale = model_width / (1.96 * total)
-
-    def turn(owner, carry):
-        span = pl.ds(pl.multiple_of(owner * block, block), block)
-        both = mine_ref[:, span].astype(jnp.float32) + other_ref[:, span].astype(jnp.float32)
-        sum_ref[owner] = (both * scale).T.astype(sum_ref.dtype)
-        return carry
-
-    lax.fori_loop(0, dp, turn, 0)
+    index = 0
+    for mine_ref, other_ref in zip(mine, other):
+        for first in range(0, mine_ref.shape[1], block):
+            both = mine_ref[:, first : first + block].astype(jnp.float32)
+            both += other_ref[:, first : first + block].astype(jnp.float32)
+            sum_ref[index] = (both * scale).T.astype(sum_ref.dtype)
+            index += 1
 
     def body(index, carry):
         span = pl.ds(pl.multiple_of(index * chunk, chunk), chunk)
         made = jnp.zeros((chunk, block), jnp.float32)
-        for owner in range(dp):
+        for owner in range(blocks):
             made += jnp.dot(
-                panel_ref[owner, span, :], sum_ref[owner], preferred_element_type=jnp.float32
+                panel[owner][span, :], sum_ref[owner], preferred_element_type=jnp.float32
             )
         if step != 2:
             made = 1.5 * held[0][span, :] - 0.5 * made
@@ -126,37 +125,34 @@
     lax.fori_loop(0, CHUNKS, body, 0)
     if last:
         return
-
-    def product(owner, carry):
-        inner_ref[:, pl.ds(pl.multiple_of(owner * block, block), block)] = jnp.dot(
-            value_ref[...], panel_ref[owner], preferred_element_type=jnp.float32
+    for index in range(blocks):
+        inner_ref[:, index * block : (index + 1) * block] = jnp.dot(
+            value_ref[...], panel[index][...], preferred_element_type=jnp.float32
         ).astype(inner_ref.dtype)
-        return carry
-
-    lax.fori_loop(0, dp, product, 0)
 
 
 def in_vmem(*values):
     return [pltpu.with_memory_space_constraint(value, pltpu.VMEM) for value in values]
 
 
-def apply_first(panel, own):
-    dp, cols, block = panel.shape
+def apply_first(own, square, panel):
+    block = panel[0].shape[1]
     return pl.pallas_call(
         first_kernel,
-        in_specs=[VMEM, VMEM],
+        in_specs=[VMEM] * (2 + len(panel)),
         out_specs=[VMEM, VMEM],
         out_shape=[
-            pltpu.VMEM((block, dp * block), jnp.bfloat16),
+            pltpu.VMEM((block, len(panel) * block), jnp.bfloat16),
             pltpu.VMEM((8, block), jnp.float32),
         ],
         compiler_params=pltpu.CompilerParams(vmem_limit_bytes=VMEM_BYTES),
         name="first",
-    )(*in_vmem(panel, own))
+    )(*in_vmem(own, square, *panel))
 
 
 def apply_next(step, panel, inner, squares, held):
-    dp, cols, block = panel.shape
+    cols, block = panel[0].shape
+    blocks = len(panel)
     last = step == 3
     if last:
         out_shape = jax.ShapeDtypeStruct((block, cols), jnp.float32)
@@ -164,18 +160,20 @@
     else:
         out_shape = [
             pltpu.VMEM((cols, block), jnp.float32),
-            pltpu.VMEM((block, dp * block), jnp.bfloat16),
+            pltpu.VMEM((block, blocks * block), jnp.bfloat16),
         ]
         value = [pltpu.VMEM((block, cols), jnp.bfloat16)]
+    mine, other = zip(*inner)
+    operands = in_vmem(*squares, *panel, *mine, *other, *held)
     return pl.pallas_call(
-        functools.partial(next_kernel, step),
-        in_specs=[VMEM] * (5 + len(held)),
+        functools.partial(next_kernel, step, blocks, len(inner)),
+        in_specs=[VMEM] * len(operands),
         out_specs=VMEM if last else [VMEM, VMEM],
         out_shape=out_shape,
-        scratch_shapes=[pltpu.VMEM((dp, block, block), jnp.bfloat16)] + value,
+        scratch_shapes=[pltpu.VMEM((blocks, block, block), jnp.bfloat16)] + value,
         compiler_params=pltpu.CompilerParams(vmem_limit_bytes=VMEM_BYTES),
         name="apply%d" % step,
-    )(*in_vmem(panel, *squares, *inner, *held))
+    )(*operands)
 
 
 def swap_cores(value):
@@ -187,6 +185,33 @@
         return value, swap_cores(value)
     total = lax.psum(value.astype(jnp.float32), "col").astype(value.dtype)
     return total, jnp.zeros_like(total)
+
+
+def gather_rounds(outer_size):
+    held = {(0, 0)}
+    last = outer_size - 1
+    rounds = []
+    for k in range(1, outer_size):
+        rounds.append([((k, 0), (k - 1, 0)), ((k - 1, 1), (k - 1, 0)), ((k - 1, 2), (k - 1, 0))])
+    held.update(key for moves in rounds for key, _ in moves)
+    rest = [(last, 1), (last, 2)] + [(k, 3) for k in range(outer_size)]
+    while rest:
+        moves, taken = [], set()
+        for key in rest:
+            ways = [("y", (key[0], key[1] ^ 2)), ("x", (key[0], key[1] ^ 1)), ("z", (key[0] - 1, key[1]))]
+            if key == (last, 1):
+                ways.reverse()
+            if key[1] == 3:
+                ways = ways[::-1] if (key[0] - 1, 3) in held else ways
+            for link, source in ways:
+                if source in held and link not in taken:
+                    taken.add(link)
+                    moves.append((key, source))
+                    break
+        held.update(key for key, _ in moves)
+        rest = [key for key in rest if key not in held]
+        rounds.append(moves)
+    return rounds
 
 
 def shards(embeddings, rotation, codes, codebooks):
@@ -210,14 +235,27 @@
         return lax.ppermute(value, "dp", pairs)
 
     steps = list(range(1, outer_size))
-    shares = []
-    for step in steps:
-        send = lax.dynamic_slice(
-            embeddings, (core * part_rows, (outer ^ step) * wide), (part_rows, wide)
-        )
-        shares.append(from_outer(send, step))
+    sends = [
+        lax.dynamic_slice(embeddings, (core * part_rows, (outer ^ step) * wide), (part_rows, wide))
+        for step in steps
+    ]
     codes_t = codes.T.astype(jnp.bfloat16)
-    group_codes = jnp.stack([codes_t] + [from_outer(codes_t, step) for step in steps])
+    group_codes = [codes_t] + [from_outer(codes_t, step) for step in steps]
+    sends[0], group_codes = lax.optimization_barrier((sends[0], group_codes))
+    shares = [from_outer(send, step) for send, step in zip(sends, steps)]
+    table = jnp.transpose(codebooks, (0, 2, 1)).astype(jnp.float32)
+    rebuilt = rebuild_rows(jnp.stack(group_codes), table)
+
+    own = rebuild_rows(codes_t[None], table)
+    rotated = lax.dot_general(
+        rotation, embeddings, (((0,), (1,)), ((), ())), preferred_element_type=jnp.float32
+    )
+    residue = rotated - own.astype(jnp.float32)
+    row_error = lax.psum(jnp.sum(residue * residue, axis=0), "col")
+    weights = 1.0 / (1.0 + row_error / (2.0 * model_width))
+    group_weights = [weights] + [from_outer(weights, step) for step in steps]
+
+    shares, rebuilt, group_weights = lax.optimization_barrier((shares, rebuilt, group_weights))
     columns = [lax.dynamic_slice_in_dim(embeddings, outer * wide, wide, 1)]
     for share in shares:
         if col == 2:
@@ -226,16 +264,6 @@
             columns.append(jnp.concatenate(pair, axis=0))
         else:
             columns.append(lax.all_gather(share, "col", axis=0, tiled=True))
-
-    table = jnp.transpose(codebooks, (0, 2, 1)).astype(jnp.float32)
-    own = rebuild_rows(codes_t[None], table)
-    rotated = lax.dot_general(
-        rotation, embeddings, (((0,), (1,)), ((), ())), preferred_element_type=jnp.float32
-    )
-    residue = rotated - own.astype(jnp.float32)
-    row_error = lax.psum(jnp.sum(residue * residue, axis=0), "col")
-    weights = 1.0 / (1.0 + row_error / (2.0 * model_width))
-    group_weights = [weights] + [from_outer(weights, step) for step in steps]
     scaled = jnp.concatenate(
         [
             (weight[:, None] * part.astype(jnp.float32)).astype(jnp.bfloat16)
@@ -244,7 +272,6 @@
         axis=0,
     )
 
-    rebuilt = rebuild_rows(group_codes, table)
 
     def group_block(step):
         part = lax.dynamic_slice_in_dim(scaled, (inner ^ step) * block, block, 1)
@@ -260,14 +287,37 @@
     for part in parts:
         start = start + part.astype(jnp.float32)
     narrow = start.astype(jnp.bfloat16)
-    panel = lax.all_gather(narrow, "dp")
-
-    inner, square = apply_first(panel, narrow.T)
+
+    def ring(value):
+        pairs = [(i, (i + inner_size) % dp) for i in range(dp)]
+        return lax.ppermute(value, "dp", pairs)
+
+    def move(key, source):
+        if key[0] != source[0]:
+            return ring(held[source])
+        return from_inner(held[source], key[1] ^ source[1])
+
+    own = narrow.T
+    held = {(0, 0): narrow}
+    order, products = [(0, 0)], []
+    square = jnp.zeros((8, block), jnp.float32)
+    fresh = [narrow]
+    for moves in gather_rounds(outer_size):
+        arrived = [move(key, source) for key, source in moves]
+        product, square = apply_first(own, square, fresh)
+        arrived, product, square = lax.optimization_barrier((arrived, product, square))
+        held.update({key: value for (key, _), value in zip(moves, arrived)})
+        order += [key for key, _ in moves]
+        products.append(both_cores(product))
+        fresh = arrived
+    product, square = apply_first(own, square, fresh)
+    products.append(both_cores(product))
+    panel = [held[key] for key in order]
     squares = both_cores(square)
-    first, inner = apply_next(0, panel, both_cores(inner), squares, [start])
-    state, inner = apply_next(1, panel, both_cores(inner), squares, [first])
-    state, inner = apply_next(2, panel, both_cores(inner), squares, [state])
-    return apply_next(3, panel, both_cores(inner), squares, [state, first])
+    first, product = apply_next(0, panel, products, squares, [start])
+    state, product = apply_next(1, panel, [both_cores(product)], squares, [first])
+    state, product = apply_next(2, panel, [both_cores(product)], squares, [state])
+    return apply_next(3, panel, [both_cores(product)], squares, [state, first])
 
 
 def solution(mesh):

time: 447 us -> 367 us (0.82)
  waiting for transfers between devices: 256 us -> 195 us
  between operations: 13.7 us -> 0.58 us
  Pallas kernels: 85.6 us -> 80.9 us
    all_gather x1 -> x0, waiting for transfers between devices: 190 us -> none  [shards(): panel = lax.all_gather(narrow, 'dp')]
    ppermute x3 -> x13, waiting for transfers between devices: 37.6 us -> 139 us  [from_inner(): return lax.ppermute(value, 'dp', pairs)]
    ppermute x9, waiting for transfers between devices: 13.4 us -> 35.7 us  [from_outer(): return lax.ppermute(value, 'dp', pairs)]
    ppermute x9, starting transfers between devices: 28 us -> 14.2 us  [from_outer(): return lax.ppermute(value, 'dp', pairs)]
    ppermute x3 -> x13, starting transfers between devices: 3.49 us -> 13.9 us  [from_inner(): return lax.ppermute(value, 'dp', pairs)]
    ppermute x0 -> x5, waiting for transfers between devices: none -> 6.79 us  [ring(): return lax.ppermute(value, 'dp', pairs)]
    pallas_call x5 -> x10, Pallas kernels: 58.4 us -> 53.7 us  [the longest x4 46.8 us: apply_next(): pl.pallas_call(functools.partial(next_kernel, step, blocks, len(inner)),...]
    ppermute x8 -> x13, waiting for transfers between devices: 15.7 us -> 13.2 us  [swap_cores(): return lax.ppermute(value, 'col', [(0, 1), (1, 0)])]
  transfers between devices with their start and end apart: 21 -> 40, of which waited for: 10 -> 22; matrix products, arithmetic and copies ran while one was open for 7% -> 8% of each run, Pallas kernels for 6% -> 9%
where the time goes in v5:
time: 367 us; the launch traced here: 362 us
  waiting for transfers between devices  195 us (53%)
  Pallas kernels  80.9 us (22%)
  starting transfers between devices  32.4 us (9%)
  matrix products  28.6 us (8%)
  local copies, waits for them, and re-layouts  11.2 us (3%)
  other arithmetic  10.9 us (3%)
    ppermute x13, waiting for transfers between devices, from_inner(): return lax.ppermute(value, 'dp', pairs)  139 us
    pallas_call x4, Pallas kernels, apply_next(): pl.pallas_call(functools.partial(next_kernel, step, blocks, len(inner)),...  46.8 us
    ppermute x9, waiting for transfers between devices, from_outer(): return lax.ppermute(value, 'dp', pairs)  35.7 us
    pallas_call x2, Pallas kernels, rebuild_rows(): pl.pallas_call(lookup_kernel, grid=(subs // tile, blocks), in_specs=[pl.B...  27.2 us
    dot_general x4, matrix products, group_block(): return jnp.dot(rebuilt, part, preferred_element_type=jnp.float32)  16 us
    ppermute x9, starting transfers between devices, from_outer(): return lax.ppermute(value, 'dp', pairs)  14.2 us
    ppermute x13, starting transfers between devices, from_inner(): return lax.ppermute(value, 'dp', pairs)  13.9 us
    ppermute x13, waiting for transfers between devices, swap_cores(): return lax.ppermute(value, 'col', [(0, 1), (1, 0)])  13.2 us
  transfers between devices with their start and end apart: 40, of which 22 were waited for; matrix products, arithmetic and copies ran while one was open for 8% of the time, Pallas kernels for 9%

profile of v5, /device:TPU:0, one launch (start us, length us, event | category | flops | bytes accessed | tf_op | source)
XLA Modules:
  0.0 361.8 jit_solution(4267485653026819440)
XLA Ops:
  2.0 5.0 %collective-permute-start.2 = (bf16[256,512]{1,0:T(8,128)(2,1)}, bf16[256,512]{1,0:T(8,128)(2,1)}, u32[]{:S(2)}, u32[]{:S(2)}) collective-permute-start(bf16[256,512]{1,0:T(8,128)(2,1)} %get-tuple-element.62), channel_id=1, source_target_pairs={{0,24},{2,26},{4,28},{6,30},{8,16},{10,18},{12,20},{14,22},{16,8},... | collective-permute-start | bytes 786440 | tf_op jit(solution)/shard_map/ppermute | solution.py:231
  10.2 3.8 %collective-permute-start.5 = (bf16[256,1024]{1,0:T(8,128)(2,1)}, bf16[256,1024]{1,0:T(8,128)(2,1)}, u32[]{:S(2)}, u32[]{:S(2)}) collective-permute-start(bf16[256,1024]{1,0:T(8,128)(2,1)} %get-tuple-element.119), channel_id=1, source_target_pairs={{0,24},{2,26},{4,28},{6,30},{8,16},{10,18},{12,20},{14,22},{16,8},... | collective-permute-start | bytes 1572872 | tf_op jit(solution)/shard_map/ppermute | solution.py:231
  14.2 5.3 %lookup.3 = bf16[2048,512]{1,0:T(8,128)(2,1)S(1)} custom-call(bf16[1,256,512]{2,1,0:T(8,128)(2,1)S(1)} %get-tuple-element.128.codes_ref, f32[256,8,256]{2,1,0:T(8,128)S(1)} %convert_bitcast_fusion.table_ref), custom_call_target="tpu_custom_call" | custom-call | tf_op jit(solution)/shard_map/lookup/pallas_call | solution.py:56
  19.5 33.6 %collective-permute-done.1 = bf16[256,512]{1,0:T(8,128)(2,1)} collective-permute-done((bf16[256,512]{1,0:T(8,128)(2,1)}, bf16[256,512]{1,0:T(8,128)(2,1)}, u32[]{:S(2)}, u32[]{:S(2)}) %collective-permute-start.1) | collective-permute-done | bytes 262176 | tf_op jit(solution)/shard_map/ppermute | solution.py:231
  53.1 12.6 %multiply_reduce_fusion = f32[512]{0:T(512)S(1)} fusion(bf16[2048,512]{1,0:T(8,128)(2,1)S(1)} %lookup.3, bf16[4096,2048]{1,0:T(8,128)(2,1)} %param.5, bf16[512,4096]{1,0:T(8,128)(2,1)S(1)} %copy-done.3), kind=kOutput, calls=%fused_computation.1 | convolution fusion | flops 8594128896 | bytes 23070720 | tf_op jit(solution)/shard_map/dot_general | solution.py:250
  76.5 21.9 %lookup.2 = bf16[2048,2048]{1,0:T(8,128)(2,1)S(1)} custom-call(bf16[4,256,512]{2,1,0:T(8,128)(2,1)S(1)} %pad_maximum_fusion.1.codes_ref, f32[256,8,256]{2,1,0:T(8,128)S(1)} %convert_bitcast_fusion.table_ref), custom_call_target="tpu_custom_call" | custom-call | tf_op jit(solution)/shard_map/lookup/pallas_call | solution.py:56
  125.1 6.0 %fusion.6 = f32[2048,256]{1,0:T(8,128)S(1)} fusion(bf16[2048,2048]{1,0:T(8,128)(2,1)} %copy-done, bf16[2048,1024]{1,0:T(8,128)(2,1)} %copy-done.2, s32[]{:T(128)S(6)} %select_n.85), kind=kOutput, calls=%fused_computation.18 | convolution fusion | flops 2147483648 | bytes 11534340 | tf_op jit(solution)/shard_map/dot_general | solution.py:278
  131.1 15.6 %collective-permute-done.12 = bf16[2048,256]{1,0:T(8,128)(2,1)S(1)} collective-permute-done((bf16[2048,256]{1,0:T(8,128)(2,1)}, bf16[2048,256]{1,0:T(8,128)(2,1)S(1)}, u32[]{:S(2)}, u32[]{:S(2)}) %collective-permute-start.12) | collective-permute-done | bytes 1048608 | tf_op jit(solution)/shard_map/ppermute | solution.py:235
  146.7 21.7 %collective-permute-done.13 = bf16[2048,256]{1,0:T(8,128)(2,1)} collective-permute-done((bf16[2048,256]{1,0:T(8,128)(2,1)}, bf16[2048,256]{1,0:T(8,128)(2,1)}, u32[]{:S(2)}, u32[]{:S(2)}) %collective-permute-start.13) | collective-permute-done | bytes 1048608 | tf_op jit(solution)/shard_map/ppermute | solution.py:235
  168.5 3.5 fusion.12
  176.1 21.0 %collective-permute-done.17.refs_2_.refs_3_ = bf16[2048,256]{1,0:T(8,128)(2,1)S(1)} collective-permute-done((bf16[2048,256]{1,0:T(8,128)(2,1)S(1)}, bf16[2048,256]{1,0:T(8,128)(2,1)S(1)}, u32[]{:S(2)}, u32[]{:S(2)}) %collective-permute-start.17) | collective-permute-done | bytes 1048608 | tf_op jit(solution)/shard_map/ppermute | solution.py:235
  205.0 18.9 %collective-permute-done.20.refs_2_.refs_6_ = bf16[2048,256]{1,0:T(8,128)(2,1)S(1)} collective-permute-done((bf16[2048,256]{1,0:T(8,128)(2,1)}, bf16[2048,256]{1,0:T(8,128)(2,1)S(1)}, u32[]{:S(2)}, u32[]{:S(2)}) %collective-permute-start.20) | collective-permute-done | bytes 1048608 | tf_op jit(solution)/shard_map/ppermute | solution.py:235
  232.0 17.4 %collective-permute-done.23.refs_2_.refs_9_ = bf16[2048,256]{1,0:T(8,128)(2,1)S(1)} collective-permute-done((bf16[2048,256]{1,0:T(8,128)(2,1)S(1)}, bf16[2048,256]{1,0:T(8,128)(2,1)S(1)}, u32[]{:S(2)}, u32[]{:S(2)}) %collective-permute-start.23) | collective-permute-done | bytes 1048608 | tf_op jit(solution)/shard_map/ppermute | solution.py:235
  249.4 5.6 %collective-permute-done.22.refs_1_.refs_8_ = bf16[2048,256]{1,0:T(8,128)(2,1)S(1)} collective-permute-done((bf16[2048,256]{1,0:T(8,128)(2,1)S(1)}, bf16[2048,256]{1,0:T(8,128)(2,1)S(1)}, u32[]{:S(2)}, u32[]{:S(2)}) %collective-permute-start.22) | collective-permute-done | bytes 1048608 | tf_op jit(solution)/shard_map/ppermute | solution.py:235
  258.1 16.6 %collective-permute-done.26.refs_2_.refs_12_ = bf16[2048,256]{1,0:T(8,128)(2,1)S(1)} collective-permute-done((bf16[2048,256]{1,0:T(8,128)(2,1)S(1)}, bf16[2048,256]{1,0:T(8,128)(2,1)S(1)}, u32[]{:S(2)}, u32[]{:S(2)}) %collective-permute-start.26) | collective-permute-done | bytes 1048608 | tf_op jit(solution)/shard_map/ppermute | solution.py:235
  274.7 6.5 %collective-permute-done.25.refs_1_.refs_11_ = bf16[2048,256]{1,0:T(8,128)(2,1)S(1)} collective-permute-done((bf16[2048,256]{1,0:T(8,128)(2,1)S(1)}, bf16[2048,256]{1,0:T(8,128)(2,1)S(1)}, u32[]{:S(2)}, u32[]{:S(2)}) %collective-permute-start.25) | collective-permute-done | bytes 1048608 | tf_op jit(solution)/shard_map/ppermute | solution.py:235
  283.0 12.8 %collective-permute-done.28.refs_1_.refs_14_ = bf16[2048,256]{1,0:T(8,128)(2,1)S(1)} collective-permute-done((bf16[2048,256]{1,0:T(8,128)(2,1)S(1)}, bf16[2048,256]{1,0:T(8,128)(2,1)S(1)}, u32[]{:S(2)}, u32[]{:S(2)}) %collective-permute-start.28) | collective-permute-done | bytes 1048608 | tf_op jit(solution)/shard_map/ppermute | solution.py:235
  302.1 12.8 %apply0.1 = (f32[2048,256]{1,0:T(8,128)S(1)}, bf16[256,4096]{1,0:T(8,128)(2,1)S(1)}) custom-call(f32[8,256]{1,0:T(8,128)S(1)} %get-tuple-element.104.mine_square_ref, f32[8,256]{1,0:T(8,128)S(1)} %collective-permute-done.30.other_square_ref, bf16[2048,256]{1,0:T(8,128)(2,1)S(1)} %get-tuple-element.117.refs_0_, ...), custom_call_target="tpu_custom_call" | custom-call | tf_op jit(solution)/shard_map/apply0/pallas_call | solution.py:168
  315.3 3.8 %collective-permute-done.37.refs_17_ = bf16[256,4096]{1,0:T(8,128)(2,1)S(1)} collective-permute-done((bf16[256,4096]{1,0:T(8,128)(2,1)S(1)}, bf16[256,4096]{1,0:T(8,128)(2,1)S(1)}, u32[]{:S(2)}, u32[]{:S(2)}) %collective-permute-start.37) | collective-permute-done | bytes 2097184 | tf_op jit(solution)/shard_map/ppermute | solution.py:180
  319.1 12.3 %apply1.1 = (f32[2048,256]{1,0:T(8,128)S(1)}, bf16[256,4096]{1,0:T(8,128)(2,1)S(1)}) custom-call(f32[8,256]{1,0:T(8,128)S(1)} %get-tuple-element.104.mine_square_ref, f32[8,256]{1,0:T(8,128)S(1)} %collective-permute-done.30.other_square_ref, bf16[2048,256]{1,0:T(8,128)(2,1)S(1)} %get-tuple-element.117.refs_0_, ...), custom_call_target="tpu_custom_call" | custom-call | tf_op jit(solution)/shard_map/apply1/pallas_call | solution.py:168
  331.9 3.8 %collective-permute-done.38.refs_17_ = bf16[256,4096]{1,0:T(8,128)(2,1)S(1)} collective-permute-done((bf16[256,4096]{1,0:T(8,128)(2,1)S(1)}, bf16[256,4096]{1,0:T(8,128)(2,1)S(1)}, u32[]{:S(2)}, u32[]{:S(2)}) %collective-permute-start.38) | collective-permute-done | bytes 2097184 | tf_op jit(solution)/shard_map/ppermute | solution.py:180
  335.7 12.5 %apply2.1 = (f32[2048,256]{1,0:T(8,128)S(1)}, bf16[256,4096]{1,0:T(8,128)(2,1)S(1)}) custom-call(f32[8,256]{1,0:T(8,128)S(1)} %get-tuple-element.104.mine_square_ref, f32[8,256]{1,0:T(8,128)S(1)} %collective-permute-done.30.other_square_ref, bf16[2048,256]{1,0:T(8,128)(2,1)S(1)} %get-tuple-element.117.refs_0_, ...), custom_call_target="tpu_custom_call" | custom-call | tf_op jit(solution)/shard_map/apply2/pallas_call | solution.py:168
  348.6 3.8 %collective-permute-done.39.refs_17_ = bf16[256,4096]{1,0:T(8,128)(2,1)S(1)} collective-permute-done((bf16[256,4096]{1,0:T(8,128)(2,1)S(1)}, bf16[256,4096]{1,0:T(8,128)(2,1)S(1)}, u32[]{:S(2)}, u32[]{:S(2)}) %collective-permute-start.39) | collective-permute-done | bytes 2097184 | tf_op jit(solution)/shard_map/ppermute | solution.py:180
  352.4 9.2 %apply3.1 = f32[256,2048]{1,0:T(8,128)} custom-call(f32[8,256]{1,0:T(8,128)S(1)} %get-tuple-element.104.mine_square_ref, f32[8,256]{1,0:T(8,128)S(1)} %collective-permute-done.30.other_square_ref, bf16[2048,256]{1,0:T(8,128)(2,1)S(1)} %get-tuple-element.117.refs_0_, bf16[2048,256]{1,0:T(8,128)(2,1)} %collective-permute-done.15.refs_0_.refs_1_, ...), custom_call_target="tpu_custom_call" | custom-call | tf_op jit(solution)/shard_map/apply3/pallas_call | solution.py:168
  (108 shorter events, 75.2 us)
Async XLA Ops:
  7.0 46.1 %collective-permute-start.1 = (bf16[256,512]{1,0:T(8,128)(2,1)}, bf16[256,512]{1,0:T(8,128)(2,1)}, u32[]{:S(2)}, u32[]{:S(2)}) collective-permute-start(bf16[256,512]{1,0:T(8,128)(2,1)} %get-tuple-element.62), channel_id=1, source_target_pairs={{0,16},{2,18},{4,20},{6,22},{8,24},{10,26},{12,28},{14,30},{16,0},... | collective-permute-start | bytes 786440 | tf_op jit(solution)/shard_map/ppermute | solution.py:231
  7.0 46.1 %collective-permute-start = (bf16[256,512]{1,0:T(8,128)(2,1)}, bf16[256,512]{1,0:T(8,128)(2,1)}, u32[]{:S(2)}, u32[]{:S(2)}) collective-permute-start(bf16[256,512]{1,0:T(8,128)(2,1)} %get-tuple-element.62), channel_id=1, source_target_pairs={{0,8},{2,10},{4,12},{6,14},{8,0},{10,2},{12,4},{14,6},{16,24},{18,... | collective-permute-start | bytes 786440 | tf_op jit(solution)/shard_map/ppermute | solution.py:231
  10.2 91.6 %collective-permute-start.5 = (bf16[256,1024]{1,0:T(8,128)(2,1)}, bf16[256,1024]{1,0:T(8,128)(2,1)}, u32[]{:S(2)}, u32[]{:S(2)}) collective-permute-start(bf16[256,1024]{1,0:T(8,128)(2,1)} %get-tuple-element.119), channel_id=1, source_target_pairs={{0,24},{2,26},{4,28},{6,30},{8,16},{10,18},{12,20},{14,22},{16,8},... | collective-permute-start | bytes 1572872 | tf_op jit(solution)/shard_map/ppermute | solution.py:231
  14.0 87.8 %collective-permute-start.4 = (bf16[256,1024]{1,0:T(8,128)(2,1)}, bf16[256,1024]{1,0:T(8,128)(2,1)}, u32[]{:S(2)}, u32[]{:S(2)}) collective-permute-start(bf16[256,1024]{1,0:T(8,128)(2,1)} %get-tuple-element.120), channel_id=1, source_target_pairs={{0,16},{2,18},{4,20},{6,22},{8,24},{10,26},{12,28},{14,30},{16,0},... | collective-permute-start | bytes 1572872 | tf_op jit(solution)/shard_map/ppermute | solution.py:231
  53.1 48.7 %collective-permute-start.3 = (bf16[256,1024]{1,0:T(8,128)(2,1)}, bf16[256,1024]{1,0:T(8,128)(2,1)S(1)}, u32[]{:S(2)}, u32[]{:S(2)}) collective-permute-start(bf16[256,1024]{1,0:T(8,128)(2,1)} %get-tuple-element.61), channel_id=1, source_target_pairs={{0,8},{2,10},{4,12},{6,14},{8,0},{10,2},{12,4},{14,6},{16,24},{18,... | collective-permute-start | bytes 1572872 | tf_op jit(solution)/shard_map/ppermute | solution.py:231
  71.0 30.7 %collective-permute-start.7 = (f32[512]{0:T(512)S(1)}, f32[512]{0:T(512)S(1)}, u32[]{:S(2)}, u32[]{:S(2)}) collective-permute-start(f32[512]{0:T(512)S(1)} %add_divide_fusion), channel_id=1, source_target_pairs={{0,16},{2,18},{4,20},{6,22},{8,24},{10,26},{12,28},{14,30},{16,0},... | collective-permute-start | bytes 6152 | tf_op jit(solution)/shard_map/ppermute | solution.py:231
  73.9 27.8 %collective-permute-start.6 = (f32[512]{0:T(512)S(1)}, f32[512]{0:T(512)S(1)}, u32[]{:S(2)}, u32[]{:S(2)}) collective-permute-start(f32[512]{0:T(512)S(1)} %add_divide_fusion), channel_id=1, source_target_pairs={{0,8},{2,10},{4,12},{6,14},{8,0},{10,2},{12,4},{14,6},{16,24},{18,... | collective-permute-start | bytes 6152 | tf_op jit(solution)/shard_map/ppermute | solution.py:231
  119.6 27.2 %collective-permute-start.12 = (bf16[2048,256]{1,0:T(8,128)(2,1)}, bf16[2048,256]{1,0:T(8,128)(2,1)S(1)}, u32[]{:S(2)}, u32[]{:S(2)}) collective-permute-start(bf16[2048,256]{1,0:T(8,128)(2,1)} %convolution_convert_fusion.2), channel_id=1, source_target_pairs={{0,6},{2,4},{4,2},{6,0},{8,14},{10,12},{12,10},{14,8},{16,22},{18,... | collective-permute-start | bytes 3145736 | tf_op jit(solution)/shard_map/ppermute | solution.py:235
  122.0 46.4 %collective-permute-start.13 = (bf16[2048,256]{1,0:T(8,128)(2,1)}, bf16[2048,256]{1,0:T(8,128)(2,1)}, u32[]{:S(2)}, u32[]{:S(2)}) collective-permute-start(bf16[2048,256]{1,0:T(8,128)(2,1)} %convolution_convert_fusion.1), channel_id=1, source_target_pairs={{0,4},{2,6},{4,0},{6,2},{8,12},{10,14},{12,8},{14,10},{16,20},{18,... | collective-permute-start | bytes 3145736 | tf_op jit(solution)/shard_map/ppermute | solution.py:235
  122.5 46.0 %collective-permute-start.14 = (bf16[2048,256]{1,0:T(8,128)(2,1)}, bf16[2048,256]{1,0:T(8,128)(2,1)}, u32[]{:S(2)}, u32[]{:S(2)}) collective-permute-start(bf16[2048,256]{1,0:T(8,128)(2,1)} %convolution_convert_fusion), channel_id=1, source_target_pairs={{0,2},{2,0},{4,6},{6,4},{8,10},{10,8},{12,14},{14,12},{16,18},{18,... | collective-permute-start | bytes 3145736 | tf_op jit(solution)/shard_map/ppermute | solution.py:235
  172.0 25.0 %collective-permute-start.17 = (bf16[2048,256]{1,0:T(8,128)(2,1)S(1)}, bf16[2048,256]{1,0:T(8,128)(2,1)S(1)}, u32[]{:S(2)}, u32[]{:S(2)}) collective-permute-start(bf16[2048,256]{1,0:T(8,128)(2,1)S(1)} %get-tuple-element.117.refs_0_), channel_id=1, source_target_pairs={{0,4},{2,6},{4,0},{6,2},{8,12},{10,14},{12,8},{14,10},{16,20},{18,... | collective-permute-start | bytes 3145736 | tf_op jit(solution)/shard_map/ppermute | solution.py:235
  173.5 24.9 %collective-permute-start.16 = (bf16[2048,256]{1,0:T(8,128)(2,1)S(1)}, bf16[2048,256]{1,0:T(8,128)(2,1)}, u32[]{:S(2)}, u32[]{:S(2)}) collective-permute-start(bf16[2048,256]{1,0:T(8,128)(2,1)S(1)} %get-tuple-element.117.refs_0_), channel_id=1, source_target_pairs={{0,2},{2,0},{4,6},{6,4},{8,10},{10,8},{12,14},{14,12},{16,18},{18,... | collective-permute-start | bytes 3145736 | tf_op jit(solution)/shard_map/ppermute | solution.py:235
  174.3 25.9 %collective-permute-start.15 = (bf16[2048,256]{1,0:T(8,128)(2,1)S(1)}, bf16[2048,256]{1,0:T(8,128)(2,1)}, u32[]{:S(2)}, u32[]{:S(2)}) collective-permute-start(bf16[2048,256]{1,0:T(8,128)(2,1)S(1)} %get-tuple-element.117.refs_0_), channel_id=1, source_target_pairs={{0,8},{2,10},{4,12},{6,14},{8,16},{10,18},{12,20},{14,22},{16,24},... | collective-permute-start | bytes 3145736 | tf_op jit(solution)/shard_map/ppermute | solution.py:293
  200.2 23.7 %collective-permute-start.20 = (bf16[2048,256]{1,0:T(8,128)(2,1)}, bf16[2048,256]{1,0:T(8,128)(2,1)S(1)}, u32[]{:S(2)}, u32[]{:S(2)}) collective-permute-start(bf16[2048,256]{1,0:T(8,128)(2,1)} %collective-permute-done.15.refs_0_.refs_1_), channel_id=1, source_target_pairs={{0,4},{2,6},{4,0},{6,2},{8,12},{10,14},{12,8},{14,10},{16,20},{18,... | collective-permute-start | bytes 3145736 | tf_op jit(solution)/shard_map/ppermute | solution.py:235
  201.9 23.4 %collective-permute-start.19 = (bf16[2048,256]{1,0:T(8,128)(2,1)}, bf16[2048,256]{1,0:T(8,128)(2,1)S(1)}, u32[]{:S(2)}, u32[]{:S(2)}) collective-permute-start(bf16[2048,256]{1,0:T(8,128)(2,1)} %collective-permute-done.15.refs_0_.refs_1_), channel_id=1, source_target_pairs={{0,2},{2,0},{4,6},{6,4},{8,10},{10,8},{12,14},{14,12},{16,18},{18,... | collective-permute-start | bytes 3145736 | tf_op jit(solution)/shard_map/ppermute | solution.py:235
  202.4 25.0 %collective-permute-start.18 = (bf16[2048,256]{1,0:T(8,128)(2,1)}, bf16[2048,256]{1,0:T(8,128)(2,1)S(1)}, u32[]{:S(2)}, u32[]{:S(2)}) collective-permute-start(bf16[2048,256]{1,0:T(8,128)(2,1)} %collective-permute-done.15.refs_0_.refs_1_), channel_id=1, source_target_pairs={{0,8},{2,10},{4,12},{6,14},{8,16},{10,18},{12,20},{14,22},{16,24},... | collective-permute-start | bytes 3145736 | tf_op jit(solution)/shard_map/ppermute | solution.py:293
  227.4 22.0 %collective-permute-start.23 = (bf16[2048,256]{1,0:T(8,128)(2,1)S(1)}, bf16[2048,256]{1,0:T(8,128)(2,1)S(1)}, u32[]{:S(2)}, u32[]{:S(2)}) collective-permute-start(bf16[2048,256]{1,0:T(8,128)(2,1)S(1)} %collective-permute-done.18.refs_0_.refs_4_), channel_id=1, source_target_pairs={{0,4},{2,6},{4,0},{6,2},{8,12},{10,14},{12,8},{14,10},{16,20},{18,... | collective-permute-start | bytes 3145736 | tf_op jit(solution)/shard_map/ppermute | solution.py:235
  229.0 26.1 %collective-permute-start.22 = (bf16[2048,256]{1,0:T(8,128)(2,1)S(1)}, bf16[2048,256]{1,0:T(8,128)(2,1)S(1)}, u32[]{:S(2)}, u32[]{:S(2)}) collective-permute-start(bf16[2048,256]{1,0:T(8,128)(2,1)S(1)} %collective-permute-done.18.refs_0_.refs_4_), channel_id=1, source_target_pairs={{0,2},{2,0},{4,6},{6,4},{8,10},{10,8},{12,14},{14,12},{16,18},{18,... | collective-permute-start | bytes 3145736 | tf_op jit(solution)/shard_map/ppermute | solution.py:235
  229.3 25.8 %collective-permute-start.21 = (bf16[2048,256]{1,0:T(8,128)(2,1)S(1)}, bf16[2048,256]{1,0:T(8,128)(2,1)S(1)}, u32[]{:S(2)}, u32[]{:S(2)}) collective-permute-start(bf16[2048,256]{1,0:T(8,128)(2,1)S(1)} %collective-permute-done.18.refs_0_.refs_4_), channel_id=1, source_target_pairs={{0,8},{2,10},{4,12},{6,14},{8,16},{10,18},{12,20},{14,22},{16,24},... | collective-permute-start | bytes 3145736 | tf_op jit(solution)/shard_map/ppermute | solution.py:293
  229.3 45.4 %collective-permute-start.26 = (bf16[2048,256]{1,0:T(8,128)(2,1)S(1)}, bf16[2048,256]{1,0:T(8,128)(2,1)S(1)}, u32[]{:S(2)}, u32[]{:S(2)}) collective-permute-start(bf16[2048,256]{1,0:T(8,128)(2,1)S(1)} %collective-permute-done.17.refs_2_.refs_3_), channel_id=1, source_target_pairs={{0,2},{2,0},{4,6},{6,4},{8,10},{10,8},{12,14},{14,12},{16,18},{18,... | collective-permute-start | bytes 3145736 | tf_op jit(solution)/shard_map/ppermute | solution.py:235
  255.1 26.1 %collective-permute-start.25 = (bf16[2048,256]{1,0:T(8,128)(2,1)S(1)}, bf16[2048,256]{1,0:T(8,128)(2,1)S(1)}, u32[]{:S(2)}, u32[]{:S(2)}) collective-permute-start(bf16[2048,256]{1,0:T(8,128)(2,1)S(1)} %collective-permute-done.21.refs_0_.refs_7_), channel_id=1, source_target_pairs={{0,4},{2,6},{4,0},{6,2},{8,12},{10,14},{12,8},{14,10},{16,20},{18,... | collective-permute-start | bytes 3145736 | tf_op jit(solution)/shard_map/ppermute | solution.py:235
  255.5 25.7 %collective-permute-start.24 = (bf16[2048,256]{1,0:T(8,128)(2,1)S(1)}, bf16[2048,256]{1,0:T(8,128)(2,1)S(1)}, u32[]{:S(2)}, u32[]{:S(2)}) collective-permute-start(bf16[2048,256]{1,0:T(8,128)(2,1)S(1)} %collective-permute-done.22.refs_1_.refs_8_), channel_id=1, source_target_pairs={{0,8},{2,10},{4,12},{6,14},{8,16},{10,18},{12,20},{14,22},{16,24},... | collective-permute-start | bytes 3145736 | tf_op jit(solution)/shard_map/ppermute | solution.py:293
  255.5 40.2 %collective-permute-start.28 = (bf16[2048,256]{1,0:T(8,128)(2,1)S(1)}, bf16[2048,256]{1,0:T(8,128)(2,1)S(1)}, u32[]{:S(2)}, u32[]{:S(2)}) collective-permute-start(bf16[2048,256]{1,0:T(8,128)(2,1)S(1)} %collective-permute-done.22.refs_1_.refs_8_), channel_id=1, source_target_pairs={{0,4},{2,6},{4,0},{6,2},{8,12},{10,14},{12,8},{14,10},{16,20},{18,... | collective-permute-start | bytes 3145736 | tf_op jit(solution)/shard_map/ppermute | solution.py:235
  281.5 18.8 %collective-permute-start.32 = (bf16[256,768]{1,0:T(8,128)(2,1)S(1)}, bf16[256,768]{1,0:T(8,128)(2,1)S(1)}, u32[]{:S(2)}, u32[]{:S(2)}) collective-permute-start(bf16[256,768]{1,0:T(8,128)(2,1)S(1)} %get-tuple-element.106.refs_17_), channel_id=1, source_target_pairs={{0,1},{1,0},{2,3},{3,2},{4,5},{5,4},{6,7},{7,6},{8,9},{9,8},{10,11... | collective-permute-start | bytes 1179656 | tf_op jit(solution)/shard_map/ppermute | solution.py:180
  (23 other events, 182.3 us)

commit v6 on v5

--- a/solution.py
+++ b/solution.py
@@ -68,16 +68,19 @@
     )(codes, table)
 
 
+def product_of(value_ref, block_ref, inner_ref, index):
+    block = block_ref.shape[1]
+    product = jnp.dot(value_ref[...], block_ref[...], preferred_element_type=jnp.float32)
+    inner_ref[index * block : (index + 1) * block, :] = product.T.astype(inner_ref.dtype)
+
+
 def first_kernel(own_ref, before_ref, *refs):
     panel, (inner_ref, square_ref) = refs[:-2], refs[-2:]
     cols, block = panel[0].shape
     square = before_ref[...]
     for index, block_ref in enumerate(panel):
-        values = block_ref[...]
-        inner_ref[:, index * block : (index + 1) * block] = jnp.dot(
-            own_ref[...], values, preferred_element_type=jnp.float32
-        ).astype(inner_ref.dtype)
-        values = values.astype(jnp.float32)
+        product_of(own_ref, block_ref, inner_ref, index)
+        values = block_ref[...].astype(jnp.float32)
         square += jnp.sum((values * values).reshape(cols // 8, 8, block), axis=0)
     square_ref[...] = square
 
@@ -97,38 +100,34 @@
     chunk = cols // CHUNKS
     total = jnp.sum(mine_square_ref[...] + other_square_ref[...], axis=(0, 1), keepdims=True)
     scale = model_width / (1.96 * total)
-    index = 0
+    first = 0
     for mine_ref, other_ref in zip(mine, other):
-        for first in range(0, mine_ref.shape[1], block):
-            both = mine_ref[:, first : first + block].astype(jnp.float32)
-            both += other_ref[:, first : first + block].astype(jnp.float32)
-            sum_ref[index] = (both * scale).T.astype(sum_ref.dtype)
-            index += 1
-
-    def body(index, carry):
-        span = pl.ds(pl.multiple_of(index * chunk, chunk), chunk)
+        sum_ref[first : first + mine_ref.shape[0], :] = mine_ref[...] + other_ref[...]
+        first += mine_ref.shape[0]
+
+    for index in range(CHUNKS):
+        span = slice(index * chunk, (index + 1) * chunk)
         made = jnp.zeros((chunk, block), jnp.float32)
         for owner in range(blocks):
             made += jnp.dot(
-                panel[owner][span, :], sum_ref[owner], preferred_element_type=jnp.float32
+                panel[owner][span, :],
+                sum_ref[owner * block : (owner + 1) * block, :],
+                preferred_element_type=jnp.float32,
             )
-        if step != 2:
-            made = 1.5 * held[0][span, :] - 0.5 * made
+        if step == 2:
+            made = made * scale
+        else:
+            made = 1.5 * held[0][span, :] - (0.5 * scale) * made
         if last:
             made = (1.5 * held[1][span, :] - 0.5 * made) * (math.sqrt(model_width) * jnp.sqrt(scale))
             out_ref[:, span] = made.T
         else:
             state_ref[span, :] = made
             value_ref[:, span] = made.T.astype(value_ref.dtype)
-        return carry
-
-    lax.fori_loop(0, CHUNKS, body, 0)
     if last:
         return
     for index in range(blocks):
-        inner_ref[:, index * block : (index + 1) * block] = jnp.dot(
-            value_ref[...], panel[index][...], preferred_element_type=jnp.float32
-        ).astype(inner_ref.dtype)
+        product_of(value_ref, panel[index], inner_ref, index)
 
 
 def in_vmem(*values):
@@ -142,7 +141,7 @@
         in_specs=[VMEM] * (2 + len(panel)),
         out_specs=[VMEM, VMEM],
         out_shape=[
-            pltpu.VMEM((block, len(panel) * block), jnp.bfloat16),
+            pltpu.VMEM((len(panel) * block, block), jnp.bfloat16),
             pltpu.VMEM((8, block), jnp.float32),
         ],
         compiler_params=pltpu.CompilerParams(vmem_limit_bytes=VMEM_BYTES),
@@ -160,7 +159,7 @@
     else:
         out_shape = [
             pltpu.VMEM((cols, block), jnp.float32),
-            pltpu.VMEM((block, blocks * block), jnp.bfloat16),
+            pltpu.VMEM((blocks * block, block), jnp.bfloat16),
         ]
         value = [pltpu.VMEM((block, cols), jnp.bfloat16)]
     mine, other = zip(*inner)
@@ -170,7 +169,7 @@
         in_specs=[VMEM] * len(operands),
         out_specs=VMEM if last else [VMEM, VMEM],
         out_shape=out_shape,
-        scratch_shapes=[pltpu.VMEM((blocks, block, block), jnp.bfloat16)] + value,
+        scratch_shapes=[pltpu.VMEM((blocks * block, block), jnp.bfloat16)] + value,
         compiler_params=pltpu.CompilerParams(vmem_limit_bytes=VMEM_BYTES),
         name="apply%d" % step,
     )(*operands)
@@ -241,19 +240,20 @@
     ]
     codes_t = codes.T.astype(jnp.bfloat16)
     group_codes = [codes_t] + [from_outer(codes_t, step) for step in steps]
-    sends[0], group_codes = lax.optimization_barrier((sends[0], group_codes))
-    shares = [from_outer(send, step) for send, step in zip(sends, steps)]
+
     table = jnp.transpose(codebooks, (0, 2, 1)).astype(jnp.float32)
-    rebuilt = rebuild_rows(jnp.stack(group_codes), table)
-
     own = rebuild_rows(codes_t[None], table)
+    sends[1:], own = lax.optimization_barrier((sends[1:], own))
     rotated = lax.dot_general(
         rotation, embeddings, (((0,), (1,)), ((), ())), preferred_element_type=jnp.float32
     )
     residue = rotated - own.astype(jnp.float32)
     row_error = lax.psum(jnp.sum(residue * residue, axis=0), "col")
     weights = 1.0 / (1.0 + row_error / (2.0 * model_width))
+    sends[0], weights, group_codes = lax.optimization_barrier((sends[0], weights, group_codes))
+    shares = [from_outer(send, step) for send, step in zip(sends, steps)]
     group_weights = [weights] + [from_outer(weights, step) for step in steps]
+    rebuilt = rebuild_rows(jnp.stack(group_codes), table)
 
     shares, rebuilt, group_weights = lax.optimization_barrier((shares, rebuilt, group_weights))
     columns = [lax.dynamic_slice_in_dim(embeddings, outer * wide, wide, 1)]

time: 367 us -> 359 us (0.978)
  starting transfers between devices: 32.4 us -> 40.1 us
  waiting for transfers between devices: 195 us -> 188 us
  Pallas kernels: 80.9 us -> 74 us
    ppermute x9, starting transfers between devices: 14.2 us -> 22.1 us  [from_outer(): return lax.ppermute(value, 'dp', pairs)]
    pallas_call x4, Pallas kernels: 46.8 us -> 39.3 us  [apply_next(): pl.pallas_call(functools.partial(next_kernel, step, blocks, len(inner)),...]
    ppermute x9, waiting for transfers between devices: 35.7 us -> 29.2 us  [from_outer(): return lax.ppermute(value, 'dp', pairs)]
  transfers between devices with their start and end apart: 40 -> 40, of which waited for: 22 -> 21; matrix products, arithmetic and copies ran while one was open for 8% -> 8% of each run, Pallas kernels for 9% -> 10%
where the time goes in v6:
time: 359 us; the launch traced here: 354 us
  waiting for transfers between devices  188 us (52%)
  Pallas kernels  74 us (21%)
  starting transfers between devices  40.1 us (11%)
  matrix products  28.6 us (8%)
  local copies, waits for them, and re-layouts  10.8 us (3%)
  other arithmetic  9.69 us (3%)
    ppermute x13, waiting for transfers between devices, from_inner(): return lax.ppermute(value, 'dp', pairs)  139 us
    pallas_call x4, Pallas kernels, apply_next(): pl.pallas_call(functools.partial(next_kernel, step, blocks, len(inner)),...  39.3 us
    ppermute x9, waiting for transfers between devices, from_outer(): return lax.ppermute(value, 'dp', pairs)  29.2 us
    pallas_call x2, Pallas kernels, rebuild_rows(): pl.pallas_call(lookup_kernel, grid=(subs // tile, blocks), in_specs=[pl.B...  27.2 us
    ppermute x9, starting transfers between devices, from_outer(): return lax.ppermute(value, 'dp', pairs)  22.1 us
    dot_general x4, matrix products, group_block(): return jnp.dot(rebuilt, part, preferred_element_type=jnp.float32)  16 us
    ppermute x13, starting transfers between devices, from_inner(): return lax.ppermute(value, 'dp', pairs)  14 us
    ppermute x13, waiting for transfers between devices, swap_cores(): return lax.ppermute(value, 'col', [(0, 1), (1, 0)])  12.8 us
  transfers between devices with their start and end apart: 40, of which 21 were waited for; matrix products, arithmetic and copies ran while one was open for 8% of the time, Pallas kernels for 10%

profile of v6, /device:TPU:0, one launch (start us, length us, event | category | flops | bytes accessed | tf_op | source)
XLA Modules:
  0.0 354.2 jit_solution(6877628235840651380)
XLA Ops:
  2.1 5.0 %collective-permute-start.2 = (bf16[256,512]{1,0:T(8,128)(2,1)}, bf16[256,512]{1,0:T(8,128)(2,1)}, u32[]{:S(2)}, u32[]{:S(2)}) collective-permute-start(bf16[256,512]{1,0:T(8,128)(2,1)} %get-tuple-element.69), channel_id=1, source_target_pairs={{0,24},{2,26},{4,28},{6,30},{8,16},{10,18},{12,20},{14,22},{16,8},... | collective-permute-start | bytes 786440 | tf_op jit(solution)/shard_map/ppermute | solution.py:230
  7.9 5.3 %lookup.2 = bf16[2048,512]{1,0:T(8,128)(2,1)S(1)} custom-call(bf16[1,256,512]{2,1,0:T(8,128)(2,1)S(1)} %get-tuple-element.137.codes_ref, f32[256,8,256]{2,1,0:T(8,128)S(1)} %convert_bitcast_fusion.table_ref), custom_call_target="tpu_custom_call" | custom-call | tf_op jit(solution)/shard_map/lookup/pallas_call | solution.py:56
  18.2 12.6 %multiply_reduce_fusion = f32[512]{0:T(512)S(1)} fusion(bf16[2048,512]{1,0:T(8,128)(2,1)S(1)} %lookup.2, bf16[4096,2048]{1,0:T(8,128)(2,1)} %param.5, bf16[512,4096]{1,0:T(8,128)(2,1)S(1)} %copy-done.3), kind=kOutput, calls=%fused_computation.1 | convolution fusion | flops 8594128896 | bytes 23070720 | tf_op jit(solution)/shard_map/dot_general | solution.py:247
  33.5 19.7 %collective-permute-done.1 = bf16[256,512]{1,0:T(8,128)(2,1)} collective-permute-done((bf16[256,512]{1,0:T(8,128)(2,1)}, bf16[256,512]{1,0:T(8,128)(2,1)}, u32[]{:S(2)}, u32[]{:S(2)}) %collective-permute-start.1) | collective-permute-done | bytes 262176 | tf_op jit(solution)/shard_map/ppermute | solution.py:230
  56.7 9.5 %collective-permute-done.8 = f32[512]{0:T(512)S(1)} collective-permute-done((f32[512]{0:T(512)S(1)}, f32[512]{0:T(512)S(1)}, u32[]{:S(2)}, u32[]{:S(2)}) %collective-permute-start.8) | collective-permute-done | bytes 2080 | tf_op jit(solution)/shard_map/ppermute | solution.py:230
  66.1 9.2 %collective-permute-start.6 = (f32[512]{0:T(512)S(1)}, f32[512]{0:T(512)S(1)}, u32[]{:S(2)}, u32[]{:S(2)}) collective-permute-start(f32[512]{0:T(512)S(1)} %add_divide_fusion), channel_id=1, source_target_pairs={{0,8},{2,10},{4,12},{6,14},{8,0},{10,2},{12,4},{14,6},{16,24},{18,... | collective-permute-start | bytes 6152 | tf_op jit(solution)/shard_map/ppermute | solution.py:230
  76.7 21.9 %lookup.3 = bf16[2048,2048]{1,0:T(8,128)(2,1)S(1)} custom-call(bf16[4,256,512]{2,1,0:T(8,128)(2,1)S(1)} %pad_maximum_fusion.1.codes_ref, f32[256,8,256]{2,1,0:T(8,128)S(1)} %convert_bitcast_fusion.table_ref), custom_call_target="tpu_custom_call" | custom-call | tf_op jit(solution)/shard_map/lookup/pallas_call | solution.py:56
  124.6 6.0 %fusion.6 = f32[2048,256]{1,0:T(8,128)S(1)} fusion(bf16[2048,2048]{1,0:T(8,128)(2,1)} %copy-done, bf16[2048,1024]{1,0:T(8,128)(2,1)} %copy-done.2, s32[]{:T(128)S(6)} %select_n.85), kind=kOutput, calls=%fused_computation.18 | convolution fusion | flops 2147483648 | bytes 11534340 | tf_op jit(solution)/shard_map/dot_general | solution.py:278
  130.6 15.6 %collective-permute-done.12 = bf16[2048,256]{1,0:T(8,128)(2,1)S(1)} collective-permute-done((bf16[2048,256]{1,0:T(8,128)(2,1)}, bf16[2048,256]{1,0:T(8,128)(2,1)S(1)}, u32[]{:S(2)}, u32[]{:S(2)}) %collective-permute-start.12) | collective-permute-done | bytes 1048608 | tf_op jit(solution)/shard_map/ppermute | solution.py:234
  146.2 22.0 %collective-permute-done.13 = bf16[2048,256]{1,0:T(8,128)(2,1)} collective-permute-done((bf16[2048,256]{1,0:T(8,128)(2,1)}, bf16[2048,256]{1,0:T(8,128)(2,1)}, u32[]{:S(2)}, u32[]{:S(2)}) %collective-permute-start.13) | collective-permute-done | bytes 1048608 | tf_op jit(solution)/shard_map/ppermute | solution.py:234
  175.2 21.6 %collective-permute-done.17.refs_2_.refs_3_ = bf16[2048,256]{1,0:T(8,128)(2,1)S(1)} collective-permute-done((bf16[2048,256]{1,0:T(8,128)(2,1)S(1)}, bf16[2048,256]{1,0:T(8,128)(2,1)S(1)}, u32[]{:S(2)}, u32[]{:S(2)}) %collective-permute-start.17) | collective-permute-done | bytes 1048608 | tf_op jit(solution)/shard_map/ppermute | solution.py:234
  204.8 18.8 %collective-permute-done.20.refs_2_.refs_6_ = bf16[2048,256]{1,0:T(8,128)(2,1)S(1)} collective-permute-done((bf16[2048,256]{1,0:T(8,128)(2,1)}, bf16[2048,256]{1,0:T(8,128)(2,1)S(1)}, u32[]{:S(2)}, u32[]{:S(2)}) %collective-permute-start.20) | collective-permute-done | bytes 1048608 | tf_op jit(solution)/shard_map/ppermute | solution.py:234
  231.8 17.4 %collective-permute-done.23.refs_2_.refs_9_ = bf16[2048,256]{1,0:T(8,128)(2,1)S(1)} collective-permute-done((bf16[2048,256]{1,0:T(8,128)(2,1)S(1)}, bf16[2048,256]{1,0:T(8,128)(2,1)S(1)}, u32[]{:S(2)}, u32[]{:S(2)}) %collective-permute-start.23) | collective-permute-done | bytes 1048608 | tf_op jit(solution)/shard_map/ppermute | solution.py:234
  249.2 5.6 %collective-permute-done.22.refs_1_.refs_8_ = bf16[2048,256]{1,0:T(8,128)(2,1)S(1)} collective-permute-done((bf16[2048,256]{1,0:T(8,128)(2,1)S(1)}, bf16[2048,256]{1,0:T(8,128)(2,1)S(1)}, u32[]{:S(2)}, u32[]{:S(2)}) %collective-permute-start.22) | collective-permute-done | bytes 1048608 | tf_op jit(solution)/shard_map/ppermute | solution.py:234
  257.9 16.1 %collective-permute-done.26.refs_2_.refs_12_ = bf16[2048,256]{1,0:T(8,128)(2,1)S(1)} collective-permute-done((bf16[2048,256]{1,0:T(8,128)(2,1)S(1)}, bf16[2048,256]{1,0:T(8,128)(2,1)S(1)}, u32[]{:S(2)}, u32[]{:S(2)}) %collective-permute-start.26) | collective-permute-done | bytes 1048608 | tf_op jit(solution)/shard_map/ppermute | solution.py:234
  274.1 6.9 %collective-permute-done.25.refs_1_.refs_11_ = bf16[2048,256]{1,0:T(8,128)(2,1)S(1)} collective-permute-done((bf16[2048,256]{1,0:T(8,128)(2,1)S(1)}, bf16[2048,256]{1,0:T(8,128)(2,1)S(1)}, u32[]{:S(2)}, u32[]{:S(2)}) %collective-permute-start.25) | collective-permute-done | bytes 1048608 | tf_op jit(solution)/shard_map/ppermute | solution.py:234
  283.3 12.2 %collective-permute-done.28.refs_1_.refs_14_ = bf16[2048,256]{1,0:T(8,128)(2,1)S(1)} collective-permute-done((bf16[2048,256]{1,0:T(8,128)(2,1)S(1)}, bf16[2048,256]{1,0:T(8,128)(2,1)S(1)}, u32[]{:S(2)}, u32[]{:S(2)}) %collective-permute-start.28) | collective-permute-done | bytes 1048608 | tf_op jit(solution)/shard_map/ppermute | solution.py:234
  302.0 10.6 %apply0.1 = (f32[2048,256]{1,0:T(8,128)S(1)}, bf16[4096,256]{1,0:T(8,128)(2,1)S(1)}) custom-call(f32[8,256]{1,0:T(8,128)S(1)} %get-tuple-element.112.mine_square_ref, f32[8,256]{1,0:T(8,128)S(1)} %collective-permute-done.30.other_square_ref, bf16[2048,256]{1,0:T(8,128)(2,1)S(1)} %get-tuple-element.125.refs_0_, ...), custom_call_target="tpu_custom_call" | custom-call | tf_op jit(solution)/shard_map/apply0/pallas_call | solution.py:167
  313.0 3.8 %collective-permute-done.37.refs_17_ = bf16[4096,256]{1,0:T(8,128)(2,1)S(1)} collective-permute-done((bf16[4096,256]{1,0:T(8,128)(2,1)S(1)}, bf16[4096,256]{1,0:T(8,128)(2,1)S(1)}, u32[]{:S(2)}, u32[]{:S(2)}) %collective-permute-start.37) | collective-permute-done | bytes 2097184 | tf_op jit(solution)/shard_map/ppermute | solution.py:179
  316.8 10.7 %apply1.1 = (f32[2048,256]{1,0:T(8,128)S(1)}, bf16[4096,256]{1,0:T(8,128)(2,1)S(1)}) custom-call(f32[8,256]{1,0:T(8,128)S(1)} %get-tuple-element.112.mine_square_ref, f32[8,256]{1,0:T(8,128)S(1)} %collective-permute-done.30.other_square_ref, bf16[2048,256]{1,0:T(8,128)(2,1)S(1)} %get-tuple-element.125.refs_0_, ...), custom_call_target="tpu_custom_call" | custom-call | tf_op jit(solution)/shard_map/apply1/pallas_call | solution.py:167
  327.9 3.8 %collective-permute-done.38.refs_17_ = bf16[4096,256]{1,0:T(8,128)(2,1)S(1)} collective-permute-done((bf16[4096,256]{1,0:T(8,128)(2,1)S(1)}, bf16[4096,256]{1,0:T(8,128)(2,1)S(1)}, u32[]{:S(2)}, u32[]{:S(2)}) %collective-permute-start.38) | collective-permute-done | bytes 2097184 | tf_op jit(solution)/shard_map/ppermute | solution.py:179
  331.7 10.5 %apply2.1 = (f32[2048,256]{1,0:T(8,128)S(1)}, bf16[4096,256]{1,0:T(8,128)(2,1)S(1)}) custom-call(f32[8,256]{1,0:T(8,128)S(1)} %get-tuple-element.112.mine_square_ref, f32[8,256]{1,0:T(8,128)S(1)} %collective-permute-done.30.other_square_ref, bf16[2048,256]{1,0:T(8,128)(2,1)S(1)} %get-tuple-element.125.refs_0_, ...), custom_call_target="tpu_custom_call" | custom-call | tf_op jit(solution)/shard_map/apply2/pallas_call | solution.py:167
  342.6 3.8 %collective-permute-done.39.refs_17_ = bf16[4096,256]{1,0:T(8,128)(2,1)S(1)} collective-permute-done((bf16[4096,256]{1,0:T(8,128)(2,1)S(1)}, bf16[4096,256]{1,0:T(8,128)(2,1)S(1)}, u32[]{:S(2)}, u32[]{:S(2)}) %collective-permute-start.39) | collective-permute-done | bytes 2097184 | tf_op jit(solution)/shard_map/ppermute | solution.py:179
  346.4 7.6 %apply3.1 = f32[256,2048]{1,0:T(8,128)} custom-call(f32[8,256]{1,0:T(8,128)S(1)} %get-tuple-element.112.mine_square_ref, f32[8,256]{1,0:T(8,128)S(1)} %collective-permute-done.30.other_square_ref, bf16[2048,256]{1,0:T(8,128)(2,1)S(1)} %get-tuple-element.125.refs_0_, bf16[2048,256]{1,0:T(8,128)(2,1)} %collective-permute-done.15.refs_0_.refs_1_, ...), custom_call_target="tpu_custom_call" | custom-call | tf_op jit(solution)/shard_map/apply3/pallas_call | solution.py:167
  (108 shorter events, 77.6 us)
Async XLA Ops:
  2.1 31.4 %collective-permute-start.2 = (bf16[256,512]{1,0:T(8,128)(2,1)}, bf16[256,512]{1,0:T(8,128)(2,1)}, u32[]{:S(2)}, u32[]{:S(2)}) collective-permute-start(bf16[256,512]{1,0:T(8,128)(2,1)} %get-tuple-element.69), channel_id=1, source_target_pairs={{0,24},{2,26},{4,28},{6,30},{8,16},{10,18},{12,20},{14,22},{16,8},... | collective-permute-start | bytes 786440 | tf_op jit(solution)/shard_map/ppermute | solution.py:230
  7.1 46.1 %collective-permute-start.1 = (bf16[256,512]{1,0:T(8,128)(2,1)}, bf16[256,512]{1,0:T(8,128)(2,1)}, u32[]{:S(2)}, u32[]{:S(2)}) collective-permute-start(bf16[256,512]{1,0:T(8,128)(2,1)} %get-tuple-element.69), channel_id=1, source_target_pairs={{0,16},{2,18},{4,20},{6,22},{8,24},{10,26},{12,28},{14,30},{16,0},... | collective-permute-start | bytes 786440 | tf_op jit(solution)/shard_map/ppermute | solution.py:230
  7.1 46.1 %collective-permute-start = (bf16[256,512]{1,0:T(8,128)(2,1)}, bf16[256,512]{1,0:T(8,128)(2,1)}, u32[]{:S(2)}, u32[]{:S(2)}) collective-permute-start(bf16[256,512]{1,0:T(8,128)(2,1)} %get-tuple-element.69), channel_id=1, source_target_pairs={{0,8},{2,10},{4,12},{6,14},{8,0},{10,2},{12,4},{14,6},{16,24},{18,... | collective-permute-start | bytes 786440 | tf_op jit(solution)/shard_map/ppermute | solution.py:230
  14.4 87.5 %collective-permute-start.4 = (bf16[256,1024]{1,0:T(8,128)(2,1)}, bf16[256,1024]{1,0:T(8,128)(2,1)S(1)}, u32[]{:S(2)}, u32[]{:S(2)}) collective-permute-start(bf16[256,1024]{1,0:T(8,128)(2,1)} %get-tuple-element.67), channel_id=1, source_target_pairs={{0,16},{2,18},{4,20},{6,22},{8,24},{10,26},{12,28},{14,30},{16,0},... | collective-permute-start | bytes 1572872 | tf_op jit(solution)/shard_map/ppermute | solution.py:230
  16.8 85.1 %collective-permute-start.5 = (bf16[256,1024]{1,0:T(8,128)(2,1)}, bf16[256,1024]{1,0:T(8,128)(2,1)S(1)}, u32[]{:S(2)}, u32[]{:S(2)}) collective-permute-start(bf16[256,1024]{1,0:T(8,128)(2,1)} %get-tuple-element.68), channel_id=1, source_target_pairs={{0,24},{2,26},{4,28},{6,30},{8,16},{10,18},{12,20},{14,22},{16,8},... | collective-permute-start | bytes 1572872 | tf_op jit(solution)/shard_map/ppermute | solution.py:230
  53.2 48.7 %collective-permute-start.3 = (bf16[256,1024]{1,0:T(8,128)(2,1)}, bf16[256,1024]{1,0:T(8,128)(2,1)}, u32[]{:S(2)}, u32[]{:S(2)}) collective-permute-start(bf16[256,1024]{1,0:T(8,128)(2,1)} %get-tuple-element.66), channel_id=1, source_target_pairs={{0,8},{2,10},{4,12},{6,14},{8,0},{10,2},{12,4},{14,6},{16,24},{18,... | collective-permute-start | bytes 1572872 | tf_op jit(solution)/shard_map/ppermute | solution.py:230
  55.8 46.0 %collective-permute-start.7 = (f32[512]{0:T(512)S(1)}, f32[512]{0:T(512)S(1)}, u32[]{:S(2)}, u32[]{:S(2)}) collective-permute-start(f32[512]{0:T(512)S(1)} %add_divide_fusion), channel_id=1, source_target_pairs={{0,16},{2,18},{4,20},{6,22},{8,24},{10,26},{12,28},{14,30},{16,0},... | collective-permute-start | bytes 6152 | tf_op jit(solution)/shard_map/ppermute | solution.py:230
  66.1 35.7 %collective-permute-start.6 = (f32[512]{0:T(512)S(1)}, f32[512]{0:T(512)S(1)}, u32[]{:S(2)}, u32[]{:S(2)}) collective-permute-start(f32[512]{0:T(512)S(1)} %add_divide_fusion), channel_id=1, source_target_pairs={{0,8},{2,10},{4,12},{6,14},{8,0},{10,2},{12,4},{14,6},{16,24},{18,... | collective-permute-start | bytes 6152 | tf_op jit(solution)/shard_map/ppermute | solution.py:230
  119.0 27.1 %collective-permute-start.12 = (bf16[2048,256]{1,0:T(8,128)(2,1)}, bf16[2048,256]{1,0:T(8,128)(2,1)S(1)}, u32[]{:S(2)}, u32[]{:S(2)}) collective-permute-start(bf16[2048,256]{1,0:T(8,128)(2,1)} %convolution_convert_fusion.2), channel_id=1, source_target_pairs={{0,6},{2,4},{4,2},{6,0},{8,14},{10,12},{12,10},{14,8},{16,22},{18,... | collective-permute-start | bytes 3145736 | tf_op jit(solution)/shard_map/ppermute | solution.py:234
  121.5 46.7 %collective-permute-start.13 = (bf16[2048,256]{1,0:T(8,128)(2,1)}, bf16[2048,256]{1,0:T(8,128)(2,1)}, u32[]{:S(2)}, u32[]{:S(2)}) collective-permute-start(bf16[2048,256]{1,0:T(8,128)(2,1)} %convolution_convert_fusion.1), channel_id=1, source_target_pairs={{0,4},{2,6},{4,0},{6,2},{8,12},{10,14},{12,8},{14,10},{16,20},{18,... | collective-permute-start | bytes 3145736 | tf_op jit(solution)/shard_map/ppermute | solution.py:234
  122.0 46.3 %collective-permute-start.14 = (bf16[2048,256]{1,0:T(8,128)(2,1)}, bf16[2048,256]{1,0:T(8,128)(2,1)}, u32[]{:S(2)}, u32[]{:S(2)}) collective-permute-start(bf16[2048,256]{1,0:T(8,128)(2,1)} %convolution_convert_fusion), channel_id=1, source_target_pairs={{0,2},{2,0},{4,6},{6,4},{8,10},{10,8},{12,14},{14,12},{16,18},{18,... | collective-permute-start | bytes 3145736 | tf_op jit(solution)/shard_map/ppermute | solution.py:234
  171.8 25.0 %collective-permute-start.17 = (bf16[2048,256]{1,0:T(8,128)(2,1)S(1)}, bf16[2048,256]{1,0:T(8,128)(2,1)S(1)}, u32[]{:S(2)}, u32[]{:S(2)}) collective-permute-start(bf16[2048,256]{1,0:T(8,128)(2,1)S(1)} %get-tuple-element.125.refs_0_), channel_id=1, source_target_pairs={{0,4},{2,6},{4,0},{6,2},{8,12},{10,14},{12,8},{14,10},{16,20},{18,... | collective-permute-start | bytes 3145736 | tf_op jit(solution)/shard_map/ppermute | solution.py:234
  173.2 24.9 %collective-permute-start.16 = (bf16[2048,256]{1,0:T(8,128)(2,1)S(1)}, bf16[2048,256]{1,0:T(8,128)(2,1)}, u32[]{:S(2)}, u32[]{:S(2)}) collective-permute-start(bf16[2048,256]{1,0:T(8,128)(2,1)S(1)} %get-tuple-element.125.refs_0_), channel_id=1, source_target_pairs={{0,2},{2,0},{4,6},{6,4},{8,10},{10,8},{12,14},{14,12},{16,18},{18,... | collective-permute-start | bytes 3145736 | tf_op jit(solution)/shard_map/ppermute | solution.py:234
  174.0 25.9 %collective-permute-start.15 = (bf16[2048,256]{1,0:T(8,128)(2,1)S(1)}, bf16[2048,256]{1,0:T(8,128)(2,1)}, u32[]{:S(2)}, u32[]{:S(2)}) collective-permute-start(bf16[2048,256]{1,0:T(8,128)(2,1)S(1)} %get-tuple-element.125.refs_0_), channel_id=1, source_target_pairs={{0,8},{2,10},{4,12},{6,14},{8,16},{10,18},{12,20},{14,22},{16,24},... | collective-permute-start | bytes 3145736 | tf_op jit(solution)/shard_map/ppermute | solution.py:293
  199.9 23.7 %collective-permute-start.20 = (bf16[2048,256]{1,0:T(8,128)(2,1)}, bf16[2048,256]{1,0:T(8,128)(2,1)S(1)}, u32[]{:S(2)}, u32[]{:S(2)}) collective-permute-start(bf16[2048,256]{1,0:T(8,128)(2,1)} %collective-permute-done.15.refs_0_.refs_1_), channel_id=1, source_target_pairs={{0,4},{2,6},{4,0},{6,2},{8,12},{10,14},{12,8},{14,10},{16,20},{18,... | collective-permute-start | bytes 3145736 | tf_op jit(solution)/shard_map/ppermute | solution.py:234
  201.6 23.4 %collective-permute-start.19 = (bf16[2048,256]{1,0:T(8,128)(2,1)}, bf16[2048,256]{1,0:T(8,128)(2,1)S(1)}, u32[]{:S(2)}, u32[]{:S(2)}) collective-permute-start(bf16[2048,256]{1,0:T(8,128)(2,1)} %collective-permute-done.15.refs_0_.refs_1_), channel_id=1, source_target_pairs={{0,2},{2,0},{4,6},{6,4},{8,10},{10,8},{12,14},{14,12},{16,18},{18,... | collective-permute-start | bytes 3145736 | tf_op jit(solution)/shard_map/ppermute | solution.py:234
  202.2 25.0 %collective-permute-start.18 = (bf16[2048,256]{1,0:T(8,128)(2,1)}, bf16[2048,256]{1,0:T(8,128)(2,1)S(1)}, u32[]{:S(2)}, u32[]{:S(2)}) collective-permute-start(bf16[2048,256]{1,0:T(8,128)(2,1)} %collective-permute-done.15.refs_0_.refs_1_), channel_id=1, source_target_pairs={{0,8},{2,10},{4,12},{6,14},{8,16},{10,18},{12,20},{14,22},{16,24},... | collective-permute-start | bytes 3145736 | tf_op jit(solution)/shard_map/ppermute | solution.py:293
  227.2 22.1 %collective-permute-start.23 = (bf16[2048,256]{1,0:T(8,128)(2,1)S(1)}, bf16[2048,256]{1,0:T(8,128)(2,1)S(1)}, u32[]{:S(2)}, u32[]{:S(2)}) collective-permute-start(bf16[2048,256]{1,0:T(8,128)(2,1)S(1)} %collective-permute-done.18.refs_0_.refs_4_), channel_id=1, source_target_pairs={{0,4},{2,6},{4,0},{6,2},{8,12},{10,14},{12,8},{14,10},{16,20},{18,... | collective-permute-start | bytes 3145736 | tf_op jit(solution)/shard_map/ppermute | solution.py:234
  228.7 26.1 %collective-permute-start.22 = (bf16[2048,256]{1,0:T(8,128)(2,1)S(1)}, bf16[2048,256]{1,0:T(8,128)(2,1)S(1)}, u32[]{:S(2)}, u32[]{:S(2)}) collective-permute-start(bf16[2048,256]{1,0:T(8,128)(2,1)S(1)} %collective-permute-done.18.refs_0_.refs_4_), channel_id=1, source_target_pairs={{0,2},{2,0},{4,6},{6,4},{8,10},{10,8},{12,14},{14,12},{16,18},{18,... | collective-permute-start | bytes 3145736 | tf_op jit(solution)/shard_map/ppermute | solution.py:234
  229.0 25.8 %collective-permute-start.21 = (bf16[2048,256]{1,0:T(8,128)(2,1)S(1)}, bf16[2048,256]{1,0:T(8,128)(2,1)S(1)}, u32[]{:S(2)}, u32[]{:S(2)}) collective-permute-start(bf16[2048,256]{1,0:T(8,128)(2,1)S(1)} %collective-permute-done.18.refs_0_.refs_4_), channel_id=1, source_target_pairs={{0,8},{2,10},{4,12},{6,14},{8,16},{10,18},{12,20},{14,22},{16,24},... | collective-permute-start | bytes 3145736 | tf_op jit(solution)/shard_map/ppermute | solution.py:293
  229.0 45.0 %collective-permute-start.26 = (bf16[2048,256]{1,0:T(8,128)(2,1)S(1)}, bf16[2048,256]{1,0:T(8,128)(2,1)S(1)}, u32[]{:S(2)}, u32[]{:S(2)}) collective-permute-start(bf16[2048,256]{1,0:T(8,128)(2,1)S(1)} %collective-permute-done.17.refs_2_.refs_3_), channel_id=1, source_target_pairs={{0,2},{2,0},{4,6},{6,4},{8,10},{10,8},{12,14},{14,12},{16,18},{18,... | collective-permute-start | bytes 3145736 | tf_op jit(solution)/shard_map/ppermute | solution.py:234
  254.8 26.1 %collective-permute-start.25 = (bf16[2048,256]{1,0:T(8,128)(2,1)S(1)}, bf16[2048,256]{1,0:T(8,128)(2,1)S(1)}, u32[]{:S(2)}, u32[]{:S(2)}) collective-permute-start(bf16[2048,256]{1,0:T(8,128)(2,1)S(1)} %collective-permute-done.21.refs_0_.refs_7_), channel_id=1, source_target_pairs={{0,4},{2,6},{4,0},{6,2},{8,12},{10,14},{12,8},{14,10},{16,20},{18,... | collective-permute-start | bytes 3145736 | tf_op jit(solution)/shard_map/ppermute | solution.py:234
  255.3 25.6 %collective-permute-start.24 = (bf16[2048,256]{1,0:T(8,128)(2,1)S(1)}, bf16[2048,256]{1,0:T(8,128)(2,1)S(1)}, u32[]{:S(2)}, u32[]{:S(2)}) collective-permute-start(bf16[2048,256]{1,0:T(8,128)(2,1)S(1)} %collective-permute-done.22.refs_1_.refs_8_), channel_id=1, source_target_pairs={{0,8},{2,10},{4,12},{6,14},{8,16},{10,18},{12,20},{14,22},{16,24},... | collective-permute-start | bytes 3145736 | tf_op jit(solution)/shard_map/ppermute | solution.py:293
  255.3 40.2 %collective-permute-start.28 = (bf16[2048,256]{1,0:T(8,128)(2,1)S(1)}, bf16[2048,256]{1,0:T(8,128)(2,1)S(1)}, u32[]{:S(2)}, u32[]{:S(2)}) collective-permute-start(bf16[2048,256]{1,0:T(8,128)(2,1)S(1)} %collective-permute-done.22.refs_1_.refs_8_), channel_id=1, source_target_pairs={{0,4},{2,6},{4,0},{6,2},{8,12},{10,14},{12,8},{14,10},{16,20},{18,... | collective-permute-start | bytes 3145736 | tf_op jit(solution)/shard_map/ppermute | solution.py:234
  (23 other events, 151.2 us)

commit v7 on v6

--- a/solution.py
+++ b/solution.py
@@ -21,11 +21,13 @@
     subs, rows = codes_ref.shape[1:]
     width = table_ref.shape[1]
     halves = table_ref.shape[2] // LANES
+    first_out = pl.program_id(0) * (subs * width)
     ids_ref[...] = codes_ref[0].astype(jnp.float32).astype(jnp.int32)
 
     def body(step, carry):
         base = pl.multiple_of(step * GROUP, GROUP)
         for first in range(0, rows, LANES):
+            lanes = pl.ds(pl.multiple_of(pl.program_id(1) * rows + first, LANES), LANES)
             ids_all = ids_ref[pl.ds(base, GROUP), first : first + LANES]
             for pair in range(0, GROUP, 2):
                 both = []
@@ -40,10 +42,10 @@
                         )
                         picked = got if half == 0 else jnp.where(ids >= half * LANES, got, picked)
                     both.append(picked)
-                out_ref[
-                    pl.ds(pl.multiple_of((base + pair) * width, 2 * width), 2 * width),
-                    first : first + LANES,
-                ] = jnp.concatenate(both, axis=0).astype(out_ref.dtype)
+                row = pl.multiple_of(first_out + (base + pair) * width, 2 * width)
+                out_ref[pl.ds(row, 2 * width), lanes] = jnp.concatenate(both, axis=0).astype(
+                    out_ref.dtype
+                )
         return carry
 
     lax.fori_loop(0, subs // GROUP, body, 0)
@@ -60,12 +62,48 @@
             pl.BlockSpec((1, tile, rows), lambda m, s: (s, m, 0)),
             pl.BlockSpec((tile, width, centroids), lambda m, s: (m, 0, 0)),
         ],
-        out_specs=pl.BlockSpec((tile * width, rows), lambda m, s: (m, s)),
+        out_specs=VMEM,
         scratch_shapes=[pltpu.VMEM((tile, rows), jnp.int32)],
-        out_shape=jax.ShapeDtypeStruct((subs * width, blocks * rows), jnp.bfloat16),
+        out_shape=pltpu.VMEM((subs * width, blocks * rows), jnp.bfloat16),
         compiler_params=pltpu.CompilerParams(vmem_limit_bytes=VMEM_BYTES),
         name="lookup",
     )(codes, table)
+
+
+def cross_kernel(targets, place_ref, rebuilt_ref, prior_ref, local_ref, *refs):
+    pieces, outs = refs[: len(refs) - len(targets)], refs[len(refs) - len(targets) :]
+    rows = local_ref.shape[0]
+    block = outs[0].shape[1]
+    part_rows, col = (pieces[0].shape[0], rows // pieces[0].shape[0]) if pieces else (rows, 1)
+    for target, out_ref in zip(targets, outs):
+        place = lax.bitwise_xor(place_ref[1], target)
+        lanes = pl.ds(pl.multiple_of(place * block, block), block)
+        total = jnp.dot(
+            rebuilt_ref[:, :rows], local_ref[:, lanes], preferred_element_type=jnp.float32
+        )
+        for index, piece_ref in enumerate(pieces):
+            step, turn = divmod(index, col)
+            first = (step + 1) * rows + lax.rem(place_ref[0] + turn, col) * part_rows
+            total += jnp.dot(
+                rebuilt_ref[:, pl.ds(pl.multiple_of(first, part_rows), part_rows)],
+                piece_ref[:, lanes],
+                preferred_element_type=jnp.float32,
+            )
+        if target == 0:
+            total += prior_ref[...]
+        out_ref[...] = total.astype(out_ref.dtype)
+
+
+def cross_blocks(targets, dtype, place, rebuilt, prior, local, pieces):
+    operands = in_vmem(rebuilt, prior, local, *pieces)
+    return pl.pallas_call(
+        functools.partial(cross_kernel, targets),
+        in_specs=[pl.BlockSpec(memory_space=pltpu.SMEM)] + [VMEM] * len(operands),
+        out_specs=[VMEM] * len(targets),
+        out_shape=[pltpu.VMEM(prior.shape, dtype) for _ in targets],
+        compiler_params=pltpu.CompilerParams(vmem_limit_bytes=VMEM_BYTES),
+        name="cross",
+    )(place, *operands)
 
 
 def product_of(value_ref, block_ref, inner_ref, index):
@@ -234,56 +272,45 @@
         return lax.ppermute(value, "dp", pairs)
 
     steps = list(range(1, outer_size))
-    sends = [
-        lax.dynamic_slice(embeddings, (core * part_rows, (outer ^ step) * wide), (part_rows, wide))
-        for step in steps
-    ]
     codes_t = codes.T.astype(jnp.bfloat16)
     group_codes = [codes_t] + [from_outer(codes_t, step) for step in steps]
 
     table = jnp.transpose(codebooks, (0, 2, 1)).astype(jnp.float32)
     own = rebuild_rows(codes_t[None], table)
-    sends[1:], own = lax.optimization_barrier((sends[1:], own))
     rotated = lax.dot_general(
         rotation, embeddings, (((0,), (1,)), ((), ())), preferred_element_type=jnp.float32
     )
     residue = rotated - own.astype(jnp.float32)
     row_error = lax.psum(jnp.sum(residue * residue, axis=0), "col")
     weights = 1.0 / (1.0 + row_error / (2.0 * model_width))
-    sends[0], weights, group_codes = lax.optimization_barrier((sends[0], weights, group_codes))
+    scaled = (weights[:, None] * embeddings.astype(jnp.float32)).astype(jnp.bfloat16)
+
+    sends = [
+        lax.dynamic_slice(scaled, (core * part_rows, (outer ^ step) * wide), (part_rows, wide))
+        for step in steps
+    ]
     shares = [from_outer(send, step) for send, step in zip(sends, steps)]
-    group_weights = [weights] + [from_outer(weights, step) for step in steps]
+    local = lax.dynamic_slice_in_dim(scaled, outer * wide, wide, 1)
     rebuilt = rebuild_rows(jnp.stack(group_codes), table)
-
-    shares, rebuilt, group_weights = lax.optimization_barrier((shares, rebuilt, group_weights))
-    columns = [lax.dynamic_slice_in_dim(embeddings, outer * wide, wide, 1)]
+    shares, rebuilt = lax.optimization_barrier((shares, rebuilt))
+    pieces = []
     for share in shares:
-        if col == 2:
-            other = swap_cores(share)
-            pair = [jnp.where(core == 0, share, other), jnp.where(core == 0, other, share)]
-            columns.append(jnp.concatenate(pair, axis=0))
-        else:
-            columns.append(lax.all_gather(share, "col", axis=0, tiled=True))
-    scaled = jnp.concatenate(
-        [
-            (weight[:, None] * part.astype(jnp.float32)).astype(jnp.bfloat16)
-            for weight, part in zip(group_weights, columns)
-        ],
-        axis=0,
-    )
-
-
-    def group_block(step):
-        part = lax.dynamic_slice_in_dim(scaled, (inner ^ step) * block, block, 1)
-        return jnp.dot(rebuilt, part, preferred_element_type=jnp.float32)
-
-    parts = [
-        from_inner(group_block(step).astype(jnp.bfloat16), step)
-        for step in reversed(range(1, inner_size))
-    ]
+        if part_rows % LANES:
+            pieces.append(lax.all_gather(share, "col", axis=0, tiled=True))
+            continue
+        pieces.append(share)
+        for turn in range(1, col):
+            pairs = [(i, (i - turn) % col) for i in range(col)]
+            pieces.append(lax.ppermute(share, "col", pairs))
+
+    place = jnp.stack([core, inner]).astype(jnp.int32)
     start_row = lax.axis_index("dp") * block
     prior = lax.dynamic_slice_in_dim(rotation, start_row, block, 0).T
-    start = lax.optimization_barrier(group_block(0)) + 0.2 * rows_total * prior.astype(jnp.float32)
+    prior = 0.2 * rows_total * prior.astype(jnp.float32)
+    targets = list(reversed(range(1, inner_size)))
+    parts = cross_blocks(targets, jnp.bfloat16, place, rebuilt, prior, local, pieces)
+    parts = [from_inner(part, target) for part, target in zip(parts, targets)]
+    (start,) = cross_blocks([0], jnp.float32, place, rebuilt, prior, local, pieces)
     for part in parts:
         start = start + part.astype(jnp.float32)
     narrow = start.astype(jnp.bfloat16)

time: 359 us -> 336 us (0.936)
  matrix products: 28.6 us -> 12.6 us
  starting transfers between devices: 40.1 us -> 27.9 us
  Pallas kernels: 74 us -> 84.7 us
  waiting for transfers between devices: 188 us -> 181 us
    dot_general x4 -> x0, matrix products: 16 us -> none  [group_block(): return jnp.dot(rebuilt, part, preferred_element_type=jnp.float32)]
    ppermute x9 -> x6, waiting for transfers between devices: 29.2 us -> 15.3 us  [from_outer(): return lax.ppermute(value, 'dp', pairs)]
    ppermute x9 -> x6, starting transfers between devices: 22.1 us -> 10 us  [from_outer(): return lax.ppermute(value, 'dp', pairs)]
    pallas_call x0 -> x2, Pallas kernels: none -> 11.5 us  [cross_blocks(): pl.pallas_call(functools.partial(cross_kernel, targets), in_specs=[pl.Blo...]
    ppermute x13, waiting for transfers between devices: 139 us -> 143 us  [from_inner(): return lax.ppermute(value, 'dp', pairs)]
    unnamed x16 -> x10, local copies, waits for them, and re-layouts: 7.71 us -> 3.79 us
    ppermute x13 -> x10, waiting for transfers between devices: 12.8 us -> 12.8 us  [swap_cores(): return lax.ppermute(value, 'col', [(0, 1), (1, 0)])]
  transfers between devices with their start and end apart: 40 -> 37, of which waited for: 21 -> 22; matrix products, arithmetic and copies ran while one was open for 8% -> 9% of each run, Pallas kernels for 10% -> 11%
where the time goes in v7:
time: 336 us; the launch traced here: 329 us
  waiting for transfers between devices  181 us (54%)
  Pallas kernels  84.7 us (25%)
  starting transfers between devices  27.9 us (8%)
  matrix products  12.6 us (4%)
  local copies, waits for them, and re-layouts  10.6 us (3%)
  other arithmetic  10 us (3%)
    ppermute x13, waiting for transfers between devices, from_inner(): return lax.ppermute(value, 'dp', pairs)  143 us
    pallas_call x4, Pallas kernels, apply_next(): pl.pallas_call(functools.partial(next_kernel, step, blocks, len(inner)),...  39.3 us
    pallas_call x2, Pallas kernels, rebuild_rows(): pl.pallas_call(lookup_kernel, grid=(subs // tile, blocks), in_specs=[pl.B...  26.4 us
    ppermute x6, waiting for transfers between devices, from_outer(): return lax.ppermute(value, 'dp', pairs)  15.3 us
    ppermute x13, starting transfers between devices, from_inner(): return lax.ppermute(value, 'dp', pairs)  14 us
    ppermute x10, waiting for transfers between devices, swap_cores(): return lax.ppermute(value, 'col', [(0, 1), (1, 0)])  12.8 us
    dot_general x1, matrix products, shards(): lax.dot_general(rotation, embeddings, (((0,), (1,)), ((), ())), preferred...  12.6 us
    pallas_call x2, Pallas kernels, cross_blocks(): pl.pallas_call(functools.partial(cross_kernel, targets), in_specs=[pl.Blo...  11.5 us
  transfers between devices with their start and end apart: 37, of which 22 were waited for; matrix products, arithmetic and copies ran while one was open for 9% of the time, Pallas kernels for 11%

profile of v7, /device:TPU:0, one launch (start us, length us, event | category | flops | bytes accessed | tf_op | source)
XLA Modules:
  0.0 329.4 jit_solution(17195838606970492746)
XLA Ops:
  2.1 4.0 %collective-permute-start.4 = (bf16[256,512]{1,0:T(8,128)(2,1)}, bf16[256,512]{1,0:T(8,128)(2,1)}, u32[]{:S(2)}, u32[]{:S(2)}) collective-permute-start(bf16[256,512]{1,0:T(8,128)(2,1)} %get-tuple-element.110), channel_id=1, source_target_pairs={{0,16},{2,18},{4,20},{6,22},{8,24},{10,26},{12,28},{14,30},{16,0},... | collective-permute-start | bytes 786440 | tf_op jit(solution)/shard_map/ppermute | solution.py:268
  7.9 5.3 %lookup.2 = bf16[2048,512]{1,0:T(8,128)(2,1)S(1)} custom-call(bf16[1,256,512]{2,1,0:T(8,128)(2,1)S(1)} %get-tuple-element.111.codes_ref, f32[256,8,256]{2,1,0:T(8,128)S(1)} %convert_bitcast_fusion.table_ref), custom_call_target="tpu_custom_call" | custom-call | tf_op jit(solution)/shard_map/lookup/pallas_call | solution.py:58
  13.2 12.6 %multiply_reduce_fusion = f32[512]{0:T(512)S(1)} fusion(bf16[2048,512]{1,0:T(8,128)(2,1)S(1)} %lookup.2, bf16[4096,2048]{1,0:T(8,128)(2,1)} %param.5, bf16[512,4096]{1,0:T(8,128)(2,1)S(1)} %copy-done.1), kind=kOutput, calls=%fused_computation.1 | convolution fusion | flops 8594128896 | bytes 23070720 | tf_op jit(solution)/shard_map/dot_general | solution.py:280
  28.3 5.6 %multiply_convert_fusion = bf16[512,4096]{1,0:T(8,128)(2,1)} fusion(bf16[512,4096]{1,0:T(8,128)(2,1)} %param.4, f32[512]{0:T(512)S(1)} %add_divide_fusion), kind=kLoop, calls=%fused_computation | loop fusion | flops 6291456 | bytes 8390656 | tf_op jit(solution)/shard_map/convert_element_type | solution.py:286
  36.5 3.8 %collective-permute-start.2 = (bf16[256,1024]{1,0:T(8,128)(2,1)}, bf16[256,1024]{1,0:T(8,128)(2,1)S(1)}, u32[]{:S(2)}, u32[]{:S(2)}) collective-permute-start(bf16[256,1024]{1,0:T(8,128)(2,1)} %get-tuple-element.107), channel_id=1, source_target_pairs={{0,24},{2,26},{4,28},{6,30},{8,16},{10,18},{12,20},{14,22},{16,8},... | collective-permute-start | bytes 1572872 | tf_op jit(solution)/shard_map/ppermute | solution.py:268
  48.3 21.1 %lookup.3.rebuilt_ref = bf16[2048,2048]{1,0:T(8,128)(2,1)S(1)} custom-call(bf16[4,256,512]{2,1,0:T(8,128)(2,1)S(1)} %pad_maximum_fusion.codes_ref, f32[256,8,256]{2,1,0:T(8,128)S(1)} %convert_bitcast_fusion.table_ref), custom_call_target="tpu_custom_call" | custom-call | tf_op jit(solution)/shard_map/lookup/pallas_call | solution.py:58
  69.4 15.3 %collective-permute-done.1.refs_2_ = bf16[256,1024]{1,0:T(8,128)(2,1)S(1)} collective-permute-done((bf16[256,1024]{1,0:T(8,128)(2,1)}, bf16[256,1024]{1,0:T(8,128)(2,1)S(1)}, u32[]{:S(2)}, u32[]{:S(2)}) %collective-permute-start.1) | collective-permute-done | bytes 524320 | tf_op jit(solution)/shard_map/ppermute | solution.py:268
  88.1 8.0 %cross.3 = (bf16[2048,256]{1,0:T(8,128)(2,1)S(1)}, bf16[2048,256]{1,0:T(8,128)(2,1)S(1)}, bf16[2048,256]{1,0:T(8,128)(2,1)S(1)}) custom-call(s32[2]{0:T(128)S(1)} %pad_add_fusion.place_ref, bf16[2048,2048]{1,0:T(8,128)(2,1)S(1)} %lookup.3.rebuilt_ref, f32[2048,256]{1,0:T(8,128)S(1)} %multiply_bitcast_fusion.prior_ref, ...), custom_call_target="tpu_custom_call" | custom-call | tf_op jit(solution)/shard_map/cross/pallas_call | solution.py:99
  103.2 19.9 %collective-permute-done.9 = bf16[2048,256]{1,0:T(8,128)(2,1)S(1)} collective-permute-done((bf16[2048,256]{1,0:T(8,128)(2,1)S(1)}, bf16[2048,256]{1,0:T(8,128)(2,1)S(1)}, u32[]{:S(2)}, u32[]{:S(2)}) %collective-permute-start.9) | collective-permute-done | bytes 1048608 | tf_op jit(solution)/shard_map/ppermute | solution.py:272
  123.1 21.8 %collective-permute-done.10 = bf16[2048,256]{1,0:T(8,128)(2,1)S(1)} collective-permute-done((bf16[2048,256]{1,0:T(8,128)(2,1)S(1)}, bf16[2048,256]{1,0:T(8,128)(2,1)S(1)}, u32[]{:S(2)}, u32[]{:S(2)}) %collective-permute-start.10) | collective-permute-done | bytes 1048608 | tf_op jit(solution)/shard_map/ppermute | solution.py:272
  150.3 21.6 %collective-permute-done.14.refs_2_.refs_3_ = bf16[2048,256]{1,0:T(8,128)(2,1)S(1)} collective-permute-done((bf16[2048,256]{1,0:T(8,128)(2,1)S(1)}, bf16[2048,256]{1,0:T(8,128)(2,1)S(1)}, u32[]{:S(2)}, u32[]{:S(2)}) %collective-permute-start.14) | collective-permute-done | bytes 1048608 | tf_op jit(solution)/shard_map/ppermute | solution.py:272
  179.9 18.8 %collective-permute-done.17.refs_2_.refs_6_ = bf16[2048,256]{1,0:T(8,128)(2,1)S(1)} collective-permute-done((bf16[2048,256]{1,0:T(8,128)(2,1)}, bf16[2048,256]{1,0:T(8,128)(2,1)S(1)}, u32[]{:S(2)}, u32[]{:S(2)}) %collective-permute-start.17) | collective-permute-done | bytes 1048608 | tf_op jit(solution)/shard_map/ppermute | solution.py:272
  207.0 17.3 %collective-permute-done.20.refs_2_.refs_9_ = bf16[2048,256]{1,0:T(8,128)(2,1)S(1)} collective-permute-done((bf16[2048,256]{1,0:T(8,128)(2,1)S(1)}, bf16[2048,256]{1,0:T(8,128)(2,1)S(1)}, u32[]{:S(2)}, u32[]{:S(2)}) %collective-permute-start.20) | collective-permute-done | bytes 1048608 | tf_op jit(solution)/shard_map/ppermute | solution.py:272
  224.3 5.7 %collective-permute-done.19.refs_1_.refs_8_ = bf16[2048,256]{1,0:T(8,128)(2,1)S(1)} collective-permute-done((bf16[2048,256]{1,0:T(8,128)(2,1)S(1)}, bf16[2048,256]{1,0:T(8,128)(2,1)S(1)}, u32[]{:S(2)}, u32[]{:S(2)}) %collective-permute-start.19) | collective-permute-done | bytes 1048608 | tf_op jit(solution)/shard_map/ppermute | solution.py:272
  233.1 16.1 %collective-permute-done.23.refs_2_.refs_12_ = bf16[2048,256]{1,0:T(8,128)(2,1)S(1)} collective-permute-done((bf16[2048,256]{1,0:T(8,128)(2,1)S(1)}, bf16[2048,256]{1,0:T(8,128)(2,1)S(1)}, u32[]{:S(2)}, u32[]{:S(2)}) %collective-permute-start.23) | collective-permute-done | bytes 1048608 | tf_op jit(solution)/shard_map/ppermute | solution.py:272
  249.2 6.9 %collective-permute-done.22.refs_1_.refs_11_ = bf16[2048,256]{1,0:T(8,128)(2,1)S(1)} collective-permute-done((bf16[2048,256]{1,0:T(8,128)(2,1)S(1)}, bf16[2048,256]{1,0:T(8,128)(2,1)S(1)}, u32[]{:S(2)}, u32[]{:S(2)}) %collective-permute-start.22) | collective-permute-done | bytes 1048608 | tf_op jit(solution)/shard_map/ppermute | solution.py:272
  258.4 12.2 %collective-permute-done.25.refs_1_.refs_14_ = bf16[2048,256]{1,0:T(8,128)(2,1)S(1)} collective-permute-done((bf16[2048,256]{1,0:T(8,128)(2,1)S(1)}, bf16[2048,256]{1,0:T(8,128)(2,1)S(1)}, u32[]{:S(2)}, u32[]{:S(2)}) %collective-permute-start.25) | collective-permute-done | bytes 1048608 | tf_op jit(solution)/shard_map/ppermute | solution.py:272
  277.2 10.6 %apply0.1 = (f32[2048,256]{1,0:T(8,128)S(1)}, bf16[4096,256]{1,0:T(8,128)(2,1)S(1)}) custom-call(f32[8,256]{1,0:T(8,128)S(1)} %get-tuple-element.92.mine_square_ref, f32[8,256]{1,0:T(8,128)S(1)} %collective-permute-done.27.other_square_ref, bf16[2048,256]{1,0:T(8,128)(2,1)S(1)} %get-tuple-element.105.refs_0_, ...), custom_call_target="tpu_custom_call" | custom-call | tf_op jit(solution)/shard_map/apply0/pallas_call | solution.py:205
  288.2 3.8 %collective-permute-done.34.refs_17_ = bf16[4096,256]{1,0:T(8,128)(2,1)S(1)} collective-permute-done((bf16[4096,256]{1,0:T(8,128)(2,1)S(1)}, bf16[4096,256]{1,0:T(8,128)(2,1)S(1)}, u32[]{:S(2)}, u32[]{:S(2)}) %collective-permute-start.34) | collective-permute-done | bytes 2097184 | tf_op jit(solution)/shard_map/ppermute | solution.py:217
  292.0 10.7 %apply1.1 = (f32[2048,256]{1,0:T(8,128)S(1)}, bf16[4096,256]{1,0:T(8,128)(2,1)S(1)}) custom-call(f32[8,256]{1,0:T(8,128)S(1)} %get-tuple-element.92.mine_square_ref, f32[8,256]{1,0:T(8,128)S(1)} %collective-permute-done.27.other_square_ref, bf16[2048,256]{1,0:T(8,128)(2,1)S(1)} %get-tuple-element.105.refs_0_, ...), custom_call_target="tpu_custom_call" | custom-call | tf_op jit(solution)/shard_map/apply1/pallas_call | solution.py:205
  303.1 3.8 %collective-permute-done.35.refs_17_ = bf16[4096,256]{1,0:T(8,128)(2,1)S(1)} collective-permute-done((bf16[4096,256]{1,0:T(8,128)(2,1)S(1)}, bf16[4096,256]{1,0:T(8,128)(2,1)S(1)}, u32[]{:S(2)}, u32[]{:S(2)}) %collective-permute-start.35) | collective-permute-done | bytes 2097184 | tf_op jit(solution)/shard_map/ppermute | solution.py:217
  306.9 10.5 %apply2.1 = (f32[2048,256]{1,0:T(8,128)S(1)}, bf16[4096,256]{1,0:T(8,128)(2,1)S(1)}) custom-call(f32[8,256]{1,0:T(8,128)S(1)} %get-tuple-element.92.mine_square_ref, f32[8,256]{1,0:T(8,128)S(1)} %collective-permute-done.27.other_square_ref, bf16[2048,256]{1,0:T(8,128)(2,1)S(1)} %get-tuple-element.105.refs_0_, ...), custom_call_target="tpu_custom_call" | custom-call | tf_op jit(solution)/shard_map/apply2/pallas_call | solution.py:205
  317.8 3.8 %collective-permute-done.36.refs_17_ = bf16[4096,256]{1,0:T(8,128)(2,1)S(1)} collective-permute-done((bf16[4096,256]{1,0:T(8,128)(2,1)S(1)}, bf16[4096,256]{1,0:T(8,128)(2,1)S(1)}, u32[]{:S(2)}, u32[]{:S(2)}) %collective-permute-start.36) | collective-permute-done | bytes 2097184 | tf_op jit(solution)/shard_map/ppermute | solution.py:217
  321.6 7.6 %apply3.1 = f32[256,2048]{1,0:T(8,128)} custom-call(f32[8,256]{1,0:T(8,128)S(1)} %get-tuple-element.92.mine_square_ref, f32[8,256]{1,0:T(8,128)S(1)} %collective-permute-done.27.other_square_ref, bf16[2048,256]{1,0:T(8,128)(2,1)S(1)} %get-tuple-element.105.refs_0_, bf16[2048,256]{1,0:T(8,128)(2,1)} %collective-permute-done.12.refs_0_.refs_1_, ...), custom_call_target="tpu_custom_call" | custom-call | tf_op jit(solution)/shard_map/apply3/pallas_call | solution.py:205
  (89 shorter events, 62.3 us)
Async XLA Ops:
  2.1 38.2 %collective-permute-start.4 = (bf16[256,512]{1,0:T(8,128)(2,1)}, bf16[256,512]{1,0:T(8,128)(2,1)}, u32[]{:S(2)}, u32[]{:S(2)}) collective-permute-start(bf16[256,512]{1,0:T(8,128)(2,1)} %get-tuple-element.110), channel_id=1, source_target_pairs={{0,16},{2,18},{4,20},{6,22},{8,24},{10,26},{12,28},{14,30},{16,0},... | collective-permute-start | bytes 786440 | tf_op jit(solution)/shard_map/ppermute | solution.py:268
  6.1 40.9 %collective-permute-start.3 = (bf16[256,512]{1,0:T(8,128)(2,1)}, bf16[256,512]{1,0:T(8,128)(2,1)}, u32[]{:S(2)}, u32[]{:S(2)}) collective-permute-start(bf16[256,512]{1,0:T(8,128)(2,1)} %get-tuple-element.110), channel_id=1, source_target_pairs={{0,8},{2,10},{4,12},{6,14},{8,0},{10,2},{12,4},{14,6},{16,24},{18,... | collective-permute-start | bytes 786440 | tf_op jit(solution)/shard_map/ppermute | solution.py:268
  7.7 39.3 %collective-permute-start.5 = (bf16[256,512]{1,0:T(8,128)(2,1)}, bf16[256,512]{1,0:T(8,128)(2,1)}, u32[]{:S(2)}, u32[]{:S(2)}) collective-permute-start(bf16[256,512]{1,0:T(8,128)(2,1)} %get-tuple-element.110), channel_id=1, source_target_pairs={{0,24},{2,26},{4,28},{6,30},{8,16},{10,18},{12,20},{14,22},{16,8},... | collective-permute-start | bytes 786440 | tf_op jit(solution)/shard_map/ppermute | solution.py:268
  36.5 32.9 %collective-permute-start.2 = (bf16[256,1024]{1,0:T(8,128)(2,1)}, bf16[256,1024]{1,0:T(8,128)(2,1)S(1)}, u32[]{:S(2)}, u32[]{:S(2)}) collective-permute-start(bf16[256,1024]{1,0:T(8,128)(2,1)} %get-tuple-element.107), channel_id=1, source_target_pairs={{0,24},{2,26},{4,28},{6,30},{8,16},{10,18},{12,20},{14,22},{16,8},... | collective-permute-start | bytes 1572872 | tf_op jit(solution)/shard_map/ppermute | solution.py:268
  40.3 44.4 %collective-permute-start.1 = (bf16[256,1024]{1,0:T(8,128)(2,1)}, bf16[256,1024]{1,0:T(8,128)(2,1)S(1)}, u32[]{:S(2)}, u32[]{:S(2)}) collective-permute-start(bf16[256,1024]{1,0:T(8,128)(2,1)} %get-tuple-element.108), channel_id=1, source_target_pairs={{0,16},{2,18},{4,20},{6,22},{8,24},{10,26},{12,28},{14,30},{16,0},... | collective-permute-start | bytes 1572872 | tf_op jit(solution)/shard_map/ppermute | solution.py:268
  40.3 44.4 %collective-permute-start = (bf16[256,1024]{1,0:T(8,128)(2,1)}, bf16[256,1024]{1,0:T(8,128)(2,1)}, u32[]{:S(2)}, u32[]{:S(2)}) collective-permute-start(bf16[256,1024]{1,0:T(8,128)(2,1)} %get-tuple-element.109), channel_id=1, source_target_pairs={{0,8},{2,10},{4,12},{6,14},{8,0},{10,2},{12,4},{14,6},{16,24},{18,... | collective-permute-start | bytes 1572872 | tf_op jit(solution)/shard_map/ppermute | solution.py:268
  96.1 27.0 %collective-permute-start.9 = (bf16[2048,256]{1,0:T(8,128)(2,1)S(1)}, bf16[2048,256]{1,0:T(8,128)(2,1)S(1)}, u32[]{:S(2)}, u32[]{:S(2)}) collective-permute-start(bf16[2048,256]{1,0:T(8,128)(2,1)S(1)} %get-tuple-element.59), channel_id=1, source_target_pairs={{0,6},{2,4},{4,2},{6,0},{8,14},{10,12},{12,10},{14,8},{16,22},{18,... | collective-permute-start | bytes 3145736 | tf_op jit(solution)/shard_map/ppermute | solution.py:272
  98.6 46.2 %collective-permute-start.10 = (bf16[2048,256]{1,0:T(8,128)(2,1)S(1)}, bf16[2048,256]{1,0:T(8,128)(2,1)S(1)}, u32[]{:S(2)}, u32[]{:S(2)}) collective-permute-start(bf16[2048,256]{1,0:T(8,128)(2,1)S(1)} %get-tuple-element.60), channel_id=1, source_target_pairs={{0,4},{2,6},{4,0},{6,2},{8,12},{10,14},{12,8},{14,10},{16,20},{18,... | collective-permute-start | bytes 3145736 | tf_op jit(solution)/shard_map/ppermute | solution.py:272
  99.1 45.8 %collective-permute-start.11 = (bf16[2048,256]{1,0:T(8,128)(2,1)S(1)}, bf16[2048,256]{1,0:T(8,128)(2,1)S(1)}, u32[]{:S(2)}, u32[]{:S(2)}) collective-permute-start(bf16[2048,256]{1,0:T(8,128)(2,1)S(1)} %get-tuple-element.61), channel_id=1, source_target_pairs={{0,2},{2,0},{4,6},{6,4},{8,10},{10,8},{12,14},{14,12},{16,18},{18,... | collective-permute-start | bytes 3145736 | tf_op jit(solution)/shard_map/ppermute | solution.py:272
  146.9 25.0 %collective-permute-start.14 = (bf16[2048,256]{1,0:T(8,128)(2,1)S(1)}, bf16[2048,256]{1,0:T(8,128)(2,1)S(1)}, u32[]{:S(2)}, u32[]{:S(2)}) collective-permute-start(bf16[2048,256]{1,0:T(8,128)(2,1)S(1)} %get-tuple-element.105.refs_0_), channel_id=1, source_target_pairs={{0,4},{2,6},{4,0},{6,2},{8,12},{10,14},{12,8},{14,10},{16,20},{18,... | collective-permute-start | bytes 3145736 | tf_op jit(solution)/shard_map/ppermute | solution.py:272
  148.3 24.9 %collective-permute-start.13 = (bf16[2048,256]{1,0:T(8,128)(2,1)S(1)}, bf16[2048,256]{1,0:T(8,128)(2,1)}, u32[]{:S(2)}, u32[]{:S(2)}) collective-permute-start(bf16[2048,256]{1,0:T(8,128)(2,1)S(1)} %get-tuple-element.105.refs_0_), channel_id=1, source_target_pairs={{0,2},{2,0},{4,6},{6,4},{8,10},{10,8},{12,14},{14,12},{16,18},{18,... | collective-permute-start | bytes 3145736 | tf_op jit(solution)/shard_map/ppermute | solution.py:272
  149.1 25.9 %collective-permute-start.12 = (bf16[2048,256]{1,0:T(8,128)(2,1)S(1)}, bf16[2048,256]{1,0:T(8,128)(2,1)}, u32[]{:S(2)}, u32[]{:S(2)}) collective-permute-start(bf16[2048,256]{1,0:T(8,128)(2,1)S(1)} %get-tuple-element.105.refs_0_), channel_id=1, source_target_pairs={{0,8},{2,10},{4,12},{6,14},{8,16},{10,18},{12,20},{14,22},{16,24},... | collective-permute-start | bytes 3145736 | tf_op jit(solution)/shard_map/ppermute | solution.py:320
  175.1 23.7 %collective-permute-start.17 = (bf16[2048,256]{1,0:T(8,128)(2,1)}, bf16[2048,256]{1,0:T(8,128)(2,1)S(1)}, u32[]{:S(2)}, u32[]{:S(2)}) collective-permute-start(bf16[2048,256]{1,0:T(8,128)(2,1)} %collective-permute-done.12.refs_0_.refs_1_), channel_id=1, source_target_pairs={{0,4},{2,6},{4,0},{6,2},{8,12},{10,14},{12,8},{14,10},{16,20},{18,... | collective-permute-start | bytes 3145736 | tf_op jit(solution)/shard_map/ppermute | solution.py:272
  176.8 23.4 %collective-permute-start.16 = (bf16[2048,256]{1,0:T(8,128)(2,1)}, bf16[2048,256]{1,0:T(8,128)(2,1)S(1)}, u32[]{:S(2)}, u32[]{:S(2)}) collective-permute-start(bf16[2048,256]{1,0:T(8,128)(2,1)} %collective-permute-done.12.refs_0_.refs_1_), channel_id=1, source_target_pairs={{0,2},{2,0},{4,6},{6,4},{8,10},{10,8},{12,14},{14,12},{16,18},{18,... | collective-permute-start | bytes 3145736 | tf_op jit(solution)/shard_map/ppermute | solution.py:272
  177.3 25.0 %collective-permute-start.15 = (bf16[2048,256]{1,0:T(8,128)(2,1)}, bf16[2048,256]{1,0:T(8,128)(2,1)S(1)}, u32[]{:S(2)}, u32[]{:S(2)}) collective-permute-start(bf16[2048,256]{1,0:T(8,128)(2,1)} %collective-permute-done.12.refs_0_.refs_1_), channel_id=1, source_target_pairs={{0,8},{2,10},{4,12},{6,14},{8,16},{10,18},{12,20},{14,22},{16,24},... | collective-permute-start | bytes 3145736 | tf_op jit(solution)/shard_map/ppermute | solution.py:320
  202.3 22.0 %collective-permute-start.20 = (bf16[2048,256]{1,0:T(8,128)(2,1)S(1)}, bf16[2048,256]{1,0:T(8,128)(2,1)S(1)}, u32[]{:S(2)}, u32[]{:S(2)}) collective-permute-start(bf16[2048,256]{1,0:T(8,128)(2,1)S(1)} %collective-permute-done.15.refs_0_.refs_4_), channel_id=1, source_target_pairs={{0,4},{2,6},{4,0},{6,2},{8,12},{10,14},{12,8},{14,10},{16,20},{18,... | collective-permute-start | bytes 3145736 | tf_op jit(solution)/shard_map/ppermute | solution.py:272
  203.9 26.1 %collective-permute-start.19 = (bf16[2048,256]{1,0:T(8,128)(2,1)S(1)}, bf16[2048,256]{1,0:T(8,128)(2,1)S(1)}, u32[]{:S(2)}, u32[]{:S(2)}) collective-permute-start(bf16[2048,256]{1,0:T(8,128)(2,1)S(1)} %collective-permute-done.15.refs_0_.refs_4_), channel_id=1, source_target_pairs={{0,2},{2,0},{4,6},{6,4},{8,10},{10,8},{12,14},{14,12},{16,18},{18,... | collective-permute-start | bytes 3145736 | tf_op jit(solution)/shard_map/ppermute | solution.py:272
  204.2 25.8 %collective-permute-start.18 = (bf16[2048,256]{1,0:T(8,128)(2,1)S(1)}, bf16[2048,256]{1,0:T(8,128)(2,1)S(1)}, u32[]{:S(2)}, u32[]{:S(2)}) collective-permute-start(bf16[2048,256]{1,0:T(8,128)(2,1)S(1)} %collective-permute-done.15.refs_0_.refs_4_), channel_id=1, source_target_pairs={{0,8},{2,10},{4,12},{6,14},{8,16},{10,18},{12,20},{14,22},{16,24},... | collective-permute-start | bytes 3145736 | tf_op jit(solution)/shard_map/ppermute | solution.py:320
  204.2 45.0 %collective-permute-start.23 = (bf16[2048,256]{1,0:T(8,128)(2,1)S(1)}, bf16[2048,256]{1,0:T(8,128)(2,1)S(1)}, u32[]{:S(2)}, u32[]{:S(2)}) collective-permute-start(bf16[2048,256]{1,0:T(8,128)(2,1)S(1)} %collective-permute-done.14.refs_2_.refs_3_), channel_id=1, source_target_pairs={{0,2},{2,0},{4,6},{6,4},{8,10},{10,8},{12,14},{14,12},{16,18},{18,... | collective-permute-start | bytes 3145736 | tf_op jit(solution)/shard_map/ppermute | solution.py:272
  230.0 26.1 %collective-permute-start.22 = (bf16[2048,256]{1,0:T(8,128)(2,1)S(1)}, bf16[2048,256]{1,0:T(8,128)(2,1)S(1)}, u32[]{:S(2)}, u32[]{:S(2)}) collective-permute-start(bf16[2048,256]{1,0:T(8,128)(2,1)S(1)} %collective-permute-done.18.refs_0_.refs_7_), channel_id=1, source_target_pairs={{0,4},{2,6},{4,0},{6,2},{8,12},{10,14},{12,8},{14,10},{16,20},{18,... | collective-permute-start | bytes 3145736 | tf_op jit(solution)/shard_map/ppermute | solution.py:272
  230.4 25.7 %collective-permute-start.21 = (bf16[2048,256]{1,0:T(8,128)(2,1)S(1)}, bf16[2048,256]{1,0:T(8,128)(2,1)S(1)}, u32[]{:S(2)}, u32[]{:S(2)}) collective-permute-start(bf16[2048,256]{1,0:T(8,128)(2,1)S(1)} %collective-permute-done.19.refs_1_.refs_8_), channel_id=1, source_target_pairs={{0,8},{2,10},{4,12},{6,14},{8,16},{10,18},{12,20},{14,22},{16,24},... | collective-permute-start | bytes 3145736 | tf_op jit(solution)/shard_map/ppermute | solution.py:320
  230.4 40.2 %collective-permute-start.25 = (bf16[2048,256]{1,0:T(8,128)(2,1)S(1)}, bf16[2048,256]{1,0:T(8,128)(2,1)S(1)}, u32[]{:S(2)}, u32[]{:S(2)}) collective-permute-start(bf16[2048,256]{1,0:T(8,128)(2,1)S(1)} %collective-permute-done.19.refs_1_.refs_8_), channel_id=1, source_target_pairs={{0,4},{2,6},{4,0},{6,2},{8,12},{10,14},{12,8},{14,10},{16,20},{18,... | collective-permute-start | bytes 3145736 | tf_op jit(solution)/shard_map/ppermute | solution.py:272
  256.8 18.4 %collective-permute-start.28 = (bf16[256,256]{1,0:T(8,128)(2,1)S(1)}, bf16[256,256]{1,0:T(8,128)(2,1)S(1)}, u32[]{:S(2)}, u32[]{:S(2)}) collective-permute-start(bf16[256,256]{1,0:T(8,128)(2,1)S(1)} %get-tuple-element.93.refs_16_), channel_id=1, source_target_pairs={{0,1},{1,0},{2,3},{3,2},{4,5},{5,4},{6,7},{7,6},{8,9},{9,8},{10,11... | collective-permute-start | bytes 393224 | tf_op jit(solution)/shard_map/ppermute | solution.py:217
  256.8 18.5 %collective-permute-start.29 = (bf16[768,256]{1,0:T(8,128)(2,1)S(1)}, bf16[768,256]{1,0:T(8,128)(2,1)S(1)}, u32[]{:S(2)}, u32[]{:S(2)}) collective-permute-start(bf16[768,256]{1,0:T(8,128)(2,1)S(1)} %get-tuple-element.94.refs_17_), channel_id=1, source_target_pairs={{0,1},{1,0},{2,3},{3,2},{4,5},{5,4},{6,7},{7,6},{8,9},{9,8},{10,11... | collective-permute-start | bytes 1179656 | tf_op jit(solution)/shard_map/ppermute | solution.py:217
  (17 other events, 123.0 us)

commit v8 on v7

--- a/solution.py
+++ b/solution.py
@@ -70,72 +70,82 @@
     )(codes, table)
 
 
-def cross_kernel(targets, place_ref, rebuilt_ref, prior_ref, local_ref, *refs):
-    pieces, outs = refs[: len(refs) - len(targets)], refs[len(refs) - len(targets) :]
+def cross_kernel(plan, place_ref, rebuilt_ref, prior_ref, local_ref, *refs):
+    pieces, outs = refs[: len(refs) - len(plan)], refs[len(refs) - len(plan) :]
     rows = local_ref.shape[0]
-    block = outs[0].shape[1]
     part_rows, col = (pieces[0].shape[0], rows // pieces[0].shape[0]) if pieces else (rows, 1)
-    for target, out_ref in zip(targets, outs):
-        place = lax.bitwise_xor(place_ref[1], target)
-        lanes = pl.ds(pl.multiple_of(place * block, block), block)
-        total = jnp.dot(
-            rebuilt_ref[:, :rows], local_ref[:, lanes], preferred_element_type=jnp.float32
-        )
-        for index, piece_ref in enumerate(pieces):
-            step, turn = divmod(index, col)
-            first = (step + 1) * rows + lax.rem(place_ref[0] + turn, col) * part_rows
-            total += jnp.dot(
-                rebuilt_ref[:, pl.ds(pl.multiple_of(first, part_rows), part_rows)],
-                piece_ref[:, lanes],
-                preferred_element_type=jnp.float32,
+    for (targets, first_row), out_ref in zip(plan, outs):
+        height, block = out_ref.shape[0] // len(targets), out_ref.shape[1]
+        span = slice(first_row, first_row + height)
+        for slot, target in enumerate(targets):
+            place = lax.bitwise_xor(place_ref[1], target)
+            lanes = pl.ds(pl.multiple_of(place * block, block), block)
+            total = jnp.dot(
+                rebuilt_ref[span, :rows], local_ref[:, lanes], preferred_element_type=jnp.float32
             )
-        if target == 0:
-            total += prior_ref[...]
-        out_ref[...] = total.astype(out_ref.dtype)
-
-
-def cross_blocks(targets, dtype, place, rebuilt, prior, local, pieces):
+            for index, piece_ref in enumerate(pieces):
+                step, turn = divmod(index, col)
+                first = (step + 1) * rows + lax.rem(place_ref[0] + turn, col) * part_rows
+                total += jnp.dot(
+                    rebuilt_ref[span, pl.ds(pl.multiple_of(first, part_rows), part_rows)],
+                    piece_ref[:, lanes],
+                    preferred_element_type=jnp.float32,
+                )
+            if target == 0:
+                total += prior_ref[span, :]
+            out_ref[slot * height : (slot + 1) * height, :] = total.astype(out_ref.dtype)
+
+
+def cross_blocks(plan, dtype, place, rebuilt, prior, local, pieces):
     operands = in_vmem(rebuilt, prior, local, *pieces)
+    half, block = prior.shape[0] // 2, prior.shape[1]
     return pl.pallas_call(
-        functools.partial(cross_kernel, targets),
+        functools.partial(cross_kernel, plan),
         in_specs=[pl.BlockSpec(memory_space=pltpu.SMEM)] + [VMEM] * len(operands),
-        out_specs=[VMEM] * len(targets),
-        out_shape=[pltpu.VMEM(prior.shape, dtype) for _ in targets],
+        out_specs=[VMEM] * len(plan),
+        out_shape=[pltpu.VMEM((len(targets) * half, block), dtype) for targets, _ in plan],
         compiler_params=pltpu.CompilerParams(vmem_limit_bytes=VMEM_BYTES),
         name="cross",
     )(place, *operands)
 
 
-def product_of(value_ref, block_ref, inner_ref, index):
-    block = block_ref.shape[1]
-    product = jnp.dot(value_ref[...], block_ref[...], preferred_element_type=jnp.float32)
+def product_of(value_ref, halves, inner_ref, index):
+    half, block = halves[0].shape
+    product = jnp.zeros((value_ref.shape[0], block), jnp.float32)
+    for first, half_ref in enumerate(halves):
+        product += jnp.dot(
+            value_ref[:, first * half : (first + 1) * half], half_ref[...],
+            preferred_element_type=jnp.float32,
+        )
     inner_ref[index * block : (index + 1) * block, :] = product.T.astype(inner_ref.dtype)
 
 
 def first_kernel(own_ref, before_ref, *refs):
     panel, (inner_ref, square_ref) = refs[:-2], refs[-2:]
-    cols, block = panel[0].shape
+    half, block = panel[0].shape
     square = before_ref[...]
-    for index, block_ref in enumerate(panel):
-        product_of(own_ref, block_ref, inner_ref, index)
-        values = block_ref[...].astype(jnp.float32)
-        square += jnp.sum((values * values).reshape(cols // 8, 8, block), axis=0)
+    for index in range(len(panel) // 2):
+        halves = panel[2 * index : 2 * index + 2]
+        product_of(own_ref, halves, inner_ref, index)
+        for half_ref in halves:
+            values = half_ref[...].astype(jnp.float32)
+            square += jnp.sum((values * values).reshape(half // 8, 8, block), axis=0)
     square_ref[...] = square
 
 
 def next_kernel(step, blocks, parts, mine_square_ref, other_square_ref, *refs):
     last = step == 3
     states = 2 if last else 1
-    panel, refs = refs[:blocks], refs[blocks:]
+    panel, refs = refs[: 2 * blocks], refs[2 * blocks :]
     mine, other, refs = refs[:parts], refs[parts : 2 * parts], refs[2 * parts :]
     held, refs = refs[:states], refs[states:]
     if last:
         out_ref, sum_ref = refs
     else:
         state_ref, inner_ref, sum_ref, value_ref = refs
-    cols, block = panel[0].shape
+    half, block = panel[0].shape
     model_width = blocks * block
-    chunk = cols // CHUNKS
+    chunk = 2 * half // CHUNKS
     total = jnp.sum(mine_square_ref[...] + other_square_ref[...], axis=(0, 1), keepdims=True)
     scale = model_width / (1.96 * total)
     first = 0
@@ -145,10 +155,11 @@
 
     for index in range(CHUNKS):
         span = slice(index * chunk, (index + 1) * chunk)
+        side, first = divmod(index * chunk, half)
         made = jnp.zeros((chunk, block), jnp.float32)
         for owner in range(blocks):
             made += jnp.dot(
-                panel[owner][span, :],
+                panel[2 * owner + side][first : first + chunk, :],
                 sum_ref[owner * block : (owner + 1) * block, :],
                 preferred_element_type=jnp.float32,
             )
@@ -165,7 +176,7 @@
     if last:
         return
     for index in range(blocks):
-        product_of(value_ref, panel[index], inner_ref, index)
+        product_of(value_ref, panel[2 * index : 2 * index + 2], inner_ref, index)
 
 
 def in_vmem(*values):
@@ -179,7 +190,7 @@
         in_specs=[VMEM] * (2 + len(panel)),
         out_specs=[VMEM, VMEM],
         out_shape=[
-            pltpu.VMEM((len(panel) * block, block), jnp.bfloat16),
+            pltpu.VMEM((len(panel) // 2 * block, block), jnp.bfloat16),
             pltpu.VMEM((8, block), jnp.float32),
         ],
         compiler_params=pltpu.CompilerParams(vmem_limit_bytes=VMEM_BYTES),
@@ -188,8 +199,8 @@
 
 
 def apply_next(step, panel, inner, squares, held):
-    cols, block = panel[0].shape
-    blocks = len(panel)
+    half, block = panel[0].shape
+    blocks, cols = len(panel) // 2, 2 * half
     last = step == 3
     if last:
         out_shape = jax.ShapeDtypeStruct((block, cols), jnp.float32)
@@ -307,39 +318,56 @@
     start_row = lax.axis_index("dp") * block
     prior = lax.dynamic_slice_in_dim(rotation, start_row, block, 0).T
     prior = 0.2 * rows_total * prior.astype(jnp.float32)
-    targets = list(reversed(range(1, inner_size)))
-    parts = cross_blocks(targets, jnp.bfloat16, place, rebuilt, prior, local, pieces)
-    parts = [from_inner(part, target) for part, target in zip(parts, targets)]
-    (start,) = cross_blocks([0], jnp.float32, place, rebuilt, prior, local, pieces)
-    for part in parts:
-        start = start + part.astype(jnp.float32)
-    narrow = start.astype(jnp.bfloat16)
+    half = prior.shape[0] // 2
+    blocks_for = functools.partial(
+        cross_blocks, place=place, rebuilt=rebuilt, prior=prior, local=local, pieces=pieces
+    )
+    near = [(1, 2), (2, 1)]
+    sent = blocks_for([((one, 3), side * half) for side, (one, _) in enumerate(near)], jnp.bfloat16)
+    came = [from_inner(value, one) for value, (one, _) in zip(sent, near)]
+    kept = blocks_for(
+        [((0,), side * half) for side in range(2)]
+        + [((two,), side * half) for side, (_, two) in enumerate(near)],
+        jnp.float32,
+    )
+    starts = []
+    for side, (_, two) in enumerate(near):
+        passed = kept[2 + side] + came[side][half:].astype(jnp.float32)
+        last = from_inner(passed.astype(jnp.bfloat16), two)
+        starts.append(kept[side] + came[side][:half].astype(jnp.float32) + last.astype(jnp.float32))
+    narrow = [value.astype(jnp.bfloat16) for value in starts]
+    start = jnp.concatenate(starts, axis=0)
 
     def ring(value):
         pairs = [(i, (i + inner_size) % dp) for i in range(dp)]
         return lax.ppermute(value, "dp", pairs)
 
-    def move(key, source):
-        if key[0] != source[0]:
-            return ring(held[source])
-        return from_inner(held[source], key[1] ^ source[1])
-
-    own = narrow.T
-    held = {(0, 0): narrow}
+    own = jnp.concatenate(narrow, axis=0).T
+    held = [{(0, 0): value} for value in narrow]
+
+    def move(side, key, source):
+        value = held[side][source]
+        return ring(value) if key[0] != source[0] else from_inner(value, key[1] ^ source[1])
+
+    def halves(keys):
+        return [held[side][key] for key in keys for side in range(2)]
+
     order, products = [(0, 0)], []
     square = jnp.zeros((8, block), jnp.float32)
-    fresh = [narrow]
+    fresh = [(0, 0)]
     for moves in gather_rounds(outer_size):
-        arrived = [move(key, source) for key, source in moves]
-        product, square = apply_first(own, square, fresh)
-        arrived, product, square = lax.optimization_barrier((arrived, product, square))
-        held.update({key: value for (key, _), value in zip(moves, arrived)})
-        order += [key for key, _ in moves]
+        arrived = [[move(side, key, source) for key, source in moves] for side in range(2)]
+        product, square = apply_first(own, square, halves(fresh))
+        arrived[0], product, square = lax.optimization_barrier((arrived[0], product, square))
+        arrived[1] = lax.optimization_barrier(arrived[1])
+        fresh = [key for key, _ in moves]
+        for side in range(2):
+            held[side].update(zip(fresh, arrived[side]))
+        order += fresh
         products.append(both_cores(product))
-        fresh = arrived
-    product, square = apply_first(own, square, fresh)
+    product, square = apply_first(own, square, halves(fresh))
     products.append(both_cores(product))
-    panel = [held[key] for key in order]
+    panel = halves(order)
     squares = both_cores(square)
     first, product = apply_next(0, panel, products, squares, [start])
     state, product = apply_next(1, panel, [both_cores(product)], squares, [first])

time: 336 us -> 314 us (0.935)
  waiting for transfers between devices: 181 us -> 143 us
  starting transfers between devices: 27.9 us -> 38.8 us
    ppermute x13 -> x24, waiting for transfers between devices: 143 us -> 95 us  [from_inner(): return lax.ppermute(value, 'dp', pairs)]
    ppermute x13 -> x24, starting transfers between devices: 14 us -> 24.9 us  [from_inner(): return lax.ppermute(value, 'dp', pairs)]
    ppermute x5 -> x10, waiting for transfers between devices: 6.81 us -> 17.1 us  [ring(): return lax.ppermute(value, 'dp', pairs)]
  transfers between devices with their start and end apart: 37 -> 53, of which waited for: 22 -> 30; matrix products, arithmetic and copies ran while one was open for 9% -> 11% of each run, Pallas kernels for 11% -> 13%
where the time goes in v8:
time: 314 us; the launch traced here: 308 us
  waiting for transfers between devices  143 us (46%)
  Pallas kernels  87 us (28%)
  starting transfers between devices  38.8 us (12%)
  matrix products  12.6 us (4%)
  local copies, waits for them, and re-layouts  12 us (4%)
  other arithmetic  11.9 us (4%)
    ppermute x24, waiting for transfers between devices, from_inner(): return lax.ppermute(value, 'dp', pairs)  95 us
    pallas_call x4, Pallas kernels, apply_next(): pl.pallas_call(functools.partial(next_kernel, step, blocks, len(inner)),...  40.7 us
    pallas_call x2, Pallas kernels, rebuild_rows(): pl.pallas_call(lookup_kernel, grid=(subs // tile, blocks), in_specs=[pl.B...  26.4 us
    ppermute x24, starting transfers between devices, from_inner(): return lax.ppermute(value, 'dp', pairs)  24.9 us
    ppermute x10, waiting for transfers between devices, ring(): return lax.ppermute(value, 'dp', pairs)  17.1 us
    ppermute x6, waiting for transfers between devices, from_outer(): return lax.ppermute(value, 'dp', pairs)  15.5 us
    ppermute x10, waiting for transfers between devices, swap_cores(): return lax.ppermute(value, 'col', [(0, 1), (1, 0)])  12.6 us
    dot_general x1, matrix products, shards(): lax.dot_general(rotation, embeddings, (((0,), (1,)), ((), ())), preferred...  12.6 us
  transfers between devices with their start and end apart: 53, of which 30 were waited for; matrix products, arithmetic and copies ran while one was open for 11% of the time, Pallas kernels for 13%

profile of v8, /device:TPU:0, one launch (start us, length us, event | category | flops | bytes accessed | tf_op | source)
XLA Modules:
  0.0 308.5 jit_solution(1321741790247947317)
XLA Ops:
  2.1 4.0 %collective-permute-start.4 = (bf16[256,512]{1,0:T(8,128)(2,1)}, bf16[256,512]{1,0:T(8,128)(2,1)}, u32[]{:S(2)}, u32[]{:S(2)}) collective-permute-start(bf16[256,512]{1,0:T(8,128)(2,1)} %get-tuple-element.148), channel_id=1, source_target_pairs={{0,16},{2,18},{4,20},{6,22},{8,24},{10,26},{12,28},{14,30},{16,0},... | collective-permute-start | bytes 786440 | tf_op jit(solution)/shard_map/ppermute | solution.py:279
  7.9 5.3 %lookup.2 = bf16[2048,512]{1,0:T(8,128)(2,1)S(1)} custom-call(bf16[1,256,512]{2,1,0:T(8,128)(2,1)S(1)} %get-tuple-element.149.codes_ref, f32[256,8,256]{2,1,0:T(8,128)S(1)} %convert_bitcast_fusion.table_ref), custom_call_target="tpu_custom_call" | custom-call | tf_op jit(solution)/shard_map/lookup/pallas_call | solution.py:58
  13.2 12.6 %multiply_reduce_fusion = f32[512]{0:T(512)S(1)} fusion(bf16[2048,512]{1,0:T(8,128)(2,1)S(1)} %lookup.2, bf16[4096,2048]{1,0:T(8,128)(2,1)} %param.5, bf16[512,4096]{1,0:T(8,128)(2,1)S(1)} %copy-done.2), kind=kOutput, calls=%fused_computation.1 | convolution fusion | flops 8594128896 | bytes 23070720 | tf_op jit(solution)/shard_map/dot_general | solution.py:291
  28.5 5.6 %multiply_convert_fusion = bf16[512,4096]{1,0:T(8,128)(2,1)} fusion(bf16[512,4096]{1,0:T(8,128)(2,1)} %param.4, f32[512]{0:T(512)S(1)} %add_divide_fusion), kind=kLoop, calls=%fused_computation | loop fusion | flops 6291456 | bytes 8390656 | tf_op jit(solution)/shard_map/convert_element_type | solution.py:297
  48.3 21.1 %lookup.3.rebuilt_ref = bf16[2048,2048]{1,0:T(8,128)(2,1)S(1)} custom-call(bf16[4,256,512]{2,1,0:T(8,128)(2,1)S(1)} %pad_maximum_fusion.1.codes_ref, f32[256,8,256]{2,1,0:T(8,128)S(1)} %convert_bitcast_fusion.table_ref), custom_call_target="tpu_custom_call" | custom-call | tf_op jit(solution)/shard_map/lookup/pallas_call | solution.py:58
  69.4 15.5 %collective-permute-done.1.refs_2_ = bf16[256,1024]{1,0:T(8,128)(2,1)S(1)} collective-permute-done((bf16[256,1024]{1,0:T(8,128)(2,1)}, bf16[256,1024]{1,0:T(8,128)(2,1)S(1)}, u32[]{:S(2)}, u32[]{:S(2)}) %collective-permute-start.1) | collective-permute-done | bytes 524320 | tf_op jit(solution)/shard_map/ppermute | solution.py:279
  88.3 5.6 %cross.3 = (bf16[2048,256]{1,0:T(8,128)(2,1)S(1)}, bf16[2048,256]{1,0:T(8,128)(2,1)S(1)}) custom-call(s32[2]{0:T(128)S(1)} %pad_add_fusion.place_ref, bf16[2048,2048]{1,0:T(8,128)(2,1)S(1)} %lookup.3.rebuilt_ref, f32[2048,256]{1,0:T(8,128)S(1)} %multiply_bitcast_fusion.prior_ref, bf16[512,1024]{1,0:T(8,128)(2,1)S(1)} %constant_dynamic-slice_fusion.local_ref, ...), custom_call_target="tpu_custom_call" | custom-call | tf_op jit(solution)/shard_map/cross/pallas_call | solution.py:102
  97.0 5.6 %cross.2 = (f32[1024,256]{1,0:T(8,128)S(1)}, f32[1024,256]{1,0:T(8,128)S(1)}, f32[1024,256]{1,0:T(8,128)S(1)}, f32[1024,256]{1,0:T(8,128)S(1)}) custom-call(s32[2]{0:T(128)S(1)} %pad_add_fusion.place_ref, bf16[2048,2048]{1,0:T(8,128)(2,1)S(1)} %lookup.3.rebuilt_ref, f32[2048,256]{1,0:T(8,128)S(1)} %multiply_bitcast_fusion.prior_ref, ...), custom_call_target="tpu_custom_call" | custom-call | tf_op jit(solution)/shard_map/cross/pallas_call | solution.py:102
  102.6 16.6 %collective-permute-done.11 = bf16[2048,256]{1,0:T(8,128)(2,1)S(1)} collective-permute-done((bf16[2048,256]{1,0:T(8,128)(2,1)S(1)}, bf16[2048,256]{1,0:T(8,128)(2,1)S(1)}, u32[]{:S(2)}, u32[]{:S(2)}) %collective-permute-start.11) | collective-permute-done | bytes 1048608 | tf_op jit(solution)/shard_map/ppermute | solution.py:283
  122.6 9.9 %collective-permute-done.12 = bf16[1024,256]{1,0:T(8,128)(2,1)S(1)} collective-permute-done((bf16[1024,256]{1,0:T(8,128)(2,1)S(1)}, bf16[1024,256]{1,0:T(8,128)(2,1)S(1)}, u32[]{:S(2)}, u32[]{:S(2)}) %collective-permute-start.12) | collective-permute-done | bytes 524320 | tf_op jit(solution)/shard_map/ppermute | solution.py:283
  138.9 9.6 %collective-permute-done.21.refs_5_.refs_7_ = bf16[1024,256]{1,0:T(8,128)(2,1)S(1)} collective-permute-done((bf16[1024,256]{1,0:T(8,128)(2,1)S(1)}, bf16[1024,256]{1,0:T(8,128)(2,1)S(1)}, u32[]{:S(2)}, u32[]{:S(2)}) %collective-permute-start.21) | collective-permute-done | bytes 524320 | tf_op jit(solution)/shard_map/ppermute | solution.py:283
  152.4 7.3 %collective-permute-done.15.refs_4_.refs_6_ = bf16[1024,256]{1,0:T(8,128)(2,1)S(1)} collective-permute-done((bf16[1024,256]{1,0:T(8,128)(2,1)S(1)}, bf16[1024,256]{1,0:T(8,128)(2,1)S(1)}, u32[]{:S(2)}, u32[]{:S(2)}) %collective-permute-start.15) | collective-permute-done | bytes 524320 | tf_op jit(solution)/shard_map/ppermute | solution.py:283
  176.8 5.4 %collective-permute-done.18.refs_4_.refs_12_ = bf16[1024,256]{1,0:T(8,128)(2,1)S(1)} collective-permute-done((bf16[1024,256]{1,0:T(8,128)(2,1)}, bf16[1024,256]{1,0:T(8,128)(2,1)S(1)}, u32[]{:S(2)}, u32[]{:S(2)}) %collective-permute-start.18) | collective-permute-done | bytes 524320 | tf_op jit(solution)/shard_map/ppermute | solution.py:283
  188.0 5.4 %collective-permute-done.33.refs_5_.refs_19_ = bf16[1024,256]{1,0:T(8,128)(2,1)S(1)} collective-permute-done((bf16[1024,256]{1,0:T(8,128)(2,1)}, bf16[1024,256]{1,0:T(8,128)(2,1)S(1)}, u32[]{:S(2)}, u32[]{:S(2)}) %collective-permute-start.33) | collective-permute-done | bytes 524320 | tf_op jit(solution)/shard_map/ppermute | solution.py:283
  198.0 6.7 %collective-permute-done.24.refs_4_.refs_18_ = bf16[1024,256]{1,0:T(8,128)(2,1)S(1)} collective-permute-done((bf16[1024,256]{1,0:T(8,128)(2,1)S(1)}, bf16[1024,256]{1,0:T(8,128)(2,1)S(1)}, u32[]{:S(2)}, u32[]{:S(2)}) %collective-permute-start.24) | collective-permute-done | bytes 524320 | tf_op jit(solution)/shard_map/ppermute | solution.py:283
  210.7 6.7 %collective-permute-done.39.refs_5_.refs_25_ = bf16[1024,256]{1,0:T(8,128)(2,1)S(1)} collective-permute-done((bf16[1024,256]{1,0:T(8,128)(2,1)S(1)}, bf16[1024,256]{1,0:T(8,128)(2,1)S(1)}, u32[]{:S(2)}, u32[]{:S(2)}) %collective-permute-start.39) | collective-permute-done | bytes 524320 | tf_op jit(solution)/shard_map/ppermute | solution.py:283
  219.5 9.2 %collective-permute-done.30.refs_4_.refs_24_ = bf16[1024,256]{1,0:T(8,128)(2,1)S(1)} collective-permute-done((bf16[1024,256]{1,0:T(8,128)(2,1)S(1)}, bf16[1024,256]{1,0:T(8,128)(2,1)S(1)}, u32[]{:S(2)}, u32[]{:S(2)}) %collective-permute-start.30) | collective-permute-done | bytes 524320 | tf_op jit(solution)/shard_map/ppermute | solution.py:283
  230.9 7.5 %collective-permute-done.41.refs_3_.refs_29_ = bf16[1024,256]{1,0:T(8,128)(2,1)S(1)} collective-permute-done((bf16[1024,256]{1,0:T(8,128)(2,1)S(1)}, bf16[1024,256]{1,0:T(8,128)(2,1)S(1)}, u32[]{:S(2)}, u32[]{:S(2)}) %collective-permute-start.41) | collective-permute-done | bytes 524320 | tf_op jit(solution)/shard_map/ppermute | solution.py:283
  239.9 5.5 %collective-permute-done.40.refs_1_.refs_27_ = bf16[1024,256]{1,0:T(8,128)(2,1)S(1)} collective-permute-done((bf16[1024,256]{1,0:T(8,128)(2,1)S(1)}, bf16[1024,256]{1,0:T(8,128)(2,1)S(1)}, u32[]{:S(2)}, u32[]{:S(2)}) %collective-permute-start.40) | collective-permute-done | bytes 524320 | tf_op jit(solution)/shard_map/ppermute | solution.py:343
  247.0 4.2 %collective-permute-done.34.refs_0_.refs_26_ = bf16[1024,256]{1,0:T(8,128)(2,1)S(1)} collective-permute-done((bf16[1024,256]{1,0:T(8,128)(2,1)S(1)}, bf16[1024,256]{1,0:T(8,128)(2,1)S(1)}, u32[]{:S(2)}, u32[]{:S(2)}) %collective-permute-start.34) | collective-permute-done | bytes 524320 | tf_op jit(solution)/shard_map/ppermute | solution.py:343
  254.8 10.9 %apply0.1 = (f32[2048,256]{1,0:T(8,128)S(1)}, bf16[4096,256]{1,0:T(8,128)(2,1)S(1)}) custom-call(f32[8,256]{1,0:T(8,128)S(1)} %get-tuple-element.128.mine_square_ref, f32[8,256]{1,0:T(8,128)S(1)} %collective-permute-done.43.other_square_ref, bf16[1024,256]{1,0:T(8,128)(2,1)S(1)} %get-tuple-element.141.refs_0_, ...), custom_call_target="tpu_custom_call" | custom-call | tf_op jit(solution)/shard_map/apply0/pallas_call | solution.py:216
  270.0 11.1 %apply1.1 = (f32[2048,256]{1,0:T(8,128)S(1)}, bf16[4096,256]{1,0:T(8,128)(2,1)S(1)}) custom-call(f32[8,256]{1,0:T(8,128)S(1)} %get-tuple-element.128.mine_square_ref, f32[8,256]{1,0:T(8,128)S(1)} %collective-permute-done.43.other_square_ref, bf16[1024,256]{1,0:T(8,128)(2,1)S(1)} %get-tuple-element.141.refs_0_, ...), custom_call_target="tpu_custom_call" | custom-call | tf_op jit(solution)/shard_map/apply1/pallas_call | solution.py:216
  285.3 10.9 %apply2.1 = (f32[2048,256]{1,0:T(8,128)S(1)}, bf16[4096,256]{1,0:T(8,128)(2,1)S(1)}) custom-call(f32[8,256]{1,0:T(8,128)S(1)} %get-tuple-element.128.mine_square_ref, f32[8,256]{1,0:T(8,128)S(1)} %collective-permute-done.43.other_square_ref, bf16[1024,256]{1,0:T(8,128)(2,1)S(1)} %get-tuple-element.141.refs_0_, ...), custom_call_target="tpu_custom_call" | custom-call | tf_op jit(solution)/shard_map/apply2/pallas_call | solution.py:216
  300.4 7.9 %apply3.1 = f32[256,2048]{1,0:T(8,128)} custom-call(f32[8,256]{1,0:T(8,128)S(1)} %get-tuple-element.128.mine_square_ref, f32[8,256]{1,0:T(8,128)S(1)} %collective-permute-done.43.other_square_ref, bf16[1024,256]{1,0:T(8,128)(2,1)S(1)} %get-tuple-element.141.refs_0_, bf16[1024,256]{1,0:T(8,128)(2,1)S(1)} %get-tuple-element.143.refs_1_, ...), custom_call_target="tpu_custom_call" | custom-call | tf_op jit(solution)/shard_map/apply3/pallas_call | solution.py:216
  (132 shorter events, 97.8 us)
Async XLA Ops:
  2.1 38.4 %collective-permute-start.4 = (bf16[256,512]{1,0:T(8,128)(2,1)}, bf16[256,512]{1,0:T(8,128)(2,1)}, u32[]{:S(2)}, u32[]{:S(2)}) collective-permute-start(bf16[256,512]{1,0:T(8,128)(2,1)} %get-tuple-element.148), channel_id=1, source_target_pairs={{0,16},{2,18},{4,20},{6,22},{8,24},{10,26},{12,28},{14,30},{16,0},... | collective-permute-start | bytes 786440 | tf_op jit(solution)/shard_map/ppermute | solution.py:279
  6.1 40.8 %collective-permute-start.3 = (bf16[256,512]{1,0:T(8,128)(2,1)}, bf16[256,512]{1,0:T(8,128)(2,1)}, u32[]{:S(2)}, u32[]{:S(2)}) collective-permute-start(bf16[256,512]{1,0:T(8,128)(2,1)} %get-tuple-element.148), channel_id=1, source_target_pairs={{0,8},{2,10},{4,12},{6,14},{8,0},{10,2},{12,4},{14,6},{16,24},{18,... | collective-permute-start | bytes 786440 | tf_op jit(solution)/shard_map/ppermute | solution.py:279
  7.7 39.3 %collective-permute-start.5 = (bf16[256,512]{1,0:T(8,128)(2,1)}, bf16[256,512]{1,0:T(8,128)(2,1)}, u32[]{:S(2)}, u32[]{:S(2)}) collective-permute-start(bf16[256,512]{1,0:T(8,128)(2,1)} %get-tuple-element.148), channel_id=1, source_target_pairs={{0,24},{2,26},{4,28},{6,30},{8,16},{10,18},{12,20},{14,22},{16,8},... | collective-permute-start | bytes 786440 | tf_op jit(solution)/shard_map/ppermute | solution.py:279
  36.7 32.8 %collective-permute-start.2 = (bf16[256,1024]{1,0:T(8,128)(2,1)}, bf16[256,1024]{1,0:T(8,128)(2,1)S(1)}, u32[]{:S(2)}, u32[]{:S(2)}) collective-permute-start(bf16[256,1024]{1,0:T(8,128)(2,1)} %get-tuple-element.145), channel_id=1, source_target_pairs={{0,24},{2,26},{4,28},{6,30},{8,16},{10,18},{12,20},{14,22},{16,8},... | collective-permute-start | bytes 1572872 | tf_op jit(solution)/shard_map/ppermute | solution.py:279
  40.5 44.4 %collective-permute-start.1 = (bf16[256,1024]{1,0:T(8,128)(2,1)}, bf16[256,1024]{1,0:T(8,128)(2,1)S(1)}, u32[]{:S(2)}, u32[]{:S(2)}) collective-permute-start(bf16[256,1024]{1,0:T(8,128)(2,1)} %get-tuple-element.146), channel_id=1, source_target_pairs={{0,16},{2,18},{4,20},{6,22},{8,24},{10,26},{12,28},{14,30},{16,0},... | collective-permute-start | bytes 1572872 | tf_op jit(solution)/shard_map/ppermute | solution.py:279
  40.5 44.4 %collective-permute-start = (bf16[256,1024]{1,0:T(8,128)(2,1)}, bf16[256,1024]{1,0:T(8,128)(2,1)}, u32[]{:S(2)}, u32[]{:S(2)}) collective-permute-start(bf16[256,1024]{1,0:T(8,128)(2,1)} %get-tuple-element.147), channel_id=1, source_target_pairs={{0,8},{2,10},{4,12},{6,14},{8,0},{10,2},{12,4},{14,6},{16,24},{18,... | collective-permute-start | bytes 1572872 | tf_op jit(solution)/shard_map/ppermute | solution.py:279
  93.9 25.3 %collective-permute-start.11 = (bf16[2048,256]{1,0:T(8,128)(2,1)S(1)}, bf16[2048,256]{1,0:T(8,128)(2,1)S(1)}, u32[]{:S(2)}, u32[]{:S(2)}) collective-permute-start(bf16[2048,256]{1,0:T(8,128)(2,1)S(1)} %get-tuple-element.81), channel_id=1, source_target_pairs={{0,4},{2,6},{4,0},{6,2},{8,12},{10,14},{12,8},{14,10},{16,20},{18,... | collective-permute-start | bytes 3145736 | tf_op jit(solution)/shard_map/ppermute | solution.py:283
  95.5 25.4 %collective-permute-start.9 = (bf16[2048,256]{1,0:T(8,128)(2,1)S(1)}, bf16[2048,256]{1,0:T(8,128)(2,1)S(1)}, u32[]{:S(2)}, u32[]{:S(2)}) collective-permute-start(bf16[2048,256]{1,0:T(8,128)(2,1)S(1)} %get-tuple-element.78), channel_id=1, source_target_pairs={{0,2},{2,0},{4,6},{6,4},{8,10},{10,8},{12,14},{14,12},{16,18},{18,... | collective-permute-start | bytes 3145736 | tf_op jit(solution)/shard_map/ppermute | solution.py:283
  137.9 21.9 %collective-permute-start.15 = (bf16[1024,256]{1,0:T(8,128)(2,1)S(1)}, bf16[1024,256]{1,0:T(8,128)(2,1)S(1)}, u32[]{:S(2)}, u32[]{:S(2)}) collective-permute-start(bf16[1024,256]{1,0:T(8,128)(2,1)S(1)} %get-tuple-element.141.refs_0_), channel_id=1, source_target_pairs={{0,4},{2,6},{4,0},{6,2},{8,12},{10,14},{12,8},{14,10},{16,20},{18,... | collective-permute-start | bytes 1572872 | tf_op jit(solution)/shard_map/ppermute | solution.py:283
  138.4 25.6 %collective-permute-start.14 = (bf16[1024,256]{1,0:T(8,128)(2,1)S(1)}, bf16[1024,256]{1,0:T(8,128)(2,1)}, u32[]{:S(2)}, u32[]{:S(2)}) collective-permute-start(bf16[1024,256]{1,0:T(8,128)(2,1)S(1)} %get-tuple-element.141.refs_0_), channel_id=1, source_target_pairs={{0,2},{2,0},{4,6},{6,4},{8,10},{10,8},{12,14},{14,12},{16,18},{18,... | collective-permute-start | bytes 1572872 | tf_op jit(solution)/shard_map/ppermute | solution.py:283
  152.4 18.7 %collective-permute-start.27 = (bf16[1024,256]{1,0:T(8,128)(2,1)}, bf16[1024,256]{1,0:T(8,128)(2,1)}, u32[]{:S(2)}, u32[]{:S(2)}) collective-permute-start(bf16[1024,256]{1,0:T(8,128)(2,1)} %collective-permute-done.19.refs_1_.refs_3_), channel_id=1, source_target_pairs={{0,4},{2,6},{4,0},{6,2},{8,12},{10,14},{12,8},{14,10},{16,20},{18,... | collective-permute-start | bytes 1572872 | tf_op jit(solution)/shard_map/ppermute | solution.py:283
  152.4 20.2 %collective-permute-start.26 = (bf16[1024,256]{1,0:T(8,128)(2,1)}, bf16[1024,256]{1,0:T(8,128)(2,1)}, u32[]{:S(2)}, u32[]{:S(2)}) collective-permute-start(bf16[1024,256]{1,0:T(8,128)(2,1)} %collective-permute-done.19.refs_1_.refs_3_), channel_id=1, source_target_pairs={{0,2},{2,0},{4,6},{6,4},{8,10},{10,8},{12,14},{14,12},{16,18},{18,... | collective-permute-start | bytes 1572872 | tf_op jit(solution)/shard_map/ppermute | solution.py:283
  165.6 19.0 %collective-permute-start.17 = (bf16[1024,256]{1,0:T(8,128)(2,1)}, bf16[1024,256]{1,0:T(8,128)(2,1)S(1)}, u32[]{:S(2)}, u32[]{:S(2)}) collective-permute-start(bf16[1024,256]{1,0:T(8,128)(2,1)} %collective-permute-done.13.refs_0_.refs_2_), channel_id=1, source_target_pairs={{0,2},{2,0},{4,6},{6,4},{8,10},{10,8},{12,14},{14,12},{16,18},{18,... | collective-permute-start | bytes 1572872 | tf_op jit(solution)/shard_map/ppermute | solution.py:283
  174.7 18.8 %collective-permute-start.33 = (bf16[1024,256]{1,0:T(8,128)(2,1)}, bf16[1024,256]{1,0:T(8,128)(2,1)S(1)}, u32[]{:S(2)}, u32[]{:S(2)}) collective-permute-start(bf16[1024,256]{1,0:T(8,128)(2,1)} %collective-permute-done.25.refs_1_.refs_9_), channel_id=1, source_target_pairs={{0,4},{2,6},{4,0},{6,2},{8,12},{10,14},{12,8},{14,10},{16,20},{18,... | collective-permute-start | bytes 1572872 | tf_op jit(solution)/shard_map/ppermute | solution.py:283
  175.3 19.7 %collective-permute-start.32 = (bf16[1024,256]{1,0:T(8,128)(2,1)}, bf16[1024,256]{1,0:T(8,128)(2,1)S(1)}, u32[]{:S(2)}, u32[]{:S(2)}) collective-permute-start(bf16[1024,256]{1,0:T(8,128)(2,1)} %collective-permute-done.25.refs_1_.refs_9_), channel_id=1, source_target_pairs={{0,2},{2,0},{4,6},{6,4},{8,10},{10,8},{12,14},{14,12},{16,18},{18,... | collective-permute-start | bytes 1572872 | tf_op jit(solution)/shard_map/ppermute | solution.py:283
  185.9 18.8 %collective-permute-start.24 = (bf16[1024,256]{1,0:T(8,128)(2,1)S(1)}, bf16[1024,256]{1,0:T(8,128)(2,1)S(1)}, u32[]{:S(2)}, u32[]{:S(2)}) collective-permute-start(bf16[1024,256]{1,0:T(8,128)(2,1)S(1)} %collective-permute-done.16.refs_0_.refs_8_), channel_id=1, source_target_pairs={{0,4},{2,6},{4,0},{6,2},{8,12},{10,14},{12,8},{14,10},{16,20},{18,... | collective-permute-start | bytes 1572872 | tf_op jit(solution)/shard_map/ppermute | solution.py:283
  186.5 19.7 %collective-permute-start.23 = (bf16[1024,256]{1,0:T(8,128)(2,1)S(1)}, bf16[1024,256]{1,0:T(8,128)(2,1)S(1)}, u32[]{:S(2)}, u32[]{:S(2)}) collective-permute-start(bf16[1024,256]{1,0:T(8,128)(2,1)S(1)} %collective-permute-done.16.refs_0_.refs_8_), channel_id=1, source_target_pairs={{0,2},{2,0},{4,6},{6,4},{8,10},{10,8},{12,14},{14,12},{16,18},{18,... | collective-permute-start | bytes 1572872 | tf_op jit(solution)/shard_map/ppermute | solution.py:283
  195.0 22.5 %collective-permute-start.39 = (bf16[1024,256]{1,0:T(8,128)(2,1)S(1)}, bf16[1024,256]{1,0:T(8,128)(2,1)S(1)}, u32[]{:S(2)}, u32[]{:S(2)}) collective-permute-start(bf16[1024,256]{1,0:T(8,128)(2,1)S(1)} %collective-permute-done.21.refs_5_.refs_7_), channel_id=1, source_target_pairs={{0,2},{2,0},{4,6},{6,4},{8,10},{10,8},{12,14},{14,12},{16,18},{18,... | collective-permute-start | bytes 1572872 | tf_op jit(solution)/shard_map/ppermute | solution.py:283
  197.4 20.1 %collective-permute-start.38 = (bf16[1024,256]{1,0:T(8,128)(2,1)S(1)}, bf16[1024,256]{1,0:T(8,128)(2,1)S(1)}, u32[]{:S(2)}, u32[]{:S(2)}) collective-permute-start(bf16[1024,256]{1,0:T(8,128)(2,1)S(1)} %collective-permute-done.31.refs_1_.refs_15_), channel_id=1, source_target_pairs={{0,4},{2,6},{4,0},{6,2},{8,12},{10,14},{12,8},{14,10},{16,20},{18,... | collective-permute-start | bytes 1572872 | tf_op jit(solution)/shard_map/ppermute | solution.py:283
  206.2 22.5 %collective-permute-start.30 = (bf16[1024,256]{1,0:T(8,128)(2,1)S(1)}, bf16[1024,256]{1,0:T(8,128)(2,1)S(1)}, u32[]{:S(2)}, u32[]{:S(2)}) collective-permute-start(bf16[1024,256]{1,0:T(8,128)(2,1)S(1)} %copy-done.1), channel_id=1, source_target_pairs={{0,2},{2,0},{4,6},{6,4},{8,10},{10,8},{12,14},{14,12},{16,18},{18,... | collective-permute-start | bytes 1572872 | tf_op jit(solution)/shard_map/ppermute | solution.py:283
  210.2 19.6 %collective-permute-start.29 = (bf16[1024,256]{1,0:T(8,128)(2,1)S(1)}, bf16[1024,256]{1,0:T(8,128)(2,1)S(1)}, u32[]{:S(2)}, u32[]{:S(2)}) collective-permute-start(bf16[1024,256]{1,0:T(8,128)(2,1)S(1)} %collective-permute-done.22.refs_0_.refs_14_), channel_id=1, source_target_pairs={{0,4},{2,6},{4,0},{6,2},{8,12},{10,14},{12,8},{14,10},{16,20},{18,... | collective-permute-start | bytes 1572872 | tf_op jit(solution)/shard_map/ppermute | solution.py:283
  217.5 20.9 %collective-permute-start.41 = (bf16[1024,256]{1,0:T(8,128)(2,1)S(1)}, bf16[1024,256]{1,0:T(8,128)(2,1)S(1)}, u32[]{:S(2)}, u32[]{:S(2)}) collective-permute-start(bf16[1024,256]{1,0:T(8,128)(2,1)S(1)} %collective-permute-done.32.refs_3_.refs_17_), channel_id=1, source_target_pairs={{0,4},{2,6},{4,0},{6,2},{8,12},{10,14},{12,8},{14,10},{16,20},{18,... | collective-permute-start | bytes 1572872 | tf_op jit(solution)/shard_map/ppermute | solution.py:283
  218.9 21.0 %collective-permute-start.42 = (bf16[1024,256]{1,0:T(8,128)(2,1)S(1)}, bf16[1024,256]{1,0:T(8,128)(2,1)S(1)}, u32[]{:S(2)}, u32[]{:S(2)}) collective-permute-start(bf16[1024,256]{1,0:T(8,128)(2,1)S(1)} %collective-permute-done.38.refs_3_.refs_23_), channel_id=1, source_target_pairs={{0,2},{2,0},{4,6},{6,4},{8,10},{10,8},{12,14},{14,12},{16,18},{18,... | collective-permute-start | bytes 1572872 | tf_op jit(solution)/shard_map/ppermute | solution.py:283
  230.4 20.9 %collective-permute-start.34 = (bf16[1024,256]{1,0:T(8,128)(2,1)S(1)}, bf16[1024,256]{1,0:T(8,128)(2,1)S(1)}, u32[]{:S(2)}, u32[]{:S(2)}) collective-permute-start(bf16[1024,256]{1,0:T(8,128)(2,1)S(1)} %collective-permute-done.30.refs_4_.refs_24_), channel_id=1, source_target_pairs={{0,8},{2,10},{4,12},{6,14},{8,16},{10,18},{12,20},{14,22},{16,24},... | collective-permute-start | bytes 1572872 | tf_op jit(solution)/shard_map/ppermute | solution.py:343
  (36 other events, 373.8 us)

commit v9 on v8

--- a/solution.py
+++ b/solution.py
@@ -133,36 +133,55 @@
     square_ref[...] = square
 
 
-def next_kernel(step, blocks, parts, mine_square_ref, other_square_ref, *refs):
-    last = step == 3
-    states = 2 if last else 1
-    panel, refs = refs[: 2 * blocks], refs[2 * blocks :]
-    mine, other, refs = refs[:parts], refs[parts : 2 * parts], refs[2 * parts :]
-    held, refs = refs[:states], refs[states:]
-    if last:
-        out_ref, sum_ref = refs
-    else:
-        state_ref, inner_ref, sum_ref, value_ref = refs
-    half, block = panel[0].shape
-    model_width = blocks * block
-    chunk = 2 * half // CHUNKS
-    total = jnp.sum(mine_square_ref[...] + other_square_ref[...], axis=(0, 1), keepdims=True)
-    scale = model_width / (1.96 * total)
+def add_up(mine, other, sum_ref):
     first = 0
     for mine_ref, other_ref in zip(mine, other):
         sum_ref[first : first + mine_ref.shape[0], :] = mine_ref[...] + other_ref[...]
         first += mine_ref.shape[0]
 
+
+def gram_rows(panel, sum_ref, index):
+    half, block = panel[0].shape
+    chunk = 2 * half // CHUNKS
+    side, first = divmod(index * chunk, half)
+    made = jnp.zeros((chunk, block), jnp.float32)
+    for owner in range(len(panel) // 2):
+        made += jnp.dot(
+            panel[2 * owner + side][first : first + chunk, :],
+            sum_ref[owner * block : (owner + 1) * block, :],
+            preferred_element_type=jnp.float32,
+        )
+    return slice(index * chunk, (index + 1) * chunk), made
+
+
+def early_kernel(blocks, parts, *refs):
+    panel, refs = refs[: 2 * blocks], refs[2 * blocks :]
+    mine, other, (out_ref, sum_ref) = refs[:parts], refs[parts : 2 * parts], refs[2 * parts :]
+    add_up(mine, other, sum_ref)
     for index in range(CHUNKS):
-        span = slice(index * chunk, (index + 1) * chunk)
-        side, first = divmod(index * chunk, half)
-        made = jnp.zeros((chunk, block), jnp.float32)
-        for owner in range(blocks):
-            made += jnp.dot(
-                panel[2 * owner + side][first : first + chunk, :],
-                sum_ref[owner * block : (owner + 1) * block, :],
-                preferred_element_type=jnp.float32,
-            )
+        span, made = gram_rows(panel, sum_ref, index)
+        out_ref[span, :] = made
+
+
+def late_kernel(step, blocks, parts, mine_square_ref, other_square_ref, *refs):
+    last = step == 3
+    states = 2 if last else 1
+    first_late, late = blocks
+    panel, refs = refs[: 2 * (first_late + late)], refs[2 * (first_late + late) :]
+    mine, other, refs = refs[:parts], refs[parts : 2 * parts], refs[2 * parts :]
+    early_ref, held, refs = refs[0], refs[1 : 1 + states], refs[1 + states :]
+    if last:
+        out_ref, sum_ref = refs
+    else:
+        state_ref, value_ref, inner_ref, sum_ref = refs
+    half, block = panel[0].shape
+    model_width = (first_late + late) * block
+    total = jnp.sum(mine_square_ref[...] + other_square_ref[...], axis=(0, 1), keepdims=True)
+    scale = model_width / (1.96 * total)
+    add_up(mine, other, sum_ref)
+    for index in range(CHUNKS):
+        span, made = gram_rows(panel[2 * first_late :], sum_ref, index)
+        made += early_ref[span, :]
         if step == 2:
             made = made * scale
         else:
@@ -175,7 +194,13 @@
             value_ref[:, span] = made.T.astype(value_ref.dtype)
     if last:
         return
-    for index in range(blocks):
+    for index in range(inner_ref.shape[0] // block):
+        product_of(value_ref, panel[2 * index : 2 * index + 2], inner_ref, index)
+
+
+def rest_kernel(value_ref, *refs):
+    panel, inner_ref = refs[:-1], refs[-1]
+    for index in range(len(panel) // 2):
         product_of(value_ref, panel[2 * index : 2 * index + 2], inner_ref, index)
 
 
@@ -198,29 +223,58 @@
     )(*in_vmem(own, square, *panel))
 
 
-def apply_next(step, panel, inner, squares, held):
+def apply_early(panel, inner):
+    half, block = panel[0].shape
+    blocks = len(panel) // 2
+    mine, other = zip(*inner)
+    operands = in_vmem(*panel, *mine, *other)
+    return pl.pallas_call(
+        functools.partial(early_kernel, blocks, len(inner)),
+        in_specs=[VMEM] * len(operands),
+        out_specs=VMEM,
+        out_shape=pltpu.VMEM((2 * half, block), jnp.float32),
+        scratch_shapes=[pltpu.VMEM((blocks * block, block), jnp.bfloat16)],
+        compiler_params=pltpu.CompilerParams(vmem_limit_bytes=VMEM_BYTES),
+        name="early",
+    )(*operands)
+
+
+def apply_late(step, early, panel, inner, squares, held):
     half, block = panel[0].shape
     blocks, cols = len(panel) // 2, 2 * half
+    late = sum(mine.shape[0] for mine, _ in inner) // block
     last = step == 3
     if last:
         out_shape = jax.ShapeDtypeStruct((block, cols), jnp.float32)
-        value = []
     else:
         out_shape = [
             pltpu.VMEM((cols, block), jnp.float32),
-            pltpu.VMEM((blocks * block, block), jnp.bfloat16),
+            pltpu.VMEM((block, cols), jnp.bfloat16),
+            pltpu.VMEM((blocks // 2 * block, block), jnp.bfloat16),
         ]
-        value = [pltpu.VMEM((block, cols), jnp.bfloat16)]
     mine, other = zip(*inner)
-    operands = in_vmem(*squares, *panel, *mine, *other, *held)
-    return pl.pallas_call(
-        functools.partial(next_kernel, step, blocks, len(inner)),
+    operands = in_vmem(*squares, *panel, *mine, *other, early, *held)
+    return pl.pallas_call(
+        functools.partial(late_kernel, step, (blocks - late, late), len(inner)),
         in_specs=[VMEM] * len(operands),
-        out_specs=VMEM if last else [VMEM, VMEM],
+        out_specs=VMEM if last else [VMEM] * 3,
         out_shape=out_shape,
-        scratch_shapes=[pltpu.VMEM((blocks * block, block), jnp.bfloat16)] + value,
-        compiler_params=pltpu.CompilerParams(vmem_limit_bytes=VMEM_BYTES),
-        name="apply%d" % step,
+        scratch_shapes=[pltpu.VMEM((late * block, block), jnp.bfloat16)],
+        compiler_params=pltpu.CompilerParams(vmem_limit_bytes=VMEM_BYTES),
+        name="late%d" % step,
+    )(*operands)
+
+
+def apply_rest(value, panel):
+    block = panel[0].shape[1]
+    operands = in_vmem(value, *panel)
+    return pl.pallas_call(
+        rest_kernel,
+        in_specs=[VMEM] * len(operands),
+        out_specs=VMEM,
+        out_shape=pltpu.VMEM((len(panel) // 2 * block, block), jnp.bfloat16),
+        compiler_params=pltpu.CompilerParams(vmem_limit_bytes=VMEM_BYTES),
+        name="rest",
     )(*operands)
 
 
@@ -369,10 +423,19 @@
     products.append(both_cores(product))
     panel = halves(order)
     squares = both_cores(square)
-    first, product = apply_next(0, panel, products, squares, [start])
-    state, product = apply_next(1, panel, [both_cores(product)], squares, [first])
-    state, product = apply_next(2, panel, [both_cores(product)], squares, [state])
-    return apply_next(3, panel, [both_cores(product)], squares, [state, first])
+
+    first_late = sum(mine.shape[0] for mine, _ in products[:-2]) // block
+    early = apply_early(panel[: 2 * first_late], products[:-2])
+    inner = products[-2:]
+    states = [start]
+    middle = len(panel) // 2
+    for step in range(3):
+        state, value, product = apply_late(step, early, panel, inner, squares, states[-1:])
+        states.append(state)
+        product = both_cores(product)
+        inner = [both_cores(apply_rest(value, panel[middle:]))]
+        early = apply_early(panel[:middle], [product])
+    return apply_late(3, early, panel, inner, squares, [states[3], states[1]])
 
 
 def solution(mesh):

time: 314 us -> 311 us (level)
  waiting for transfers between devices: 143 us -> 130 us
  Pallas kernels: 87 us -> 96.4 us
    ppermute x10 -> x13, waiting for transfers between devices: 12.6 us -> 0.03 us  [swap_cores(): return lax.ppermute(value, 'col', [(0, 1), (1, 0)])]
    pallas_call x4 -> x11, Pallas kernels: 40.7 us -> 50.2 us  [the longest x4 25.5 us: apply_late(): pl.pallas_call(functools.partial(late_kernel, step, (blocks - late, late)...]
  transfers between devices with their start and end apart: 53 -> 56, of which waited for: 30 -> 26; matrix products, arithmetic and copies ran while one was open for 11% -> 11% of each run, Pallas kernels for 13% -> 21%
where the time goes in v9:
time: 311 us; the launch traced here: 306 us
  waiting for transfers between devices  130 us (42%)
  Pallas kernels  96.4 us (31%)
  starting transfers between devices  40.1 us (13%)
  matrix products  12.6 us (4%)
  local copies, waits for them, and re-layouts  12.1 us (4%)
  other arithmetic  12 us (4%)
    ppermute x24, waiting for transfers between devices, from_inner(): return lax.ppermute(value, 'dp', pairs)  94.3 us
    pallas_call x2, Pallas kernels, rebuild_rows(): pl.pallas_call(lookup_kernel, grid=(subs // tile, blocks), in_specs=[pl.B...  26.4 us
    ppermute x24, starting transfers between devices, from_inner(): return lax.ppermute(value, 'dp', pairs)  25.5 us
    pallas_call x4, Pallas kernels, apply_late(): pl.pallas_call(functools.partial(late_kernel, step, (blocks - late, late)...  25.5 us
    pallas_call x4, Pallas kernels, apply_early(): pl.pallas_call(functools.partial(early_kernel, blocks, len(inner)), in_sp...  17.4 us
    ppermute x10, waiting for transfers between devices, ring(): return lax.ppermute(value, 'dp', pairs)  17.2 us
    ppermute x6, waiting for transfers between devices, from_outer(): return lax.ppermute(value, 'dp', pairs)  15.5 us
    dot_general x1, matrix products, shards(): lax.dot_general(rotation, embeddings, (((0,), (1,)), ((), ())), preferred...  12.6 us
  transfers between devices with their start and end apart: 56, of which 26 were waited for; matrix products, arithmetic and copies ran while one was open for 11% of the time, Pallas kernels for 21%

profile of v9, /device:TPU:0, one launch (start us, length us, event | category | flops | bytes accessed | tf_op | source)
XLA Modules:
  0.0 306.2 jit_solution(3295128283919484919)
XLA Ops:
  7.9 5.3 %lookup.2 = bf16[2048,512]{1,0:T(8,128)(2,1)S(1)} custom-call(bf16[1,256,512]{2,1,0:T(8,128)(2,1)S(1)} %get-tuple-element.155.codes_ref, f32[256,8,256]{2,1,0:T(8,128)S(1)} %convert_bitcast_fusion.table_ref), custom_call_target="tpu_custom_call" | custom-call | tf_op jit(solution)/shard_map/lookup/pallas_call | solution.py:58
  13.2 12.6 %multiply_reduce_fusion = f32[512]{0:T(512)S(1)} fusion(bf16[2048,512]{1,0:T(8,128)(2,1)S(1)} %lookup.2, bf16[4096,2048]{1,0:T(8,128)(2,1)} %param.5, bf16[512,4096]{1,0:T(8,128)(2,1)S(1)} %copy-done.4), kind=kOutput, calls=%fused_computation.1 | convolution fusion | flops 8594128896 | bytes 23070720 | tf_op jit(solution)/shard_map/dot_general | solution.py:345
  28.5 5.6 %multiply_convert_fusion = bf16[512,4096]{1,0:T(8,128)(2,1)} fusion(bf16[512,4096]{1,0:T(8,128)(2,1)} %param.4, f32[512]{0:T(512)S(1)} %add_divide_fusion), kind=kLoop, calls=%fused_computation | loop fusion | flops 6291456 | bytes 8390656 | tf_op jit(solution)/shard_map/convert_element_type | solution.py:351
  48.3 21.1 %lookup.3.rebuilt_ref = bf16[2048,2048]{1,0:T(8,128)(2,1)S(1)} custom-call(bf16[4,256,512]{2,1,0:T(8,128)(2,1)S(1)} %pad_maximum_fusion.1.codes_ref, f32[256,8,256]{2,1,0:T(8,128)S(1)} %convert_bitcast_fusion.table_ref), custom_call_target="tpu_custom_call" | custom-call | tf_op jit(solution)/shard_map/lookup/pallas_call | solution.py:58
  69.5 15.5 %collective-permute-done.1.refs_2_ = bf16[256,1024]{1,0:T(8,128)(2,1)S(1)} collective-permute-done((bf16[256,1024]{1,0:T(8,128)(2,1)}, bf16[256,1024]{1,0:T(8,128)(2,1)S(1)}, u32[]{:S(2)}, u32[]{:S(2)}) %collective-permute-start.1) | collective-permute-done | bytes 524320 | tf_op jit(solution)/shard_map/ppermute | solution.py:333
  88.4 5.6 %cross.3 = (bf16[2048,256]{1,0:T(8,128)(2,1)S(1)}, bf16[2048,256]{1,0:T(8,128)(2,1)S(1)}) custom-call(s32[2]{0:T(128)S(1)} %pad_add_fusion.place_ref, bf16[2048,2048]{1,0:T(8,128)(2,1)S(1)} %lookup.3.rebuilt_ref, f32[2048,256]{1,0:T(8,128)S(1)} %multiply_bitcast_fusion.prior_ref, bf16[512,1024]{1,0:T(8,128)(2,1)S(1)} %constant_dynamic-slice_fusion.local_ref, ...), custom_call_target="tpu_custom_call" | custom-call | tf_op jit(solution)/shard_map/cross/pallas_call | solution.py:102
  97.0 5.6 %cross.2 = (f32[1024,256]{1,0:T(8,128)S(1)}, f32[1024,256]{1,0:T(8,128)S(1)}, f32[1024,256]{1,0:T(8,128)S(1)}, f32[1024,256]{1,0:T(8,128)S(1)}) custom-call(s32[2]{0:T(128)S(1)} %pad_add_fusion.place_ref, bf16[2048,2048]{1,0:T(8,128)(2,1)S(1)} %lookup.3.rebuilt_ref, f32[2048,256]{1,0:T(8,128)S(1)} %multiply_bitcast_fusion.prior_ref, ...), custom_call_target="tpu_custom_call" | custom-call | tf_op jit(solution)/shard_map/cross/pallas_call | solution.py:102
  102.6 16.6 %collective-permute-done.11 = bf16[2048,256]{1,0:T(8,128)(2,1)S(1)} collective-permute-done((bf16[2048,256]{1,0:T(8,128)(2,1)S(1)}, bf16[2048,256]{1,0:T(8,128)(2,1)S(1)}, u32[]{:S(2)}, u32[]{:S(2)}) %collective-permute-start.11) | collective-permute-done | bytes 1048608 | tf_op jit(solution)/shard_map/ppermute | solution.py:337
  122.7 9.9 %collective-permute-done.12 = bf16[1024,256]{1,0:T(8,128)(2,1)S(1)} collective-permute-done((bf16[1024,256]{1,0:T(8,128)(2,1)S(1)}, bf16[1024,256]{1,0:T(8,128)(2,1)S(1)}, u32[]{:S(2)}, u32[]{:S(2)}) %collective-permute-start.12) | collective-permute-done | bytes 524320 | tf_op jit(solution)/shard_map/ppermute | solution.py:337
  139.0 9.6 %collective-permute-done.21.refs_5_.refs_7_ = bf16[1024,256]{1,0:T(8,128)(2,1)S(1)} collective-permute-done((bf16[1024,256]{1,0:T(8,128)(2,1)S(1)}, bf16[1024,256]{1,0:T(8,128)(2,1)S(1)}, u32[]{:S(2)}, u32[]{:S(2)}) %collective-permute-start.21) | collective-permute-done | bytes 524320 | tf_op jit(solution)/shard_map/ppermute | solution.py:337
  152.5 7.3 %collective-permute-done.15.refs_4_.refs_6_ = bf16[1024,256]{1,0:T(8,128)(2,1)S(1)} collective-permute-done((bf16[1024,256]{1,0:T(8,128)(2,1)S(1)}, bf16[1024,256]{1,0:T(8,128)(2,1)S(1)}, u32[]{:S(2)}, u32[]{:S(2)}) %collective-permute-start.15) | collective-permute-done | bytes 524320 | tf_op jit(solution)/shard_map/ppermute | solution.py:337
  177.0 5.3 %collective-permute-done.18.refs_4_.refs_12_ = bf16[1024,256]{1,0:T(8,128)(2,1)S(1)} collective-permute-done((bf16[1024,256]{1,0:T(8,128)(2,1)}, bf16[1024,256]{1,0:T(8,128)(2,1)S(1)}, u32[]{:S(2)}, u32[]{:S(2)}) %collective-permute-start.18) | collective-permute-done | bytes 524320 | tf_op jit(solution)/shard_map/ppermute | solution.py:337
  188.3 5.3 %collective-permute-done.33.refs_5_.refs_19_.refs_3_ = bf16[1024,256]{1,0:T(8,128)(2,1)S(1)} collective-permute-done((bf16[1024,256]{1,0:T(8,128)(2,1)}, bf16[1024,256]{1,0:T(8,128)(2,1)S(1)}, u32[]{:S(2)}, u32[]{:S(2)}) %collective-permute-start.33) | collective-permute-done | bytes 524320 | tf_op jit(solution)/shard_map/ppermute | solution.py:337
  198.2 6.6 %collective-permute-done.24.refs_4_.refs_18_.refs_2_ = bf16[1024,256]{1,0:T(8,128)(2,1)S(1)} collective-permute-done((bf16[1024,256]{1,0:T(8,128)(2,1)S(1)}, bf16[1024,256]{1,0:T(8,128)(2,1)S(1)}, u32[]{:S(2)}, u32[]{:S(2)}) %collective-permute-start.24) | collective-permute-done | bytes 524320 | tf_op jit(solution)/shard_map/ppermute | solution.py:337
  210.8 6.7 %collective-permute-done.39.refs_5_.refs_25_.refs_9_ = bf16[1024,256]{1,0:T(8,128)(2,1)S(1)} collective-permute-done((bf16[1024,256]{1,0:T(8,128)(2,1)S(1)}, bf16[1024,256]{1,0:T(8,128)(2,1)S(1)}, u32[]{:S(2)}, u32[]{:S(2)}) %collective-permute-start.39) | collective-permute-done | bytes 524320 | tf_op jit(solution)/shard_map/ppermute | solution.py:337
  219.7 9.1 %collective-permute-done.30.refs_4_.refs_24_.refs_8_ = bf16[1024,256]{1,0:T(8,128)(2,1)S(1)} collective-permute-done((bf16[1024,256]{1,0:T(8,128)(2,1)S(1)}, bf16[1024,256]{1,0:T(8,128)(2,1)S(1)}, u32[]{:S(2)}, u32[]{:S(2)}) %collective-permute-start.30) | collective-permute-done | bytes 524320 | tf_op jit(solution)/shard_map/ppermute | solution.py:337
  231.1 7.4 %collective-permute-done.41.refs_3_.refs_29_.refs_13_ = bf16[1024,256]{1,0:T(8,128)(2,1)S(1)} collective-permute-done((bf16[1024,256]{1,0:T(8,128)(2,1)S(1)}, bf16[1024,256]{1,0:T(8,128)(2,1)S(1)}, u32[]{:S(2)}, u32[]{:S(2)}) %collective-permute-start.41) | collective-permute-done | bytes 524320 | tf_op jit(solution)/shard_map/ppermute | solution.py:337
  240.0 5.5 %collective-permute-done.40.refs_1_.refs_27_.refs_11_ = bf16[1024,256]{1,0:T(8,128)(2,1)S(1)} collective-permute-done((bf16[1024,256]{1,0:T(8,128)(2,1)S(1)}, bf16[1024,256]{1,0:T(8,128)(2,1)S(1)}, u32[]{:S(2)}, u32[]{:S(2)}) %collective-permute-start.40) | collective-permute-done | bytes 524320 | tf_op jit(solution)/shard_map/ppermute | solution.py:397
  253.7 4.7 %early.4.refs_36_ = f32[2048,256]{1,0:T(8,128)S(1)} custom-call(bf16[1024,256]{1,0:T(8,128)(2,1)S(1)} %get-tuple-element.147.refs_0_, bf16[1024,256]{1,0:T(8,128)(2,1)S(1)} %get-tuple-element.149.refs_1_, bf16[1024,256]{1,0:T(8,128)(2,1)} %collective-permute-done.13.refs_0_.refs_2_, bf16[1024,256]{1,0:T(8,128)(2,1)} %collective-permute-done.19.refs_1_.refs_3_, ...), custom_call_target="tpu_custom_call" | custom-call | tf_op jit(solution)/shard_map/early/pallas_call | solution.py:231
  258.5 6.2 %late0.1 = (f32[2048,256]{1,0:T(8,128)S(1)}, bf16[256,2048]{1,0:T(8,128)(2,1)S(1)}, bf16[2048,256]{1,0:T(8,128)(2,1)S(1)}) custom-call(f32[8,256]{1,0:T(8,128)S(1)} %get-tuple-element.131.mine_square_ref, f32[8,256]{1,0:T(8,128)S(1)} %collective-permute-done.43.other_square_ref, bf16[1024,256]{1,0:T(8,128)(2,1)S(1)} %get-tuple-element.147.refs_0_, ...), custom_call_target="tpu_custom_call" | custom-call | tf_op jit(solution)/shard_map/late0/pallas_call | solution.py:257
  267.8 4.3 %early.5.refs_34_ = f32[2048,256]{1,0:T(8,128)S(1)} custom-call(bf16[1024,256]{1,0:T(8,128)(2,1)S(1)} %get-tuple-element.147.refs_0_, bf16[1024,256]{1,0:T(8,128)(2,1)S(1)} %get-tuple-element.149.refs_1_, bf16[1024,256]{1,0:T(8,128)(2,1)} %collective-permute-done.13.refs_0_.refs_2_, bf16[1024,256]{1,0:T(8,128)(2,1)} %collective-permute-done.19.refs_1_.refs_3_, ...), custom_call_target="tpu_custom_call" | custom-call | tf_op jit(solution)/shard_map/early/pallas_call | solution.py:231
  272.2 6.8 %late1.1 = (f32[2048,256]{1,0:T(8,128)S(1)}, bf16[256,2048]{1,0:T(8,128)(2,1)S(1)}, bf16[2048,256]{1,0:T(8,128)(2,1)S(1)}) custom-call(f32[8,256]{1,0:T(8,128)S(1)} %get-tuple-element.131.mine_square_ref, f32[8,256]{1,0:T(8,128)S(1)} %collective-permute-done.43.other_square_ref, bf16[1024,256]{1,0:T(8,128)(2,1)S(1)} %get-tuple-element.147.refs_0_, ...), custom_call_target="tpu_custom_call" | custom-call | tf_op jit(solution)/shard_map/late1/pallas_call | solution.py:257
  286.3 6.6 %late2.1 = (f32[2048,256]{1,0:T(8,128)S(1)}, bf16[256,2048]{1,0:T(8,128)(2,1)S(1)}, bf16[2048,256]{1,0:T(8,128)(2,1)S(1)}) custom-call(f32[8,256]{1,0:T(8,128)S(1)} %get-tuple-element.131.mine_square_ref, f32[8,256]{1,0:T(8,128)S(1)} %collective-permute-done.43.other_square_ref, bf16[1024,256]{1,0:T(8,128)(2,1)S(1)} %get-tuple-element.147.refs_0_, ...), custom_call_target="tpu_custom_call" | custom-call | tf_op jit(solution)/shard_map/late2/pallas_call | solution.py:257
  300.2 5.8 %late3.1 = f32[256,2048]{1,0:T(8,128)} custom-call(f32[8,256]{1,0:T(8,128)S(1)} %get-tuple-element.131.mine_square_ref, f32[8,256]{1,0:T(8,128)S(1)} %collective-permute-done.43.other_square_ref, bf16[1024,256]{1,0:T(8,128)(2,1)S(1)} %get-tuple-element.147.refs_0_, bf16[1024,256]{1,0:T(8,128)(2,1)S(1)} %get-tuple-element.149.refs_1_, ...), custom_call_target="tpu_custom_call" | custom-call | tf_op jit(solution)/shard_map/late3/pallas_call | solution.py:257
  (149 shorter events, 110.5 us)
Async XLA Ops:
  2.1 38.4 %collective-permute-start.4 = (bf16[256,512]{1,0:T(8,128)(2,1)}, bf16[256,512]{1,0:T(8,128)(2,1)}, u32[]{:S(2)}, u32[]{:S(2)}) collective-permute-start(bf16[256,512]{1,0:T(8,128)(2,1)} %get-tuple-element.154), channel_id=1, source_target_pairs={{0,16},{2,18},{4,20},{6,22},{8,24},{10,26},{12,28},{14,30},{16,0},... | collective-permute-start | bytes 786440 | tf_op jit(solution)/shard_map/ppermute | solution.py:333
  6.2 40.9 %collective-permute-start.3 = (bf16[256,512]{1,0:T(8,128)(2,1)}, bf16[256,512]{1,0:T(8,128)(2,1)}, u32[]{:S(2)}, u32[]{:S(2)}) collective-permute-start(bf16[256,512]{1,0:T(8,128)(2,1)} %get-tuple-element.154), channel_id=1, source_target_pairs={{0,8},{2,10},{4,12},{6,14},{8,0},{10,2},{12,4},{14,6},{16,24},{18,... | collective-permute-start | bytes 786440 | tf_op jit(solution)/shard_map/ppermute | solution.py:333
  7.7 39.3 %collective-permute-start.5 = (bf16[256,512]{1,0:T(8,128)(2,1)}, bf16[256,512]{1,0:T(8,128)(2,1)}, u32[]{:S(2)}, u32[]{:S(2)}) collective-permute-start(bf16[256,512]{1,0:T(8,128)(2,1)} %get-tuple-element.154), channel_id=1, source_target_pairs={{0,24},{2,26},{4,28},{6,30},{8,16},{10,18},{12,20},{14,22},{16,8},... | collective-permute-start | bytes 786440 | tf_op jit(solution)/shard_map/ppermute | solution.py:333
  36.7 32.8 %collective-permute-start.2 = (bf16[256,1024]{1,0:T(8,128)(2,1)}, bf16[256,1024]{1,0:T(8,128)(2,1)S(1)}, u32[]{:S(2)}, u32[]{:S(2)}) collective-permute-start(bf16[256,1024]{1,0:T(8,128)(2,1)} %get-tuple-element.151), channel_id=1, source_target_pairs={{0,24},{2,26},{4,28},{6,30},{8,16},{10,18},{12,20},{14,22},{16,8},... | collective-permute-start | bytes 1572872 | tf_op jit(solution)/shard_map/ppermute | solution.py:333
  40.6 44.4 %collective-permute-start.1 = (bf16[256,1024]{1,0:T(8,128)(2,1)}, bf16[256,1024]{1,0:T(8,128)(2,1)S(1)}, u32[]{:S(2)}, u32[]{:S(2)}) collective-permute-start(bf16[256,1024]{1,0:T(8,128)(2,1)} %get-tuple-element.152), channel_id=1, source_target_pairs={{0,16},{2,18},{4,20},{6,22},{8,24},{10,26},{12,28},{14,30},{16,0},... | collective-permute-start | bytes 1572872 | tf_op jit(solution)/shard_map/ppermute | solution.py:333
  40.6 44.4 %collective-permute-start = (bf16[256,1024]{1,0:T(8,128)(2,1)}, bf16[256,1024]{1,0:T(8,128)(2,1)}, u32[]{:S(2)}, u32[]{:S(2)}) collective-permute-start(bf16[256,1024]{1,0:T(8,128)(2,1)} %get-tuple-element.153), channel_id=1, source_target_pairs={{0,8},{2,10},{4,12},{6,14},{8,0},{10,2},{12,4},{14,6},{16,24},{18,... | collective-permute-start | bytes 1572872 | tf_op jit(solution)/shard_map/ppermute | solution.py:333
  94.0 25.3 %collective-permute-start.11 = (bf16[2048,256]{1,0:T(8,128)(2,1)S(1)}, bf16[2048,256]{1,0:T(8,128)(2,1)S(1)}, u32[]{:S(2)}, u32[]{:S(2)}) collective-permute-start(bf16[2048,256]{1,0:T(8,128)(2,1)S(1)} %get-tuple-element.84), channel_id=1, source_target_pairs={{0,4},{2,6},{4,0},{6,2},{8,12},{10,14},{12,8},{14,10},{16,20},{18,... | collective-permute-start | bytes 3145736 | tf_op jit(solution)/shard_map/ppermute | solution.py:337
  95.6 25.4 %collective-permute-start.9 = (bf16[2048,256]{1,0:T(8,128)(2,1)S(1)}, bf16[2048,256]{1,0:T(8,128)(2,1)S(1)}, u32[]{:S(2)}, u32[]{:S(2)}) collective-permute-start(bf16[2048,256]{1,0:T(8,128)(2,1)S(1)} %get-tuple-element.81), channel_id=1, source_target_pairs={{0,2},{2,0},{4,6},{6,4},{8,10},{10,8},{12,14},{14,12},{16,18},{18,... | collective-permute-start | bytes 3145736 | tf_op jit(solution)/shard_map/ppermute | solution.py:337
  138.0 21.9 %collective-permute-start.15 = (bf16[1024,256]{1,0:T(8,128)(2,1)S(1)}, bf16[1024,256]{1,0:T(8,128)(2,1)S(1)}, u32[]{:S(2)}, u32[]{:S(2)}) collective-permute-start(bf16[1024,256]{1,0:T(8,128)(2,1)S(1)} %get-tuple-element.147.refs_0_), channel_id=1, source_target_pairs={{0,4},{2,6},{4,0},{6,2},{8,12},{10,14},{12,8},{14,10},{16,20},{18,... | collective-permute-start | bytes 1572872 | tf_op jit(solution)/shard_map/ppermute | solution.py:337
  138.5 25.7 %collective-permute-start.14 = (bf16[1024,256]{1,0:T(8,128)(2,1)S(1)}, bf16[1024,256]{1,0:T(8,128)(2,1)}, u32[]{:S(2)}, u32[]{:S(2)}) collective-permute-start(bf16[1024,256]{1,0:T(8,128)(2,1)S(1)} %get-tuple-element.147.refs_0_), channel_id=1, source_target_pairs={{0,2},{2,0},{4,6},{6,4},{8,10},{10,8},{12,14},{14,12},{16,18},{18,... | collective-permute-start | bytes 1572872 | tf_op jit(solution)/shard_map/ppermute | solution.py:337
  152.5 18.7 %collective-permute-start.27 = (bf16[1024,256]{1,0:T(8,128)(2,1)}, bf16[1024,256]{1,0:T(8,128)(2,1)}, u32[]{:S(2)}, u32[]{:S(2)}) collective-permute-start(bf16[1024,256]{1,0:T(8,128)(2,1)} %collective-permute-done.19.refs_1_.refs_3_), channel_id=1, source_target_pairs={{0,4},{2,6},{4,0},{6,2},{8,12},{10,14},{12,8},{14,10},{16,20},{18,... | collective-permute-start | bytes 1572872 | tf_op jit(solution)/shard_map/ppermute | solution.py:337
  152.5 20.2 %collective-permute-start.26 = (bf16[1024,256]{1,0:T(8,128)(2,1)}, bf16[1024,256]{1,0:T(8,128)(2,1)}, u32[]{:S(2)}, u32[]{:S(2)}) collective-permute-start(bf16[1024,256]{1,0:T(8,128)(2,1)} %collective-permute-done.19.refs_1_.refs_3_), channel_id=1, source_target_pairs={{0,2},{2,0},{4,6},{6,4},{8,10},{10,8},{12,14},{14,12},{16,18},{18,... | collective-permute-start | bytes 1572872 | tf_op jit(solution)/shard_map/ppermute | solution.py:337
  165.8 19.0 %collective-permute-start.17 = (bf16[1024,256]{1,0:T(8,128)(2,1)}, bf16[1024,256]{1,0:T(8,128)(2,1)S(1)}, u32[]{:S(2)}, u32[]{:S(2)}) collective-permute-start(bf16[1024,256]{1,0:T(8,128)(2,1)} %collective-permute-done.13.refs_0_.refs_2_), channel_id=1, source_target_pairs={{0,2},{2,0},{4,6},{6,4},{8,10},{10,8},{12,14},{14,12},{16,18},{18,... | collective-permute-start | bytes 1572872 | tf_op jit(solution)/shard_map/ppermute | solution.py:337
  174.8 18.8 %collective-permute-start.33 = (bf16[1024,256]{1,0:T(8,128)(2,1)}, bf16[1024,256]{1,0:T(8,128)(2,1)S(1)}, u32[]{:S(2)}, u32[]{:S(2)}) collective-permute-start(bf16[1024,256]{1,0:T(8,128)(2,1)} %collective-permute-done.25.refs_1_.refs_9_), channel_id=1, source_target_pairs={{0,4},{2,6},{4,0},{6,2},{8,12},{10,14},{12,8},{14,10},{16,20},{18,... | collective-permute-start | bytes 1572872 | tf_op jit(solution)/shard_map/ppermute | solution.py:337
  175.5 19.5 %collective-permute-start.32 = (bf16[1024,256]{1,0:T(8,128)(2,1)}, bf16[1024,256]{1,0:T(8,128)(2,1)S(1)}, u32[]{:S(2)}, u32[]{:S(2)}) collective-permute-start(bf16[1024,256]{1,0:T(8,128)(2,1)} %collective-permute-done.25.refs_1_.refs_9_), channel_id=1, source_target_pairs={{0,2},{2,0},{4,6},{6,4},{8,10},{10,8},{12,14},{14,12},{16,18},{18,... | collective-permute-start | bytes 1572872 | tf_op jit(solution)/shard_map/ppermute | solution.py:337
  186.0 18.8 %collective-permute-start.24 = (bf16[1024,256]{1,0:T(8,128)(2,1)S(1)}, bf16[1024,256]{1,0:T(8,128)(2,1)S(1)}, u32[]{:S(2)}, u32[]{:S(2)}) collective-permute-start(bf16[1024,256]{1,0:T(8,128)(2,1)S(1)} %collective-permute-done.16.refs_0_.refs_8_), channel_id=1, source_target_pairs={{0,4},{2,6},{4,0},{6,2},{8,12},{10,14},{12,8},{14,10},{16,20},{18,... | collective-permute-start | bytes 1572872 | tf_op jit(solution)/shard_map/ppermute | solution.py:337
  186.8 19.5 %collective-permute-start.23 = (bf16[1024,256]{1,0:T(8,128)(2,1)S(1)}, bf16[1024,256]{1,0:T(8,128)(2,1)S(1)}, u32[]{:S(2)}, u32[]{:S(2)}) collective-permute-start(bf16[1024,256]{1,0:T(8,128)(2,1)S(1)} %collective-permute-done.16.refs_0_.refs_8_), channel_id=1, source_target_pairs={{0,2},{2,0},{4,6},{6,4},{8,10},{10,8},{12,14},{14,12},{16,18},{18,... | collective-permute-start | bytes 1572872 | tf_op jit(solution)/shard_map/ppermute | solution.py:337
  195.1 22.5 %collective-permute-start.39 = (bf16[1024,256]{1,0:T(8,128)(2,1)S(1)}, bf16[1024,256]{1,0:T(8,128)(2,1)S(1)}, u32[]{:S(2)}, u32[]{:S(2)}) collective-permute-start(bf16[1024,256]{1,0:T(8,128)(2,1)S(1)} %collective-permute-done.21.refs_5_.refs_7_), channel_id=1, source_target_pairs={{0,2},{2,0},{4,6},{6,4},{8,10},{10,8},{12,14},{14,12},{16,18},{18,... | collective-permute-start | bytes 1572872 | tf_op jit(solution)/shard_map/ppermute | solution.py:337
  197.4 20.1 %collective-permute-start.38 = (bf16[1024,256]{1,0:T(8,128)(2,1)S(1)}, bf16[1024,256]{1,0:T(8,128)(2,1)S(1)}, u32[]{:S(2)}, u32[]{:S(2)}) collective-permute-start(bf16[1024,256]{1,0:T(8,128)(2,1)S(1)} %collective-permute-done.31.refs_1_.refs_15_), channel_id=1, source_target_pairs={{0,4},{2,6},{4,0},{6,2},{8,12},{10,14},{12,8},{14,10},{16,20},{18,... | collective-permute-start | bytes 1572872 | tf_op jit(solution)/shard_map/ppermute | solution.py:337
  206.3 22.5 %collective-permute-start.30 = (bf16[1024,256]{1,0:T(8,128)(2,1)S(1)}, bf16[1024,256]{1,0:T(8,128)(2,1)S(1)}, u32[]{:S(2)}, u32[]{:S(2)}) collective-permute-start(bf16[1024,256]{1,0:T(8,128)(2,1)S(1)} %copy-done.1), channel_id=1, source_target_pairs={{0,2},{2,0},{4,6},{6,4},{8,10},{10,8},{12,14},{14,12},{16,18},{18,... | collective-permute-start | bytes 1572872 | tf_op jit(solution)/shard_map/ppermute | solution.py:337
  210.2 19.6 %collective-permute-start.29 = (bf16[1024,256]{1,0:T(8,128)(2,1)S(1)}, bf16[1024,256]{1,0:T(8,128)(2,1)S(1)}, u32[]{:S(2)}, u32[]{:S(2)}) collective-permute-start(bf16[1024,256]{1,0:T(8,128)(2,1)S(1)} %collective-permute-done.22.refs_0_.refs_14_), channel_id=1, source_target_pairs={{0,4},{2,6},{4,0},{6,2},{8,12},{10,14},{12,8},{14,10},{16,20},{18,... | collective-permute-start | bytes 1572872 | tf_op jit(solution)/shard_map/ppermute | solution.py:337
  217.5 20.9 %collective-permute-start.41 = (bf16[1024,256]{1,0:T(8,128)(2,1)S(1)}, bf16[1024,256]{1,0:T(8,128)(2,1)S(1)}, u32[]{:S(2)}, u32[]{:S(2)}) collective-permute-start(bf16[1024,256]{1,0:T(8,128)(2,1)S(1)} %collective-permute-done.32.refs_3_.refs_17_.refs_1_), channel_id=1, source_target_pairs={{0,4},{2,6},{4,0},{6,2},{8,12},{10,14},{12,8},{14,10},{16,20},{18,... | collective-permute-start | bytes 1572872 | tf_op jit(solution)/shard_map/ppermute | solution.py:337
  219.0 21.0 %collective-permute-start.42 = (bf16[1024,256]{1,0:T(8,128)(2,1)S(1)}, bf16[1024,256]{1,0:T(8,128)(2,1)S(1)}, u32[]{:S(2)}, u32[]{:S(2)}) collective-permute-start(bf16[1024,256]{1,0:T(8,128)(2,1)S(1)} %collective-permute-done.38.refs_3_.refs_23_.refs_7_), channel_id=1, source_target_pairs={{0,2},{2,0},{4,6},{6,4},{8,10},{10,8},{12,14},{14,12},{16,18},{18,... | collective-permute-start | bytes 1572872 | tf_op jit(solution)/shard_map/ppermute | solution.py:337
  230.4 20.9 %collective-permute-start.34 = (bf16[1024,256]{1,0:T(8,128)(2,1)S(1)}, bf16[1024,256]{1,0:T(8,128)(2,1)S(1)}, u32[]{:S(2)}, u32[]{:S(2)}) collective-permute-start(bf16[1024,256]{1,0:T(8,128)(2,1)S(1)} %collective-permute-done.30.refs_4_.refs_24_.refs_8_), channel_id=1, source_target_pairs={{0,8},{2,10},{4,12},{6,14},{8,16},{10,18},{12,20},{14,22},{16,24},... | collective-permute-start | bytes 1572872 | tf_op jit(solution)/shard_map/ppermute | solution.py:397
  (41 other events, 402.1 us)

commit v10 on v9

--- a/solution.py
+++ b/solution.py
@@ -17,7 +17,7 @@
 VMEM = pl.BlockSpec(memory_space=pltpu.VMEM)
 
 
-def lookup_kernel(codes_ref, table_ref, out_ref, ids_ref):
+def lookup_kernel(codes_ref, table_ref, weights_ref, out_ref, ids_ref):
     subs, rows = codes_ref.shape[1:]
     width = table_ref.shape[1]
     halves = table_ref.shape[2] // LANES
@@ -29,6 +29,7 @@
         for first in range(0, rows, LANES):
             lanes = pl.ds(pl.multiple_of(pl.program_id(1) * rows + first, LANES), LANES)
             ids_all = ids_ref[pl.ds(base, GROUP), first : first + LANES]
+            scale = jnp.broadcast_to(weights_ref[0, :, first : first + LANES], (width, LANES))
             for pair in range(0, GROUP, 2):
                 both = []
                 for sub in (pair, pair + 1):
@@ -41,7 +42,7 @@
                             entries, lane, axis=1, mode="promise_in_bounds"
                         )
                         picked = got if half == 0 else jnp.where(ids >= half * LANES, got, picked)
-                    both.append(picked)
+                    both.append(picked * scale)
                 row = pl.multiple_of(first_out + (base + pair) * width, 2 * width)
                 out_ref[pl.ds(row, 2 * width), lanes] = jnp.concatenate(both, axis=0).astype(
                     out_ref.dtype
@@ -51,7 +52,7 @@
     lax.fori_loop(0, subs // GROUP, body, 0)
 
 
-def rebuild_rows(codes, table):
+def rebuild_rows(codes, table, weights):
     blocks, subs, rows = codes.shape
     width, centroids = table.shape[1:]
     tile = min(64, subs)
@@ -61,43 +62,43 @@
         in_specs=[
             pl.BlockSpec((1, tile, rows), lambda m, s: (s, m, 0)),
             pl.BlockSpec((tile, width, centroids), lambda m, s: (m, 0, 0)),
+            pl.BlockSpec((1, 1, rows), lambda m, s: (s, 0, 0)),
         ],
         out_specs=VMEM,
         scratch_shapes=[pltpu.VMEM((tile, rows), jnp.int32)],
         out_shape=pltpu.VMEM((subs * width, blocks * rows), jnp.bfloat16),
         compiler_params=pltpu.CompilerParams(vmem_limit_bytes=VMEM_BYTES),
         name="lookup",
-    )(codes, table)
-
-
-def cross_kernel(plan, place_ref, rebuilt_ref, prior_ref, local_ref, *refs):
+    )(codes, table, weights[:, None, :])
+
+
+def cross_kernel(plan, place_ref, own_ref, rebuilt_ref, prior_ref, local_ref, *refs):
     pieces, outs = refs[: len(refs) - len(plan)], refs[len(refs) - len(plan) :]
     rows = local_ref.shape[0]
     part_rows, col = (pieces[0].shape[0], rows // pieces[0].shape[0]) if pieces else (rows, 1)
     for (targets, first_row), out_ref in zip(plan, outs):
         height, block = out_ref.shape[0] // len(targets), out_ref.shape[1]
         span = slice(first_row, first_row + height)
+        left = [own_ref[span, :]]
+        for index in range(len(pieces)):
+            step, turn = divmod(index, col)
+            first = step * rows + lax.rem(place_ref[0] + turn, col) * part_rows
+            left.append(rebuilt_ref[span, pl.ds(pl.multiple_of(first, part_rows), part_rows)])
+        left = jnp.concatenate(left, axis=1)
         for slot, target in enumerate(targets):
             place = lax.bitwise_xor(place_ref[1], target)
             lanes = pl.ds(pl.multiple_of(place * block, block), block)
+            right = [local_ref[:, lanes]] + [piece_ref[:, lanes] for piece_ref in pieces]
             total = jnp.dot(
-                rebuilt_ref[span, :rows], local_ref[:, lanes], preferred_element_type=jnp.float32
+                left, jnp.concatenate(right, axis=0), preferred_element_type=jnp.float32
             )
-            for index, piece_ref in enumerate(pieces):
-                step, turn = divmod(index, col)
-                first = (step + 1) * rows + lax.rem(place_ref[0] + turn, col) * part_rows
-                total += jnp.dot(
-                    rebuilt_ref[span, pl.ds(pl.multiple_of(first, part_rows), part_rows)],
-                    piece_ref[:, lanes],
-                    preferred_element_type=jnp.float32,
-                )
             if target == 0:
                 total += prior_ref[span, :]
             out_ref[slot * height : (slot + 1) * height, :] = total.astype(out_ref.dtype)
 
 
-def cross_blocks(plan, dtype, place, rebuilt, prior, local, pieces):
-    operands = in_vmem(rebuilt, prior, local, *pieces)
+def cross_blocks(plan, dtype, place, own, rebuilt, prior, local, pieces):
+    operands = in_vmem(own, rebuilt, prior, local, *pieces)
     half, block = prior.shape[0] // 2, prior.shape[1]
     return pl.pallas_call(
         functools.partial(cross_kernel, plan),
@@ -141,16 +142,13 @@
 
 
 def gram_rows(panel, sum_ref, index):
-    half, block = panel[0].shape
+    half = panel[0].shape[0]
     chunk = 2 * half // CHUNKS
     side, first = divmod(index * chunk, half)
-    made = jnp.zeros((chunk, block), jnp.float32)
-    for owner in range(len(panel) // 2):
-        made += jnp.dot(
-            panel[2 * owner + side][first : first + chunk, :],
-            sum_ref[owner * block : (owner + 1) * block, :],
-            preferred_element_type=jnp.float32,
-        )
+    rows = [half_ref[first : first + chunk, :] for half_ref in panel[side::2]]
+    made = jnp.dot(
+        jnp.concatenate(rows, axis=1), sum_ref[...], preferred_element_type=jnp.float32
+    )
     return slice(index * chunk, (index + 1) * chunk), made
 
 
@@ -338,28 +336,35 @@
 
     steps = list(range(1, outer_size))
     codes_t = codes.T.astype(jnp.bfloat16)
-    group_codes = [codes_t] + [from_outer(codes_t, step) for step in steps]
+    group_codes = [from_outer(codes_t, step) for step in steps]
 
     table = jnp.transpose(codebooks, (0, 2, 1)).astype(jnp.float32)
-    own = rebuild_rows(codes_t[None], table)
+    own = rebuild_rows(codes_t[None], table, jnp.ones((1, tok_rows), jnp.float32))
     rotated = lax.dot_general(
         rotation, embeddings, (((0,), (1,)), ((), ())), preferred_element_type=jnp.float32
     )
     residue = rotated - own.astype(jnp.float32)
-    row_error = lax.psum(jnp.sum(residue * residue, axis=0), "col")
-    weights = 1.0 / (1.0 + row_error / (2.0 * model_width))
-    scaled = (weights[:, None] * embeddings.astype(jnp.float32)).astype(jnp.bfloat16)
+    row_error = jnp.sum(residue * residue, axis=0)
 
     sends = [
-        lax.dynamic_slice(scaled, (core * part_rows, (outer ^ step) * wide), (part_rows, wide))
+        lax.dynamic_slice(embeddings, (core * part_rows, (outer ^ step) * wide), (part_rows, wide))
         for step in steps
     ]
-    shares = [from_outer(send, step) for send, step in zip(sends, steps)]
-    local = lax.dynamic_slice_in_dim(scaled, outer * wide, wide, 1)
-    rebuilt = rebuild_rows(jnp.stack(group_codes), table)
-    shares, rebuilt = lax.optimization_barrier((shares, rebuilt))
+    sends[:-1], row_error, group_codes = lax.optimization_barrier(
+        (sends[:-1], row_error, group_codes)
+    )
+    shares = [from_outer(send, step) for send, step in zip(sends[:-1], steps)]
+    weights = 1.0 / (1.0 + lax.psum(row_error, "col") / (2.0 * model_width))
+    weights, shares = lax.optimization_barrier((weights, shares))
+    group_weights = [from_outer(weights, step) for step in steps]
+    sends[-1:], group_weights = lax.optimization_barrier((sends[-1:], group_weights))
+    rebuilt = rebuild_rows(jnp.stack(group_codes), table, jnp.stack(group_weights))
+    own = (own.astype(jnp.float32) * weights[None, :]).astype(jnp.bfloat16)
+    late = [from_outer(send, step) for send, step in zip(sends[-1:], steps[-1:])]
+    late, rebuilt = lax.optimization_barrier((late, rebuilt))
+    local = lax.dynamic_slice_in_dim(embeddings, outer * wide, wide, 1)
     pieces = []
-    for share in shares:
+    for share in shares + late:
         if part_rows % LANES:
             pieces.append(lax.all_gather(share, "col", axis=0, tiled=True))
             continue
@@ -374,7 +379,7 @@
     prior = 0.2 * rows_total * prior.astype(jnp.float32)
     half = prior.shape[0] // 2
     blocks_for = functools.partial(
-        cross_blocks, place=place, rebuilt=rebuilt, prior=prior, local=local, pieces=pieces
+        cross_blocks, place=place, own=own, rebuilt=rebuilt, prior=prior, local=local, pieces=pieces
     )
     near = [(1, 2), (2, 1)]
     sent = blocks_for([((one, 3), side * half) for side, (one, _) in enumerate(near)], jnp.bfloat16)

time: 311 us -> 323 us (1.039)
  waiting for transfers between devices: 130 us -> 136 us
  starting transfers between devices: 40.1 us -> 44.3 us
    ppermute x6 -> x9, starting transfers between devices: 10 us -> 17 us  [from_outer(): return lax.ppermute(value, 'dp', pairs)]
    convert_element_type x1, other arithmetic: 5.63 us -> 0.48 us  [shards(): own = (own.astype(jnp.float32) * weights[None, :]).astype(jnp.bfloat16)]
    ppermute x6 -> x9, waiting for transfers between devices: 15.5 us -> 19.7 us  [from_outer(): return lax.ppermute(value, 'dp', pairs)]
  transfers between devices with their start and end apart: 56 -> 59, of which waited for: 26 -> 26; matrix products, arithmetic and copies ran while one was open for 11% -> 10% of each run, Pallas kernels for 21% -> 22%
where the time goes in v10:
time: 323 us; the launch traced here: 317 us
  waiting for transfers between devices  136 us (42%)
  Pallas kernels  99.2 us (31%)
  starting transfers between devices  44.3 us (14%)
  matrix products  13.4 us (4%)
  local copies, waits for them, and re-layouts  12.2 us (4%)
  other arithmetic  9.13 us (3%)
    ppermute x24, waiting for transfers between devices, from_inner(): return lax.ppermute(value, 'dp', pairs)  97.1 us
    pallas_call x2, Pallas kernels, rebuild_rows(): pl.pallas_call(lookup_kernel, grid=(subs // tile, blocks), in_specs=[pl.B...  29.5 us
    pallas_call x4, Pallas kernels, apply_late(): pl.pallas_call(functools.partial(late_kernel, step, (blocks - late, late)...  25.4 us
    ppermute x24, starting transfers between devices, from_inner(): return lax.ppermute(value, 'dp', pairs)  23.2 us
    ppermute x9, waiting for transfers between devices, from_outer(): return lax.ppermute(value, 'dp', pairs)  19.7 us
    ppermute x10, waiting for transfers between devices, ring(): return lax.ppermute(value, 'dp', pairs)  17.4 us
    pallas_call x4, Pallas kernels, apply_early(): pl.pallas_call(functools.partial(early_kernel, blocks, len(inner)), in_sp...  17.4 us
    ppermute x9, starting transfers between devices, from_outer(): return lax.ppermute(value, 'dp', pairs)  17 us
  transfers between devices with their start and end apart: 59, of which 26 were waited for; matrix products, arithmetic and copies ran while one was open for 10% of the time, Pallas kernels for 22%

profile of v10, /device:TPU:0, one launch (start us, length us, event | category | flops | bytes accessed | tf_op | source)
XLA Modules:
  0.0 317.3 jit_solution(15200508749893138903)
XLA Ops:
  7.9 7.4 %lookup.2 = bf16[2048,512]{1,0:T(8,128)(2,1)S(1)} custom-call(bf16[1,256,512]{2,1,0:T(8,128)(2,1)S(1)} %get-tuple-element.177.codes_ref, f32[256,8,256]{2,1,0:T(8,128)S(1)} %convert_bitcast_fusion.table_ref, f32[1,1,512]{2,1,0:T(1,128)S(1)} %broadcast_in_dim_broadcast_in_dim.3.weights_ref), custom_call_target="tpu_custom_call" | custom-call | tf_op jit(solution)/shard_map/lookup/pallas_call | solution.py:59
  15.3 13.4 %fusion.1 = f32[512]{0:T(512)S(1)} fusion(bf16[2048,512]{1,0:T(8,128)(2,1)S(1)} %lookup.2, bf16[4096,2048]{1,0:T(8,128)(2,1)} %param.5, bf16[512,4096]{1,0:T(8,128)(2,1)S(1)} %copy-done.9), kind=kOutput, calls=%fused_computation.3 | convolution fusion | flops 8594128896 | bytes 23070720 | tf_op jit(solution)/shard_map/dot_general | solution.py:343
  38.4 17.3 %collective-permute-done.3.refs_0_ = bf16[256,1024]{1,0:T(8,128)(2,1)S(1)} collective-permute-done((bf16[256,1024]{1,0:T(8,128)(2,1)}, bf16[256,1024]{1,0:T(8,128)(2,1)S(1)}, u32[]{:S(2)}, u32[]{:S(2)}) %collective-permute-start.3) | collective-permute-done | bytes 524320 | tf_op jit(solution)/shard_map/ppermute | solution.py:331
  75.4 22.1 %lookup.3.rebuilt_ref = bf16[2048,1536]{1,0:T(8,128)(2,1)S(1)} custom-call(bf16[3,256,512]{2,1,0:T(8,128)(2,1)S(1)} %pad_maximum_fusion.1.codes_ref, f32[256,8,256]{2,1,0:T(8,128)S(1)} %convert_bitcast_fusion.table_ref, f32[3,1,512]{2,1,0:T(1,128)S(1)} %broadcast_in_dim.11.weights_ref), custom_call_target="tpu_custom_call" | custom-call | tf_op jit(solution)/shard_map/lookup/pallas_call | solution.py:59
  99.8 5.5 %cross.3 = (bf16[2048,256]{1,0:T(8,128)(2,1)S(1)}, bf16[2048,256]{1,0:T(8,128)(2,1)S(1)}) custom-call(s32[2]{0:T(128)S(1)} %pad_add_fusion.place_ref, bf16[2048,512]{1,0:T(8,128)(2,1)S(1)} %fusion.2.own_ref, bf16[2048,1536]{1,0:T(8,128)(2,1)S(1)} %lookup.3.rebuilt_ref, f32[2048,256]{1,0:T(8,128)S(1)} %copy-done.2, ...), custom_call_target="tpu_custom_call" | custom-call | tf_op jit(solution)/shard_map/cross/pallas_call | solution.py:103
  108.4 5.6 %cross.2 = (f32[1024,256]{1,0:T(8,128)S(1)}, f32[1024,256]{1,0:T(8,128)S(1)}, f32[1024,256]{1,0:T(8,128)S(1)}, f32[1024,256]{1,0:T(8,128)S(1)}) custom-call(s32[2]{0:T(128)S(1)} %pad_add_fusion.place_ref, bf16[2048,512]{1,0:T(8,128)(2,1)S(1)} %fusion.2.own_ref, bf16[2048,1536]{1,0:T(8,128)(2,1)S(1)} %lookup.3.rebuilt_ref, f32[2048,256]{1,0:T(8,128)S(1)} %copy-done.2, ...), custom_call_target="tpu_custom_call" | custom-call | tf_op jit(solution)/shard_map/cross/pallas_call | solution.py:103
  114.0 16.6 %collective-permute-done.14 = bf16[2048,256]{1,0:T(8,128)(2,1)S(1)} collective-permute-done((bf16[2048,256]{1,0:T(8,128)(2,1)S(1)}, bf16[2048,256]{1,0:T(8,128)(2,1)S(1)}, u32[]{:S(2)}, u32[]{:S(2)}) %collective-permute-start.14) | collective-permute-done | bytes 1048608 | tf_op jit(solution)/shard_map/ppermute | solution.py:335
  134.0 9.9 %collective-permute-done.15 = bf16[1024,256]{1,0:T(8,128)(2,1)S(1)} collective-permute-done((bf16[1024,256]{1,0:T(8,128)(2,1)S(1)}, bf16[1024,256]{1,0:T(8,128)(2,1)S(1)}, u32[]{:S(2)}, u32[]{:S(2)}) %collective-permute-start.15) | collective-permute-done | bytes 524320 | tf_op jit(solution)/shard_map/ppermute | solution.py:335
  150.3 9.6 %collective-permute-done.24.refs_5_.refs_7_ = bf16[1024,256]{1,0:T(8,128)(2,1)S(1)} collective-permute-done((bf16[1024,256]{1,0:T(8,128)(2,1)S(1)}, bf16[1024,256]{1,0:T(8,128)(2,1)S(1)}, u32[]{:S(2)}, u32[]{:S(2)}) %collective-permute-start.24) | collective-permute-done | bytes 524320 | tf_op jit(solution)/shard_map/ppermute | solution.py:335
  163.9 7.3 %collective-permute-done.18.refs_4_.refs_6_ = bf16[1024,256]{1,0:T(8,128)(2,1)S(1)} collective-permute-done((bf16[1024,256]{1,0:T(8,128)(2,1)S(1)}, bf16[1024,256]{1,0:T(8,128)(2,1)S(1)}, u32[]{:S(2)}, u32[]{:S(2)}) %collective-permute-start.18) | collective-permute-done | bytes 524320 | tf_op jit(solution)/shard_map/ppermute | solution.py:335
  178.2 4.4 %collective-permute-done.30.refs_5_.refs_13_ = bf16[1024,256]{1,0:T(8,128)(2,1)} collective-permute-done((bf16[1024,256]{1,0:T(8,128)(2,1)}, bf16[1024,256]{1,0:T(8,128)(2,1)}, u32[]{:S(2)}, u32[]{:S(2)}) %collective-permute-start.30) | collective-permute-done | bytes 524320 | tf_op jit(solution)/shard_map/ppermute | solution.py:335
  187.5 6.2 %collective-permute-done.21.refs_4_.refs_12_ = bf16[1024,256]{1,0:T(8,128)(2,1)S(1)} collective-permute-done((bf16[1024,256]{1,0:T(8,128)(2,1)}, bf16[1024,256]{1,0:T(8,128)(2,1)S(1)}, u32[]{:S(2)}, u32[]{:S(2)}) %collective-permute-start.21) | collective-permute-done | bytes 524320 | tf_op jit(solution)/shard_map/ppermute | solution.py:335
  199.2 5.7 %collective-permute-done.36.refs_5_.refs_19_.refs_3_ = bf16[1024,256]{1,0:T(8,128)(2,1)S(1)} collective-permute-done((bf16[1024,256]{1,0:T(8,128)(2,1)}, bf16[1024,256]{1,0:T(8,128)(2,1)S(1)}, u32[]{:S(2)}, u32[]{:S(2)}) %collective-permute-start.36) | collective-permute-done | bytes 524320 | tf_op jit(solution)/shard_map/ppermute | solution.py:335
  208.8 7.3 %collective-permute-done.27.refs_4_.refs_18_.refs_2_ = bf16[1024,256]{1,0:T(8,128)(2,1)S(1)} collective-permute-done((bf16[1024,256]{1,0:T(8,128)(2,1)S(1)}, bf16[1024,256]{1,0:T(8,128)(2,1)S(1)}, u32[]{:S(2)}, u32[]{:S(2)}) %collective-permute-start.27) | collective-permute-done | bytes 524320 | tf_op jit(solution)/shard_map/ppermute | solution.py:335
  222.2 6.7 %collective-permute-done.42.refs_5_.refs_25_.refs_9_ = bf16[1024,256]{1,0:T(8,128)(2,1)S(1)} collective-permute-done((bf16[1024,256]{1,0:T(8,128)(2,1)S(1)}, bf16[1024,256]{1,0:T(8,128)(2,1)S(1)}, u32[]{:S(2)}, u32[]{:S(2)}) %collective-permute-start.42) | collective-permute-done | bytes 524320 | tf_op jit(solution)/shard_map/ppermute | solution.py:335
  230.9 9.2 %collective-permute-done.33.refs_4_.refs_24_.refs_8_ = bf16[1024,256]{1,0:T(8,128)(2,1)S(1)} collective-permute-done((bf16[1024,256]{1,0:T(8,128)(2,1)S(1)}, bf16[1024,256]{1,0:T(8,128)(2,1)S(1)}, u32[]{:S(2)}, u32[]{:S(2)}) %collective-permute-start.33) | collective-permute-done | bytes 524320 | tf_op jit(solution)/shard_map/ppermute | solution.py:335
  242.2 7.6 %collective-permute-done.44.refs_3_.refs_29_.refs_13_ = bf16[1024,256]{1,0:T(8,128)(2,1)S(1)} collective-permute-done((bf16[1024,256]{1,0:T(8,128)(2,1)S(1)}, bf16[1024,256]{1,0:T(8,128)(2,1)S(1)}, u32[]{:S(2)}, u32[]{:S(2)}) %collective-permute-start.44) | collective-permute-done | bytes 524320 | tf_op jit(solution)/shard_map/ppermute | solution.py:335
  251.3 5.4 %collective-permute-done.43.refs_1_.refs_27_.refs_11_ = bf16[1024,256]{1,0:T(8,128)(2,1)S(1)} collective-permute-done((bf16[1024,256]{1,0:T(8,128)(2,1)S(1)}, bf16[1024,256]{1,0:T(8,128)(2,1)S(1)}, u32[]{:S(2)}, u32[]{:S(2)}) %collective-permute-start.43) | collective-permute-done | bytes 524320 | tf_op jit(solution)/shard_map/ppermute | solution.py:402
  265.0 4.7 %early.4.refs_36_ = f32[2048,256]{1,0:T(8,128)S(1)} custom-call(bf16[1024,256]{1,0:T(8,128)(2,1)S(1)} %get-tuple-element.169.refs_0_, bf16[1024,256]{1,0:T(8,128)(2,1)S(1)} %get-tuple-element.171.refs_1_, bf16[1024,256]{1,0:T(8,128)(2,1)} %collective-permute-done.16.refs_0_.refs_2_, bf16[1024,256]{1,0:T(8,128)(2,1)} %collective-permute-done.22.refs_1_.refs_3_, ...), custom_call_target="tpu_custom_call" | custom-call | tf_op jit(solution)/shard_map/early/pallas_call | solution.py:229
  269.8 6.1 %late0.1 = (f32[2048,256]{1,0:T(8,128)S(1)}, bf16[256,2048]{1,0:T(8,128)(2,1)S(1)}, bf16[2048,256]{1,0:T(8,128)(2,1)S(1)}) custom-call(f32[8,256]{1,0:T(8,128)S(1)} %get-tuple-element.153.mine_square_ref, f32[8,256]{1,0:T(8,128)S(1)} %collective-permute-done.46.other_square_ref, bf16[1024,256]{1,0:T(8,128)(2,1)S(1)} %get-tuple-element.169.refs_0_, ...), custom_call_target="tpu_custom_call" | custom-call | tf_op jit(solution)/shard_map/late0/pallas_call | solution.py:255
  279.0 4.3 %early.5.refs_34_ = f32[2048,256]{1,0:T(8,128)S(1)} custom-call(bf16[1024,256]{1,0:T(8,128)(2,1)S(1)} %get-tuple-element.169.refs_0_, bf16[1024,256]{1,0:T(8,128)(2,1)S(1)} %get-tuple-element.171.refs_1_, bf16[1024,256]{1,0:T(8,128)(2,1)} %collective-permute-done.16.refs_0_.refs_2_, bf16[1024,256]{1,0:T(8,128)(2,1)} %collective-permute-done.22.refs_1_.refs_3_, ...), custom_call_target="tpu_custom_call" | custom-call | tf_op jit(solution)/shard_map/early/pallas_call | solution.py:229
  283.4 6.8 %late1.1 = (f32[2048,256]{1,0:T(8,128)S(1)}, bf16[256,2048]{1,0:T(8,128)(2,1)S(1)}, bf16[2048,256]{1,0:T(8,128)(2,1)S(1)}) custom-call(f32[8,256]{1,0:T(8,128)S(1)} %get-tuple-element.153.mine_square_ref, f32[8,256]{1,0:T(8,128)S(1)} %collective-permute-done.46.other_square_ref, bf16[1024,256]{1,0:T(8,128)(2,1)S(1)} %get-tuple-element.169.refs_0_, ...), custom_call_target="tpu_custom_call" | custom-call | tf_op jit(solution)/shard_map/late1/pallas_call | solution.py:255
  297.5 6.6 %late2.1 = (f32[2048,256]{1,0:T(8,128)S(1)}, bf16[256,2048]{1,0:T(8,128)(2,1)S(1)}, bf16[2048,256]{1,0:T(8,128)(2,1)S(1)}) custom-call(f32[8,256]{1,0:T(8,128)S(1)} %get-tuple-element.153.mine_square_ref, f32[8,256]{1,0:T(8,128)S(1)} %collective-permute-done.46.other_square_ref, bf16[1024,256]{1,0:T(8,128)(2,1)S(1)} %get-tuple-element.169.refs_0_, ...), custom_call_target="tpu_custom_call" | custom-call | tf_op jit(solution)/shard_map/late2/pallas_call | solution.py:255
  311.3 5.8 %late3.1 = f32[256,2048]{1,0:T(8,128)} custom-call(f32[8,256]{1,0:T(8,128)S(1)} %get-tuple-element.153.mine_square_ref, f32[8,256]{1,0:T(8,128)S(1)} %collective-permute-done.46.other_square_ref, bf16[1024,256]{1,0:T(8,128)(2,1)S(1)} %get-tuple-element.169.refs_0_, bf16[1024,256]{1,0:T(8,128)(2,1)S(1)} %get-tuple-element.171.refs_1_, ...), custom_call_target="tpu_custom_call" | custom-call | tf_op jit(solution)/shard_map/late3/pallas_call | solution.py:255
  (162 shorter events, 115.0 us)
Async XLA Ops:
  2.1 29.3 %collective-permute-start.1 = (bf16[256,512]{1,0:T(8,128)(2,1)}, bf16[256,512]{1,0:T(8,128)(2,1)S(1)}, u32[]{:S(2)}, u32[]{:S(2)}) collective-permute-start(bf16[256,512]{1,0:T(8,128)(2,1)} %get-tuple-element.176), channel_id=1, source_target_pairs={{0,16},{2,18},{4,20},{6,22},{8,24},{10,26},{12,28},{14,30},{16,0},... | collective-permute-start | bytes 786440 | tf_op jit(solution)/shard_map/ppermute | solution.py:331
  6.1 25.2 %collective-permute-start = (bf16[256,512]{1,0:T(8,128)(2,1)}, bf16[256,512]{1,0:T(8,128)(2,1)}, u32[]{:S(2)}, u32[]{:S(2)}) collective-permute-start(bf16[256,512]{1,0:T(8,128)(2,1)} %get-tuple-element.176), channel_id=1, source_target_pairs={{0,8},{2,10},{4,12},{6,14},{8,0},{10,2},{12,4},{14,6},{16,24},{18,... | collective-permute-start | bytes 786440 | tf_op jit(solution)/shard_map/ppermute | solution.py:331
  7.7 23.6 %collective-permute-start.2 = (bf16[256,512]{1,0:T(8,128)(2,1)}, bf16[256,512]{1,0:T(8,128)(2,1)}, u32[]{:S(2)}, u32[]{:S(2)}) collective-permute-start(bf16[256,512]{1,0:T(8,128)(2,1)} %get-tuple-element.176), channel_id=1, source_target_pairs={{0,24},{2,26},{4,28},{6,30},{8,16},{10,18},{12,20},{14,22},{16,8},... | collective-permute-start | bytes 786440 | tf_op jit(solution)/shard_map/ppermute | solution.py:331
  31.4 24.4 %collective-permute-start.3 = (bf16[256,1024]{1,0:T(8,128)(2,1)}, bf16[256,1024]{1,0:T(8,128)(2,1)S(1)}, u32[]{:S(2)}, u32[]{:S(2)}) collective-permute-start(bf16[256,1024]{1,0:T(8,128)(2,1)} %get-tuple-element.88), channel_id=1, source_target_pairs={{0,8},{2,10},{4,12},{6,14},{8,0},{10,2},{12,4},{14,6},{16,24},{18,... | collective-permute-start | bytes 1572872 | tf_op jit(solution)/shard_map/ppermute | solution.py:331
  32.3 25.8 %collective-permute-start.4 = (bf16[256,1024]{1,0:T(8,128)(2,1)}, bf16[256,1024]{1,0:T(8,128)(2,1)S(1)}, u32[]{:S(2)}, u32[]{:S(2)}) collective-permute-start(bf16[256,1024]{1,0:T(8,128)(2,1)} %get-tuple-element.89), channel_id=1, source_target_pairs={{0,16},{2,18},{4,20},{6,22},{8,24},{10,26},{12,28},{14,30},{16,0},... | collective-permute-start | bytes 1572872 | tf_op jit(solution)/shard_map/ppermute | solution.py:331
  67.1 30.5 %collective-permute-start.8 = (bf16[256,1024]{1,0:T(8,128)(2,1)}, bf16[256,1024]{1,0:T(8,128)(2,1)}, u32[]{:S(2)}, u32[]{:S(2)}) collective-permute-start(bf16[256,1024]{1,0:T(8,128)(2,1)} %get-tuple-element.91), channel_id=1, source_target_pairs={{0,24},{2,26},{4,28},{6,30},{8,16},{10,18},{12,20},{14,22},{16,8},... | collective-permute-start | bytes 1572872 | tf_op jit(solution)/shard_map/ppermute | solution.py:331
  74.8 23.4 %collective-permute-start.9 = (bf16[256,1024]{1,0:T(8,128)(2,1)S(1)}, bf16[256,1024]{1,0:T(8,128)(2,1)S(1)}, u32[]{:S(2)}, u32[]{:S(2)}) collective-permute-start(bf16[256,1024]{1,0:T(8,128)(2,1)S(1)} %collective-permute-done.3.refs_0_), channel_id=1, source_target_pairs={{0,1},{1,0},{2,3},{3,2},{4,5},{5,4},{6,7},{7,6},{8,9},{9,8},{10,11... | collective-permute-start | bytes 1572872 | tf_op jit(solution)/shard_map/ppermute | solution.py:374
  74.9 23.3 %collective-permute-start.10 = (bf16[256,1024]{1,0:T(8,128)(2,1)S(1)}, bf16[256,1024]{1,0:T(8,128)(2,1)S(1)}, u32[]{:S(2)}, u32[]{:S(2)}) collective-permute-start(bf16[256,1024]{1,0:T(8,128)(2,1)S(1)} %collective-permute-done.4.refs_2_), channel_id=1, source_target_pairs={{0,1},{1,0},{2,3},{3,2},{4,5},{5,4},{6,7},{7,6},{8,9},{9,8},{10,11... | collective-permute-start | bytes 1572872 | tf_op jit(solution)/shard_map/ppermute | solution.py:374
  105.3 25.3 %collective-permute-start.14 = (bf16[2048,256]{1,0:T(8,128)(2,1)S(1)}, bf16[2048,256]{1,0:T(8,128)(2,1)S(1)}, u32[]{:S(2)}, u32[]{:S(2)}) collective-permute-start(bf16[2048,256]{1,0:T(8,128)(2,1)S(1)} %get-tuple-element.106), channel_id=1, source_target_pairs={{0,4},{2,6},{4,0},{6,2},{8,12},{10,14},{12,8},{14,10},{16,20},{18,... | collective-permute-start | bytes 3145736 | tf_op jit(solution)/shard_map/ppermute | solution.py:335
  106.9 25.4 %collective-permute-start.12 = (bf16[2048,256]{1,0:T(8,128)(2,1)S(1)}, bf16[2048,256]{1,0:T(8,128)(2,1)S(1)}, u32[]{:S(2)}, u32[]{:S(2)}) collective-permute-start(bf16[2048,256]{1,0:T(8,128)(2,1)S(1)} %get-tuple-element.103), channel_id=1, source_target_pairs={{0,2},{2,0},{4,6},{6,4},{8,10},{10,8},{12,14},{14,12},{16,18},{18,... | collective-permute-start | bytes 3145736 | tf_op jit(solution)/shard_map/ppermute | solution.py:335
  149.3 21.9 %collective-permute-start.18 = (bf16[1024,256]{1,0:T(8,128)(2,1)S(1)}, bf16[1024,256]{1,0:T(8,128)(2,1)S(1)}, u32[]{:S(2)}, u32[]{:S(2)}) collective-permute-start(bf16[1024,256]{1,0:T(8,128)(2,1)S(1)} %get-tuple-element.169.refs_0_), channel_id=1, source_target_pairs={{0,4},{2,6},{4,0},{6,2},{8,12},{10,14},{12,8},{14,10},{16,20},{18,... | collective-permute-start | bytes 1572872 | tf_op jit(solution)/shard_map/ppermute | solution.py:335
  149.8 25.2 %collective-permute-start.17 = (bf16[1024,256]{1,0:T(8,128)(2,1)S(1)}, bf16[1024,256]{1,0:T(8,128)(2,1)}, u32[]{:S(2)}, u32[]{:S(2)}) collective-permute-start(bf16[1024,256]{1,0:T(8,128)(2,1)S(1)} %get-tuple-element.169.refs_0_), channel_id=1, source_target_pairs={{0,2},{2,0},{4,6},{6,4},{8,10},{10,8},{12,14},{14,12},{16,18},{18,... | collective-permute-start | bytes 1572872 | tf_op jit(solution)/shard_map/ppermute | solution.py:335
  163.9 20.1 %collective-permute-start.29 = (bf16[1024,256]{1,0:T(8,128)(2,1)}, bf16[1024,256]{1,0:T(8,128)(2,1)}, u32[]{:S(2)}, u32[]{:S(2)}) collective-permute-start(bf16[1024,256]{1,0:T(8,128)(2,1)} %collective-permute-done.22.refs_1_.refs_3_), channel_id=1, source_target_pairs={{0,2},{2,0},{4,6},{6,4},{8,10},{10,8},{12,14},{14,12},{16,18},{18,... | collective-permute-start | bytes 1572872 | tf_op jit(solution)/shard_map/ppermute | solution.py:335
  176.7 19.4 %collective-permute-start.20 = (bf16[1024,256]{1,0:T(8,128)(2,1)}, bf16[1024,256]{1,0:T(8,128)(2,1)S(1)}, u32[]{:S(2)}, u32[]{:S(2)}) collective-permute-start(bf16[1024,256]{1,0:T(8,128)(2,1)} %collective-permute-done.16.refs_0_.refs_2_), channel_id=1, source_target_pairs={{0,2},{2,0},{4,6},{6,4},{8,10},{10,8},{12,14},{14,12},{16,18},{18,... | collective-permute-start | bytes 1572872 | tf_op jit(solution)/shard_map/ppermute | solution.py:335
  186.2 20.2 %collective-permute-start.35 = (bf16[1024,256]{1,0:T(8,128)(2,1)}, bf16[1024,256]{1,0:T(8,128)(2,1)S(1)}, u32[]{:S(2)}, u32[]{:S(2)}) collective-permute-start(bf16[1024,256]{1,0:T(8,128)(2,1)} %collective-permute-done.28.refs_1_.refs_9_), channel_id=1, source_target_pairs={{0,2},{2,0},{4,6},{6,4},{8,10},{10,8},{12,14},{14,12},{16,18},{18,... | collective-permute-start | bytes 1572872 | tf_op jit(solution)/shard_map/ppermute | solution.py:335
  197.4 18.7 %collective-permute-start.27 = (bf16[1024,256]{1,0:T(8,128)(2,1)S(1)}, bf16[1024,256]{1,0:T(8,128)(2,1)S(1)}, u32[]{:S(2)}, u32[]{:S(2)}) collective-permute-start(bf16[1024,256]{1,0:T(8,128)(2,1)S(1)} %collective-permute-done.19.refs_0_.refs_8_), channel_id=1, source_target_pairs={{0,4},{2,6},{4,0},{6,2},{8,12},{10,14},{12,8},{14,10},{16,20},{18,... | collective-permute-start | bytes 1572872 | tf_op jit(solution)/shard_map/ppermute | solution.py:335
  197.7 19.9 %collective-permute-start.26 = (bf16[1024,256]{1,0:T(8,128)(2,1)S(1)}, bf16[1024,256]{1,0:T(8,128)(2,1)S(1)}, u32[]{:S(2)}, u32[]{:S(2)}) collective-permute-start(bf16[1024,256]{1,0:T(8,128)(2,1)S(1)} %collective-permute-done.19.refs_0_.refs_8_), channel_id=1, source_target_pairs={{0,2},{2,0},{4,6},{6,4},{8,10},{10,8},{12,14},{14,12},{16,18},{18,... | collective-permute-start | bytes 1572872 | tf_op jit(solution)/shard_map/ppermute | solution.py:335
  206.4 22.5 %collective-permute-start.42 = (bf16[1024,256]{1,0:T(8,128)(2,1)S(1)}, bf16[1024,256]{1,0:T(8,128)(2,1)S(1)}, u32[]{:S(2)}, u32[]{:S(2)}) collective-permute-start(bf16[1024,256]{1,0:T(8,128)(2,1)S(1)} %collective-permute-done.24.refs_5_.refs_7_), channel_id=1, source_target_pairs={{0,2},{2,0},{4,6},{6,4},{8,10},{10,8},{12,14},{14,12},{16,18},{18,... | collective-permute-start | bytes 1572872 | tf_op jit(solution)/shard_map/ppermute | solution.py:335
  208.8 20.1 %collective-permute-start.41 = (bf16[1024,256]{1,0:T(8,128)(2,1)S(1)}, bf16[1024,256]{1,0:T(8,128)(2,1)S(1)}, u32[]{:S(2)}, u32[]{:S(2)}) collective-permute-start(bf16[1024,256]{1,0:T(8,128)(2,1)S(1)} %collective-permute-done.34.refs_1_.refs_15_), channel_id=1, source_target_pairs={{0,4},{2,6},{4,0},{6,2},{8,12},{10,14},{12,8},{14,10},{16,20},{18,... | collective-permute-start | bytes 1572872 | tf_op jit(solution)/shard_map/ppermute | solution.py:335
  217.6 22.5 %collective-permute-start.33 = (bf16[1024,256]{1,0:T(8,128)(2,1)S(1)}, bf16[1024,256]{1,0:T(8,128)(2,1)S(1)}, u32[]{:S(2)}, u32[]{:S(2)}) collective-permute-start(bf16[1024,256]{1,0:T(8,128)(2,1)S(1)} %copy-done.1), channel_id=1, source_target_pairs={{0,2},{2,0},{4,6},{6,4},{8,10},{10,8},{12,14},{14,12},{16,18},{18,... | collective-permute-start | bytes 1572872 | tf_op jit(solution)/shard_map/ppermute | solution.py:335
  221.6 19.6 %collective-permute-start.32 = (bf16[1024,256]{1,0:T(8,128)(2,1)S(1)}, bf16[1024,256]{1,0:T(8,128)(2,1)S(1)}, u32[]{:S(2)}, u32[]{:S(2)}) collective-permute-start(bf16[1024,256]{1,0:T(8,128)(2,1)S(1)} %collective-permute-done.25.refs_0_.refs_14_), channel_id=1, source_target_pairs={{0,4},{2,6},{4,0},{6,2},{8,12},{10,14},{12,8},{14,10},{16,20},{18,... | collective-permute-start | bytes 1572872 | tf_op jit(solution)/shard_map/ppermute | solution.py:335
  228.9 20.9 %collective-permute-start.44 = (bf16[1024,256]{1,0:T(8,128)(2,1)S(1)}, bf16[1024,256]{1,0:T(8,128)(2,1)S(1)}, u32[]{:S(2)}, u32[]{:S(2)}) collective-permute-start(bf16[1024,256]{1,0:T(8,128)(2,1)S(1)} %collective-permute-done.35.refs_3_.refs_17_.refs_1_), channel_id=1, source_target_pairs={{0,4},{2,6},{4,0},{6,2},{8,12},{10,14},{12,8},{14,10},{16,20},{18,... | collective-permute-start | bytes 1572872 | tf_op jit(solution)/shard_map/ppermute | solution.py:335
  230.3 21.0 %collective-permute-start.45 = (bf16[1024,256]{1,0:T(8,128)(2,1)S(1)}, bf16[1024,256]{1,0:T(8,128)(2,1)S(1)}, u32[]{:S(2)}, u32[]{:S(2)}) collective-permute-start(bf16[1024,256]{1,0:T(8,128)(2,1)S(1)} %collective-permute-done.41.refs_3_.refs_23_.refs_7_), channel_id=1, source_target_pairs={{0,2},{2,0},{4,6},{6,4},{8,10},{10,8},{12,14},{14,12},{16,18},{18,... | collective-permute-start | bytes 1572872 | tf_op jit(solution)/shard_map/ppermute | solution.py:335
  241.8 20.9 %collective-permute-start.37 = (bf16[1024,256]{1,0:T(8,128)(2,1)S(1)}, bf16[1024,256]{1,0:T(8,128)(2,1)S(1)}, u32[]{:S(2)}, u32[]{:S(2)}) collective-permute-start(bf16[1024,256]{1,0:T(8,128)(2,1)S(1)} %collective-permute-done.33.refs_4_.refs_24_.refs_8_), channel_id=1, source_target_pairs={{0,8},{2,10},{4,12},{6,14},{8,16},{10,18},{12,20},{14,22},{16,24},... | collective-permute-start | bytes 1572872 | tf_op jit(solution)/shard_map/ppermute | solution.py:402
  (46 other events, 458.5 us)

commit v11 on v9

--- a/solution.py
+++ b/solution.py
@@ -12,7 +12,7 @@
 GROUP = 8
 CHUNKS = 4
 INNER = 4
-VMEM_BYTES = 24 * 1024 * 1024
+VMEM_BYTES = 22 * 1024 * 1024
 ANY = pl.BlockSpec(memory_space=pl.ANY)
 VMEM = pl.BlockSpec(memory_space=pltpu.VMEM)
 
@@ -68,6 +68,43 @@
         compiler_params=pltpu.CompilerParams(vmem_limit_bytes=VMEM_BYTES),
         name="lookup",
     )(codes, table)
+
+
+def slices_kernel(steps, place_ref, weights_ref, rows_ref, local_ref, *sends):
+    part_rows, wide = sends[0].shape
+
+    def scaled(first, rows, step):
+        lanes = pl.ds(pl.multiple_of(lax.bitwise_xor(place_ref[2], step) * wide, wide), wide)
+        column = jnp.broadcast_to(weights_ref[:, pl.ds(first, rows)], (LANES, rows)).T
+        values = rows_ref[pl.ds(first, rows), lanes].astype(jnp.float32)
+        column = jnp.concatenate([column] * (wide // LANES), axis=1)
+        return (values * column).astype(local_ref.dtype)
+
+    first = pl.multiple_of(place_ref[0] * part_rows, part_rows)
+    for step, send_ref in zip(steps, sends):
+        send_ref[...] = scaled(first, part_rows, step)
+    for first in range(0, local_ref.shape[0], part_rows):
+        local_ref[first : first + part_rows, :] = scaled(first, part_rows, 0)
+
+
+def weighted_slices(place, weights, embeddings, part_rows, wide, steps):
+    rows = embeddings.shape[0]
+    if part_rows % LANES:
+        scaled = (weights[:, None] * embeddings.astype(jnp.float32)).astype(jnp.bfloat16)
+        first = place[0] * part_rows
+        return [lax.dynamic_slice_in_dim(scaled, place[2] * wide, wide, 1)] + [
+            lax.dynamic_slice(scaled, (first, (place[2] ^ step) * wide), (part_rows, wide))
+            for step in steps
+        ]
+    return pl.pallas_call(
+        functools.partial(slices_kernel, steps),
+        in_specs=[pl.BlockSpec(memory_space=pltpu.SMEM), VMEM, VMEM],
+        out_specs=[VMEM] * (1 + len(steps)),
+        out_shape=[pltpu.VMEM((rows, wide), jnp.bfloat16)]
+        + [pltpu.VMEM((part_rows, wide), jnp.bfloat16)] * len(steps),
+        compiler_params=pltpu.CompilerParams(vmem_limit_bytes=VMEM_BYTES),
+        name="slices",
+    )(place, *in_vmem(weights[None, :], embeddings))
 
 
 def cross_kernel(plan, place_ref, rebuilt_ref, prior_ref, local_ref, *refs):
@@ -117,7 +154,7 @@
             value_ref[:, first * half : (first + 1) * half], half_ref[...],
             preferred_element_type=jnp.float32,
         )
-    inner_ref[index * block : (index + 1) * block, :] = product.T.astype(inner_ref.dtype)
+    inner_ref[:, index * block : (index + 1) * block] = product.astype(inner_ref.dtype)
 
 
 def first_kernel(own_ref, before_ref, *refs):
@@ -136,21 +173,20 @@
 def add_up(mine, other, sum_ref):
     first = 0
     for mine_ref, other_ref in zip(mine, other):
-        sum_ref[first : first + mine_ref.shape[0], :] = mine_ref[...] + other_ref[...]
-        first += mine_ref.shape[0]
-
-
-def gram_rows(panel, sum_ref, index):
-    half, block = panel[0].shape
+        width = mine_ref.shape[1]
+        sum_ref[:, first : first + width] = mine_ref[...] + other_ref[...]
+        first += width
+
+
+def gram_columns(panel, sum_ref, index):
+    half = panel[0].shape[0]
     chunk = 2 * half // CHUNKS
     side, first = divmod(index * chunk, half)
-    made = jnp.zeros((chunk, block), jnp.float32)
-    for owner in range(len(panel) // 2):
-        made += jnp.dot(
-            panel[2 * owner + side][first : first + chunk, :],
-            sum_ref[owner * block : (owner + 1) * block, :],
-            preferred_element_type=jnp.float32,
-        )
+    rows = [half_ref[first : first + chunk, :] for half_ref in panel[side::2]]
+    made = lax.dot_general(
+        sum_ref[...], jnp.concatenate(rows, axis=1), (((1,), (1,)), ((), ())),
+        preferred_element_type=jnp.float32,
+    )
     return slice(index * chunk, (index + 1) * chunk), made
 
 
@@ -159,8 +195,8 @@
     mine, other, (out_ref, sum_ref) = refs[:parts], refs[parts : 2 * parts], refs[2 * parts :]
     add_up(mine, other, sum_ref)
     for index in range(CHUNKS):
-        span, made = gram_rows(panel, sum_ref, index)
-        out_ref[span, :] = made
+        span, made = gram_columns(panel, sum_ref, index)
+        out_ref[:, span] = made
 
 
 def late_kernel(step, blocks, parts, mine_square_ref, other_square_ref, *refs):
@@ -180,21 +216,21 @@
     scale = model_width / (1.96 * total)
     add_up(mine, other, sum_ref)
     for index in range(CHUNKS):
-        span, made = gram_rows(panel[2 * first_late :], sum_ref, index)
-        made += early_ref[span, :]
+        span, made = gram_columns(panel[2 * first_late :], sum_ref, index)
+        made += early_ref[:, span]
         if step == 2:
             made = made * scale
         else:
-            made = 1.5 * held[0][span, :] - (0.5 * scale) * made
+            made = 1.5 * held[0][:, span] - (0.5 * scale) * made
         if last:
-            made = (1.5 * held[1][span, :] - 0.5 * made) * (math.sqrt(model_width) * jnp.sqrt(scale))
-            out_ref[:, span] = made.T
+            made = (1.5 * held[1][:, span] - 0.5 * made) * (math.sqrt(model_width) * jnp.sqrt(scale))
+            out_ref[:, span] = made
         else:
-            state_ref[span, :] = made
-            value_ref[:, span] = made.T.astype(value_ref.dtype)
+            state_ref[:, span] = made
+            value_ref[:, span] = made.astype(value_ref.dtype)
     if last:
         return
-    for index in range(inner_ref.shape[0] // block):
+    for index in range(inner_ref.shape[1] // block):
         product_of(value_ref, panel[2 * index : 2 * index + 2], inner_ref, index)
 
 
@@ -215,7 +251,7 @@
         in_specs=[VMEM] * (2 + len(panel)),
         out_specs=[VMEM, VMEM],
         out_shape=[
-            pltpu.VMEM((len(panel) // 2 * block, block), jnp.bfloat16),
+            pltpu.VMEM((block, len(panel) // 2 * block), jnp.bfloat16),
             pltpu.VMEM((8, block), jnp.float32),
         ],
         compiler_params=pltpu.CompilerParams(vmem_limit_bytes=VMEM_BYTES),
@@ -232,8 +268,8 @@
         functools.partial(early_kernel, blocks, len(inner)),
         in_specs=[VMEM] * len(operands),
         out_specs=VMEM,
-        out_shape=pltpu.VMEM((2 * half, block), jnp.float32),
-        scratch_shapes=[pltpu.VMEM((blocks * block, block), jnp.bfloat16)],
+        out_shape=pltpu.VMEM((block, 2 * half), jnp.float32),
+        scratch_shapes=[pltpu.VMEM((block, blocks * block), jnp.bfloat16)],
         compiler_params=pltpu.CompilerParams(vmem_limit_bytes=VMEM_BYTES),
         name="early",
     )(*operands)
@@ -242,15 +278,15 @@
 def apply_late(step, early, panel, inner, squares, held):
     half, block = panel[0].shape
     blocks, cols = len(panel) // 2, 2 * half
-    late = sum(mine.shape[0] for mine, _ in inner) // block
+    late = sum(mine.shape[1] for mine, _ in inner) // block
     last = step == 3
     if last:
         out_shape = jax.ShapeDtypeStruct((block, cols), jnp.float32)
     else:
         out_shape = [
-            pltpu.VMEM((cols, block), jnp.float32),
+            pltpu.VMEM((block, cols), jnp.float32),
             pltpu.VMEM((block, cols), jnp.bfloat16),
-            pltpu.VMEM((blocks // 2 * block, block), jnp.bfloat16),
+            pltpu.VMEM((block, blocks // 2 * block), jnp.bfloat16),
         ]
     mine, other = zip(*inner)
     operands = in_vmem(*squares, *panel, *mine, *other, early, *held)
@@ -259,7 +295,7 @@
         in_specs=[VMEM] * len(operands),
         out_specs=VMEM if last else [VMEM] * 3,
         out_shape=out_shape,
-        scratch_shapes=[pltpu.VMEM((late * block, block), jnp.bfloat16)],
+        scratch_shapes=[pltpu.VMEM((block, late * block), jnp.bfloat16)],
         compiler_params=pltpu.CompilerParams(vmem_limit_bytes=VMEM_BYTES),
         name="late%d" % step,
     )(*operands)
@@ -272,7 +308,7 @@
         rest_kernel,
         in_specs=[VMEM] * len(operands),
         out_specs=VMEM,
-        out_shape=pltpu.VMEM((len(panel) // 2 * block, block), jnp.bfloat16),
+        out_shape=pltpu.VMEM((block, len(panel) // 2 * block), jnp.bfloat16),
         compiler_params=pltpu.CompilerParams(vmem_limit_bytes=VMEM_BYTES),
         name="rest",
     )(*operands)
@@ -348,14 +384,11 @@
     residue = rotated - own.astype(jnp.float32)
     row_error = lax.psum(jnp.sum(residue * residue, axis=0), "col")
     weights = 1.0 / (1.0 + row_error / (2.0 * model_width))
-    scaled = (weights[:, None] * embeddings.astype(jnp.float32)).astype(jnp.bfloat16)
-
-    sends = [
-        lax.dynamic_slice(scaled, (core * part_rows, (outer ^ step) * wide), (part_rows, wide))
-        for step in steps
-    ]
+
+    place = jnp.stack([core, inner, outer]).astype(jnp.int32)
+    weights, group_codes = lax.optimization_barrier((weights, group_codes))
+    local, *sends = weighted_slices(place, weights, embeddings, part_rows, wide, steps)
     shares = [from_outer(send, step) for send, step in zip(sends, steps)]
-    local = lax.dynamic_slice_in_dim(scaled, outer * wide, wide, 1)
     rebuilt = rebuild_rows(jnp.stack(group_codes), table)
     shares, rebuilt = lax.optimization_barrier((shares, rebuilt))
     pieces = []
@@ -368,7 +401,6 @@
             pairs = [(i, (i - turn) % col) for i in range(col)]
             pieces.append(lax.ppermute(share, "col", pairs))
 
-    place = jnp.stack([core, inner]).astype(jnp.int32)
     start_row = lax.axis_index("dp") * block
     prior = lax.dynamic_slice_in_dim(rotation, start_row, block, 0).T
     prior = 0.2 * rows_total * prior.astype(jnp.float32)
@@ -390,13 +422,13 @@
         last = from_inner(passed.astype(jnp.bfloat16), two)
         starts.append(kept[side] + came[side][:half].astype(jnp.float32) + last.astype(jnp.float32))
     narrow = [value.astype(jnp.bfloat16) for value in starts]
-    start = jnp.concatenate(starts, axis=0)
+    start = jnp.concatenate(starts, axis=0).T
 
     def ring(value):
         pairs = [(i, (i + inner_size) % dp) for i in range(dp)]
         return lax.ppermute(value, "dp", pairs)
 
-    own = jnp.concatenate(narrow, axis=0).T
+    own = start.astype(jnp.bfloat16)
     held = [{(0, 0): value} for value in narrow]
 
     def move(side, key, source):
@@ -409,11 +441,19 @@
     order, products = [(0, 0)], []
     square = jnp.zeros((8, block), jnp.float32)
     fresh = [(0, 0)]
-    for moves in gather_rounds(outer_size):
+    rounds = gather_rounds(outer_size)
+    for moves in rounds:
         arrived = [[move(side, key, source) for key, source in moves] for side in range(2)]
         product, square = apply_first(own, square, halves(fresh))
         arrived[0], product, square = lax.optimization_barrier((arrived[0], product, square))
-        arrived[1] = lax.optimization_barrier(arrived[1])
+        beside = [products[-1]] if products else []
+        if moves is rounds[-1]:
+            beside = [apply_early(halves(order[: -len(fresh)]), products)]
+        arrived[1], beside = lax.optimization_barrier((arrived[1], beside))
+        if moves is rounds[-1]:
+            early = beside[0]
+        elif products:
+            products[-1] = beside[0]
         fresh = [key for key, _ in moves]
         for side in range(2):
             held[side].update(zip(fresh, arrived[side]))
@@ -424,8 +464,6 @@
     panel = halves(order)
     squares = both_cores(square)
 
-    first_late = sum(mine.shape[0] for mine, _ in products[:-2]) // block
-    early = apply_early(panel[: 2 * first_late], products[:-2])
     inner = products[-2:]
     states = [start]
     middle = len(panel) // 2

time: 311 us -> 340 us (1.093)
  starting transfers between devices: 40.1 us -> 100 us
  waiting for transfers between devices: 130 us -> 75.2 us
  local copies, waits for them, and re-layouts: 12.1 us -> 41.1 us
  other arithmetic: 12 us -> 5.73 us
    ppermute x10, starting transfers between devices: 1.1 us -> 54.5 us  [ring(): return lax.ppermute(value, 'dp', pairs)]
    ppermute x24, waiting for transfers between devices: 94.3 us -> 42.4 us  [from_inner(): return lax.ppermute(value, 'dp', pairs)]
    unnamed x20 -> x152, local copies, waits for them, and re-layouts: 4.44 us -> 34.2 us
    ppermute x6, waiting for transfers between devices: 15.5 us -> 8.53 us  [from_outer(): return lax.ppermute(value, 'dp', pairs)]
    ppermute x24, starting transfers between devices: 25.5 us -> 32.3 us  [from_inner(): return lax.ppermute(value, 'dp', pairs)]
    convert_element_type x1, other arithmetic: 5.63 us -> 1.07 us  [shards(): own = start.astype(jnp.bfloat16)]
    dynamic_slice x2 -> x0, local copies, waits for them, and re-layouts: 3.86 us -> none  [the longest x1 2.56 us: shards(): lax.dynamic_slice(scaled, (core * part_rows, (outer ^ step) * wide), (par...]
  transfers between devices with their start and end apart: 56 -> 56, of which waited for: 26 -> 21; matrix products, arithmetic and copies ran while one was open for 11% -> 8% of each run, Pallas kernels for 21% -> 18%
where the time goes in v11:
time: 340 us; the launch traced here: 334 us
  starting transfers between devices  100 us (29%)
  Pallas kernels  95.1 us (28%)
  waiting for transfers between devices  75.2 us (22%)
  local copies, waits for them, and re-layouts  41.1 us (12%)
  matrix products  12.6 us (4%)
  other arithmetic  5.73 us (2%)
    ppermute x10, starting transfers between devices, ring(): return lax.ppermute(value, 'dp', pairs)  54.5 us
    ppermute x24, waiting for transfers between devices, from_inner(): return lax.ppermute(value, 'dp', pairs)  42.4 us
    unnamed x152, local copies, waits for them, and re-layouts  34.2 us
    ppermute x24, starting transfers between devices, from_inner(): return lax.ppermute(value, 'dp', pairs)  32.3 us
    pallas_call x2, Pallas kernels, rebuild_rows(): pl.pallas_call(lookup_kernel, grid=(subs // tile, blocks), in_specs=[pl.B...  26.4 us
    pallas_call x4, Pallas kernels, apply_late(): pl.pallas_call(functools.partial(late_kernel, step, (blocks - late, late)...  23.9 us
    ppermute x10, waiting for transfers between devices, ring(): return lax.ppermute(value, 'dp', pairs)  19.9 us
    pallas_call x4, Pallas kernels, apply_early(): pl.pallas_call(functools.partial(early_kernel, blocks, len(inner)), in_sp...  16.2 us
  transfers between devices with their start and end apart: 56, of which 21 were waited for; matrix products, arithmetic and copies ran while one was open for 8% of the time, Pallas kernels for 18%

profile of v11, /device:TPU:0, one launch (start us, length us, event | category | flops | bytes accessed | tf_op | source)
XLA Modules:
  0.0 334.0 jit_solution(17087905956622320855)
XLA Ops:
  2.1 5.0 %collective-permute-start.2 = (bf16[256,512]{1,0:T(8,128)(2,1)}, bf16[256,512]{1,0:T(8,128)(2,1)}, u32[]{:S(2)}, u32[]{:S(2)}) collective-permute-start(bf16[256,512]{1,0:T(8,128)(2,1)} %get-tuple-element.96), channel_id=1, source_target_pairs={{0,24},{2,26},{4,28},{6,30},{8,16},{10,18},{12,20},{14,22},{16,8},... | collective-permute-start | bytes 786440 | tf_op jit(solution)/shard_map/ppermute | solution.py:369
  7.9 5.3 %lookup.2 = bf16[2048,512]{1,0:T(8,128)(2,1)S(1)} custom-call(bf16[1,256,512]{2,1,0:T(8,128)(2,1)S(1)} %get-tuple-element.184.codes_ref, f32[256,8,256]{2,1,0:T(8,128)S(1)} %convert_bitcast_fusion.table_ref), custom_call_target="tpu_custom_call" | custom-call | tf_op jit(solution)/shard_map/lookup/pallas_call | solution.py:58
  13.2 12.6 %multiply_reduce_fusion = f32[512]{0:T(512)S(1)} fusion(bf16[2048,512]{1,0:T(8,128)(2,1)S(1)} %lookup.2, bf16[4096,2048]{1,0:T(8,128)(2,1)} %param.5, bf16[512,4096]{1,0:T(8,128)(2,1)S(1)} %copy-done.67), kind=kOutput, calls=%fused_computation | convolution fusion | flops 8594128896 | bytes 23070720 | tf_op jit(solution)/shard_map/dot_general | solution.py:381
  44.1 21.1 %lookup.3.rebuilt_ref = bf16[2048,2048]{1,0:T(8,128)(2,1)S(1)} custom-call(bf16[4,256,512]{2,1,0:T(8,128)(2,1)S(1)} %pad_maximum_fusion.codes_ref, f32[256,8,256]{2,1,0:T(8,128)S(1)} %convert_bitcast_fusion.table_ref), custom_call_target="tpu_custom_call" | custom-call | tf_op jit(solution)/shard_map/lookup/pallas_call | solution.py:58
  65.3 7.6 %collective-permute-done.4.refs_2_ = bf16[256,1024]{1,0:T(8,128)(2,1)} collective-permute-done((bf16[256,1024]{1,0:T(8,128)(2,1)}, bf16[256,1024]{1,0:T(8,128)(2,1)}, u32[]{:S(2)}, u32[]{:S(2)}) %collective-permute-start.4) | collective-permute-done | bytes 524320 | tf_op jit(solution)/shard_map/ppermute | solution.py:369
  76.5 5.9 %cross.3 = (bf16[2048,256]{1,0:T(8,128)(2,1)S(1)}, bf16[2048,256]{1,0:T(8,128)(2,1)S(1)}) custom-call(s32[3]{0:T(128)S(1)} %pad_add_fusion.place_ref, bf16[2048,2048]{1,0:T(8,128)(2,1)S(1)} %lookup.3.rebuilt_ref, f32[2048,256]{1,0:T(8,128)S(1)} %multiply_bitcast_fusion.prior_ref, bf16[512,1024]{1,0:T(8,128)(2,1)S(1)} %get-tuple-element.101.local_ref, ...), custom_call_target="tpu_custom_call" | custom-call | tf_op jit(solution)/shard_map/cross/pallas_call | solution.py:139
  85.5 5.9 %cross.2 = (f32[1024,256]{1,0:T(8,128)S(1)}, f32[1024,256]{1,0:T(8,128)S(1)}, f32[1024,256]{1,0:T(8,128)S(1)}, f32[1024,256]{1,0:T(8,128)S(1)}) custom-call(s32[3]{0:T(128)S(1)} %pad_add_fusion.place_ref, bf16[2048,2048]{1,0:T(8,128)(2,1)S(1)} %lookup.3.rebuilt_ref, f32[2048,256]{1,0:T(8,128)S(1)} %multiply_bitcast_fusion.prior_ref, ...), custom_call_target="tpu_custom_call" | custom-call | tf_op jit(solution)/shard_map/cross/pallas_call | solution.py:139
  91.4 16.3 %collective-permute-done.9 = bf16[2048,256]{1,0:T(8,128)(2,1)S(1)} collective-permute-done((bf16[2048,256]{1,0:T(8,128)(2,1)S(1)}, bf16[2048,256]{1,0:T(8,128)(2,1)S(1)}, u32[]{:S(2)}, u32[]{:S(2)}) %collective-permute-start.9) | collective-permute-done | bytes 1048608 | tf_op jit(solution)/shard_map/ppermute | solution.py:373
  111.1 9.9 %collective-permute-done.10 = bf16[1024,256]{1,0:T(8,128)(2,1)S(1)} collective-permute-done((bf16[1024,256]{1,0:T(8,128)(2,1)S(1)}, bf16[1024,256]{1,0:T(8,128)(2,1)S(1)}, u32[]{:S(2)}, u32[]{:S(2)}) %collective-permute-start.10) | collective-permute-done | bytes 524320 | tf_op jit(solution)/shard_map/ppermute | solution.py:373
  124.3 11.0 %collective-permute-start.13 = (bf16[1024,256]{1,0:T(8,128)(2,1)S(1)}, bf16[1024,256]{1,0:T(8,128)(2,1)}, u32[]{:S(2)}, u32[]{:S(2)}) collective-permute-start(bf16[1024,256]{1,0:T(8,128)(2,1)S(1)} %get-tuple-element.181.refs_0_), channel_id=1, source_target_pairs={{0,8},{2,10},{4,12},{6,14},{8,16},{10,18},{12,20},{14,22},{16,24},... | collective-permute-start | bytes 1572872 | tf_op jit(solution)/shard_map/ppermute | solution.py:429
  136.7 10.5 %collective-permute-start.19 = (bf16[1024,256]{1,0:T(8,128)(2,1)S(1)}, bf16[1024,256]{1,0:T(8,128)(2,1)}, u32[]{:S(2)}, u32[]{:S(2)}) collective-permute-start(bf16[1024,256]{1,0:T(8,128)(2,1)S(1)} %get-tuple-element.179.refs_1_), channel_id=1, source_target_pairs={{0,8},{2,10},{4,12},{6,14},{8,16},{10,18},{12,20},{14,22},{16,24},... | collective-permute-start | bytes 1572872 | tf_op jit(solution)/shard_map/ppermute | solution.py:429
  153.3 5.2 %collective-permute-start.16 = (bf16[1024,256]{1,0:T(8,128)(2,1)}, bf16[1024,256]{1,0:T(8,128)(2,1)S(1)}, u32[]{:S(2)}, u32[]{:S(2)}) collective-permute-start(bf16[1024,256]{1,0:T(8,128)(2,1)} %collective-permute-done.13.refs_0_.refs_2_), channel_id=1, source_target_pairs={{0,8},{2,10},{4,12},{6,14},{8,16},{10,18},{12,20},{14,22},{16,24},... | collective-permute-start | bytes 1572872 | tf_op jit(solution)/shard_map/ppermute | solution.py:429
  163.4 6.4 %collective-permute-start.25 = (bf16[1024,256]{1,0:T(8,128)(2,1)}, bf16[1024,256]{1,0:T(8,128)(2,1)S(1)}, u32[]{:S(2)}, u32[]{:S(2)}) collective-permute-start(bf16[1024,256]{1,0:T(8,128)(2,1)} %collective-permute-done.19.refs_1_.refs_3_), channel_id=1, source_target_pairs={{0,8},{2,10},{4,12},{6,14},{8,16},{10,18},{12,20},{14,22},{16,24},... | collective-permute-start | bytes 1572872 | tf_op jit(solution)/shard_map/ppermute | solution.py:429
  176.8 4.1 %collective-permute-start.22 = (bf16[1024,256]{1,0:T(8,128)(2,1)S(1)}, bf16[1024,256]{1,0:T(8,128)(2,1)S(1)}, u32[]{:S(2)}, u32[]{:S(2)}) collective-permute-start(bf16[1024,256]{1,0:T(8,128)(2,1)S(1)} %collective-permute-done.16.refs_0_.refs_8_), channel_id=1, source_target_pairs={{0,8},{2,10},{4,12},{6,14},{8,16},{10,18},{12,20},{14,22},{16,24},... | collective-permute-start | bytes 1572872 | tf_op jit(solution)/shard_map/ppermute | solution.py:429
  196.7 6.6 %collective-permute-start.29 = (bf16[1024,256]{1,0:T(8,128)(2,1)S(1)}, bf16[1024,256]{1,0:T(8,128)(2,1)S(1)}, u32[]{:S(2)}, u32[]{:S(2)}) collective-permute-start(bf16[1024,256]{1,0:T(8,128)(2,1)S(1)} %collective-permute-done.23.refs_2_.refs_16_.refs_0_), channel_id=1, source_target_pairs={{0,8},{2,10},{4,12},{6,14},{8,16},{10,18},{12,20},{14,22},{16,24},... | collective-permute-start | bytes 1572872 | tf_op jit(solution)/shard_map/ppermute | solution.py:429
  204.8 4.1 %collective-permute-done.32.refs_1_.refs_15_ = bf16[1024,256]{1,0:T(8,128)(2,1)S(1)} collective-permute-done((bf16[1024,256]{1,0:T(8,128)(2,1)S(1)}, bf16[1024,256]{1,0:T(8,128)(2,1)S(1)}, u32[]{:S(2)}, u32[]{:S(2)}) %collective-permute-start.32) | collective-permute-done | bytes 524320 | tf_op jit(solution)/shard_map/ppermute | solution.py:429
  212.5 5.7 %collective-permute-start.39 = (bf16[1024,256]{1,0:T(8,128)(2,1)S(1)}, bf16[1024,256]{1,0:T(8,128)(2,1)S(1)}, u32[]{:S(2)}, u32[]{:S(2)}) collective-permute-start(bf16[1024,256]{1,0:T(8,128)(2,1)S(1)} %collective-permute-done.33.refs_3_.refs_17_.refs_1_), channel_id=1, source_target_pairs={{0,8},{2,10},{4,12},{6,14},{8,16},{10,18},{12,20},{14,22},{16,24},... | collective-permute-start | bytes 1572872 | tf_op jit(solution)/shard_map/ppermute | solution.py:429
  223.8 5.6 %collective-permute-done.39.refs_1_.refs_21_.refs_5_ = bf16[1024,256]{1,0:T(8,128)(2,1)S(1)} collective-permute-done((bf16[1024,256]{1,0:T(8,128)(2,1)S(1)}, bf16[1024,256]{1,0:T(8,128)(2,1)S(1)}, u32[]{:S(2)}, u32[]{:S(2)}) %collective-permute-start.39) | collective-permute-done | bytes 524320 | tf_op jit(solution)/shard_map/ppermute | solution.py:429
  240.5 4.4 %early.4.refs_36_ = f32[256,2048]{1,0:T(8,128)S(1)} custom-call(bf16[1024,256]{1,0:T(8,128)(2,1)S(1)} %get-tuple-element.181.refs_0_, bf16[1024,256]{1,0:T(8,128)(2,1)S(1)} %get-tuple-element.179.refs_1_, bf16[1024,256]{1,0:T(8,128)(2,1)} %collective-permute-done.13.refs_0_.refs_2_, bf16[1024,256]{1,0:T(8,128)(2,1)} %collective-permute-done.19.refs_1_.refs_3_, ...), custom_call_target="tpu_custom_call" | custom-call | tf_op jit(solution)/shard_map/early/pallas_call | solution.py:267
  246.5 8.4 %collective-permute-done.36.refs_0_.refs_26_.refs_10_ = bf16[1024,256]{1,0:T(8,128)(2,1)S(1)} collective-permute-done((bf16[1024,256]{1,0:T(8,128)(2,1)S(1)}, bf16[1024,256]{1,0:T(8,128)(2,1)S(1)}, u32[]{:S(2)}, u32[]{:S(2)}) %collective-permute-start.36) | collective-permute-done | bytes 524320 | tf_op jit(solution)/shard_map/ppermute | solution.py:429
  288.2 6.2 %late0.1 = (f32[256,2048]{1,0:T(8,128)S(1)}, bf16[256,2048]{1,0:T(8,128)(2,1)S(1)}, bf16[256,2048]{1,0:T(8,128)(2,1)S(1)}) custom-call(f32[8,256]{1,0:T(8,128)S(1)} %get-tuple-element.166.mine_square_ref, f32[8,256]{1,0:T(8,128)S(1)} %collective-permute-done.47.other_square_ref, bf16[1024,256]{1,0:T(8,128)(2,1)S(1)} %get-tuple-element.181.refs_0_, ...), custom_call_target="tpu_custom_call" | custom-call | tf_op jit(solution)/shard_map/late0/pallas_call | solution.py:293
  301.7 6.2 %late1.1 = (f32[256,2048]{1,0:T(8,128)S(1)}, bf16[256,2048]{1,0:T(8,128)(2,1)S(1)}, bf16[256,2048]{1,0:T(8,128)(2,1)S(1)}) custom-call(f32[8,256]{1,0:T(8,128)S(1)} %get-tuple-element.166.mine_square_ref, f32[8,256]{1,0:T(8,128)S(1)} %collective-permute-done.47.other_square_ref, bf16[1024,256]{1,0:T(8,128)(2,1)S(1)} %get-tuple-element.181.refs_0_, ...), custom_call_target="tpu_custom_call" | custom-call | tf_op jit(solution)/shard_map/late1/pallas_call | solution.py:293
  315.1 6.1 %late2.1 = (f32[256,2048]{1,0:T(8,128)S(1)}, bf16[256,2048]{1,0:T(8,128)(2,1)S(1)}, bf16[256,2048]{1,0:T(8,128)(2,1)S(1)}) custom-call(f32[8,256]{1,0:T(8,128)S(1)} %get-tuple-element.166.mine_square_ref, f32[8,256]{1,0:T(8,128)S(1)} %collective-permute-done.47.other_square_ref, bf16[1024,256]{1,0:T(8,128)(2,1)S(1)} %get-tuple-element.181.refs_0_, ...), custom_call_target="tpu_custom_call" | custom-call | tf_op jit(solution)/shard_map/late2/pallas_call | solution.py:293
  328.1 5.4 %late3.1 = f32[256,2048]{1,0:T(8,128)} custom-call(f32[8,256]{1,0:T(8,128)S(1)} %get-tuple-element.166.mine_square_ref, f32[8,256]{1,0:T(8,128)S(1)} %collective-permute-done.47.other_square_ref, bf16[1024,256]{1,0:T(8,128)(2,1)S(1)} %get-tuple-element.181.refs_0_, bf16[1024,256]{1,0:T(8,128)(2,1)S(1)} %get-tuple-element.179.refs_1_, ...), custom_call_target="tpu_custom_call" | custom-call | tf_op jit(solution)/shard_map/late3/pallas_call | solution.py:293
  (280 shorter events, 147.1 us)
Async XLA Ops:
  2.1 26.7 %collective-permute-start.2 = (bf16[256,512]{1,0:T(8,128)(2,1)}, bf16[256,512]{1,0:T(8,128)(2,1)}, u32[]{:S(2)}, u32[]{:S(2)}) collective-permute-start(bf16[256,512]{1,0:T(8,128)(2,1)} %get-tuple-element.96), channel_id=1, source_target_pairs={{0,24},{2,26},{4,28},{6,30},{8,16},{10,18},{12,20},{14,22},{16,8},... | collective-permute-start | bytes 786440 | tf_op jit(solution)/shard_map/ppermute | solution.py:369
  7.1 22.6 %collective-permute-start.1 = (bf16[256,512]{1,0:T(8,128)(2,1)}, bf16[256,512]{1,0:T(8,128)(2,1)}, u32[]{:S(2)}, u32[]{:S(2)}) collective-permute-start(bf16[256,512]{1,0:T(8,128)(2,1)} %get-tuple-element.96), channel_id=1, source_target_pairs={{0,16},{2,18},{4,20},{6,22},{8,24},{10,26},{12,28},{14,30},{16,0},... | collective-permute-start | bytes 786440 | tf_op jit(solution)/shard_map/ppermute | solution.py:369
  7.1 22.6 %collective-permute-start = (bf16[256,512]{1,0:T(8,128)(2,1)}, bf16[256,512]{1,0:T(8,128)(2,1)}, u32[]{:S(2)}, u32[]{:S(2)}) collective-permute-start(bf16[256,512]{1,0:T(8,128)(2,1)} %get-tuple-element.96), channel_id=1, source_target_pairs={{0,8},{2,10},{4,12},{6,14},{8,0},{10,2},{12,4},{14,6},{16,24},{18,... | collective-permute-start | bytes 786440 | tf_op jit(solution)/shard_map/ppermute | solution.py:369
  33.8 31.5 %collective-permute-start.3 = (bf16[256,1024]{1,0:T(8,128)(2,1)}, bf16[256,1024]{1,0:T(8,128)(2,1)}, u32[]{:S(2)}, u32[]{:S(2)}) collective-permute-start(bf16[256,1024]{1,0:T(8,128)(2,1)} %get-tuple-element.93), channel_id=1, source_target_pairs={{0,8},{2,10},{4,12},{6,14},{8,0},{10,2},{12,4},{14,6},{16,24},{18,... | collective-permute-start | bytes 1572872 | tf_op jit(solution)/shard_map/ppermute | solution.py:369
  34.4 38.5 %collective-permute-start.4 = (bf16[256,1024]{1,0:T(8,128)(2,1)}, bf16[256,1024]{1,0:T(8,128)(2,1)}, u32[]{:S(2)}, u32[]{:S(2)}) collective-permute-start(bf16[256,1024]{1,0:T(8,128)(2,1)} %get-tuple-element.94), channel_id=1, source_target_pairs={{0,16},{2,18},{4,20},{6,22},{8,24},{10,26},{12,28},{14,30},{16,0},... | collective-permute-start | bytes 1572872 | tf_op jit(solution)/shard_map/ppermute | solution.py:369
  37.3 35.6 %collective-permute-start.5 = (bf16[256,1024]{1,0:T(8,128)(2,1)}, bf16[256,1024]{1,0:T(8,128)(2,1)}, u32[]{:S(2)}, u32[]{:S(2)}) collective-permute-start(bf16[256,1024]{1,0:T(8,128)(2,1)} %get-tuple-element.95), channel_id=1, source_target_pairs={{0,24},{2,26},{4,28},{6,30},{8,16},{10,18},{12,20},{14,22},{16,8},... | collective-permute-start | bytes 1572872 | tf_op jit(solution)/shard_map/ppermute | solution.py:369
  82.4 25.3 %collective-permute-start.9 = (bf16[2048,256]{1,0:T(8,128)(2,1)S(1)}, bf16[2048,256]{1,0:T(8,128)(2,1)S(1)}, u32[]{:S(2)}, u32[]{:S(2)}) collective-permute-start(bf16[2048,256]{1,0:T(8,128)(2,1)S(1)} %get-tuple-element.106), channel_id=1, source_target_pairs={{0,2},{2,0},{4,6},{6,4},{8,10},{10,8},{12,14},{14,12},{16,18},{18,... | collective-permute-start | bytes 3145736 | tf_op jit(solution)/shard_map/ppermute | solution.py:373
  83.9 25.4 %collective-permute-start.11 = (bf16[2048,256]{1,0:T(8,128)(2,1)S(1)}, bf16[2048,256]{1,0:T(8,128)(2,1)S(1)}, u32[]{:S(2)}, u32[]{:S(2)}) collective-permute-start(bf16[2048,256]{1,0:T(8,128)(2,1)S(1)} %get-tuple-element.109), channel_id=1, source_target_pairs={{0,4},{2,6},{4,0},{6,2},{8,12},{10,14},{12,8},{14,10},{16,20},{18,... | collective-permute-start | bytes 3145736 | tf_op jit(solution)/shard_map/ppermute | solution.py:373
  109.5 25.8 %collective-permute-start.12 = (bf16[1024,256]{1,0:T(8,128)(2,1)S(1)}, bf16[1024,256]{1,0:T(8,128)(2,1)S(1)}, u32[]{:S(2)}, u32[]{:S(2)}) collective-permute-start(bf16[1024,256]{1,0:T(8,128)(2,1)S(1)} %add_convert_fusion), channel_id=1, source_target_pairs={{0,2},{2,0},{4,6},{6,4},{8,10},{10,8},{12,14},{14,12},{16,18},{18,... | collective-permute-start | bytes 1572872 | tf_op jit(solution)/shard_map/ppermute | solution.py:373
  122.8 27.4 %collective-permute-start.14 = (bf16[1024,256]{1,0:T(8,128)(2,1)S(1)}, bf16[1024,256]{1,0:T(8,128)(2,1)S(1)}, u32[]{:S(2)}, u32[]{:S(2)}) collective-permute-start(bf16[1024,256]{1,0:T(8,128)(2,1)S(1)} %get-tuple-element.181.refs_0_), channel_id=1, source_target_pairs={{0,2},{2,0},{4,6},{6,4},{8,10},{10,8},{12,14},{14,12},{16,18},{18,... | collective-permute-start | bytes 1572872 | tf_op jit(solution)/shard_map/ppermute | solution.py:373
  124.3 25.9 %collective-permute-start.13 = (bf16[1024,256]{1,0:T(8,128)(2,1)S(1)}, bf16[1024,256]{1,0:T(8,128)(2,1)}, u32[]{:S(2)}, u32[]{:S(2)}) collective-permute-start(bf16[1024,256]{1,0:T(8,128)(2,1)S(1)} %get-tuple-element.181.refs_0_), channel_id=1, source_target_pairs={{0,8},{2,10},{4,12},{6,14},{8,16},{10,18},{12,20},{14,22},{16,24},... | collective-permute-start | bytes 1572872 | tf_op jit(solution)/shard_map/ppermute | solution.py:429
  136.1 22.4 %collective-permute-start.20 = (bf16[1024,256]{1,0:T(8,128)(2,1)S(1)}, bf16[1024,256]{1,0:T(8,128)(2,1)}, u32[]{:S(2)}, u32[]{:S(2)}) collective-permute-start(bf16[1024,256]{1,0:T(8,128)(2,1)S(1)} %get-tuple-element.179.refs_1_), channel_id=1, source_target_pairs={{0,2},{2,0},{4,6},{6,4},{8,10},{10,8},{12,14},{14,12},{16,18},{18,... | collective-permute-start | bytes 1572872 | tf_op jit(solution)/shard_map/ppermute | solution.py:373
  136.7 21.8 %collective-permute-start.19 = (bf16[1024,256]{1,0:T(8,128)(2,1)S(1)}, bf16[1024,256]{1,0:T(8,128)(2,1)}, u32[]{:S(2)}, u32[]{:S(2)}) collective-permute-start(bf16[1024,256]{1,0:T(8,128)(2,1)S(1)} %get-tuple-element.179.refs_1_), channel_id=1, source_target_pairs={{0,8},{2,10},{4,12},{6,14},{8,16},{10,18},{12,20},{14,22},{16,24},... | collective-permute-start | bytes 1572872 | tf_op jit(solution)/shard_map/ppermute | solution.py:429
  151.8 20.5 %collective-permute-start.17 = (bf16[1024,256]{1,0:T(8,128)(2,1)}, bf16[1024,256]{1,0:T(8,128)(2,1)S(1)}, u32[]{:S(2)}, u32[]{:S(2)}) collective-permute-start(bf16[1024,256]{1,0:T(8,128)(2,1)} %collective-permute-done.13.refs_0_.refs_2_), channel_id=1, source_target_pairs={{0,2},{2,0},{4,6},{6,4},{8,10},{10,8},{12,14},{14,12},{16,18},{18,... | collective-permute-start | bytes 1572872 | tf_op jit(solution)/shard_map/ppermute | solution.py:373
  153.3 19.0 %collective-permute-start.16 = (bf16[1024,256]{1,0:T(8,128)(2,1)}, bf16[1024,256]{1,0:T(8,128)(2,1)S(1)}, u32[]{:S(2)}, u32[]{:S(2)}) collective-permute-start(bf16[1024,256]{1,0:T(8,128)(2,1)} %collective-permute-done.13.refs_0_.refs_2_), channel_id=1, source_target_pairs={{0,8},{2,10},{4,12},{6,14},{8,16},{10,18},{12,20},{14,22},{16,24},... | collective-permute-start | bytes 1572872 | tf_op jit(solution)/shard_map/ppermute | solution.py:429
  158.5 18.2 %collective-permute-start.27 = (bf16[1024,256]{1,0:T(8,128)(2,1)}, bf16[1024,256]{1,0:T(8,128)(2,1)S(1)}, u32[]{:S(2)}, u32[]{:S(2)}) collective-permute-start(bf16[1024,256]{1,0:T(8,128)(2,1)} %collective-permute-done.19.refs_1_.refs_3_), channel_id=1, source_target_pairs={{0,4},{2,6},{4,0},{6,2},{8,12},{10,14},{12,8},{14,10},{16,20},{18,... | collective-permute-start | bytes 1572872 | tf_op jit(solution)/shard_map/ppermute | solution.py:373
  160.0 20.8 %collective-permute-start.26 = (bf16[1024,256]{1,0:T(8,128)(2,1)}, bf16[1024,256]{1,0:T(8,128)(2,1)S(1)}, u32[]{:S(2)}, u32[]{:S(2)}) collective-permute-start(bf16[1024,256]{1,0:T(8,128)(2,1)} %collective-permute-done.19.refs_1_.refs_3_), channel_id=1, source_target_pairs={{0,2},{2,0},{4,6},{6,4},{8,10},{10,8},{12,14},{14,12},{16,18},{18,... | collective-permute-start | bytes 1572872 | tf_op jit(solution)/shard_map/ppermute | solution.py:373
  183.8 19.6 %collective-permute-start.33 = (bf16[1024,256]{1,0:T(8,128)(2,1)S(1)}, bf16[1024,256]{1,0:T(8,128)(2,1)S(1)}, u32[]{:S(2)}, u32[]{:S(2)}) collective-permute-start(bf16[1024,256]{1,0:T(8,128)(2,1)S(1)} %collective-permute-done.25.refs_1_.refs_9_), channel_id=1, source_target_pairs={{0,2},{2,0},{4,6},{6,4},{8,10},{10,8},{12,14},{14,12},{16,18},{18,... | collective-permute-start | bytes 1572872 | tf_op jit(solution)/shard_map/ppermute | solution.py:373
  190.0 22.5 %collective-permute-start.31 = (bf16[1024,256]{1,0:T(8,128)(2,1)S(1)}, bf16[1024,256]{1,0:T(8,128)(2,1)S(1)}, u32[]{:S(2)}, u32[]{:S(2)}) collective-permute-start(bf16[1024,256]{1,0:T(8,128)(2,1)S(1)} %collective-permute-done.15.refs_4_.refs_6_), channel_id=1, source_target_pairs={{0,2},{2,0},{4,6},{6,4},{8,10},{10,8},{12,14},{14,12},{16,18},{18,... | collective-permute-start | bytes 1572872 | tf_op jit(solution)/shard_map/ppermute | solution.py:373
  195.1 23.1 %collective-permute-start.30 = (bf16[1024,256]{1,0:T(8,128)(2,1)S(1)}, bf16[1024,256]{1,0:T(8,128)(2,1)S(1)}, u32[]{:S(2)}, u32[]{:S(2)}) collective-permute-start(bf16[1024,256]{1,0:T(8,128)(2,1)S(1)} %collective-permute-done.22.refs_0_.refs_14_), channel_id=1, source_target_pairs={{0,4},{2,6},{4,0},{6,2},{8,12},{10,14},{12,8},{14,10},{16,20},{18,... | collective-permute-start | bytes 1572872 | tf_op jit(solution)/shard_map/ppermute | solution.py:373
  196.7 23.4 %collective-permute-start.29 = (bf16[1024,256]{1,0:T(8,128)(2,1)S(1)}, bf16[1024,256]{1,0:T(8,128)(2,1)S(1)}, u32[]{:S(2)}, u32[]{:S(2)}) collective-permute-start(bf16[1024,256]{1,0:T(8,128)(2,1)S(1)} %collective-permute-done.23.refs_2_.refs_16_.refs_0_), channel_id=1, source_target_pairs={{0,8},{2,10},{4,12},{6,14},{8,16},{10,18},{12,20},{14,22},{16,24},... | collective-permute-start | bytes 1572872 | tf_op jit(solution)/shard_map/ppermute | solution.py:429
  203.3 19.6 %collective-permute-start.41 = (bf16[1024,256]{1,0:T(8,128)(2,1)}, bf16[1024,256]{1,0:T(8,128)(2,1)S(1)}, u32[]{:S(2)}, u32[]{:S(2)}) collective-permute-start(bf16[1024,256]{1,0:T(8,128)(2,1)} %collective-permute-done.21.refs_5_.refs_7_), channel_id=1, source_target_pairs={{0,2},{2,0},{4,6},{6,4},{8,10},{10,8},{12,14},{14,12},{16,18},{18,... | collective-permute-start | bytes 1572872 | tf_op jit(solution)/shard_map/ppermute | solution.py:373
  222.9 23.6 %collective-permute-start.37 = (bf16[1024,256]{1,0:T(8,128)(2,1)S(1)}, bf16[1024,256]{1,0:T(8,128)(2,1)S(1)}, u32[]{:S(2)}, u32[]{:S(2)}) collective-permute-start(bf16[1024,256]{1,0:T(8,128)(2,1)S(1)} %collective-permute-done.23.refs_2_.refs_16_.refs_0_), channel_id=1, source_target_pairs={{0,4},{2,6},{4,0},{6,2},{8,12},{10,14},{12,8},{14,10},{16,20},{18,... | collective-permute-start | bytes 1572872 | tf_op jit(solution)/shard_map/ppermute | solution.py:373
  233.9 21.0 %collective-permute-start.36 = (bf16[1024,256]{1,0:T(8,128)(2,1)S(1)}, bf16[1024,256]{1,0:T(8,128)(2,1)S(1)}, u32[]{:S(2)}, u32[]{:S(2)}) collective-permute-start(bf16[1024,256]{1,0:T(8,128)(2,1)S(1)} %collective-permute-done.31.refs_4_.refs_24_.refs_8_), channel_id=1, source_target_pairs={{0,8},{2,10},{4,12},{6,14},{8,16},{10,18},{12,20},{14,22},{16,24},... | collective-permute-start | bytes 1572872 | tf_op jit(solution)/shard_map/ppermute | solution.py:429
  (107 other events, 1324.4 us)

commit v12 on v9

v12 whole, which is shorter than its diff:
```python
import functools
import math

import jax
import jax.numpy as jnp
from jax import lax
from jax.experimental import pallas as pl
from jax.experimental.pallas import tpu as pltpu
from jax.sharding import PartitionSpec as P

LANES = 128
GROUP = 8
CHUNKS = 4
INNER = 4
VMEM_BYTES = 24 * 1024 * 1024
ANY = pl.BlockSpec(memory_space=pl.ANY)
VMEM = pl.BlockSpec(memory_space=pltpu.VMEM)


def lookup_kernel(codes_ref, table_ref, out_ref, ids_ref):
    subs, rows = codes_ref.shape[1:]
    width = table_ref.shape[1]
    halves = table_ref.shape[2] // LANES
    first_out = pl.program_id(0) * (subs * width)
    ids_ref[...] = codes_ref[0].astype(jnp.float32).astype(jnp.int32)

    def body(step, carry):
        base = pl.multiple_of(step * GROUP, GROUP)
        for first in range(0, rows, LANES):
            lanes = pl.ds(pl.multiple_of(pl.program_id(1) * rows + first, LANES), LANES)
            ids_all = ids_ref[pl.ds(base, GROUP), first : first + LANES]
            for pair in range(0, GROUP, 2):
                both = []
                for sub in (pair, pair + 1):
                    ids = jnp.broadcast_to(ids_all[sub : sub + 1], (width, LANES))
                    lane = jnp.bitwise_and(ids, LANES - 1)
                    picked = None
                    for half in range(halves):
                        entries = table_ref[base + sub, :, half * LANES : (half + 1) * LANES]
                        got = jnp.take_along_axis(
                            entries, lane, axis=1, mode="promise_in_bounds"
                        )
                        picked = got if half == 0 else jnp.where(ids >= half * LANES, got, picked)
                    both.append(picked)
                row = pl.multiple_of(first_out + (base + pair) * width, 2 * width)
                out_ref[pl.ds(row, 2 * width), lanes] = jnp.concatenate(both, axis=0).astype(
                    out_ref.dtype
                )
        return carry

    lax.fori_loop(0, subs // GROUP, body, 0)


def rebuild_rows(codes, table):
    blocks, subs, rows = codes.shape
    width, centroids = table.shape[1:]
    tile = min(64, subs)
    return pl.pallas_call(
        lookup_kernel,
        grid=(subs // tile, blocks),
        in_specs=[
            pl.BlockSpec((1, tile, rows), lambda m, s: (s, m, 0)),
            pl.BlockSpec((tile, width, centroids), lambda m, s: (m, 0, 0)),
        ],
        out_specs=VMEM,
        scratch_shapes=[pltpu.VMEM((tile, rows), jnp.int32)],
        out_shape=pltpu.VMEM((subs * width, blocks * rows), jnp.bfloat16),
        compiler_params=pltpu.CompilerParams(vmem_limit_bytes=VMEM_BYTES),
        name="lookup",
    )(codes, table)


def slices_kernel(steps, streams, inner_size, place_ref, weights_ref, rows_ref, *outs):
    width = outs[0].shape[1] // inner_size
    wide = width * streams * inner_size
    rows, part_rows = outs[0].shape[0], outs[-1].shape[0]

    def scaled(first, step, stream):
        base = lax.bitwise_xor(place_ref[2], step) * wide + stream * width
        column = jnp.broadcast_to(weights_ref[:, pl.ds(first, part_rows)], (LANES, part_rows)).T
        for index in range(inner_size):
            lanes = pl.ds(pl.multiple_of(base + index * width * streams, LANES), width)
            values = rows_ref[pl.ds(first, part_rows), lanes].astype(jnp.float32)
            yield slice(index * width, (index + 1) * width), (values * column).astype(outs[0].dtype)

    for index, out_ref in enumerate(outs):
        stream, slot = divmod(index, 1 + len(steps))
        if slot:
            first = pl.multiple_of(place_ref[0] * part_rows, part_rows)
            for span, values in scaled(first, steps[slot - 1], stream):
                out_ref[:, span] = values
        else:
            for first in range(0, rows, part_rows):
                for span, values in scaled(first, 0, stream):
                    out_ref[first : first + part_rows, span] = values


def weighted_slices(place, weights, embeddings, part_rows, steps, streams, inner_size, wide):
    rows = embeddings.shape[0]
    count = 1 + len(steps)
    if part_rows % LANES or wide // streams // inner_size != LANES:
        scaled = (weights[:, None] * embeddings.astype(jnp.float32)).astype(jnp.bfloat16)
        parts = [lax.dynamic_slice_in_dim(scaled, place[2] * wide, wide, 1)]
        for step in steps:
            start = (place[0] * part_rows, (place[2] ^ step) * wide)
            parts.append(lax.dynamic_slice(scaled, start, (part_rows, wide)))
        split = [part.reshape(part.shape[0], inner_size, streams, -1) for part in parts]
        return [
            [part[:, :, stream].reshape(part.shape[0], -1) for part in split]
            for stream in range(streams)
        ]
    shapes = [(rows, wide // streams)] + [(part_rows, wide // streams)] * len(steps)
    outs = pl.pallas_call(
        functools.partial(slices_kernel, steps, streams, inner_size),
        in_specs=[pl.BlockSpec(memory_space=pltpu.SMEM), VMEM, VMEM],
        out_specs=[VMEM] * (count * streams),
        out_shape=[pltpu.VMEM(shape, jnp.bfloat16) for shape in shapes] * streams,
        compiler_params=pltpu.CompilerParams(vmem_limit_bytes=VMEM_BYTES),
        name="slices",
    )(place, *in_vmem(weights[None, :], embeddings))
    return [list(outs[first : first + count]) for first in range(0, count * streams, count)]


def cross_kernel(plan, place_ref, own_ref, rebuilt_ref, prior_ref, local_ref, *refs):
    pieces, outs = refs[: len(refs) - len(plan)], refs[len(refs) - len(plan) :]
    rows = local_ref.shape[0]
    part_rows, col = (pieces[0].shape[0], rows // pieces[0].shape[0]) if pieces else (rows, 1)
    for (targets, first_row), out_ref in zip(plan, outs):
        span = slice(first_row, first_row + out_ref.shape[0])
        width = out_ref.shape[1] // len(targets)
        left = [own_ref[span, :]]
        for index in range(len(pieces)):
            step, turn = divmod(index, col)
            first = step * rows + lax.rem(place_ref[0] + turn, col) * part_rows
            left.append(rebuilt_ref[span, pl.ds(pl.multiple_of(first, part_rows), part_rows)])
        right = []
        for target in targets:
            place = lax.bitwise_xor(place_ref[1], target)
            lanes = pl.ds(pl.multiple_of(place * width, width), width)
            right.append(
                jnp.concatenate([part[:, lanes] for part in (local_ref, *pieces)], axis=0)
            )
        total = jnp.dot(
            jnp.concatenate(left, axis=1), jnp.concatenate(right, axis=1),
            preferred_element_type=jnp.float32,
        )
        if targets[0] == 0:
            out_ref[:, :width] = (total[:, :width] + prior_ref[span, :]).astype(out_ref.dtype)
            out_ref[:, width:] = total[:, width:].astype(out_ref.dtype)
        else:
            out_ref[...] = total.astype(out_ref.dtype)


def cross_blocks(plan, dtype, place, own, rebuilt, prior, local, pieces):
    operands = in_vmem(own, rebuilt, prior, local, *pieces)
    half, width = prior.shape[0] // 2, prior.shape[1]
    return pl.pallas_call(
        functools.partial(cross_kernel, plan),
        in_specs=[pl.BlockSpec(memory_space=pltpu.SMEM)] + [VMEM] * len(operands),
        out_specs=[VMEM] * len(plan),
        out_shape=[pltpu.VMEM((half, len(targets) * width), dtype) for targets, _ in plan],
        compiler_params=pltpu.CompilerParams(vmem_limit_bytes=VMEM_BYTES),
        name="cross",
    )(place, *operands)


def product_of(value_ref, pieces, inner_ref, index):
    block_values = jnp.concatenate([piece_ref[...] for piece_ref in pieces], axis=1)
    block = block_values.shape[1]
    product = jnp.dot(value_ref[...], block_values, preferred_element_type=jnp.float32)
    inner_ref[index * block : (index + 1) * block, :] = product.T.astype(inner_ref.dtype)


def first_kernel(streams, own_ref, before_ref, *refs):
    panel, (inner_ref, square_ref) = refs[:-2], refs[-2:]
    cols, width = panel[0].shape
    square = before_ref[...]
    for index in range(len(panel) // streams):
        pieces = panel[streams * index : streams * (index + 1)]
        product_of(own_ref, pieces, inner_ref, index)
        for piece_ref in pieces:
            values = piece_ref[...].astype(jnp.float32)
            square += jnp.sum((values * values).reshape(cols // 8, 8, width), axis=0)
    square_ref[...] = square


def add_up(mine, other, sum_ref):
    first = 0
    for mine_ref, other_ref in zip(mine, other):
        sum_ref[first : first + mine_ref.shape[0], :] = mine_ref[...] + other_ref[...]
        first += mine_ref.shape[0]


def gram_rows(panel, sum_ref, index):
    chunk = panel[0].shape[0] // CHUNKS
    span = slice(index * chunk, (index + 1) * chunk)
    rows = jnp.concatenate([piece_ref[span, :] for piece_ref in panel], axis=1)
    return span, jnp.dot(rows, sum_ref[...], preferred_element_type=jnp.float32)


def early_kernel(count, parts, *refs):
    panel, refs = refs[:count], refs[count:]
    mine, other, (out_ref, sum_ref) = refs[:parts], refs[parts : 2 * parts], refs[2 * parts :]
    add_up(mine, other, sum_ref)
    for index in range(CHUNKS):
        span, made = gram_rows(panel, sum_ref, index)
        out_ref[span, :] = made


def late_kernel(step, streams, counts, parts, mine_square_ref, other_square_ref, *refs):
    last = step == 3
    states = 2 if last else 1
    first_late, late = counts
    panel, refs = refs[: first_late + late], refs[first_late + late :]
    mine, other, refs = refs[:parts], refs[parts : 2 * parts], refs[2 * parts :]
    early_ref, held, refs = refs[0], refs[1 : 1 + states], refs[1 + states :]
    if last:
        out_ref, sum_ref = refs
    else:
        state_ref, value_ref, inner_ref, sum_ref = refs
    width = panel[0].shape[1]
    model_width = len(panel) * width
    total = jnp.sum(mine_square_ref[...] + other_square_ref[...], axis=(0, 1), keepdims=True)
    scale = model_width / (1.96 * total)
    add_up(mine, other, sum_ref)
    for index in range(CHUNKS):
        span, made = gram_rows(panel[first_late:], sum_ref, index)
        made += early_ref[span, :]
        if step == 2:
            made = made * scale
        else:
            made = 1.5 * held[0][span, :] - (0.5 * scale) * made
        if last:
            made = (1.5 * held[1][span, :] - 0.5 * made) * (math.sqrt(model_width) * jnp.sqrt(scale))
            out_ref[:, span] = made.T
        else:
            state_ref[span, :] = made
            value_ref[:, span] = made.T.astype(value_ref.dtype)
    if last:
        return
    for index in range(inner_ref.shape[0] // (streams * width)):
        product_of(value_ref, panel[streams * index : streams * (index + 1)], inner_ref, index)


def rest_kernel(streams, value_ref, *refs):
    panel, inner_ref = refs[:-1], refs[-1]
    for index in range(len(panel) // streams):
        product_of(value_ref, panel[streams * index : streams * (index + 1)], inner_ref, index)


def in_vmem(*values):
    return [pltpu.with_memory_space_constraint(value, pltpu.VMEM) for value in values]


def apply_first(own, square, panel):
    block = own.shape[0]
    streams = block // panel[0].shape[1]
    return pl.pallas_call(
        functools.partial(first_kernel, streams),
        in_specs=[VMEM] * (2 + len(panel)),
        out_specs=[VMEM, VMEM],
        out_shape=[
            pltpu.VMEM((len(panel) // streams * block, block), jnp.bfloat16),
            pltpu.VMEM(square.shape, jnp.float32),
        ],
        compiler_params=pltpu.CompilerParams(vmem_limit_bytes=VMEM_BYTES),
        name="first",
    )(*in_vmem(own, square, *panel))


def apply_early(panel, inner):
    cols, width = panel[0].shape
    mine, other = zip(*inner)
    operands = in_vmem(*panel, *mine, *other)
    return pl.pallas_call(
        functools.partial(early_kernel, len(panel), len(inner)),
        in_specs=[VMEM] * len(operands),
        out_specs=VMEM,
        out_shape=pltpu.VMEM((cols, mine[0].shape[1]), jnp.float32),
        scratch_shapes=[pltpu.VMEM((len(panel) * width, mine[0].shape[1]), jnp.bfloat16)],
        compiler_params=pltpu.CompilerParams(vmem_limit_bytes=VMEM_BYTES),
        name="early",
    )(*operands)


def apply_late(step, early, panel, inner, squares, held):
    mine, other = zip(*inner)
    cols, width = panel[0].shape
    block = mine[0].shape[1]
    late = sum(part.shape[0] for part in mine) // width
    last = step == 3
    if last:
        out_shape = jax.ShapeDtypeStruct((block, cols), jnp.float32)
    else:
        out_shape = [
            pltpu.VMEM((cols, block), jnp.float32),
            pltpu.VMEM((block, cols), jnp.bfloat16),
            pltpu.VMEM((len(panel) // 2 * width, block), jnp.bfloat16),
        ]
    operands = in_vmem(*squares, *panel, *mine, *other, early, *held)
    return pl.pallas_call(
        functools.partial(late_kernel, step, block // width, (len(panel) - late, late), len(inner)),
        in_specs=[VMEM] * len(operands),
        out_specs=VMEM if last else [VMEM] * 3,
        out_shape=out_shape,
        scratch_shapes=[pltpu.VMEM((late * width, block), jnp.bfloat16)],
        compiler_params=pltpu.CompilerParams(vmem_limit_bytes=VMEM_BYTES),
        name="late%d" % step,
    )(*operands)


def apply_rest(value, panel):
    block = value.shape[0]
    width = panel[0].shape[1]
    operands = in_vmem(value, *panel)
    return pl.pallas_call(
        functools.partial(rest_kernel, block // width),
        in_specs=[VMEM] * len(operands),
        out_specs=VMEM,
        out_shape=pltpu.VMEM((len(panel) * width, block), jnp.bfloat16),
        compiler_params=pltpu.CompilerParams(vmem_limit_bytes=VMEM_BYTES),
        name="rest",
    )(*operands)


def swap_cores(value):
    return lax.ppermute(value, "col", [(0, 1), (1, 0)])


def both_cores(value):
    if lax.axis_size("col") == 2:
        return value, swap_cores(value)
    total = lax.psum(value.astype(jnp.float32), "col").astype(value.dtype)
    return total, jnp.zeros_like(total)


def gather_rounds(outer_size):
    held = {(0, 0)}
    last = outer_size - 1
    rounds = []
    for k in range(1, outer_size):
        rounds.append([((k, 0), (k - 1, 0)), ((k - 1, 1), (k - 1, 0)), ((k - 1, 2), (k - 1, 0))])
    held.update(key for moves in rounds for key, _ in moves)
    rest = [(last, 1), (last, 2)] + [(k, 3) for k in range(outer_size)]
    while rest:
        moves, taken = [], set()
        for key in rest:
            ways = [("y", (key[0], key[1] ^ 2)), ("x", (key[0], key[1] ^ 1)), ("z", (key[0] - 1, key[1]))]
            if key == (last, 1):
                ways.reverse()
            if key[1] == 3:
                ways = ways[::-1] if (key[0] - 1, 3) in held else ways
            for link, source in ways:
                if source in held and link not in taken:
                    taken.add(link)
                    moves.append((key, source))
                    break
        held.update(key for key, _ in moves)
        rest = [key for key in rest if key not in held]
        rounds.append(moves)
    return rounds


def shards(embeddings, rotation, codes, codebooks):
    tok_rows, model_width = embeddings.shape
    dp, col = lax.axis_size("dp"), lax.axis_size("col")
    rows_total = tok_rows * dp
    block = model_width // dp
    inner_size = math.gcd(dp, INNER)
    outer_size = dp // inner_size
    wide = model_width // outer_size
    part_rows = tok_rows // col
    outer, inner = lax.axis_index("dp") // inner_size, lax.axis_index("dp") % inner_size
    core = lax.axis_index("col")

    def from_outer(value, step):
        pairs = [(i, (i // inner_size ^ step) * inner_size + i % inner_size) for i in range(dp)]
        return lax.ppermute(value, "dp", pairs)

    def from_inner(value, step):
        pairs = [(i, i // inner_size * inner_size + (i % inner_size ^ step)) for i in range(dp)]
        return lax.ppermute(value, "dp", pairs)

    steps = list(range(1, outer_size))
    codes_t = codes.T.astype(jnp.bfloat16)
    group_codes = [from_outer(codes_t, step) for step in steps]

    table = jnp.transpose(codebooks, (0, 2, 1)).astype(jnp.float32)
    own = rebuild_rows(codes_t[None], table)
    rotated = lax.dot_general(
        rotation, embeddings, (((0,), (1,)), ((), ())), preferred_element_type=jnp.float32
    )
    residue = rotated - own.astype(jnp.float32)
    row_error = lax.psum(jnp.sum(residue * residue, axis=0), "col")
    weights = 1.0 / (1.0 + row_error / (2.0 * model_width))
    weights, group_codes = lax.optimization_barrier((weights, group_codes))

    streams = 2 if block % (2 * LANES) == 0 else 1
    width = block // streams
    place = jnp.stack([core, inner, outer]).astype(jnp.int32)
    slices = weighted_slices(
        place, weights, embeddings, part_rows, steps, streams, inner_size, wide
    )
    rebuilt = rebuild_rows(jnp.stack(group_codes), table)
    start_row = lax.axis_index("dp") * block
    prior = lax.dynamic_slice_in_dim(rotation, start_row, block, 0).T
    prior = 0.2 * rows_total * prior.astype(jnp.float32)
    half = prior.shape[0] // 2
    near = [(1, 2), (2, 1)]
    fetched, shares = [], []
    for stream, (_, *sends) in enumerate(slices):
        if stream:
            sends, rebuilt, shares = lax.optimization_barrier((sends, rebuilt, shares))
            fetched.append(shares)
        shares = [from_outer(send, step) for send, step in zip(sends, steps)]
    fetched.append(shares)
    starts, narrow = [], []
    for stream in range(streams):
        pieces = []
        for share in fetched[stream]:
            if part_rows % LANES:
                pieces.append(lax.all_gather(share, "col", axis=0, tiled=True))
                continue
            pieces.append(share)
            for turn in range(1, col):
                pairs = [(i, (i - turn) % col) for i in range(col)]
                pieces.append(lax.ppermute(share, "col", pairs))
        if stream:
            pieces, narrow = lax.optimization_barrier((pieces, narrow))
        blocks_for = functools.partial(
            cross_blocks,
            place=place,
            own=own,
            rebuilt=rebuilt,
            prior=prior[:, stream * width : (stream + 1) * width],
            local=slices[stream][0],
            pieces=pieces,
        )
        sent = blocks_for([((one, 3), side * half) for side, (one, _) in enumerate(near)], jnp.bfloat16)
        came = [from_inner(value, one) for value, (one, _) in zip(sent, near)]
        kept = blocks_for([((0, two), side * half) for side, (_, two) in enumerate(near)], jnp.float32)
        if stream + 1 < streams:
            fetched[stream + 1], came = lax.optimization_barrier((fetched[stream + 1], came))
        sums = []
        for side, (_, two) in enumerate(near):
            total = kept[side] + came[side].astype(jnp.float32)
            last = from_inner(total[:, width:].astype(jnp.bfloat16), two)
            sums.append(total[:, :width] + last.astype(jnp.float32))
        starts.append(jnp.concatenate(sums, axis=0))
        narrow.append(starts[-1].astype(jnp.bfloat16))
    start = jnp.concatenate(starts, axis=1)

    def ring(value):
        pairs = [(i, (i + inner_size) % dp) for i in range(dp)]
        return lax.ppermute(value, "dp", pairs)

    own = jnp.concatenate(narrow, axis=1).T
    held = [{(0, 0): value} for value in narrow]

    def move(stream, key, source):
        value = held[stream][source]
        return ring(value) if key[0] != source[0] else from_inner(value, key[1] ^ source[1])

    def pieces_of(keys):
        return [held[stream][key] for key in keys for stream in range(streams)]

    order, products = [(0, 0)], []
    square = jnp.zeros((8, width), jnp.float32)
    fresh = [(0, 0)]
    for moves in gather_rounds(outer_size):
        arrived = [
            [move(stream, key, source) for key, source in moves] for stream in range(streams)
        ]
        product, square = apply_first(own, square, pieces_of(fresh))
        for stream in range(streams - 1):
            arrived[stream] = lax.optimization_barrier(arrived[stream])
        arrived[-1], product, square = lax.optimization_barrier((arrived[-1], product, square))
        fresh = [key for key, _ in moves]
        for stream in range(streams):
            held[stream].update(zip(fresh, arrived[stream]))
        order += fresh
        products.append(both_cores(product))
    product, square = apply_first(own, square, pieces_of(fresh))
    products.append(both_cores(product))
    panel = pieces_of(order)
    squares = both_cores(square)

    first_late = sum(mine.shape[0] for mine, _ in products[:-2]) // width
    early = apply_early(panel[:first_late], products[:-2])
    inner = products[-2:]
    states = [start]
    middle = len(panel) // 2
    for step in range(3):
        state, value, product = apply_late(step, early, panel, inner, squares, states[-1:])
        states.append(state)
        product = both_cores(product)
        inner = [both_cores(apply_rest(value, panel[middle:]))]
        early = apply_early(panel[:middle], [product])
    return apply_late(3, early, panel, inner, squares, [states[3], states[1]])


def solution(mesh):
    placed = (P("dp", None), P(None, "col"), P("dp", "col"), P("col", None, None))
    return jax.shard_map(
        shards, mesh=mesh, in_specs=placed, out_specs=P("dp", "col"), check_vma=False
    )
```

time: 311 us -> 301 us (0.968)
  waiting for transfers between devices: 130 us -> 76.4 us
  starting transfers between devices: 40.1 us -> 92.9 us
  other arithmetic: 12 us -> 3.82 us
    ppermute x24 -> x28, waiting for transfers between devices: 94.3 us -> 47.7 us  [from_inner(): return lax.ppermute(value, 'dp', pairs)]
    ppermute x10, starting transfers between devices: 1.1 us -> 39.3 us  [ring(): return lax.ppermute(value, 'dp', pairs)]
    convert_element_type x5 -> x2, other arithmetic: 8.3 us -> 0.11 us  [shards(): narrow.append(starts[-1].astype(jnp.bfloat16))]
    ppermute x6 -> x9, starting transfers between devices: 10 us -> 18 us  [from_outer(): return lax.ppermute(value, 'dp', pairs)]
    ppermute x10, waiting for transfers between devices: 17.2 us -> 10 us  [ring(): return lax.ppermute(value, 'dp', pairs)]
    ppermute x24 -> x28, starting transfers between devices: 25.5 us -> 31 us  [from_inner(): return lax.ppermute(value, 'dp', pairs)]
    pallas_call x2, Pallas kernels: 26.4 us -> 21.1 us  [rebuild_rows(): pl.pallas_call(lookup_kernel, grid=(subs // tile, blocks), in_specs=[pl.B...]
    dynamic_slice x2 -> x0, local copies, waits for them, and re-layouts: 3.86 us -> none  [the longest x1 2.56 us: shards(): lax.dynamic_slice(scaled, (core * part_rows, (outer ^ step) * wide), (par...]
  transfers between devices with their start and end apart: 56 -> 66, of which waited for: 26 -> 22; matrix products, arithmetic and copies ran while one was open for 11% -> 8% of each run, Pallas kernels for 21% -> 21%
where the time goes in v12:
time: 301 us; the launch traced here: 296 us
  Pallas kernels  94.7 us (31%)
  starting transfers between devices  92.9 us (31%)
  waiting for transfers between devices  76.4 us (25%)
  matrix products  12.6 us (4%)
  local copies, waits for them, and re-layouts  12.2 us (4%)
  other arithmetic  3.82 us (1%)
    ppermute x28, waiting for transfers between devices, from_inner(): return lax.ppermute(value, 'dp', pairs)  47.7 us
    ppermute x10, starting transfers between devices, ring(): return lax.ppermute(value, 'dp', pairs)  39.3 us
    ppermute x28, starting transfers between devices, from_inner(): return lax.ppermute(value, 'dp', pairs)  31 us
    pallas_call x4, Pallas kernels, apply_late(): pl.pallas_call(functools.partial(late_kernel, step, block // width, (len(...  25.7 us
    pallas_call x2, Pallas kernels, rebuild_rows(): pl.pallas_call(lookup_kernel, grid=(subs // tile, blocks), in_specs=[pl.B...  21.1 us
    ppermute x9, starting transfers between devices, from_outer(): return lax.ppermute(value, 'dp', pairs)  18 us
    pallas_call x4, Pallas kernels, apply_early(): pl.pallas_call(functools.partial(early_kernel, len(panel), len(inner)), i...  17.5 us
    ppermute x9, waiting for transfers between devices, from_outer(): return lax.ppermute(value, 'dp', pairs)  17 us
  transfers between devices with their start and end apart: 66, of which 22 were waited for; matrix products, arithmetic and copies ran while one was open for 8% of the time, Pallas kernels for 21%

profile of v12, /device:TPU:0, one launch (start us, length us, event | category | flops | bytes accessed | tf_op | source)
XLA Modules:
  0.0 296.1 jit_solution(2491025406600563801)
XLA Ops:
  11.0 5.3 %lookup.2.own_ref = bf16[2048,512]{1,0:T(8,128)(2,1)S(1)} custom-call(bf16[1,256,512]{2,1,0:T(8,128)(2,1)S(1)} %get-tuple-element.208.codes_ref, f32[256,8,256]{2,1,0:T(8,128)S(1)} %copy-done.2), custom_call_target="tpu_custom_call" | custom-call | tf_op jit(solution)/shard_map/lookup/pallas_call | solution.py:58
  16.3 12.6 %multiply_reduce_fusion = f32[512]{0:T(512)S(1)} fusion(bf16[2048,512]{1,0:T(8,128)(2,1)S(1)} %lookup.2.own_ref, bf16[4096,2048]{1,0:T(8,128)(2,1)} %param.5, bf16[512,4096]{1,0:T(8,128)(2,1)S(1)} %copy-done.4), kind=kOutput, calls=%fused_computation | convolution fusion | flops 8594128896 | bytes 23070720 | tf_op jit(solution)/shard_map/dot_general | solution.py:390
  43.5 15.8 %lookup.3.rebuilt_ref = bf16[2048,1536]{1,0:T(8,128)(2,1)S(1)} custom-call(bf16[3,256,512]{2,1,0:T(8,128)(2,1)S(1)} %pad_maximum_fusion.codes_ref, f32[256,8,256]{2,1,0:T(8,128)S(1)} %copy-done.3), custom_call_target="tpu_custom_call" | custom-call | tf_op jit(solution)/shard_map/lookup/pallas_call | solution.py:58
  68.6 5.4 %collective-permute-start.6 = (bf16[256,512]{1,0:T(8,128)(2,1)S(1)}, bf16[256,512]{1,0:T(8,128)(2,1)S(1)}, u32[]{:S(2)}, u32[]{:S(2)}) collective-permute-start(bf16[256,512]{1,0:T(8,128)(2,1)S(1)} %get-tuple-element.115), channel_id=1, source_target_pairs={{0,8},{2,10},{4,12},{6,14},{8,0},{10,2},{12,4},{14,6},{16,24},{18,... | collective-permute-start | bytes 786440 | tf_op jit(solution)/shard_map/ppermute | solution.py:378
  79.3 5.4 %collective-permute-done.6.refs_0_ = bf16[256,512]{1,0:T(8,128)(2,1)S(1)} collective-permute-done((bf16[256,512]{1,0:T(8,128)(2,1)S(1)}, bf16[256,512]{1,0:T(8,128)(2,1)S(1)}, u32[]{:S(2)}, u32[]{:S(2)}) %collective-permute-start.6) | collective-permute-done | bytes 262176 | tf_op jit(solution)/shard_map/ppermute | solution.py:378
  84.7 10.6 %collective-permute-done.7.refs_2_ = bf16[256,512]{1,0:T(8,128)(2,1)S(1)} collective-permute-done((bf16[256,512]{1,0:T(8,128)(2,1)S(1)}, bf16[256,512]{1,0:T(8,128)(2,1)S(1)}, u32[]{:S(2)}, u32[]{:S(2)}) %collective-permute-start.7) | collective-permute-done | bytes 262176 | tf_op jit(solution)/shard_map/ppermute | solution.py:378
  97.4 4.6 %collective-permute-done.17 = bf16[1024,128]{1,0:T(8,128)(2,1)S(1)} collective-permute-done((bf16[1024,128]{1,0:T(8,128)(2,1)S(1)}, bf16[1024,128]{1,0:T(8,128)(2,1)S(1)}, u32[]{:S(2)}, u32[]{:S(2)}) %collective-permute-start.17) | collective-permute-done | bytes 262176 | tf_op jit(solution)/shard_map/ppermute | solution.py:382
  110.8 5.3 %collective-permute-done.19 = bf16[1024,256]{1,0:T(8,128)(2,1)S(1)} collective-permute-done((bf16[1024,256]{1,0:T(8,128)(2,1)S(1)}, bf16[1024,256]{1,0:T(8,128)(2,1)S(1)}, u32[]{:S(2)}, u32[]{:S(2)}) %collective-permute-start.19) | collective-permute-done | bytes 524320 | tf_op jit(solution)/shard_map/ppermute | solution.py:382
  131.3 5.6 %collective-permute-done.31.refs_4_.refs_6_ = bf16[2048,128]{1,0:T(8,128)(2,1)S(1)} collective-permute-done((bf16[2048,128]{1,0:T(8,128)(2,1)S(1)}, bf16[2048,128]{1,0:T(8,128)(2,1)S(1)}, u32[]{:S(2)}, u32[]{:S(2)}) %collective-permute-start.31) | collective-permute-done | bytes 524320 | tf_op jit(solution)/shard_map/ppermute | solution.py:382
  136.9 5.2 %collective-permute-start.23 = (bf16[2048,128]{1,0:T(8,128)(2,1)S(1)}, bf16[2048,128]{1,0:T(8,128)(2,1)}, u32[]{:S(2)}, u32[]{:S(2)}) collective-permute-start(bf16[2048,128]{1,0:T(8,128)(2,1)S(1)} %maximum_convert_fusion.1.refs_1_), channel_id=1, source_target_pairs={{0,8},{2,10},{4,12},{6,14},{8,16},{10,18},{12,20},{14,22},{16,24},... | collective-permute-start | bytes 1572872 | tf_op jit(solution)/shard_map/ppermute | solution.py:455
  149.0 5.2 %collective-permute-start.35 = (bf16[2048,128]{1,0:T(8,128)(2,1)}, bf16[2048,128]{1,0:T(8,128)(2,1)}, u32[]{:S(2)}, u32[]{:S(2)}) collective-permute-start(bf16[2048,128]{1,0:T(8,128)(2,1)} %collective-permute-done.29.refs_0_.refs_2_), channel_id=1, source_target_pairs={{0,8},{2,10},{4,12},{6,14},{8,16},{10,18},{12,20},{14,22},{16,24},... | collective-permute-start | bytes 1572872 | tf_op jit(solution)/shard_map/ppermute | solution.py:455
  159.5 5.2 %collective-permute-start.26 = (bf16[2048,128]{1,0:T(8,128)(2,1)}, bf16[2048,128]{1,0:T(8,128)(2,1)S(1)}, u32[]{:S(2)}, u32[]{:S(2)}) collective-permute-start(bf16[2048,128]{1,0:T(8,128)(2,1)} %collective-permute-done.23.refs_1_.refs_3_), channel_id=1, source_target_pairs={{0,8},{2,10},{4,12},{6,14},{8,16},{10,18},{12,20},{14,22},{16,24},... | collective-permute-start | bytes 1572872 | tf_op jit(solution)/shard_map/ppermute | solution.py:455
  166.9 5.6 %collective-permute-done.28.refs_5_.refs_13_ = bf16[2048,128]{1,0:T(8,128)(2,1)S(1)} collective-permute-done((bf16[2048,128]{1,0:T(8,128)(2,1)}, bf16[2048,128]{1,0:T(8,128)(2,1)S(1)}, u32[]{:S(2)}, u32[]{:S(2)}) %collective-permute-start.28) | collective-permute-done | bytes 524320 | tf_op jit(solution)/shard_map/ppermute | solution.py:382
  207.0 4.2 %collective-permute-start.38 = (bf16[2048,128]{1,0:T(8,128)(2,1)S(1)}, bf16[2048,128]{1,0:T(8,128)(2,1)S(1)}, u32[]{:S(2)}, u32[]{:S(2)}) collective-permute-start(bf16[2048,128]{1,0:T(8,128)(2,1)S(1)} %collective-permute-done.33.refs_3_.refs_17_.refs_1_), channel_id=1, source_target_pairs={{0,8},{2,10},{4,12},{6,14},{8,16},{10,18},{12,20},{14,22},{16,24},... | collective-permute-start | bytes 1572872 | tf_op jit(solution)/shard_map/ppermute | solution.py:455
  212.6 5.6 %collective-permute-done.40.refs_5_.refs_25_.refs_9_ = bf16[2048,128]{1,0:T(8,128)(2,1)S(1)} collective-permute-done((bf16[2048,128]{1,0:T(8,128)(2,1)S(1)}, bf16[2048,128]{1,0:T(8,128)(2,1)S(1)}, u32[]{:S(2)}, u32[]{:S(2)}) %collective-permute-start.40) | collective-permute-done | bytes 524320 | tf_op jit(solution)/shard_map/ppermute | solution.py:382
  218.2 4.3 %collective-permute-start.50 = (bf16[2048,128]{1,0:T(8,128)(2,1)S(1)}, bf16[2048,128]{1,0:T(8,128)(2,1)S(1)}, u32[]{:S(2)}, u32[]{:S(2)}) collective-permute-start(bf16[2048,128]{1,0:T(8,128)(2,1)S(1)} %collective-permute-done.49.refs_4_.refs_24_.refs_8_), channel_id=1, source_target_pairs={{0,8},{2,10},{4,12},{6,14},{8,16},{10,18},{12,20},{14,22},{16,24},... | collective-permute-start | bytes 1572872 | tf_op jit(solution)/shard_map/ppermute | solution.py:455
  229.2 5.6 %collective-permute-done.50.refs_0_.refs_26_.refs_10_ = bf16[2048,128]{1,0:T(8,128)(2,1)S(1)} collective-permute-done((bf16[2048,128]{1,0:T(8,128)(2,1)S(1)}, bf16[2048,128]{1,0:T(8,128)(2,1)S(1)}, u32[]{:S(2)}, u32[]{:S(2)}) %collective-permute-start.50) | collective-permute-done | bytes 524320 | tf_op jit(solution)/shard_map/ppermute | solution.py:455
  243.1 4.7 %early.4.refs_36_ = f32[2048,256]{1,0:T(8,128)S(1)} custom-call(bf16[2048,128]{1,0:T(8,128)(2,1)S(1)} %maximum_convert_fusion.refs_0_, bf16[2048,128]{1,0:T(8,128)(2,1)S(1)} %maximum_convert_fusion.1.refs_1_, bf16[2048,128]{1,0:T(8,128)(2,1)} %collective-permute-done.29.refs_0_.refs_2_, bf16[2048,128]{1,0:T(8,128)(2,1)} %collective-permute-done.23.refs_1_.refs_3_, ...), custom_call_target="tpu_custom_call" | custom-call | tf_op jit(solution)/shard_map/early/pallas_call | solution.py:275
  247.9 6.2 %late0.1 = (f32[2048,256]{1,0:T(8,128)S(1)}, bf16[256,2048]{1,0:T(8,128)(2,1)S(1)}, bf16[2048,256]{1,0:T(8,128)(2,1)S(1)}) custom-call(f32[8,128]{1,0:T(8,128)S(1)} %get-tuple-element.189.mine_square_ref, f32[8,128]{1,0:T(8,128)S(1)} %collective-permute-done.53.other_square_ref, bf16[2048,128]{1,0:T(8,128)(2,1)S(1)} %maximum_convert_fusion.refs_0_, ...), custom_call_target="tpu_custom_call" | custom-call | tf_op jit(solution)/shard_map/late0/pallas_call | solution.py:301
  257.3 4.2 %early.5.refs_34_ = f32[2048,256]{1,0:T(8,128)S(1)} custom-call(bf16[2048,128]{1,0:T(8,128)(2,1)S(1)} %maximum_convert_fusion.refs_0_, bf16[2048,128]{1,0:T(8,128)(2,1)S(1)} %maximum_convert_fusion.1.refs_1_, bf16[2048,128]{1,0:T(8,128)(2,1)} %collective-permute-done.29.refs_0_.refs_2_, bf16[2048,128]{1,0:T(8,128)(2,1)} %collective-permute-done.23.refs_1_.refs_3_, ...), custom_call_target="tpu_custom_call" | custom-call | tf_op jit(solution)/shard_map/early/pallas_call | solution.py:275
  261.5 6.9 %late1.1 = (f32[2048,256]{1,0:T(8,128)S(1)}, bf16[256,2048]{1,0:T(8,128)(2,1)S(1)}, bf16[2048,256]{1,0:T(8,128)(2,1)S(1)}) custom-call(f32[8,128]{1,0:T(8,128)S(1)} %get-tuple-element.189.mine_square_ref, f32[8,128]{1,0:T(8,128)S(1)} %collective-permute-done.53.other_square_ref, bf16[2048,128]{1,0:T(8,128)(2,1)S(1)} %maximum_convert_fusion.refs_0_, ...), custom_call_target="tpu_custom_call" | custom-call | tf_op jit(solution)/shard_map/late1/pallas_call | solution.py:301
  275.7 6.6 %late2.1 = (f32[2048,256]{1,0:T(8,128)S(1)}, bf16[256,2048]{1,0:T(8,128)(2,1)S(1)}, bf16[2048,256]{1,0:T(8,128)(2,1)S(1)}) custom-call(f32[8,128]{1,0:T(8,128)S(1)} %get-tuple-element.189.mine_square_ref, f32[8,128]{1,0:T(8,128)S(1)} %collective-permute-done.53.other_square_ref, bf16[2048,128]{1,0:T(8,128)(2,1)S(1)} %maximum_convert_fusion.refs_0_, ...), custom_call_target="tpu_custom_call" | custom-call | tf_op jit(solution)/shard_map/late2/pallas_call | solution.py:301
  285.5 4.4 %early.7.refs_34_ = f32[2048,256]{1,0:T(8,128)S(1)} custom-call(bf16[2048,128]{1,0:T(8,128)(2,1)S(1)} %maximum_convert_fusion.refs_0_, bf16[2048,128]{1,0:T(8,128)(2,1)S(1)} %maximum_convert_fusion.1.refs_1_, bf16[2048,128]{1,0:T(8,128)(2,1)} %collective-permute-done.29.refs_0_.refs_2_, bf16[2048,128]{1,0:T(8,128)(2,1)} %collective-permute-done.23.refs_1_.refs_3_, ...), custom_call_target="tpu_custom_call" | custom-call | tf_op jit(solution)/shard_map/early/pallas_call | solution.py:275
  289.9 5.9 %late3.1 = f32[256,2048]{1,0:T(8,128)} custom-call(f32[8,128]{1,0:T(8,128)S(1)} %get-tuple-element.189.mine_square_ref, f32[8,128]{1,0:T(8,128)S(1)} %collective-permute-done.53.other_square_ref, bf16[2048,128]{1,0:T(8,128)(2,1)S(1)} %maximum_convert_fusion.refs_0_, bf16[2048,128]{1,0:T(8,128)(2,1)S(1)} %maximum_convert_fusion.1.refs_1_, ...), custom_call_target="tpu_custom_call" | custom-call | tf_op jit(solution)/shard_map/late3/pallas_call | solution.py:301
  (194 shorter events, 144.6 us)
Async XLA Ops:
  1.4 32.5 %collective-permute-start.1 = (bf16[256,512]{1,0:T(8,128)(2,1)S(1)}, bf16[256,512]{1,0:T(8,128)(2,1)S(1)}, u32[]{:S(2)}, u32[]{:S(2)}) collective-permute-start(bf16[256,512]{1,0:T(8,128)(2,1)S(1)} %get-tuple-element.207), channel_id=1, source_target_pairs={{0,16},{2,18},{4,20},{6,22},{8,24},{10,26},{12,28},{14,30},{16,0},... | collective-permute-start | bytes 786440 | tf_op jit(solution)/shard_map/ppermute | solution.py:378
  5.5 28.4 %collective-permute-start = (bf16[256,512]{1,0:T(8,128)(2,1)S(1)}, bf16[256,512]{1,0:T(8,128)(2,1)S(1)}, u32[]{:S(2)}, u32[]{:S(2)}) collective-permute-start(bf16[256,512]{1,0:T(8,128)(2,1)S(1)} %get-tuple-element.207), channel_id=1, source_target_pairs={{0,8},{2,10},{4,12},{6,14},{8,0},{10,2},{12,4},{14,6},{16,24},{18,... | collective-permute-start | bytes 786440 | tf_op jit(solution)/shard_map/ppermute | solution.py:378
  7.1 26.9 %collective-permute-start.2 = (bf16[256,512]{1,0:T(8,128)(2,1)S(1)}, bf16[256,512]{1,0:T(8,128)(2,1)S(1)}, u32[]{:S(2)}, u32[]{:S(2)}) collective-permute-start(bf16[256,512]{1,0:T(8,128)(2,1)S(1)} %get-tuple-element.207), channel_id=1, source_target_pairs={{0,24},{2,26},{4,28},{6,30},{8,16},{10,18},{12,20},{14,22},{16,8},... | collective-permute-start | bytes 786440 | tf_op jit(solution)/shard_map/ppermute | solution.py:378
  37.5 21.9 %collective-permute-start.3 = (bf16[256,512]{1,0:T(8,128)(2,1)S(1)}, bf16[256,512]{1,0:T(8,128)(2,1)S(1)}, u32[]{:S(2)}, u32[]{:S(2)}) collective-permute-start(bf16[256,512]{1,0:T(8,128)(2,1)S(1)} %get-tuple-element.112), channel_id=1, source_target_pairs={{0,8},{2,10},{4,12},{6,14},{8,0},{10,2},{12,4},{14,6},{16,24},{18,... | collective-permute-start | bytes 786440 | tf_op jit(solution)/shard_map/ppermute | solution.py:378
  38.4 21.9 %collective-permute-start.4 = (bf16[256,512]{1,0:T(8,128)(2,1)S(1)}, bf16[256,512]{1,0:T(8,128)(2,1)S(1)}, u32[]{:S(2)}, u32[]{:S(2)}) collective-permute-start(bf16[256,512]{1,0:T(8,128)(2,1)S(1)} %get-tuple-element.113), channel_id=1, source_target_pairs={{0,16},{2,18},{4,20},{6,22},{8,24},{10,26},{12,28},{14,30},{16,0},... | collective-permute-start | bytes 786440 | tf_op jit(solution)/shard_map/ppermute | solution.py:378
  41.9 18.4 %collective-permute-start.5 = (bf16[256,512]{1,0:T(8,128)(2,1)S(1)}, bf16[256,512]{1,0:T(8,128)(2,1)S(1)}, u32[]{:S(2)}, u32[]{:S(2)}) collective-permute-start(bf16[256,512]{1,0:T(8,128)(2,1)S(1)} %get-tuple-element.114), channel_id=1, source_target_pairs={{0,24},{2,26},{4,28},{6,30},{8,16},{10,18},{12,20},{14,22},{16,8},... | collective-permute-start | bytes 786440 | tf_op jit(solution)/shard_map/ppermute | solution.py:378
  65.5 29.9 %collective-permute-start.12 = (bf16[1024,256]{1,0:T(8,128)(2,1)S(1)}, bf16[1024,256]{1,0:T(8,128)(2,1)S(1)}, u32[]{:S(2)}, u32[]{:S(2)}) collective-permute-start(bf16[1024,256]{1,0:T(8,128)(2,1)S(1)} %get-tuple-element.123), channel_id=1, source_target_pairs={{0,2},{2,0},{4,6},{6,4},{8,10},{10,8},{12,14},{14,12},{16,18},{18,... | collective-permute-start | bytes 1572872 | tf_op jit(solution)/shard_map/ppermute | solution.py:382
  67.1 28.3 %collective-permute-start.13 = (bf16[1024,256]{1,0:T(8,128)(2,1)S(1)}, bf16[1024,256]{1,0:T(8,128)(2,1)S(1)}, u32[]{:S(2)}, u32[]{:S(2)}) collective-permute-start(bf16[1024,256]{1,0:T(8,128)(2,1)S(1)} %get-tuple-element.124), channel_id=1, source_target_pairs={{0,4},{2,6},{4,0},{6,2},{8,12},{10,14},{12,8},{14,10},{16,20},{18,... | collective-permute-start | bytes 1572872 | tf_op jit(solution)/shard_map/ppermute | solution.py:382
  74.0 21.4 %collective-permute-start.7 = (bf16[256,512]{1,0:T(8,128)(2,1)S(1)}, bf16[256,512]{1,0:T(8,128)(2,1)S(1)}, u32[]{:S(2)}, u32[]{:S(2)}) collective-permute-start(bf16[256,512]{1,0:T(8,128)(2,1)S(1)} %get-tuple-element.116), channel_id=1, source_target_pairs={{0,16},{2,18},{4,20},{6,22},{8,24},{10,26},{12,28},{14,30},{16,0},... | collective-permute-start | bytes 786440 | tf_op jit(solution)/shard_map/ppermute | solution.py:378
  75.0 20.4 %collective-permute-start.8 = (bf16[256,512]{1,0:T(8,128)(2,1)S(1)}, bf16[256,512]{1,0:T(8,128)(2,1)S(1)}, u32[]{:S(2)}, u32[]{:S(2)}) collective-permute-start(bf16[256,512]{1,0:T(8,128)(2,1)S(1)} %get-tuple-element.117), channel_id=1, source_target_pairs={{0,24},{2,26},{4,28},{6,30},{8,16},{10,18},{12,20},{14,22},{16,8},... | collective-permute-start | bytes 786440 | tf_op jit(solution)/shard_map/ppermute | solution.py:378
  121.9 20.2 %collective-permute-start.30 = (bf16[2048,128]{1,0:T(8,128)(2,1)S(1)}, bf16[2048,128]{1,0:T(8,128)(2,1)S(1)}, u32[]{:S(2)}, u32[]{:S(2)}) collective-permute-start(bf16[2048,128]{1,0:T(8,128)(2,1)S(1)} %maximum_convert_fusion.refs_0_), channel_id=1, source_target_pairs={{0,2},{2,0},{4,6},{6,4},{8,10},{10,8},{12,14},{14,12},{16,18},{18,... | collective-permute-start | bytes 1572872 | tf_op jit(solution)/shard_map/ppermute | solution.py:382
  123.9 18.3 %collective-permute-start.29 = (bf16[2048,128]{1,0:T(8,128)(2,1)S(1)}, bf16[2048,128]{1,0:T(8,128)(2,1)}, u32[]{:S(2)}, u32[]{:S(2)}) collective-permute-start(bf16[2048,128]{1,0:T(8,128)(2,1)S(1)} %maximum_convert_fusion.refs_0_), channel_id=1, source_target_pairs={{0,8},{2,10},{4,12},{6,14},{8,16},{10,18},{12,20},{14,22},{16,24},... | collective-permute-start | bytes 1572872 | tf_op jit(solution)/shard_map/ppermute | solution.py:455
  129.7 18.5 %collective-permute-start.25 = (bf16[2048,128]{1,0:T(8,128)(2,1)S(1)}, bf16[2048,128]{1,0:T(8,128)(2,1)S(1)}, u32[]{:S(2)}, u32[]{:S(2)}) collective-permute-start(bf16[2048,128]{1,0:T(8,128)(2,1)S(1)} %maximum_convert_fusion.1.refs_1_), channel_id=1, source_target_pairs={{0,4},{2,6},{4,0},{6,2},{8,12},{10,14},{12,8},{14,10},{16,20},{18,... | collective-permute-start | bytes 1572872 | tf_op jit(solution)/shard_map/ppermute | solution.py:382
  131.3 26.0 %collective-permute-start.24 = (bf16[2048,128]{1,0:T(8,128)(2,1)S(1)}, bf16[2048,128]{1,0:T(8,128)(2,1)}, u32[]{:S(2)}, u32[]{:S(2)}) collective-permute-start(bf16[2048,128]{1,0:T(8,128)(2,1)S(1)} %maximum_convert_fusion.1.refs_1_), channel_id=1, source_target_pairs={{0,2},{2,0},{4,6},{6,4},{8,10},{10,8},{12,14},{14,12},{16,18},{18,... | collective-permute-start | bytes 1572872 | tf_op jit(solution)/shard_map/ppermute | solution.py:382
  136.9 20.4 %collective-permute-start.23 = (bf16[2048,128]{1,0:T(8,128)(2,1)S(1)}, bf16[2048,128]{1,0:T(8,128)(2,1)}, u32[]{:S(2)}, u32[]{:S(2)}) collective-permute-start(bf16[2048,128]{1,0:T(8,128)(2,1)S(1)} %maximum_convert_fusion.1.refs_1_), channel_id=1, source_target_pairs={{0,8},{2,10},{4,12},{6,14},{8,16},{10,18},{12,20},{14,22},{16,24},... | collective-permute-start | bytes 1572872 | tf_op jit(solution)/shard_map/ppermute | solution.py:455
  144.0 20.7 %collective-permute-start.36 = (bf16[2048,128]{1,0:T(8,128)(2,1)}, bf16[2048,128]{1,0:T(8,128)(2,1)}, u32[]{:S(2)}, u32[]{:S(2)}) collective-permute-start(bf16[2048,128]{1,0:T(8,128)(2,1)} %collective-permute-done.29.refs_0_.refs_2_), channel_id=1, source_target_pairs={{0,2},{2,0},{4,6},{6,4},{8,10},{10,8},{12,14},{14,12},{16,18},{18,... | collective-permute-start | bytes 1572872 | tf_op jit(solution)/shard_map/ppermute | solution.py:382
  159.2 19.8 %collective-permute-start.27 = (bf16[2048,128]{1,0:T(8,128)(2,1)}, bf16[2048,128]{1,0:T(8,128)(2,1)S(1)}, u32[]{:S(2)}, u32[]{:S(2)}) collective-permute-start(bf16[2048,128]{1,0:T(8,128)(2,1)} %collective-permute-done.23.refs_1_.refs_3_), channel_id=1, source_target_pairs={{0,2},{2,0},{4,6},{6,4},{8,10},{10,8},{12,14},{14,12},{16,18},{18,... | collective-permute-start | bytes 1572872 | tf_op jit(solution)/shard_map/ppermute | solution.py:382
  159.5 19.5 %collective-permute-start.26 = (bf16[2048,128]{1,0:T(8,128)(2,1)}, bf16[2048,128]{1,0:T(8,128)(2,1)S(1)}, u32[]{:S(2)}, u32[]{:S(2)}) collective-permute-start(bf16[2048,128]{1,0:T(8,128)(2,1)} %collective-permute-done.23.refs_1_.refs_3_), channel_id=1, source_target_pairs={{0,8},{2,10},{4,12},{6,14},{8,16},{10,18},{12,20},{14,22},{16,24},... | collective-permute-start | bytes 1572872 | tf_op jit(solution)/shard_map/ppermute | solution.py:455
  164.7 18.9 %collective-permute-start.43 = (bf16[2048,128]{1,0:T(8,128)(2,1)}, bf16[2048,128]{1,0:T(8,128)(2,1)S(1)}, u32[]{:S(2)}, u32[]{:S(2)}) collective-permute-start(bf16[2048,128]{1,0:T(8,128)(2,1)} %collective-permute-done.35.refs_0_.refs_8_), channel_id=1, source_target_pairs={{0,4},{2,6},{4,0},{6,2},{8,12},{10,14},{12,8},{14,10},{16,20},{18,... | collective-permute-start | bytes 1572872 | tf_op jit(solution)/shard_map/ppermute | solution.py:382
  166.5 20.5 %collective-permute-start.42 = (bf16[2048,128]{1,0:T(8,128)(2,1)}, bf16[2048,128]{1,0:T(8,128)(2,1)S(1)}, u32[]{:S(2)}, u32[]{:S(2)}) collective-permute-start(bf16[2048,128]{1,0:T(8,128)(2,1)} %collective-permute-done.35.refs_0_.refs_8_), channel_id=1, source_target_pairs={{0,2},{2,0},{4,6},{6,4},{8,10},{10,8},{12,14},{14,12},{16,18},{18,... | collective-permute-start | bytes 1572872 | tf_op jit(solution)/shard_map/ppermute | solution.py:382
  187.1 20.0 %collective-permute-start.49 = (bf16[2048,128]{1,0:T(8,128)(2,1)S(1)}, bf16[2048,128]{1,0:T(8,128)(2,1)S(1)}, u32[]{:S(2)}, u32[]{:S(2)}) collective-permute-start(bf16[2048,128]{1,0:T(8,128)(2,1)S(1)} %collective-permute-done.31.refs_4_.refs_6_), channel_id=1, source_target_pairs={{0,2},{2,0},{4,6},{6,4},{8,10},{10,8},{12,14},{14,12},{16,18},{18,... | collective-permute-start | bytes 1572872 | tf_op jit(solution)/shard_map/ppermute | solution.py:382
  188.4 22.8 %collective-permute-start.48 = (bf16[2048,128]{1,0:T(8,128)(2,1)S(1)}, bf16[2048,128]{1,0:T(8,128)(2,1)S(1)}, u32[]{:S(2)}, u32[]{:S(2)}) collective-permute-start(bf16[2048,128]{1,0:T(8,128)(2,1)S(1)} %collective-permute-done.41.refs_0_.refs_14_), channel_id=1, source_target_pairs={{0,4},{2,6},{4,0},{6,2},{8,12},{10,14},{12,8},{14,10},{16,20},{18,... | collective-permute-start | bytes 1572872 | tf_op jit(solution)/shard_map/ppermute | solution.py:382
  198.3 19.9 %collective-permute-start.40 = (bf16[2048,128]{1,0:T(8,128)(2,1)S(1)}, bf16[2048,128]{1,0:T(8,128)(2,1)S(1)}, u32[]{:S(2)}, u32[]{:S(2)}) collective-permute-start(bf16[2048,128]{1,0:T(8,128)(2,1)S(1)} %copy-done.1), channel_id=1, source_target_pairs={{0,2},{2,0},{4,6},{6,4},{8,10},{10,8},{12,14},{14,12},{16,18},{18,... | collective-permute-start | bytes 1572872 | tf_op jit(solution)/shard_map/ppermute | solution.py:382
  201.7 22.2 %collective-permute-start.39 = (bf16[2048,128]{1,0:T(8,128)(2,1)S(1)}, bf16[2048,128]{1,0:T(8,128)(2,1)S(1)}, u32[]{:S(2)}, u32[]{:S(2)}) collective-permute-start(bf16[2048,128]{1,0:T(8,128)(2,1)S(1)} %collective-permute-done.32.refs_1_.refs_15_), channel_id=1, source_target_pairs={{0,4},{2,6},{4,0},{6,2},{8,12},{10,14},{12,8},{14,10},{16,20},{18,... | collective-permute-start | bytes 1572872 | tf_op jit(solution)/shard_map/ppermute | solution.py:382
  (58 other events, 513.3 us)

commit v13 on v12

--- a/solution.py
+++ b/solution.py
@@ -198,34 +198,23 @@
     return span, jnp.dot(rows, sum_ref[...], preferred_element_type=jnp.float32)
 
 
-def early_kernel(count, parts, *refs):
-    panel, refs = refs[:count], refs[count:]
-    mine, other, (out_ref, sum_ref) = refs[:parts], refs[parts : 2 * parts], refs[2 * parts :]
-    add_up(mine, other, sum_ref)
-    for index in range(CHUNKS):
-        span, made = gram_rows(panel, sum_ref, index)
-        out_ref[span, :] = made
-
-
-def late_kernel(step, streams, counts, parts, mine_square_ref, other_square_ref, *refs):
+def apply_kernel(step, streams, count, parts, mine_square_ref, other_square_ref, *refs):
     last = step == 3
     states = 2 if last else 1
-    first_late, late = counts
-    panel, refs = refs[: first_late + late], refs[first_late + late :]
+    panel, refs = refs[:count], refs[count:]
     mine, other, refs = refs[:parts], refs[parts : 2 * parts], refs[2 * parts :]
-    early_ref, held, refs = refs[0], refs[1 : 1 + states], refs[1 + states :]
+    held, refs = refs[:states], refs[states:]
     if last:
         out_ref, sum_ref = refs
     else:
         state_ref, value_ref, inner_ref, sum_ref = refs
     width = panel[0].shape[1]
-    model_width = len(panel) * width
+    model_width = count * width
     total = jnp.sum(mine_square_ref[...] + other_square_ref[...], axis=(0, 1), keepdims=True)
     scale = model_width / (1.96 * total)
     add_up(mine, other, sum_ref)
     for index in range(CHUNKS):
-        span, made = gram_rows(panel[first_late:], sum_ref, index)
-        made += early_ref[span, :]
+        span, made = gram_rows(panel, sum_ref, index)
         if step == 2:
             made = made * scale
         else:
@@ -268,26 +257,10 @@
     )(*in_vmem(own, square, *panel))
 
 
-def apply_early(panel, inner):
-    cols, width = panel[0].shape
-    mine, other = zip(*inner)
-    operands = in_vmem(*panel, *mine, *other)
-    return pl.pallas_call(
-        functools.partial(early_kernel, len(panel), len(inner)),
-        in_specs=[VMEM] * len(operands),
-        out_specs=VMEM,
-        out_shape=pltpu.VMEM((cols, mine[0].shape[1]), jnp.float32),
-        scratch_shapes=[pltpu.VMEM((len(panel) * width, mine[0].shape[1]), jnp.bfloat16)],
-        compiler_params=pltpu.CompilerParams(vmem_limit_bytes=VMEM_BYTES),
-        name="early",
-    )(*operands)
-
-
-def apply_late(step, early, panel, inner, squares, held):
+def apply_gram(step, panel, inner, squares, held):
     mine, other = zip(*inner)
     cols, width = panel[0].shape
     block = mine[0].shape[1]
-    late = sum(part.shape[0] for part in mine) // width
     last = step == 3
     if last:
         out_shape = jax.ShapeDtypeStruct((block, cols), jnp.float32)
@@ -297,15 +270,15 @@
             pltpu.VMEM((block, cols), jnp.bfloat16),
             pltpu.VMEM((len(panel) // 2 * width, block), jnp.bfloat16),
         ]
-    operands = in_vmem(*squares, *panel, *mine, *other, early, *held)
+    operands = in_vmem(*squares, *panel, *mine, *other, *held)
     return pl.pallas_call(
-        functools.partial(late_kernel, step, block // width, (len(panel) - late, late), len(inner)),
+        functools.partial(apply_kernel, step, block // width, len(panel), len(inner)),
         in_specs=[VMEM] * len(operands),
         out_specs=VMEM if last else [VMEM] * 3,
         out_shape=out_shape,
-        scratch_shapes=[pltpu.VMEM((late * width, block), jnp.bfloat16)],
-        compiler_params=pltpu.CompilerParams(vmem_limit_bytes=VMEM_BYTES),
-        name="late%d" % step,
+        scratch_shapes=[pltpu.VMEM((len(panel) * width, block), jnp.bfloat16)],
+        compiler_params=pltpu.CompilerParams(vmem_limit_bytes=VMEM_BYTES),
+        name="apply%d" % step,
     )(*operands)
 
 
@@ -402,7 +375,7 @@
         place, weights, embeddings, part_rows, steps, streams, inner_size, wide
     )
     rebuilt = rebuild_rows(jnp.stack(group_codes), table)
-    start_row = lax.axis_index("dp") * block
+    start_row, rebuilt = lax.optimization_barrier((lax.axis_index("dp") * block, rebuilt))
     prior = lax.dynamic_slice_in_dim(rotation, start_row, block, 0).T
     prior = 0.2 * rows_total * prior.astype(jnp.float32)
     half = prior.shape[0] // 2
@@ -485,18 +458,16 @@
     panel = pieces_of(order)
     squares = both_cores(square)
 
-    first_late = sum(mine.shape[0] for mine, _ in products[:-2]) // width
-    early = apply_early(panel[:first_late], products[:-2])
-    inner = products[-2:]
     states = [start]
     middle = len(panel) // 2
     for step in range(3):
-        state, value, product = apply_late(step, early, panel, inner, squares, states[-1:])
+        state, value, product = apply_gram(step, panel, products, squares, states[-1:])
         states.append(state)
-        product = both_cores(product)
-        inner = [both_cores(apply_rest(value, panel[middle:]))]
-        early = apply_early(panel[:middle], [product])
-    return apply_late(3, early, panel, inner, squares, [states[3], states[1]])
+        early, rest = lax.optimization_barrier(
+            (both_cores(product), apply_rest(value, panel[middle:]))
+        )
+        products = [early, both_cores(rest)]
+    return apply_gram(3, panel, products, squares, [states[3], states[1]])
 
 
 def solution(mesh):

time: 301 us -> 306 us (1.017)
  Pallas kernels: 94.7 us -> 87.9 us
  local copies, waits for them, and re-layouts: 12.2 us -> 18.7 us
  waiting for transfers between devices: 76.4 us -> 80.9 us
    pallas_call x8 -> x4, Pallas kernels: 43.2 us -> 34.5 us  [apply_gram(): pl.pallas_call(functools.partial(apply_kernel, step, block // width, len(...]
    ppermute x13, waiting for transfers between devices: 0.03 us -> 8.63 us  [swap_cores(): return lax.ppermute(value, 'col', [(0, 1), (1, 0)])]
    unnamed x34 -> x60, local copies, waits for them, and re-layouts: 7.95 us -> 14.5 us
    ppermute x10, starting transfers between devices: 39.3 us -> 44.5 us  [ring(): return lax.ppermute(value, 'dp', pairs)]
    ppermute x9, starting transfers between devices: 18 us -> 14.5 us  [from_outer(): return lax.ppermute(value, 'dp', pairs)]
  transfers between devices with their start and end apart: 66 -> 66, of which waited for: 22 -> 26; matrix products, arithmetic and copies ran while one was open for 8% -> 8% of each run, Pallas kernels for 21% -> 15%
where the time goes in v13:
time: 306 us; the launch traced here: 301 us
  starting transfers between devices  92.4 us (30%)
  Pallas kernels  87.9 us (29%)
  waiting for transfers between devices  80.9 us (26%)
  local copies, waits for them, and re-layouts  18.7 us (6%)
  matrix products  12.6 us (4%)
  other arithmetic  5.19 us (2%)
    ppermute x28, waiting for transfers between devices, from_inner(): return lax.ppermute(value, 'dp', pairs)  44.8 us
    ppermute x10, starting transfers between devices, ring(): return lax.ppermute(value, 'dp', pairs)  44.5 us
    pallas_call x4, Pallas kernels, apply_gram(): pl.pallas_call(functools.partial(apply_kernel, step, block // width, len(...  34.5 us
    ppermute x28, starting transfers between devices, from_inner(): return lax.ppermute(value, 'dp', pairs)  28.7 us
    pallas_call x2, Pallas kernels, rebuild_rows(): pl.pallas_call(lookup_kernel, grid=(subs // tile, blocks), in_specs=[pl.B...  21.2 us
    ppermute x9, waiting for transfers between devices, from_outer(): return lax.ppermute(value, 'dp', pairs)  14.8 us
    unnamed x60, local copies, waits for them, and re-layouts  14.5 us
    ppermute x9, starting transfers between devices, from_outer(): return lax.ppermute(value, 'dp', pairs)  14.5 us
  transfers between devices with their start and end apart: 66, of which 26 were waited for; matrix products, arithmetic and copies ran while one was open for 8% of the time, Pallas kernels for 15%

profile of v13, /device:TPU:0, one launch (start us, length us, event | category | flops | bytes accessed | tf_op | source)
XLA Modules:
  0.0 301.3 jit_solution(12881729022592748952)
XLA Ops:
  1.4 4.1 %collective-permute-start.1 = (bf16[256,512]{1,0:T(8,128)(2,1)S(1)}, bf16[256,512]{1,0:T(8,128)(2,1)S(1)}, u32[]{:S(2)}, u32[]{:S(2)}) collective-permute-start(bf16[256,512]{1,0:T(8,128)(2,1)S(1)} %get-tuple-element.229), channel_id=1, source_target_pairs={{0,16},{2,18},{4,20},{6,22},{8,24},{10,26},{12,28},{14,30},{16,0},... | collective-permute-start | bytes 786440 | tf_op jit(solution)/shard_map/ppermute | solution.py:351
  10.1 5.3 %lookup.2.own_ref = bf16[2048,512]{1,0:T(8,128)(2,1)S(1)} custom-call(bf16[1,256,512]{2,1,0:T(8,128)(2,1)S(1)} %get-tuple-element.230.codes_ref, f32[256,8,256]{2,1,0:T(8,128)S(1)} %copy-done.2), custom_call_target="tpu_custom_call" | custom-call | tf_op jit(solution)/shard_map/lookup/pallas_call | solution.py:58
  15.5 12.6 %multiply_reduce_fusion = f32[512]{0:T(512)S(1)} fusion(bf16[2048,512]{1,0:T(8,128)(2,1)S(1)} %lookup.2.own_ref, bf16[4096,2048]{1,0:T(8,128)(2,1)} %param.5, bf16[512,4096]{1,0:T(8,128)(2,1)S(1)} %copy-done.6), kind=kOutput, calls=%fused_computation | convolution fusion | flops 8594128896 | bytes 23070720 | tf_op jit(solution)/shard_map/dot_general | solution.py:363
  43.3 15.9 %lookup.3.rebuilt_ref = bf16[2048,1536]{1,0:T(8,128)(2,1)S(1)} custom-call(bf16[3,256,512]{2,1,0:T(8,128)(2,1)S(1)} %pad_maximum_fusion.codes_ref, f32[256,8,256]{2,1,0:T(8,128)S(1)} %copy-done.3), custom_call_target="tpu_custom_call" | custom-call | tf_op jit(solution)/shard_map/lookup/pallas_call | solution.py:58
  77.8 3.8 %collective-permute-start.7 = (bf16[256,512]{1,0:T(8,128)(2,1)S(1)}, bf16[256,512]{1,0:T(8,128)(2,1)S(1)}, u32[]{:S(2)}, u32[]{:S(2)}) collective-permute-start(bf16[256,512]{1,0:T(8,128)(2,1)S(1)} %copy-done.11), channel_id=1, source_target_pairs={{0,16},{2,18},{4,20},{6,22},{8,24},{10,26},{12,28},{14,30},{16,0},... | collective-permute-start | bytes 786440 | tf_op jit(solution)/shard_map/ppermute | solution.py:351
  85.2 4.8 %collective-permute-done.6.refs_0_ = bf16[256,512]{1,0:T(8,128)(2,1)S(1)} collective-permute-done((bf16[256,512]{1,0:T(8,128)(2,1)S(1)}, bf16[256,512]{1,0:T(8,128)(2,1)S(1)}, u32[]{:S(2)}, u32[]{:S(2)}) %collective-permute-start.6) | collective-permute-done | bytes 262176 | tf_op jit(solution)/shard_map/ppermute | solution.py:351
  90.1 10.0 %collective-permute-done.7.refs_2_ = bf16[256,512]{1,0:T(8,128)(2,1)S(1)} collective-permute-done((bf16[256,512]{1,0:T(8,128)(2,1)S(1)}, bf16[256,512]{1,0:T(8,128)(2,1)S(1)}, u32[]{:S(2)}, u32[]{:S(2)}) %collective-permute-start.7) | collective-permute-done | bytes 262176 | tf_op jit(solution)/shard_map/ppermute | solution.py:351
  102.1 4.6 %collective-permute-done.17 = bf16[1024,128]{1,0:T(8,128)(2,1)S(1)} collective-permute-done((bf16[1024,128]{1,0:T(8,128)(2,1)S(1)}, bf16[1024,128]{1,0:T(8,128)(2,1)S(1)}, u32[]{:S(2)}, u32[]{:S(2)}) %collective-permute-start.17) | collective-permute-done | bytes 262176 | tf_op jit(solution)/shard_map/ppermute | solution.py:355
  115.5 5.3 %collective-permute-done.19 = bf16[1024,256]{1,0:T(8,128)(2,1)S(1)} collective-permute-done((bf16[1024,256]{1,0:T(8,128)(2,1)S(1)}, bf16[1024,256]{1,0:T(8,128)(2,1)S(1)}, u32[]{:S(2)}, u32[]{:S(2)}) %collective-permute-start.19) | collective-permute-done | bytes 524320 | tf_op jit(solution)/shard_map/ppermute | solution.py:355
  136.0 5.7 %collective-permute-done.31.refs_4_.refs_6_ = bf16[2048,128]{1,0:T(8,128)(2,1)S(1)} collective-permute-done((bf16[2048,128]{1,0:T(8,128)(2,1)S(1)}, bf16[2048,128]{1,0:T(8,128)(2,1)S(1)}, u32[]{:S(2)}, u32[]{:S(2)}) %collective-permute-start.31) | collective-permute-done | bytes 524320 | tf_op jit(solution)/shard_map/ppermute | solution.py:355
  141.7 6.0 %collective-permute-start.23 = (bf16[2048,128]{1,0:T(8,128)(2,1)S(1)}, bf16[2048,128]{1,0:T(8,128)(2,1)}, u32[]{:S(2)}, u32[]{:S(2)}) collective-permute-start(bf16[2048,128]{1,0:T(8,128)(2,1)S(1)} %maximum_convert_fusion.1.refs_1_), channel_id=1, source_target_pairs={{0,8},{2,10},{4,12},{6,14},{8,16},{10,18},{12,20},{14,22},{16,24},... | collective-permute-start | bytes 1572872 | tf_op jit(solution)/shard_map/ppermute | solution.py:428
  153.7 6.4 %collective-permute-start.35 = (bf16[2048,128]{1,0:T(8,128)(2,1)}, bf16[2048,128]{1,0:T(8,128)(2,1)}, u32[]{:S(2)}, u32[]{:S(2)}) collective-permute-start(bf16[2048,128]{1,0:T(8,128)(2,1)} %collective-permute-done.29.refs_0_.refs_2_), channel_id=1, source_target_pairs={{0,8},{2,10},{4,12},{6,14},{8,16},{10,18},{12,20},{14,22},{16,24},... | collective-permute-start | bytes 1572872 | tf_op jit(solution)/shard_map/ppermute | solution.py:428
  165.4 4.8 %collective-permute-start.26 = (bf16[2048,128]{1,0:T(8,128)(2,1)}, bf16[2048,128]{1,0:T(8,128)(2,1)S(1)}, u32[]{:S(2)}, u32[]{:S(2)}) collective-permute-start(bf16[2048,128]{1,0:T(8,128)(2,1)} %collective-permute-done.23.refs_1_.refs_3_), channel_id=1, source_target_pairs={{0,8},{2,10},{4,12},{6,14},{8,16},{10,18},{12,20},{14,22},{16,24},... | collective-permute-start | bytes 1572872 | tf_op jit(solution)/shard_map/ppermute | solution.py:428
  172.3 5.9 %collective-permute-done.28.refs_5_.refs_13_ = bf16[2048,128]{1,0:T(8,128)(2,1)S(1)} collective-permute-done((bf16[2048,128]{1,0:T(8,128)(2,1)}, bf16[2048,128]{1,0:T(8,128)(2,1)S(1)}, u32[]{:S(2)}, u32[]{:S(2)}) %collective-permute-start.28) | collective-permute-done | bytes 524320 | tf_op jit(solution)/shard_map/ppermute | solution.py:355
  188.2 4.4 %collective-permute-start.32 = (bf16[2048,128]{1,0:T(8,128)(2,1)S(1)}, bf16[2048,128]{1,0:T(8,128)(2,1)S(1)}, u32[]{:S(2)}, u32[]{:S(2)}) collective-permute-start(bf16[2048,128]{1,0:T(8,128)(2,1)S(1)} %collective-permute-done.26.refs_1_.refs_9_), channel_id=1, source_target_pairs={{0,8},{2,10},{4,12},{6,14},{8,16},{10,18},{12,20},{14,22},{16,24},... | collective-permute-start | bytes 1572872 | tf_op jit(solution)/shard_map/ppermute | solution.py:428
  199.4 4.4 %collective-permute-start.47 = (bf16[2048,128]{1,0:T(8,128)(2,1)S(1)}, bf16[2048,128]{1,0:T(8,128)(2,1)S(1)}, u32[]{:S(2)}, u32[]{:S(2)}) collective-permute-start(bf16[2048,128]{1,0:T(8,128)(2,1)S(1)} %collective-permute-done.42.refs_2_.refs_16_.refs_0_), channel_id=1, source_target_pairs={{0,8},{2,10},{4,12},{6,14},{8,16},{10,18},{12,20},{14,22},{16,24},... | collective-permute-start | bytes 1572872 | tf_op jit(solution)/shard_map/ppermute | solution.py:428
  211.8 4.9 %collective-permute-start.38 = (bf16[2048,128]{1,0:T(8,128)(2,1)S(1)}, bf16[2048,128]{1,0:T(8,128)(2,1)S(1)}, u32[]{:S(2)}, u32[]{:S(2)}) collective-permute-start(bf16[2048,128]{1,0:T(8,128)(2,1)S(1)} %collective-permute-done.33.refs_3_.refs_17_.refs_1_), channel_id=1, source_target_pairs={{0,8},{2,10},{4,12},{6,14},{8,16},{10,18},{12,20},{14,22},{16,24},... | collective-permute-start | bytes 1572872 | tf_op jit(solution)/shard_map/ppermute | solution.py:428
  217.5 5.6 %collective-permute-done.40.refs_5_.refs_25_.refs_9_ = bf16[2048,128]{1,0:T(8,128)(2,1)S(1)} collective-permute-done((bf16[2048,128]{1,0:T(8,128)(2,1)S(1)}, bf16[2048,128]{1,0:T(8,128)(2,1)S(1)}, u32[]{:S(2)}, u32[]{:S(2)}) %collective-permute-start.40) | collective-permute-done | bytes 524320 | tf_op jit(solution)/shard_map/ppermute | solution.py:355
  223.1 4.9 %collective-permute-start.50 = (bf16[2048,128]{1,0:T(8,128)(2,1)S(1)}, bf16[2048,128]{1,0:T(8,128)(2,1)S(1)}, u32[]{:S(2)}, u32[]{:S(2)}) collective-permute-start(bf16[2048,128]{1,0:T(8,128)(2,1)S(1)} %collective-permute-done.49.refs_4_.refs_24_.refs_8_), channel_id=1, source_target_pairs={{0,8},{2,10},{4,12},{6,14},{8,16},{10,18},{12,20},{14,22},{16,24},... | collective-permute-start | bytes 1572872 | tf_op jit(solution)/shard_map/ppermute | solution.py:428
  234.5 5.7 %collective-permute-done.50.refs_0_.refs_26_.refs_10_ = bf16[2048,128]{1,0:T(8,128)(2,1)S(1)} collective-permute-done((bf16[2048,128]{1,0:T(8,128)(2,1)S(1)}, bf16[2048,128]{1,0:T(8,128)(2,1)S(1)}, u32[]{:S(2)}, u32[]{:S(2)}) %collective-permute-start.50) | collective-permute-done | bytes 524320 | tf_op jit(solution)/shard_map/ppermute | solution.py:428
  249.8 8.8 %apply0.1 = (f32[2048,256]{1,0:T(8,128)S(1)}, bf16[256,2048]{1,0:T(8,128)(2,1)S(1)}, bf16[2048,256]{1,0:T(8,128)(2,1)S(1)}) custom-call(f32[8,128]{1,0:T(8,128)S(1)} %get-tuple-element.202.mine_square_ref, f32[8,128]{1,0:T(8,128)S(1)} %collective-permute-done.53.other_square_ref, bf16[2048,128]{1,0:T(8,128)(2,1)S(1)} %maximum_convert_fusion.refs_0_, ...), custom_call_target="tpu_custom_call" | custom-call | tf_op jit(solution)/shard_map/apply0/pallas_call | solution.py:274
  264.3 9.0 %apply1.1 = (f32[2048,256]{1,0:T(8,128)S(1)}, bf16[256,2048]{1,0:T(8,128)(2,1)S(1)}, bf16[2048,256]{1,0:T(8,128)(2,1)S(1)}) custom-call(f32[8,128]{1,0:T(8,128)S(1)} %get-tuple-element.202.mine_square_ref, f32[8,128]{1,0:T(8,128)S(1)} %collective-permute-done.53.other_square_ref, bf16[2048,128]{1,0:T(8,128)(2,1)S(1)} %maximum_convert_fusion.refs_0_, ...), custom_call_target="tpu_custom_call" | custom-call | tf_op jit(solution)/shard_map/apply1/pallas_call | solution.py:274
  278.7 8.7 %apply2.1 = (f32[2048,256]{1,0:T(8,128)S(1)}, bf16[256,2048]{1,0:T(8,128)(2,1)S(1)}, bf16[2048,256]{1,0:T(8,128)(2,1)S(1)}) custom-call(f32[8,128]{1,0:T(8,128)S(1)} %get-tuple-element.202.mine_square_ref, f32[8,128]{1,0:T(8,128)S(1)} %collective-permute-done.53.other_square_ref, bf16[2048,128]{1,0:T(8,128)(2,1)S(1)} %maximum_convert_fusion.refs_0_, ...), custom_call_target="tpu_custom_call" | custom-call | tf_op jit(solution)/shard_map/apply2/pallas_call | solution.py:274
  293.0 8.0 %apply3.1 = f32[256,2048]{1,0:T(8,128)} custom-call(f32[8,128]{1,0:T(8,128)S(1)} %get-tuple-element.202.mine_square_ref, f32[8,128]{1,0:T(8,128)S(1)} %collective-permute-done.53.other_square_ref, bf16[2048,128]{1,0:T(8,128)(2,1)S(1)} %maximum_convert_fusion.refs_0_, bf16[2048,128]{1,0:T(8,128)(2,1)S(1)} %maximum_convert_fusion.1.refs_1_, ...), custom_call_target="tpu_custom_call" | custom-call | tf_op jit(solution)/shard_map/apply3/pallas_call | solution.py:274
  (216 shorter events, 141.0 us)
Async XLA Ops:
  1.4 29.4 %collective-permute-start.1 = (bf16[256,512]{1,0:T(8,128)(2,1)S(1)}, bf16[256,512]{1,0:T(8,128)(2,1)S(1)}, u32[]{:S(2)}, u32[]{:S(2)}) collective-permute-start(bf16[256,512]{1,0:T(8,128)(2,1)S(1)} %get-tuple-element.229), channel_id=1, source_target_pairs={{0,16},{2,18},{4,20},{6,22},{8,24},{10,26},{12,28},{14,30},{16,0},... | collective-permute-start | bytes 786440 | tf_op jit(solution)/shard_map/ppermute | solution.py:351
  5.5 25.4 %collective-permute-start = (bf16[256,512]{1,0:T(8,128)(2,1)S(1)}, bf16[256,512]{1,0:T(8,128)(2,1)S(1)}, u32[]{:S(2)}, u32[]{:S(2)}) collective-permute-start(bf16[256,512]{1,0:T(8,128)(2,1)S(1)} %get-tuple-element.229), channel_id=1, source_target_pairs={{0,8},{2,10},{4,12},{6,14},{8,0},{10,2},{12,4},{14,6},{16,24},{18,... | collective-permute-start | bytes 786440 | tf_op jit(solution)/shard_map/ppermute | solution.py:351
  7.1 23.8 %collective-permute-start.2 = (bf16[256,512]{1,0:T(8,128)(2,1)S(1)}, bf16[256,512]{1,0:T(8,128)(2,1)S(1)}, u32[]{:S(2)}, u32[]{:S(2)}) collective-permute-start(bf16[256,512]{1,0:T(8,128)(2,1)S(1)} %get-tuple-element.229), channel_id=1, source_target_pairs={{0,24},{2,26},{4,28},{6,30},{8,16},{10,18},{12,20},{14,22},{16,8},... | collective-permute-start | bytes 786440 | tf_op jit(solution)/shard_map/ppermute | solution.py:351
  38.8 29.3 %collective-permute-start.3 = (bf16[256,512]{1,0:T(8,128)(2,1)}, bf16[256,512]{1,0:T(8,128)(2,1)S(1)}, u32[]{:S(2)}, u32[]{:S(2)}) collective-permute-start(bf16[256,512]{1,0:T(8,128)(2,1)} %get-tuple-element.124), channel_id=1, source_target_pairs={{0,8},{2,10},{4,12},{6,14},{8,0},{10,2},{12,4},{14,6},{16,24},{18,... | collective-permute-start | bytes 786440 | tf_op jit(solution)/shard_map/ppermute | solution.py:351
  39.7 28.4 %collective-permute-start.4 = (bf16[256,512]{1,0:T(8,128)(2,1)}, bf16[256,512]{1,0:T(8,128)(2,1)}, u32[]{:S(2)}, u32[]{:S(2)}) collective-permute-start(bf16[256,512]{1,0:T(8,128)(2,1)} %get-tuple-element.125), channel_id=1, source_target_pairs={{0,16},{2,18},{4,20},{6,22},{8,24},{10,26},{12,28},{14,30},{16,0},... | collective-permute-start | bytes 786440 | tf_op jit(solution)/shard_map/ppermute | solution.py:351
  43.2 25.0 %collective-permute-start.5 = (bf16[256,512]{1,0:T(8,128)(2,1)}, bf16[256,512]{1,0:T(8,128)(2,1)}, u32[]{:S(2)}, u32[]{:S(2)}) collective-permute-start(bf16[256,512]{1,0:T(8,128)(2,1)} %get-tuple-element.126), channel_id=1, source_target_pairs={{0,24},{2,26},{4,28},{6,30},{8,16},{10,18},{12,20},{14,22},{16,8},... | collective-permute-start | bytes 786440 | tf_op jit(solution)/shard_map/ppermute | solution.py:351
  74.2 25.9 %collective-permute-start.12 = (bf16[1024,256]{1,0:T(8,128)(2,1)S(1)}, bf16[1024,256]{1,0:T(8,128)(2,1)S(1)}, u32[]{:S(2)}, u32[]{:S(2)}) collective-permute-start(bf16[1024,256]{1,0:T(8,128)(2,1)S(1)} %get-tuple-element.136), channel_id=1, source_target_pairs={{0,2},{2,0},{4,6},{6,4},{8,10},{10,8},{12,14},{14,12},{16,18},{18,... | collective-permute-start | bytes 1572872 | tf_op jit(solution)/shard_map/ppermute | solution.py:355
  75.9 24.1 %collective-permute-start.13 = (bf16[1024,256]{1,0:T(8,128)(2,1)S(1)}, bf16[1024,256]{1,0:T(8,128)(2,1)S(1)}, u32[]{:S(2)}, u32[]{:S(2)}) collective-permute-start(bf16[1024,256]{1,0:T(8,128)(2,1)S(1)} %get-tuple-element.137), channel_id=1, source_target_pairs={{0,4},{2,6},{4,0},{6,2},{8,12},{10,14},{12,8},{14,10},{16,20},{18,... | collective-permute-start | bytes 1572872 | tf_op jit(solution)/shard_map/ppermute | solution.py:355
  77.8 22.3 %collective-permute-start.7 = (bf16[256,512]{1,0:T(8,128)(2,1)S(1)}, bf16[256,512]{1,0:T(8,128)(2,1)S(1)}, u32[]{:S(2)}, u32[]{:S(2)}) collective-permute-start(bf16[256,512]{1,0:T(8,128)(2,1)S(1)} %copy-done.11), channel_id=1, source_target_pairs={{0,16},{2,18},{4,20},{6,22},{8,24},{10,26},{12,28},{14,30},{16,0},... | collective-permute-start | bytes 786440 | tf_op jit(solution)/shard_map/ppermute | solution.py:351
  81.6 18.4 %collective-permute-start.8 = (bf16[256,512]{1,0:T(8,128)(2,1)S(1)}, bf16[256,512]{1,0:T(8,128)(2,1)S(1)}, u32[]{:S(2)}, u32[]{:S(2)}) collective-permute-start(bf16[256,512]{1,0:T(8,128)(2,1)S(1)} %copy-done.9), channel_id=1, source_target_pairs={{0,24},{2,26},{4,28},{6,30},{8,16},{10,18},{12,20},{14,22},{16,8},... | collective-permute-start | bytes 786440 | tf_op jit(solution)/shard_map/ppermute | solution.py:351
  126.6 21.0 %collective-permute-start.30 = (bf16[2048,128]{1,0:T(8,128)(2,1)S(1)}, bf16[2048,128]{1,0:T(8,128)(2,1)S(1)}, u32[]{:S(2)}, u32[]{:S(2)}) collective-permute-start(bf16[2048,128]{1,0:T(8,128)(2,1)S(1)} %maximum_convert_fusion.refs_0_), channel_id=1, source_target_pairs={{0,2},{2,0},{4,6},{6,4},{8,10},{10,8},{12,14},{14,12},{16,18},{18,... | collective-permute-start | bytes 1572872 | tf_op jit(solution)/shard_map/ppermute | solution.py:355
  128.6 19.0 %collective-permute-start.29 = (bf16[2048,128]{1,0:T(8,128)(2,1)S(1)}, bf16[2048,128]{1,0:T(8,128)(2,1)}, u32[]{:S(2)}, u32[]{:S(2)}) collective-permute-start(bf16[2048,128]{1,0:T(8,128)(2,1)S(1)} %maximum_convert_fusion.refs_0_), channel_id=1, source_target_pairs={{0,8},{2,10},{4,12},{6,14},{8,16},{10,18},{12,20},{14,22},{16,24},... | collective-permute-start | bytes 1572872 | tf_op jit(solution)/shard_map/ppermute | solution.py:428
  134.3 18.6 %collective-permute-start.25 = (bf16[2048,128]{1,0:T(8,128)(2,1)S(1)}, bf16[2048,128]{1,0:T(8,128)(2,1)S(1)}, u32[]{:S(2)}, u32[]{:S(2)}) collective-permute-start(bf16[2048,128]{1,0:T(8,128)(2,1)S(1)} %maximum_convert_fusion.1.refs_1_), channel_id=1, source_target_pairs={{0,4},{2,6},{4,0},{6,2},{8,12},{10,14},{12,8},{14,10},{16,20},{18,... | collective-permute-start | bytes 1572872 | tf_op jit(solution)/shard_map/ppermute | solution.py:355
  136.0 27.2 %collective-permute-start.24 = (bf16[2048,128]{1,0:T(8,128)(2,1)S(1)}, bf16[2048,128]{1,0:T(8,128)(2,1)}, u32[]{:S(2)}, u32[]{:S(2)}) collective-permute-start(bf16[2048,128]{1,0:T(8,128)(2,1)S(1)} %maximum_convert_fusion.1.refs_1_), channel_id=1, source_target_pairs={{0,2},{2,0},{4,6},{6,4},{8,10},{10,8},{12,14},{14,12},{16,18},{18,... | collective-permute-start | bytes 1572872 | tf_op jit(solution)/shard_map/ppermute | solution.py:355
  141.7 21.6 %collective-permute-start.23 = (bf16[2048,128]{1,0:T(8,128)(2,1)S(1)}, bf16[2048,128]{1,0:T(8,128)(2,1)}, u32[]{:S(2)}, u32[]{:S(2)}) collective-permute-start(bf16[2048,128]{1,0:T(8,128)(2,1)S(1)} %maximum_convert_fusion.1.refs_1_), channel_id=1, source_target_pairs={{0,8},{2,10},{4,12},{6,14},{8,16},{10,18},{12,20},{14,22},{16,24},... | collective-permute-start | bytes 1572872 | tf_op jit(solution)/shard_map/ppermute | solution.py:428
  149.2 21.0 %collective-permute-start.36 = (bf16[2048,128]{1,0:T(8,128)(2,1)}, bf16[2048,128]{1,0:T(8,128)(2,1)}, u32[]{:S(2)}, u32[]{:S(2)}) collective-permute-start(bf16[2048,128]{1,0:T(8,128)(2,1)} %collective-permute-done.29.refs_0_.refs_2_), channel_id=1, source_target_pairs={{0,2},{2,0},{4,6},{6,4},{8,10},{10,8},{12,14},{14,12},{16,18},{18,... | collective-permute-start | bytes 1572872 | tf_op jit(solution)/shard_map/ppermute | solution.py:355
  164.9 19.2 %collective-permute-start.27 = (bf16[2048,128]{1,0:T(8,128)(2,1)}, bf16[2048,128]{1,0:T(8,128)(2,1)S(1)}, u32[]{:S(2)}, u32[]{:S(2)}) collective-permute-start(bf16[2048,128]{1,0:T(8,128)(2,1)} %collective-permute-done.23.refs_1_.refs_3_), channel_id=1, source_target_pairs={{0,2},{2,0},{4,6},{6,4},{8,10},{10,8},{12,14},{14,12},{16,18},{18,... | collective-permute-start | bytes 1572872 | tf_op jit(solution)/shard_map/ppermute | solution.py:355
  165.4 18.7 %collective-permute-start.26 = (bf16[2048,128]{1,0:T(8,128)(2,1)}, bf16[2048,128]{1,0:T(8,128)(2,1)S(1)}, u32[]{:S(2)}, u32[]{:S(2)}) collective-permute-start(bf16[2048,128]{1,0:T(8,128)(2,1)} %collective-permute-done.23.refs_1_.refs_3_), channel_id=1, source_target_pairs={{0,8},{2,10},{4,12},{6,14},{8,16},{10,18},{12,20},{14,22},{16,24},... | collective-permute-start | bytes 1572872 | tf_op jit(solution)/shard_map/ppermute | solution.py:428
  172.3 20.3 %collective-permute-start.42 = (bf16[2048,128]{1,0:T(8,128)(2,1)}, bf16[2048,128]{1,0:T(8,128)(2,1)S(1)}, u32[]{:S(2)}, u32[]{:S(2)}) collective-permute-start(bf16[2048,128]{1,0:T(8,128)(2,1)} %collective-permute-done.35.refs_0_.refs_8_), channel_id=1, source_target_pairs={{0,2},{2,0},{4,6},{6,4},{8,10},{10,8},{12,14},{14,12},{16,18},{18,... | collective-permute-start | bytes 1572872 | tf_op jit(solution)/shard_map/ppermute | solution.py:355
  188.2 18.9 %collective-permute-start.32 = (bf16[2048,128]{1,0:T(8,128)(2,1)S(1)}, bf16[2048,128]{1,0:T(8,128)(2,1)S(1)}, u32[]{:S(2)}, u32[]{:S(2)}) collective-permute-start(bf16[2048,128]{1,0:T(8,128)(2,1)S(1)} %collective-permute-done.26.refs_1_.refs_9_), channel_id=1, source_target_pairs={{0,8},{2,10},{4,12},{6,14},{8,16},{10,18},{12,20},{14,22},{16,24},... | collective-permute-start | bytes 1572872 | tf_op jit(solution)/shard_map/ppermute | solution.py:428
  192.6 19.3 %collective-permute-start.49 = (bf16[2048,128]{1,0:T(8,128)(2,1)S(1)}, bf16[2048,128]{1,0:T(8,128)(2,1)S(1)}, u32[]{:S(2)}, u32[]{:S(2)}) collective-permute-start(bf16[2048,128]{1,0:T(8,128)(2,1)S(1)} %collective-permute-done.31.refs_4_.refs_6_), channel_id=1, source_target_pairs={{0,2},{2,0},{4,6},{6,4},{8,10},{10,8},{12,14},{14,12},{16,18},{18,... | collective-permute-start | bytes 1572872 | tf_op jit(solution)/shard_map/ppermute | solution.py:355
  194.2 22.5 %collective-permute-start.48 = (bf16[2048,128]{1,0:T(8,128)(2,1)S(1)}, bf16[2048,128]{1,0:T(8,128)(2,1)S(1)}, u32[]{:S(2)}, u32[]{:S(2)}) collective-permute-start(bf16[2048,128]{1,0:T(8,128)(2,1)S(1)} %collective-permute-done.41.refs_0_.refs_14_), channel_id=1, source_target_pairs={{0,4},{2,6},{4,0},{6,2},{8,12},{10,14},{12,8},{14,10},{16,20},{18,... | collective-permute-start | bytes 1572872 | tf_op jit(solution)/shard_map/ppermute | solution.py:355
  203.8 19.3 %collective-permute-start.40 = (bf16[2048,128]{1,0:T(8,128)(2,1)S(1)}, bf16[2048,128]{1,0:T(8,128)(2,1)S(1)}, u32[]{:S(2)}, u32[]{:S(2)}) collective-permute-start(bf16[2048,128]{1,0:T(8,128)(2,1)S(1)} %copy-done.5), channel_id=1, source_target_pairs={{0,2},{2,0},{4,6},{6,4},{8,10},{10,8},{12,14},{14,12},{16,18},{18,... | collective-permute-start | bytes 1572872 | tf_op jit(solution)/shard_map/ppermute | solution.py:355
  207.1 22.3 %collective-permute-start.39 = (bf16[2048,128]{1,0:T(8,128)(2,1)S(1)}, bf16[2048,128]{1,0:T(8,128)(2,1)S(1)}, u32[]{:S(2)}, u32[]{:S(2)}) collective-permute-start(bf16[2048,128]{1,0:T(8,128)(2,1)S(1)} %collective-permute-done.32.refs_1_.refs_15_), channel_id=1, source_target_pairs={{0,4},{2,6},{4,0},{6,2},{8,12},{10,14},{12,8},{14,10},{16,20},{18,... | collective-permute-start | bytes 1572872 | tf_op jit(solution)/shard_map/ppermute | solution.py:355
  (71 other events, 584.2 us)

commit v14 on v13

--- a/solution.py
+++ b/solution.py
@@ -68,6 +68,50 @@
         compiler_params=pltpu.CompilerParams(vmem_limit_bytes=VMEM_BYTES),
         name="lookup",
     )(codes, table)
+
+
+def prior_kernel(factor, place_ref, rotation_any, *refs):
+    outs, (rows_ref, sem) = refs[:-2], refs[-2:]
+    block = rows_ref.shape[0]
+    width = block // len(outs)
+    first = pl.multiple_of(place_ref[0] * block, block)
+    copy = pltpu.make_async_copy(rotation_any.at[pl.ds(first, block)], rows_ref, sem)
+    copy.start()
+    copy.wait()
+    for stream, out_ref in enumerate(outs):
+        rows = rows_ref[stream * width : (stream + 1) * width, :].astype(jnp.float32)
+        out_ref[...] = factor * rows.T
+
+
+def prior_blocks(place, rotation, block, streams, factor):
+    cols = rotation.shape[1]
+    return pl.pallas_call(
+        functools.partial(prior_kernel, factor),
+        in_specs=[pl.BlockSpec(memory_space=pltpu.SMEM), ANY],
+        out_specs=[VMEM] * streams,
+        out_shape=[pltpu.VMEM((cols, block // streams), jnp.float32)] * streams,
+        scratch_shapes=[pltpu.VMEM((block, cols), rotation.dtype), pltpu.SemaphoreType.DMA],
+        compiler_params=pltpu.CompilerParams(vmem_limit_bytes=VMEM_BYTES),
+        name="prior",
+    )(place, pltpu.with_memory_space_constraint(rotation, pltpu.HBM))
+
+
+def turn_kernel(*refs):
+    pieces, out_ref = refs[:-1], refs[-1]
+    values = jnp.concatenate([piece_ref[...] for piece_ref in pieces], axis=1)
+    out_ref[...] = values.astype(jnp.float32).T.astype(out_ref.dtype)
+
+
+def turned(pieces):
+    cols, width = pieces[0].shape
+    return pl.pallas_call(
+        turn_kernel,
+        in_specs=[VMEM] * len(pieces),
+        out_specs=VMEM,
+        out_shape=pltpu.VMEM((len(pieces) * width, cols), pieces[0].dtype),
+        compiler_params=pltpu.CompilerParams(vmem_limit_bytes=VMEM_BYTES),
+        name="turn",
+    )(*in_vmem(*pieces))
 
 
 def slices_kernel(steps, streams, inner_size, place_ref, weights_ref, rows_ref, *outs):
@@ -364,7 +408,8 @@
         rotation, embeddings, (((0,), (1,)), ((), ())), preferred_element_type=jnp.float32
     )
     residue = rotated - own.astype(jnp.float32)
-    row_error = lax.psum(jnp.sum(residue * residue, axis=0), "col")
+    row_error = jnp.sum(residue * residue, axis=0)
+    row_error = row_error + swap_cores(row_error) if col == 2 else lax.psum(row_error, "col")
     weights = 1.0 / (1.0 + row_error / (2.0 * model_width))
     weights, group_codes = lax.optimization_barrier((weights, group_codes))
 
@@ -375,10 +420,11 @@
         place, weights, embeddings, part_rows, steps, streams, inner_size, wide
     )
     rebuilt = rebuild_rows(jnp.stack(group_codes), table)
-    start_row, rebuilt = lax.optimization_barrier((lax.axis_index("dp") * block, rebuilt))
-    prior = lax.dynamic_slice_in_dim(rotation, start_row, block, 0).T
-    prior = 0.2 * rows_total * prior.astype(jnp.float32)
-    half = prior.shape[0] // 2
+    dp_index, rebuilt = lax.optimization_barrier((lax.axis_index("dp"), rebuilt))
+    prior = prior_blocks(
+        dp_index[None].astype(jnp.int32), rotation, block, streams, 0.2 * rows_total
+    )
+    half = prior[0].shape[0] // 2
     near = [(1, 2), (2, 1)]
     fetched, shares = [], []
     for stream, (_, *sends) in enumerate(slices):
@@ -405,7 +451,7 @@
             place=place,
             own=own,
             rebuilt=rebuilt,
-            prior=prior[:, stream * width : (stream + 1) * width],
+            prior=prior[stream],
             local=slices[stream][0],
             pieces=pieces,
         )
@@ -427,7 +473,7 @@
         pairs = [(i, (i + inner_size) % dp) for i in range(dp)]
         return lax.ppermute(value, "dp", pairs)
 
-    own = jnp.concatenate(narrow, axis=1).T
+    own = turned(narrow)
     held = [{(0, 0): value} for value in narrow]
 
     def move(stream, key, source):

time: 306 us -> 294 us (0.961)
  starting transfers between devices: 92.4 us -> 111 us
  local copies, waits for them, and re-layouts: 18.7 us -> 4.99 us
  waiting for transfers between devices: 80.9 us -> 68.8 us
  other arithmetic: 5.19 us -> 1.22 us
    ppermute x10, starting transfers between devices: 44.5 us -> 59.2 us  [ring(): return lax.ppermute(value, 'dp', pairs)]
    ppermute x28, waiting for transfers between devices: 44.8 us -> 33.5 us  [from_inner(): return lax.ppermute(value, 'dp', pairs)]
    pallas_call x2, Pallas kernels: 21.2 us -> 32.3 us  [rebuild_rows(): pl.pallas_call(lookup_kernel, grid=(subs // tile, blocks), in_specs=[pl.B...]
    unnamed x60 -> x11, local copies, waits for them, and re-layouts: 14.5 us -> 4.84 us
    pallas_call x4, Pallas kernels: 34.5 us -> 27.2 us  [apply_gram(): pl.pallas_call(functools.partial(apply_kernel, step, block // width, len(...]
    ppermute x28, starting transfers between devices: 28.7 us -> 32.1 us  [from_inner(): return lax.ppermute(value, 'dp', pairs)]
    ppermute x13 -> x14, waiting for transfers between devices: 8.63 us -> 9.66 us  [swap_cores(): return lax.ppermute(value, 'col', [(0, 1), (1, 0)])]
  transfers between devices with their start and end apart: 66 -> 67, of which waited for: 26 -> 23; matrix products, arithmetic and copies ran while one was open for 8% -> 5% of each run, Pallas kernels for 15% -> 19%
where the time goes in v14:
time: 294 us; the launch traced here: 289 us
  starting transfers between devices  111 us (38%)
  Pallas kernels  89 us (30%)
  waiting for transfers between devices  68.8 us (23%)
  matrix products  12.6 us (4%)
  local copies, waits for them, and re-layouts  4.99 us (2%)
    ppermute x10, starting transfers between devices, ring(): return lax.ppermute(value, 'dp', pairs)  59.2 us
    ppermute x28, waiting for transfers between devices, from_inner(): return lax.ppermute(value, 'dp', pairs)  33.5 us
    pallas_call x2, Pallas kernels, rebuild_rows(): pl.pallas_call(lookup_kernel, grid=(subs // tile, blocks), in_specs=[pl.B...  32.3 us
    ppermute x28, starting transfers between devices, from_inner(): return lax.ppermute(value, 'dp', pairs)  32.1 us
    pallas_call x4, Pallas kernels, apply_gram(): pl.pallas_call(functools.partial(apply_kernel, step, block // width, len(...  27.2 us
    ppermute x9, starting transfers between devices, from_outer(): return lax.ppermute(value, 'dp', pairs)  15.1 us
    ppermute x9, waiting for transfers between devices, from_outer(): return lax.ppermute(value, 'dp', pairs)  14.9 us
    dot_general x1, matrix products, shards(): lax.dot_general(rotation, embeddings, (((0,), (1,)), ((), ())), preferred...  12.6 us
  transfers between devices with their start and end apart: 67, of which 23 were waited for; matrix products, arithmetic and copies ran while one was open for 5% of the time, Pallas kernels for 19%

profile of v14, /device:TPU:0, one launch (start us, length us, event | category | flops | bytes accessed | tf_op | source)
XLA Modules:
  0.0 288.5 jit_solution(4003188177633784320)
XLA Ops:
  1.4 4.1 %collective-permute-start.2 = (bf16[256,512]{1,0:T(8,128)(2,1)S(1)}, bf16[256,512]{1,0:T(8,128)(2,1)S(1)}, u32[]{:S(2)}, u32[]{:S(2)}) collective-permute-start(bf16[256,512]{1,0:T(8,128)(2,1)S(1)} %get-tuple-element.231), channel_id=1, source_target_pairs={{0,16},{2,18},{4,20},{6,22},{8,24},{10,26},{12,28},{14,30},{16,0},... | collective-permute-start | bytes 786440 | tf_op jit(solution)/shard_map/ppermute | solution.py:395
  7.2 5.3 %lookup.2.own_ref = bf16[2048,512]{1,0:T(8,128)(2,1)S(1)} custom-call(bf16[1,256,512]{2,1,0:T(8,128)(2,1)S(1)} %get-tuple-element.232.codes_ref, f32[256,8,256]{2,1,0:T(8,128)S(1)} %convert_bitcast_fusion.table_ref), custom_call_target="tpu_custom_call" | custom-call | tf_op jit(solution)/shard_map/lookup/pallas_call | solution.py:58
  13.9 12.6 %multiply_reduce_fusion = f32[512]{0:T(512)S(1)} fusion(bf16[2048,512]{1,0:T(8,128)(2,1)S(1)} %lookup.2.own_ref, bf16[4096,2048]{1,0:T(8,128)(2,1)} %rotation_any.1, bf16[512,4096]{1,0:T(8,128)(2,1)S(1)} %copy-done.2), kind=kOutput, calls=%fused_computation | convolution fusion | flops 8594128896 | bytes 23070720 | tf_op jit(solution)/shard_map/dot_general | solution.py:407
  36.4 27.0 %lookup.3.rebuilt_ref = bf16[2048,1536]{1,0:T(8,128)(2,1)S(1)} custom-call(bf16[3,256,512]{2,1,0:T(8,128)(2,1)S(1)} %pad_maximum_fusion.codes_ref, f32[256,8,256]{2,1,0:T(8,128)S(1)} %copy-done.1), custom_call_target="tpu_custom_call" | custom-call | tf_op jit(solution)/shard_map/lookup/pallas_call | solution.py:58
  79.0 5.7 %collective-permute-done.7.refs_0_ = bf16[256,512]{1,0:T(8,128)(2,1)S(1)} collective-permute-done((bf16[256,512]{1,0:T(8,128)(2,1)S(1)}, bf16[256,512]{1,0:T(8,128)(2,1)S(1)}, u32[]{:S(2)}, u32[]{:S(2)}) %collective-permute-start.7) | collective-permute-done | bytes 262176 | tf_op jit(solution)/shard_map/ppermute | solution.py:395
  84.7 9.2 %collective-permute-done.8.refs_2_ = bf16[256,512]{1,0:T(8,128)(2,1)S(1)} collective-permute-done((bf16[256,512]{1,0:T(8,128)(2,1)S(1)}, bf16[256,512]{1,0:T(8,128)(2,1)S(1)}, u32[]{:S(2)}, u32[]{:S(2)}) %collective-permute-start.8) | collective-permute-done | bytes 262176 | tf_op jit(solution)/shard_map/ppermute | solution.py:395
  96.0 4.6 %collective-permute-done.18 = bf16[1024,128]{1,0:T(8,128)(2,1)S(1)} collective-permute-done((bf16[1024,128]{1,0:T(8,128)(2,1)S(1)}, bf16[1024,128]{1,0:T(8,128)(2,1)S(1)}, u32[]{:S(2)}, u32[]{:S(2)}) %collective-permute-start.18) | collective-permute-done | bytes 262176 | tf_op jit(solution)/shard_map/ppermute | solution.py:399
  109.3 5.3 %collective-permute-done.20 = bf16[1024,256]{1,0:T(8,128)(2,1)S(1)} collective-permute-done((bf16[1024,256]{1,0:T(8,128)(2,1)S(1)}, bf16[1024,256]{1,0:T(8,128)(2,1)S(1)}, u32[]{:S(2)}, u32[]{:S(2)}) %collective-permute-start.20) | collective-permute-done | bytes 524320 | tf_op jit(solution)/shard_map/ppermute | solution.py:399
  122.5 4.1 %collective-permute-start.30 = (bf16[2048,128]{1,0:T(8,128)(2,1)S(1)}, bf16[2048,128]{1,0:T(8,128)(2,1)S(1)}, u32[]{:S(2)}, u32[]{:S(2)}) collective-permute-start(bf16[2048,128]{1,0:T(8,128)(2,1)S(1)} %maximum_convert_fusion.refs_0_), channel_id=1, source_target_pairs={{0,8},{2,10},{4,12},{6,14},{8,16},{10,18},{12,20},{14,22},{16,24},... | collective-permute-start | bytes 1572872 | tf_op jit(solution)/shard_map/ppermute | solution.py:474
  129.9 5.7 %collective-permute-done.32.refs_4_.refs_6_ = bf16[2048,128]{1,0:T(8,128)(2,1)S(1)} collective-permute-done((bf16[2048,128]{1,0:T(8,128)(2,1)S(1)}, bf16[2048,128]{1,0:T(8,128)(2,1)S(1)}, u32[]{:S(2)}, u32[]{:S(2)}) %collective-permute-start.32) | collective-permute-done | bytes 524320 | tf_op jit(solution)/shard_map/ppermute | solution.py:399
  135.5 6.7 %collective-permute-start.24 = (bf16[2048,128]{1,0:T(8,128)(2,1)S(1)}, bf16[2048,128]{1,0:T(8,128)(2,1)S(1)}, u32[]{:S(2)}, u32[]{:S(2)}) collective-permute-start(bf16[2048,128]{1,0:T(8,128)(2,1)S(1)} %maximum_convert_fusion.1.refs_1_), channel_id=1, source_target_pairs={{0,8},{2,10},{4,12},{6,14},{8,16},{10,18},{12,20},{14,22},{16,24},... | collective-permute-start | bytes 1572872 | tf_op jit(solution)/shard_map/ppermute | solution.py:474
  146.8 6.7 %collective-permute-start.36 = (bf16[2048,128]{1,0:T(8,128)(2,1)S(1)}, bf16[2048,128]{1,0:T(8,128)(2,1)S(1)}, u32[]{:S(2)}, u32[]{:S(2)}) collective-permute-start(bf16[2048,128]{1,0:T(8,128)(2,1)S(1)} %collective-permute-done.30.refs_0_.refs_2_), channel_id=1, source_target_pairs={{0,8},{2,10},{4,12},{6,14},{8,16},{10,18},{12,20},{14,22},{16,24},... | collective-permute-start | bytes 1572872 | tf_op jit(solution)/shard_map/ppermute | solution.py:474
  158.0 6.7 %collective-permute-start.27 = (bf16[2048,128]{1,0:T(8,128)(2,1)S(1)}, bf16[2048,128]{1,0:T(8,128)(2,1)S(1)}, u32[]{:S(2)}, u32[]{:S(2)}) collective-permute-start(bf16[2048,128]{1,0:T(8,128)(2,1)S(1)} %collective-permute-done.24.refs_1_.refs_3_), channel_id=1, source_target_pairs={{0,8},{2,10},{4,12},{6,14},{8,16},{10,18},{12,20},{14,22},{16,24},... | collective-permute-start | bytes 1572872 | tf_op jit(solution)/shard_map/ppermute | solution.py:474
  169.2 6.7 %collective-permute-start.42 = (bf16[2048,128]{1,0:T(8,128)(2,1)S(1)}, bf16[2048,128]{1,0:T(8,128)(2,1)S(1)}, u32[]{:S(2)}, u32[]{:S(2)}) collective-permute-start(bf16[2048,128]{1,0:T(8,128)(2,1)S(1)} %collective-permute-done.36.refs_0_.refs_8_), channel_id=1, source_target_pairs={{0,8},{2,10},{4,12},{6,14},{8,16},{10,18},{12,20},{14,22},{16,24},... | collective-permute-start | bytes 1572872 | tf_op jit(solution)/shard_map/ppermute | solution.py:474
  180.5 6.7 %collective-permute-start.33 = (bf16[2048,128]{1,0:T(8,128)(2,1)S(1)}, bf16[2048,128]{1,0:T(8,128)(2,1)S(1)}, u32[]{:S(2)}, u32[]{:S(2)}) collective-permute-start(bf16[2048,128]{1,0:T(8,128)(2,1)S(1)} %collective-permute-done.27.refs_1_.refs_9_), channel_id=1, source_target_pairs={{0,8},{2,10},{4,12},{6,14},{8,16},{10,18},{12,20},{14,22},{16,24},... | collective-permute-start | bytes 1572872 | tf_op jit(solution)/shard_map/ppermute | solution.py:474
  192.2 6.1 %collective-permute-start.48 = (bf16[2048,128]{1,0:T(8,128)(2,1)S(1)}, bf16[2048,128]{1,0:T(8,128)(2,1)S(1)}, u32[]{:S(2)}, u32[]{:S(2)}) collective-permute-start(bf16[2048,128]{1,0:T(8,128)(2,1)S(1)} %collective-permute-done.43.refs_2_.refs_16_.refs_0_), channel_id=1, source_target_pairs={{0,8},{2,10},{4,12},{6,14},{8,16},{10,18},{12,20},{14,22},{16,24},... | collective-permute-start | bytes 1572872 | tf_op jit(solution)/shard_map/ppermute | solution.py:474
  204.4 7.0 %collective-permute-start.39 = (bf16[2048,128]{1,0:T(8,128)(2,1)S(1)}, bf16[2048,128]{1,0:T(8,128)(2,1)S(1)}, u32[]{:S(2)}, u32[]{:S(2)}) collective-permute-start(bf16[2048,128]{1,0:T(8,128)(2,1)S(1)} %collective-permute-done.34.refs_3_.refs_17_.refs_1_), channel_id=1, source_target_pairs={{0,8},{2,10},{4,12},{6,14},{8,16},{10,18},{12,20},{14,22},{16,24},... | collective-permute-start | bytes 1572872 | tf_op jit(solution)/shard_map/ppermute | solution.py:474
  215.6 7.0 %collective-permute-start.51 = (bf16[2048,128]{1,0:T(8,128)(2,1)S(1)}, bf16[2048,128]{1,0:T(8,128)(2,1)S(1)}, u32[]{:S(2)}, u32[]{:S(2)}) collective-permute-start(bf16[2048,128]{1,0:T(8,128)(2,1)S(1)} %collective-permute-done.50.refs_4_.refs_24_.refs_8_), channel_id=1, source_target_pairs={{0,8},{2,10},{4,12},{6,14},{8,16},{10,18},{12,20},{14,22},{16,24},... | collective-permute-start | bytes 1572872 | tf_op jit(solution)/shard_map/ppermute | solution.py:474
  228.0 6.9 %collective-permute-done.51.refs_0_.refs_26_.refs_10_ = bf16[2048,128]{1,0:T(8,128)(2,1)S(1)} collective-permute-done((bf16[2048,128]{1,0:T(8,128)(2,1)S(1)}, bf16[2048,128]{1,0:T(8,128)(2,1)S(1)}, u32[]{:S(2)}, u32[]{:S(2)}) %collective-permute-start.51) | collective-permute-done | bytes 524320 | tf_op jit(solution)/shard_map/ppermute | solution.py:474
  236.9 3.6 %collective-permute-done.45.refs_1_.refs_27_.refs_11_ = bf16[2048,128]{1,0:T(8,128)(2,1)S(1)} collective-permute-done((bf16[2048,128]{1,0:T(8,128)(2,1)S(1)}, bf16[2048,128]{1,0:T(8,128)(2,1)S(1)}, u32[]{:S(2)}, u32[]{:S(2)}) %collective-permute-start.45) | collective-permute-done | bytes 524320 | tf_op jit(solution)/shard_map/ppermute | solution.py:474
  244.4 7.0 %apply0.1 = (f32[2048,256]{1,0:T(8,128)S(1)}, bf16[256,2048]{1,0:T(8,128)(2,1)S(1)}, bf16[2048,256]{1,0:T(8,128)(2,1)S(1)}) custom-call(f32[8,128]{1,0:T(8,128)S(1)} %get-tuple-element.206.mine_square_ref, f32[8,128]{1,0:T(8,128)S(1)} %collective-permute-done.54.other_square_ref, bf16[2048,128]{1,0:T(8,128)(2,1)S(1)} %maximum_convert_fusion.refs_0_, ...), custom_call_target="tpu_custom_call" | custom-call | tf_op jit(solution)/shard_map/apply0/pallas_call | solution.py:318
  257.1 7.1 %apply1.1 = (f32[2048,256]{1,0:T(8,128)S(1)}, bf16[256,2048]{1,0:T(8,128)(2,1)S(1)}, bf16[2048,256]{1,0:T(8,128)(2,1)S(1)}) custom-call(f32[8,128]{1,0:T(8,128)S(1)} %get-tuple-element.206.mine_square_ref, f32[8,128]{1,0:T(8,128)S(1)} %collective-permute-done.54.other_square_ref, bf16[2048,128]{1,0:T(8,128)(2,1)S(1)} %maximum_convert_fusion.refs_0_, ...), custom_call_target="tpu_custom_call" | custom-call | tf_op jit(solution)/shard_map/apply1/pallas_call | solution.py:318
  269.6 6.9 %apply2.1 = (f32[2048,256]{1,0:T(8,128)S(1)}, bf16[256,2048]{1,0:T(8,128)(2,1)S(1)}, bf16[2048,256]{1,0:T(8,128)(2,1)S(1)}) custom-call(f32[8,128]{1,0:T(8,128)S(1)} %get-tuple-element.206.mine_square_ref, f32[8,128]{1,0:T(8,128)S(1)} %collective-permute-done.54.other_square_ref, bf16[2048,128]{1,0:T(8,128)(2,1)S(1)} %maximum_convert_fusion.refs_0_, ...), custom_call_target="tpu_custom_call" | custom-call | tf_op jit(solution)/shard_map/apply2/pallas_call | solution.py:318
  282.2 6.2 %apply3.1 = f32[256,2048]{1,0:T(8,128)} custom-call(f32[8,128]{1,0:T(8,128)S(1)} %get-tuple-element.206.mine_square_ref, f32[8,128]{1,0:T(8,128)S(1)} %collective-permute-done.54.other_square_ref, bf16[2048,128]{1,0:T(8,128)(2,1)S(1)} %maximum_convert_fusion.refs_0_, bf16[2048,128]{1,0:T(8,128)(2,1)S(1)} %maximum_convert_fusion.1.refs_1_, ...), custom_call_target="tpu_custom_call" | custom-call | tf_op jit(solution)/shard_map/apply3/pallas_call | solution.py:318
  (165 shorter events, 113.0 us)
Async XLA Ops:
  1.4 26.3 %collective-permute-start.2 = (bf16[256,512]{1,0:T(8,128)(2,1)S(1)}, bf16[256,512]{1,0:T(8,128)(2,1)S(1)}, u32[]{:S(2)}, u32[]{:S(2)}) collective-permute-start(bf16[256,512]{1,0:T(8,128)(2,1)S(1)} %get-tuple-element.231), channel_id=1, source_target_pairs={{0,16},{2,18},{4,20},{6,22},{8,24},{10,26},{12,28},{14,30},{16,0},... | collective-permute-start | bytes 786440 | tf_op jit(solution)/shard_map/ppermute | solution.py:395
  5.5 22.2 %collective-permute-start.1 = (bf16[256,512]{1,0:T(8,128)(2,1)S(1)}, bf16[256,512]{1,0:T(8,128)(2,1)S(1)}, u32[]{:S(2)}, u32[]{:S(2)}) collective-permute-start(bf16[256,512]{1,0:T(8,128)(2,1)S(1)} %get-tuple-element.231), channel_id=1, source_target_pairs={{0,8},{2,10},{4,12},{6,14},{8,0},{10,2},{12,4},{14,6},{16,24},{18,... | collective-permute-start | bytes 786440 | tf_op jit(solution)/shard_map/ppermute | solution.py:395
  7.1 20.7 %collective-permute-start.3 = (bf16[256,512]{1,0:T(8,128)(2,1)S(1)}, bf16[256,512]{1,0:T(8,128)(2,1)S(1)}, u32[]{:S(2)}, u32[]{:S(2)}) collective-permute-start(bf16[256,512]{1,0:T(8,128)(2,1)S(1)} %get-tuple-element.231), channel_id=1, source_target_pairs={{0,24},{2,26},{4,28},{6,30},{8,16},{10,18},{12,20},{14,22},{16,8},... | collective-permute-start | bytes 786440 | tf_op jit(solution)/shard_map/ppermute | solution.py:395
  31.3 32.2 %collective-permute-start.4 = (bf16[256,512]{1,0:T(8,128)(2,1)S(1)}, bf16[256,512]{1,0:T(8,128)(2,1)S(1)}, u32[]{:S(2)}, u32[]{:S(2)}) collective-permute-start(bf16[256,512]{1,0:T(8,128)(2,1)S(1)} %get-tuple-element.126), channel_id=1, source_target_pairs={{0,8},{2,10},{4,12},{6,14},{8,0},{10,2},{12,4},{14,6},{16,24},{18,... | collective-permute-start | bytes 786440 | tf_op jit(solution)/shard_map/ppermute | solution.py:395
  33.0 30.5 %collective-permute-start.5 = (bf16[256,512]{1,0:T(8,128)(2,1)S(1)}, bf16[256,512]{1,0:T(8,128)(2,1)S(1)}, u32[]{:S(2)}, u32[]{:S(2)}) collective-permute-start(bf16[256,512]{1,0:T(8,128)(2,1)S(1)} %get-tuple-element.127), channel_id=1, source_target_pairs={{0,16},{2,18},{4,20},{6,22},{8,24},{10,26},{12,28},{14,30},{16,0},... | collective-permute-start | bytes 786440 | tf_op jit(solution)/shard_map/ppermute | solution.py:395
  35.7 27.7 %collective-permute-start.6 = (bf16[256,512]{1,0:T(8,128)(2,1)S(1)}, bf16[256,512]{1,0:T(8,128)(2,1)S(1)}, u32[]{:S(2)}, u32[]{:S(2)}) collective-permute-start(bf16[256,512]{1,0:T(8,128)(2,1)S(1)} %get-tuple-element.128), channel_id=1, source_target_pairs={{0,24},{2,26},{4,28},{6,30},{8,16},{10,18},{12,20},{14,22},{16,8},... | collective-permute-start | bytes 786440 | tf_op jit(solution)/shard_map/ppermute | solution.py:395
  68.7 25.3 %collective-permute-start.13 = (bf16[1024,256]{1,0:T(8,128)(2,1)S(1)}, bf16[1024,256]{1,0:T(8,128)(2,1)S(1)}, u32[]{:S(2)}, u32[]{:S(2)}) collective-permute-start(bf16[1024,256]{1,0:T(8,128)(2,1)S(1)} %get-tuple-element.139), channel_id=1, source_target_pairs={{0,2},{2,0},{4,6},{6,4},{8,10},{10,8},{12,14},{14,12},{16,18},{18,... | collective-permute-start | bytes 1572872 | tf_op jit(solution)/shard_map/ppermute | solution.py:399
  70.2 23.7 %collective-permute-start.14 = (bf16[1024,256]{1,0:T(8,128)(2,1)S(1)}, bf16[1024,256]{1,0:T(8,128)(2,1)S(1)}, u32[]{:S(2)}, u32[]{:S(2)}) collective-permute-start(bf16[1024,256]{1,0:T(8,128)(2,1)S(1)} %get-tuple-element.140), channel_id=1, source_target_pairs={{0,4},{2,6},{4,0},{6,2},{8,12},{10,14},{12,8},{14,10},{16,20},{18,... | collective-permute-start | bytes 1572872 | tf_op jit(solution)/shard_map/ppermute | solution.py:399
  72.3 21.6 %collective-permute-start.8 = (bf16[256,512]{1,0:T(8,128)(2,1)S(1)}, bf16[256,512]{1,0:T(8,128)(2,1)S(1)}, u32[]{:S(2)}, u32[]{:S(2)}) collective-permute-start(bf16[256,512]{1,0:T(8,128)(2,1)S(1)} %get-tuple-element.130), channel_id=1, source_target_pairs={{0,16},{2,18},{4,20},{6,22},{8,24},{10,26},{12,28},{14,30},{16,0},... | collective-permute-start | bytes 786440 | tf_op jit(solution)/shard_map/ppermute | solution.py:395
  120.5 21.7 %collective-permute-start.31 = (bf16[2048,128]{1,0:T(8,128)(2,1)S(1)}, bf16[2048,128]{1,0:T(8,128)(2,1)S(1)}, u32[]{:S(2)}, u32[]{:S(2)}) collective-permute-start(bf16[2048,128]{1,0:T(8,128)(2,1)S(1)} %maximum_convert_fusion.refs_0_), channel_id=1, source_target_pairs={{0,2},{2,0},{4,6},{6,4},{8,10},{10,8},{12,14},{14,12},{16,18},{18,... | collective-permute-start | bytes 1572872 | tf_op jit(solution)/shard_map/ppermute | solution.py:399
  122.5 19.8 %collective-permute-start.30 = (bf16[2048,128]{1,0:T(8,128)(2,1)S(1)}, bf16[2048,128]{1,0:T(8,128)(2,1)S(1)}, u32[]{:S(2)}, u32[]{:S(2)}) collective-permute-start(bf16[2048,128]{1,0:T(8,128)(2,1)S(1)} %maximum_convert_fusion.refs_0_), channel_id=1, source_target_pairs={{0,8},{2,10},{4,12},{6,14},{8,16},{10,18},{12,20},{14,22},{16,24},... | collective-permute-start | bytes 1572872 | tf_op jit(solution)/shard_map/ppermute | solution.py:474
  127.3 19.5 %collective-permute-start.26 = (bf16[2048,128]{1,0:T(8,128)(2,1)S(1)}, bf16[2048,128]{1,0:T(8,128)(2,1)S(1)}, u32[]{:S(2)}, u32[]{:S(2)}) collective-permute-start(bf16[2048,128]{1,0:T(8,128)(2,1)S(1)} %maximum_convert_fusion.1.refs_1_), channel_id=1, source_target_pairs={{0,4},{2,6},{4,0},{6,2},{8,12},{10,14},{12,8},{14,10},{16,20},{18,... | collective-permute-start | bytes 1572872 | tf_op jit(solution)/shard_map/ppermute | solution.py:399
  129.3 25.0 %collective-permute-start.25 = (bf16[2048,128]{1,0:T(8,128)(2,1)S(1)}, bf16[2048,128]{1,0:T(8,128)(2,1)S(1)}, u32[]{:S(2)}, u32[]{:S(2)}) collective-permute-start(bf16[2048,128]{1,0:T(8,128)(2,1)S(1)} %maximum_convert_fusion.1.refs_1_), channel_id=1, source_target_pairs={{0,2},{2,0},{4,6},{6,4},{8,10},{10,8},{12,14},{14,12},{16,18},{18,... | collective-permute-start | bytes 1572872 | tf_op jit(solution)/shard_map/ppermute | solution.py:399
  143.7 21.0 %collective-permute-start.37 = (bf16[2048,128]{1,0:T(8,128)(2,1)S(1)}, bf16[2048,128]{1,0:T(8,128)(2,1)S(1)}, u32[]{:S(2)}, u32[]{:S(2)}) collective-permute-start(bf16[2048,128]{1,0:T(8,128)(2,1)S(1)} %collective-permute-done.30.refs_0_.refs_2_), channel_id=1, source_target_pairs={{0,2},{2,0},{4,6},{6,4},{8,10},{10,8},{12,14},{14,12},{16,18},{18,... | collective-permute-start | bytes 1572872 | tf_op jit(solution)/shard_map/ppermute | solution.py:399
  155.9 21.4 %collective-permute-start.28 = (bf16[2048,128]{1,0:T(8,128)(2,1)S(1)}, bf16[2048,128]{1,0:T(8,128)(2,1)S(1)}, u32[]{:S(2)}, u32[]{:S(2)}) collective-permute-start(bf16[2048,128]{1,0:T(8,128)(2,1)S(1)} %collective-permute-done.24.refs_1_.refs_3_), channel_id=1, source_target_pairs={{0,2},{2,0},{4,6},{6,4},{8,10},{10,8},{12,14},{14,12},{16,18},{18,... | collective-permute-start | bytes 1572872 | tf_op jit(solution)/shard_map/ppermute | solution.py:399
  158.0 19.3 %collective-permute-start.27 = (bf16[2048,128]{1,0:T(8,128)(2,1)S(1)}, bf16[2048,128]{1,0:T(8,128)(2,1)S(1)}, u32[]{:S(2)}, u32[]{:S(2)}) collective-permute-start(bf16[2048,128]{1,0:T(8,128)(2,1)S(1)} %collective-permute-done.24.refs_1_.refs_3_), channel_id=1, source_target_pairs={{0,8},{2,10},{4,12},{6,14},{8,16},{10,18},{12,20},{14,22},{16,24},... | collective-permute-start | bytes 1572872 | tf_op jit(solution)/shard_map/ppermute | solution.py:474
  166.2 21.0 %collective-permute-start.43 = (bf16[2048,128]{1,0:T(8,128)(2,1)S(1)}, bf16[2048,128]{1,0:T(8,128)(2,1)S(1)}, u32[]{:S(2)}, u32[]{:S(2)}) collective-permute-start(bf16[2048,128]{1,0:T(8,128)(2,1)S(1)} %collective-permute-done.36.refs_0_.refs_8_), channel_id=1, source_target_pairs={{0,2},{2,0},{4,6},{6,4},{8,10},{10,8},{12,14},{14,12},{16,18},{18,... | collective-permute-start | bytes 1572872 | tf_op jit(solution)/shard_map/ppermute | solution.py:399
  178.9 19.5 %collective-permute-start.34 = (bf16[2048,128]{1,0:T(8,128)(2,1)S(1)}, bf16[2048,128]{1,0:T(8,128)(2,1)S(1)}, u32[]{:S(2)}, u32[]{:S(2)}) collective-permute-start(bf16[2048,128]{1,0:T(8,128)(2,1)S(1)} %collective-permute-done.27.refs_1_.refs_9_), channel_id=1, source_target_pairs={{0,2},{2,0},{4,6},{6,4},{8,10},{10,8},{12,14},{14,12},{16,18},{18,... | collective-permute-start | bytes 1572872 | tf_op jit(solution)/shard_map/ppermute | solution.py:399
  180.5 19.8 %collective-permute-start.33 = (bf16[2048,128]{1,0:T(8,128)(2,1)S(1)}, bf16[2048,128]{1,0:T(8,128)(2,1)S(1)}, u32[]{:S(2)}, u32[]{:S(2)}) collective-permute-start(bf16[2048,128]{1,0:T(8,128)(2,1)S(1)} %collective-permute-done.27.refs_1_.refs_9_), channel_id=1, source_target_pairs={{0,8},{2,10},{4,12},{6,14},{8,16},{10,18},{12,20},{14,22},{16,24},... | collective-permute-start | bytes 1572872 | tf_op jit(solution)/shard_map/ppermute | solution.py:474
  187.7 23.6 %collective-permute-start.49 = (bf16[2048,128]{1,0:T(8,128)(2,1)S(1)}, bf16[2048,128]{1,0:T(8,128)(2,1)S(1)}, u32[]{:S(2)}, u32[]{:S(2)}) collective-permute-start(bf16[2048,128]{1,0:T(8,128)(2,1)S(1)} %collective-permute-done.42.refs_0_.refs_14_), channel_id=1, source_target_pairs={{0,4},{2,6},{4,0},{6,2},{8,12},{10,14},{12,8},{14,10},{16,20},{18,... | collective-permute-start | bytes 1572872 | tf_op jit(solution)/shard_map/ppermute | solution.py:399
  192.2 20.1 %collective-permute-start.48 = (bf16[2048,128]{1,0:T(8,128)(2,1)S(1)}, bf16[2048,128]{1,0:T(8,128)(2,1)S(1)}, u32[]{:S(2)}, u32[]{:S(2)}) collective-permute-start(bf16[2048,128]{1,0:T(8,128)(2,1)S(1)} %collective-permute-done.43.refs_2_.refs_16_.refs_0_), channel_id=1, source_target_pairs={{0,8},{2,10},{4,12},{6,14},{8,16},{10,18},{12,20},{14,22},{16,24},... | collective-permute-start | bytes 1572872 | tf_op jit(solution)/shard_map/ppermute | solution.py:474
  200.3 23.6 %collective-permute-start.40 = (bf16[2048,128]{1,0:T(8,128)(2,1)S(1)}, bf16[2048,128]{1,0:T(8,128)(2,1)S(1)}, u32[]{:S(2)}, u32[]{:S(2)}) collective-permute-start(bf16[2048,128]{1,0:T(8,128)(2,1)S(1)} %collective-permute-done.33.refs_1_.refs_15_), channel_id=1, source_target_pairs={{0,4},{2,6},{4,0},{6,2},{8,12},{10,14},{12,8},{14,10},{16,20},{18,... | collective-permute-start | bytes 1572872 | tf_op jit(solution)/shard_map/ppermute | solution.py:399
  204.4 20.7 %collective-permute-start.39 = (bf16[2048,128]{1,0:T(8,128)(2,1)S(1)}, bf16[2048,128]{1,0:T(8,128)(2,1)S(1)}, u32[]{:S(2)}, u32[]{:S(2)}) collective-permute-start(bf16[2048,128]{1,0:T(8,128)(2,1)S(1)} %collective-permute-done.34.refs_3_.refs_17_.refs_1_), channel_id=1, source_target_pairs={{0,8},{2,10},{4,12},{6,14},{8,16},{10,18},{12,20},{14,22},{16,24},... | collective-permute-start | bytes 1572872 | tf_op jit(solution)/shard_map/ppermute | solution.py:474
  215.6 19.3 %collective-permute-start.51 = (bf16[2048,128]{1,0:T(8,128)(2,1)S(1)}, bf16[2048,128]{1,0:T(8,128)(2,1)S(1)}, u32[]{:S(2)}, u32[]{:S(2)}) collective-permute-start(bf16[2048,128]{1,0:T(8,128)(2,1)S(1)} %collective-permute-done.50.refs_4_.refs_24_.refs_8_), channel_id=1, source_target_pairs={{0,8},{2,10},{4,12},{6,14},{8,16},{10,18},{12,20},{14,22},{16,24},... | collective-permute-start | bytes 1572872 | tf_op jit(solution)/shard_map/ppermute | solution.py:474
  (48 other events, 431.7 us)

commit v15 on v14

--- a/solution.py
+++ b/solution.py
@@ -67,7 +67,7 @@
         out_shape=pltpu.VMEM((subs * width, blocks * rows), jnp.bfloat16),
         compiler_params=pltpu.CompilerParams(vmem_limit_bytes=VMEM_BYTES),
         name="lookup",
-    )(codes, table)
+    )(codes, pltpu.with_memory_space_constraint(table, pltpu.HBM))
 
 
 def prior_kernel(factor, place_ref, rotation_any, *refs):

time: 294 us -> 296 us (level)
  transfers between devices with their start and end apart: 67 -> 67, of which waited for: 23 -> 23; matrix products, arithmetic and copies ran while one was open for 5% -> 5% of each run, Pallas kernels for 19% -> 20%
where the time goes in v15:
time: 296 us; the launch traced here: 291 us
  starting transfers between devices  111 us (38%)
  Pallas kernels  91.3 us (31%)
  waiting for transfers between devices  68.7 us (23%)
  matrix products  12.6 us (4%)
  local copies, waits for them, and re-layouts  3.67 us (1%)
    ppermute x10, starting transfers between devices, ring(): return lax.ppermute(value, 'dp', pairs)  59.8 us
    pallas_call x2, Pallas kernels, rebuild_rows(): pl.pallas_call(lookup_kernel, grid=(subs // tile, blocks), in_specs=[pl.B...  34.5 us
    ppermute x28, waiting for transfers between devices, from_inner(): return lax.ppermute(value, 'dp', pairs)  33.6 us
    ppermute x28, starting transfers between devices, from_inner(): return lax.ppermute(value, 'dp', pairs)  32.1 us
    pallas_call x4, Pallas kernels, apply_gram(): pl.pallas_call(functools.partial(apply_kernel, step, block // width, len(...  27.2 us
    ppermute x9, waiting for transfers between devices, from_outer(): return lax.ppermute(value, 'dp', pairs)  15.3 us
    ppermute x9, starting transfers between devices, from_outer(): return lax.ppermute(value, 'dp', pairs)  14.5 us
    dot_general x1, matrix products, shards(): lax.dot_general(rotation, embeddings, (((0,), (1,)), ((), ())), preferred...  12.6 us
  transfers between devices with their start and end apart: 67, of which 23 were waited for; matrix products, arithmetic and copies ran while one was open for 5% of the time, Pallas kernels for 20%

profile of v15, /device:TPU:0, one launch (start us, length us, event | category | flops | bytes accessed | tf_op | source)
XLA Modules:
  0.0 290.8 jit_solution(14391315000781929801)
XLA Ops:
  1.4 4.1 %collective-permute-start.2 = (bf16[256,512]{1,0:T(8,128)(2,1)S(1)}, bf16[256,512]{1,0:T(8,128)(2,1)S(1)}, u32[]{:S(2)}, u32[]{:S(2)}) collective-permute-start(bf16[256,512]{1,0:T(8,128)(2,1)S(1)} %get-tuple-element.231), channel_id=1, source_target_pairs={{0,16},{2,18},{4,20},{6,22},{8,24},{10,26},{12,28},{14,30},{16,0},... | collective-permute-start | bytes 786440 | tf_op jit(solution)/shard_map/ppermute | solution.py:395
  8.6 6.5 %lookup.2.own_ref = bf16[2048,512]{1,0:T(8,128)(2,1)S(1)} custom-call(bf16[1,256,512]{2,1,0:T(8,128)(2,1)S(1)} %get-tuple-element.232.codes_ref, f32[256,8,256]{2,1,0:T(8,128)} %convert_bitcast_fusion.table_ref), custom_call_target="tpu_custom_call" | custom-call | tf_op jit(solution)/shard_map/lookup/pallas_call | solution.py:58
  15.1 12.6 %multiply_reduce_fusion = f32[512]{0:T(512)S(1)} fusion(bf16[2048,512]{1,0:T(8,128)(2,1)S(1)} %lookup.2.own_ref, bf16[4096,2048]{1,0:T(8,128)(2,1)} %rotation_any.1, bf16[512,4096]{1,0:T(8,128)(2,1)S(1)} %copy-done), kind=kOutput, calls=%fused_computation | convolution fusion | flops 8594128896 | bytes 23070720 | tf_op jit(solution)/shard_map/dot_general | solution.py:407
  37.0 28.0 %lookup.3.rebuilt_ref = bf16[2048,1536]{1,0:T(8,128)(2,1)S(1)} custom-call(bf16[3,256,512]{2,1,0:T(8,128)(2,1)S(1)} %pad_maximum_fusion.codes_ref, f32[256,8,256]{2,1,0:T(8,128)} %convert_bitcast_fusion.table_ref), custom_call_target="tpu_custom_call" | custom-call | tf_op jit(solution)/shard_map/lookup/pallas_call | solution.py:58
  73.9 3.8 %collective-permute-start.8 = (bf16[256,512]{1,0:T(8,128)(2,1)S(1)}, bf16[256,512]{1,0:T(8,128)(2,1)S(1)}, u32[]{:S(2)}, u32[]{:S(2)}) collective-permute-start(bf16[256,512]{1,0:T(8,128)(2,1)S(1)} %get-tuple-element.130), channel_id=1, source_target_pairs={{0,16},{2,18},{4,20},{6,22},{8,24},{10,26},{12,28},{14,30},{16,0},... | collective-permute-start | bytes 786440 | tf_op jit(solution)/shard_map/ppermute | solution.py:395
  80.8 5.7 %collective-permute-done.7.refs_0_ = bf16[256,512]{1,0:T(8,128)(2,1)S(1)} collective-permute-done((bf16[256,512]{1,0:T(8,128)(2,1)S(1)}, bf16[256,512]{1,0:T(8,128)(2,1)S(1)}, u32[]{:S(2)}, u32[]{:S(2)}) %collective-permute-start.7) | collective-permute-done | bytes 262176 | tf_op jit(solution)/shard_map/ppermute | solution.py:395
  86.5 9.7 %collective-permute-done.8.refs_2_ = bf16[256,512]{1,0:T(8,128)(2,1)S(1)} collective-permute-done((bf16[256,512]{1,0:T(8,128)(2,1)S(1)}, bf16[256,512]{1,0:T(8,128)(2,1)S(1)}, u32[]{:S(2)}, u32[]{:S(2)}) %collective-permute-start.8) | collective-permute-done | bytes 262176 | tf_op jit(solution)/shard_map/ppermute | solution.py:395
  98.2 4.6 %collective-permute-done.18 = bf16[1024,128]{1,0:T(8,128)(2,1)S(1)} collective-permute-done((bf16[1024,128]{1,0:T(8,128)(2,1)S(1)}, bf16[1024,128]{1,0:T(8,128)(2,1)S(1)}, u32[]{:S(2)}, u32[]{:S(2)}) %collective-permute-start.18) | collective-permute-done | bytes 262176 | tf_op jit(solution)/shard_map/ppermute | solution.py:399
  111.5 5.6 %collective-permute-done.20 = bf16[1024,256]{1,0:T(8,128)(2,1)S(1)} collective-permute-done((bf16[1024,256]{1,0:T(8,128)(2,1)S(1)}, bf16[1024,256]{1,0:T(8,128)(2,1)S(1)}, u32[]{:S(2)}, u32[]{:S(2)}) %collective-permute-start.20) | collective-permute-done | bytes 524320 | tf_op jit(solution)/shard_map/ppermute | solution.py:399
  124.2 4.6 %collective-permute-start.30 = (bf16[2048,128]{1,0:T(8,128)(2,1)S(1)}, bf16[2048,128]{1,0:T(8,128)(2,1)S(1)}, u32[]{:S(2)}, u32[]{:S(2)}) collective-permute-start(bf16[2048,128]{1,0:T(8,128)(2,1)S(1)} %maximum_convert_fusion.refs_0_), channel_id=1, source_target_pairs={{0,8},{2,10},{4,12},{6,14},{8,16},{10,18},{12,20},{14,22},{16,24},... | collective-permute-start | bytes 1572872 | tf_op jit(solution)/shard_map/ppermute | solution.py:474
  131.6 6.2 %collective-permute-done.32.refs_4_.refs_6_ = bf16[2048,128]{1,0:T(8,128)(2,1)S(1)} collective-permute-done((bf16[2048,128]{1,0:T(8,128)(2,1)S(1)}, bf16[2048,128]{1,0:T(8,128)(2,1)S(1)}, u32[]{:S(2)}, u32[]{:S(2)}) %collective-permute-start.32) | collective-permute-done | bytes 524320 | tf_op jit(solution)/shard_map/ppermute | solution.py:399
  137.8 6.6 %collective-permute-start.24 = (bf16[2048,128]{1,0:T(8,128)(2,1)S(1)}, bf16[2048,128]{1,0:T(8,128)(2,1)S(1)}, u32[]{:S(2)}, u32[]{:S(2)}) collective-permute-start(bf16[2048,128]{1,0:T(8,128)(2,1)S(1)} %maximum_convert_fusion.1.refs_1_), channel_id=1, source_target_pairs={{0,8},{2,10},{4,12},{6,14},{8,16},{10,18},{12,20},{14,22},{16,24},... | collective-permute-start | bytes 1572872 | tf_op jit(solution)/shard_map/ppermute | solution.py:474
  149.0 6.6 %collective-permute-start.36 = (bf16[2048,128]{1,0:T(8,128)(2,1)S(1)}, bf16[2048,128]{1,0:T(8,128)(2,1)S(1)}, u32[]{:S(2)}, u32[]{:S(2)}) collective-permute-start(bf16[2048,128]{1,0:T(8,128)(2,1)S(1)} %collective-permute-done.30.refs_0_.refs_2_), channel_id=1, source_target_pairs={{0,8},{2,10},{4,12},{6,14},{8,16},{10,18},{12,20},{14,22},{16,24},... | collective-permute-start | bytes 1572872 | tf_op jit(solution)/shard_map/ppermute | solution.py:474
  160.2 6.6 %collective-permute-start.27 = (bf16[2048,128]{1,0:T(8,128)(2,1)S(1)}, bf16[2048,128]{1,0:T(8,128)(2,1)S(1)}, u32[]{:S(2)}, u32[]{:S(2)}) collective-permute-start(bf16[2048,128]{1,0:T(8,128)(2,1)S(1)} %collective-permute-done.24.refs_1_.refs_3_), channel_id=1, source_target_pairs={{0,8},{2,10},{4,12},{6,14},{8,16},{10,18},{12,20},{14,22},{16,24},... | collective-permute-start | bytes 1572872 | tf_op jit(solution)/shard_map/ppermute | solution.py:474
  171.5 6.6 %collective-permute-start.42 = (bf16[2048,128]{1,0:T(8,128)(2,1)S(1)}, bf16[2048,128]{1,0:T(8,128)(2,1)S(1)}, u32[]{:S(2)}, u32[]{:S(2)}) collective-permute-start(bf16[2048,128]{1,0:T(8,128)(2,1)S(1)} %collective-permute-done.36.refs_0_.refs_8_), channel_id=1, source_target_pairs={{0,8},{2,10},{4,12},{6,14},{8,16},{10,18},{12,20},{14,22},{16,24},... | collective-permute-start | bytes 1572872 | tf_op jit(solution)/shard_map/ppermute | solution.py:474
  182.7 6.6 %collective-permute-start.33 = (bf16[2048,128]{1,0:T(8,128)(2,1)S(1)}, bf16[2048,128]{1,0:T(8,128)(2,1)S(1)}, u32[]{:S(2)}, u32[]{:S(2)}) collective-permute-start(bf16[2048,128]{1,0:T(8,128)(2,1)S(1)} %collective-permute-done.27.refs_1_.refs_9_), channel_id=1, source_target_pairs={{0,8},{2,10},{4,12},{6,14},{8,16},{10,18},{12,20},{14,22},{16,24},... | collective-permute-start | bytes 1572872 | tf_op jit(solution)/shard_map/ppermute | solution.py:474
  194.5 6.1 %collective-permute-start.48 = (bf16[2048,128]{1,0:T(8,128)(2,1)S(1)}, bf16[2048,128]{1,0:T(8,128)(2,1)S(1)}, u32[]{:S(2)}, u32[]{:S(2)}) collective-permute-start(bf16[2048,128]{1,0:T(8,128)(2,1)S(1)} %collective-permute-done.43.refs_2_.refs_16_.refs_0_), channel_id=1, source_target_pairs={{0,8},{2,10},{4,12},{6,14},{8,16},{10,18},{12,20},{14,22},{16,24},... | collective-permute-start | bytes 1572872 | tf_op jit(solution)/shard_map/ppermute | solution.py:474
  206.6 7.0 %collective-permute-start.39 = (bf16[2048,128]{1,0:T(8,128)(2,1)S(1)}, bf16[2048,128]{1,0:T(8,128)(2,1)S(1)}, u32[]{:S(2)}, u32[]{:S(2)}) collective-permute-start(bf16[2048,128]{1,0:T(8,128)(2,1)S(1)} %collective-permute-done.34.refs_3_.refs_17_.refs_1_), channel_id=1, source_target_pairs={{0,8},{2,10},{4,12},{6,14},{8,16},{10,18},{12,20},{14,22},{16,24},... | collective-permute-start | bytes 1572872 | tf_op jit(solution)/shard_map/ppermute | solution.py:474
  217.8 7.0 %collective-permute-start.51 = (bf16[2048,128]{1,0:T(8,128)(2,1)S(1)}, bf16[2048,128]{1,0:T(8,128)(2,1)S(1)}, u32[]{:S(2)}, u32[]{:S(2)}) collective-permute-start(bf16[2048,128]{1,0:T(8,128)(2,1)S(1)} %collective-permute-done.50.refs_4_.refs_24_.refs_8_), channel_id=1, source_target_pairs={{0,8},{2,10},{4,12},{6,14},{8,16},{10,18},{12,20},{14,22},{16,24},... | collective-permute-start | bytes 1572872 | tf_op jit(solution)/shard_map/ppermute | solution.py:474
  230.8 6.3 %collective-permute-done.51.refs_0_.refs_26_.refs_10_ = bf16[2048,128]{1,0:T(8,128)(2,1)S(1)} collective-permute-done((bf16[2048,128]{1,0:T(8,128)(2,1)S(1)}, bf16[2048,128]{1,0:T(8,128)(2,1)S(1)}, u32[]{:S(2)}, u32[]{:S(2)}) %collective-permute-start.51) | collective-permute-done | bytes 524320 | tf_op jit(solution)/shard_map/ppermute | solution.py:474
  246.6 7.0 %apply0.1 = (f32[2048,256]{1,0:T(8,128)S(1)}, bf16[256,2048]{1,0:T(8,128)(2,1)S(1)}, bf16[2048,256]{1,0:T(8,128)(2,1)S(1)}) custom-call(f32[8,128]{1,0:T(8,128)S(1)} %get-tuple-element.206.mine_square_ref, f32[8,128]{1,0:T(8,128)S(1)} %collective-permute-done.54.other_square_ref, bf16[2048,128]{1,0:T(8,128)(2,1)S(1)} %maximum_convert_fusion.refs_0_, ...), custom_call_target="tpu_custom_call" | custom-call | tf_op jit(solution)/shard_map/apply0/pallas_call | solution.py:318
  259.3 7.1 %apply1.1 = (f32[2048,256]{1,0:T(8,128)S(1)}, bf16[256,2048]{1,0:T(8,128)(2,1)S(1)}, bf16[2048,256]{1,0:T(8,128)(2,1)S(1)}) custom-call(f32[8,128]{1,0:T(8,128)S(1)} %get-tuple-element.206.mine_square_ref, f32[8,128]{1,0:T(8,128)S(1)} %collective-permute-done.54.other_square_ref, bf16[2048,128]{1,0:T(8,128)(2,1)S(1)} %maximum_convert_fusion.refs_0_, ...), custom_call_target="tpu_custom_call" | custom-call | tf_op jit(solution)/shard_map/apply1/pallas_call | solution.py:318
  271.9 6.9 %apply2.1 = (f32[2048,256]{1,0:T(8,128)S(1)}, bf16[256,2048]{1,0:T(8,128)(2,1)S(1)}, bf16[2048,256]{1,0:T(8,128)(2,1)S(1)}) custom-call(f32[8,128]{1,0:T(8,128)S(1)} %get-tuple-element.206.mine_square_ref, f32[8,128]{1,0:T(8,128)S(1)} %collective-permute-done.54.other_square_ref, bf16[2048,128]{1,0:T(8,128)(2,1)S(1)} %maximum_convert_fusion.refs_0_, ...), custom_call_target="tpu_custom_call" | custom-call | tf_op jit(solution)/shard_map/apply2/pallas_call | solution.py:318
  284.4 6.2 %apply3.1 = f32[256,2048]{1,0:T(8,128)} custom-call(f32[8,128]{1,0:T(8,128)S(1)} %get-tuple-element.206.mine_square_ref, f32[8,128]{1,0:T(8,128)S(1)} %collective-permute-done.54.other_square_ref, bf16[2048,128]{1,0:T(8,128)(2,1)S(1)} %maximum_convert_fusion.refs_0_, bf16[2048,128]{1,0:T(8,128)(2,1)S(1)} %maximum_convert_fusion.1.refs_1_, ...), custom_call_target="tpu_custom_call" | custom-call | tf_op jit(solution)/shard_map/apply3/pallas_call | solution.py:318
  (161 shorter events, 111.9 us)
Async XLA Ops:
  1.4 27.5 %collective-permute-start.2 = (bf16[256,512]{1,0:T(8,128)(2,1)S(1)}, bf16[256,512]{1,0:T(8,128)(2,1)S(1)}, u32[]{:S(2)}, u32[]{:S(2)}) collective-permute-start(bf16[256,512]{1,0:T(8,128)(2,1)S(1)} %get-tuple-element.231), channel_id=1, source_target_pairs={{0,16},{2,18},{4,20},{6,22},{8,24},{10,26},{12,28},{14,30},{16,0},... | collective-permute-start | bytes 786440 | tf_op jit(solution)/shard_map/ppermute | solution.py:395
  5.5 23.4 %collective-permute-start.1 = (bf16[256,512]{1,0:T(8,128)(2,1)S(1)}, bf16[256,512]{1,0:T(8,128)(2,1)S(1)}, u32[]{:S(2)}, u32[]{:S(2)}) collective-permute-start(bf16[256,512]{1,0:T(8,128)(2,1)S(1)} %get-tuple-element.231), channel_id=1, source_target_pairs={{0,8},{2,10},{4,12},{6,14},{8,0},{10,2},{12,4},{14,6},{16,24},{18,... | collective-permute-start | bytes 786440 | tf_op jit(solution)/shard_map/ppermute | solution.py:395
  7.1 21.9 %collective-permute-start.3 = (bf16[256,512]{1,0:T(8,128)(2,1)S(1)}, bf16[256,512]{1,0:T(8,128)(2,1)S(1)}, u32[]{:S(2)}, u32[]{:S(2)}) collective-permute-start(bf16[256,512]{1,0:T(8,128)(2,1)S(1)} %get-tuple-element.231), channel_id=1, source_target_pairs={{0,24},{2,26},{4,28},{6,30},{8,16},{10,18},{12,20},{14,22},{16,8},... | collective-permute-start | bytes 786440 | tf_op jit(solution)/shard_map/ppermute | solution.py:395
  32.5 32.6 %collective-permute-start.4 = (bf16[256,512]{1,0:T(8,128)(2,1)S(1)}, bf16[256,512]{1,0:T(8,128)(2,1)S(1)}, u32[]{:S(2)}, u32[]{:S(2)}) collective-permute-start(bf16[256,512]{1,0:T(8,128)(2,1)S(1)} %get-tuple-element.126), channel_id=1, source_target_pairs={{0,8},{2,10},{4,12},{6,14},{8,0},{10,2},{12,4},{14,6},{16,24},{18,... | collective-permute-start | bytes 786440 | tf_op jit(solution)/shard_map/ppermute | solution.py:395
  33.4 31.6 %collective-permute-start.5 = (bf16[256,512]{1,0:T(8,128)(2,1)S(1)}, bf16[256,512]{1,0:T(8,128)(2,1)S(1)}, u32[]{:S(2)}, u32[]{:S(2)}) collective-permute-start(bf16[256,512]{1,0:T(8,128)(2,1)S(1)} %get-tuple-element.127), channel_id=1, source_target_pairs={{0,16},{2,18},{4,20},{6,22},{8,24},{10,26},{12,28},{14,30},{16,0},... | collective-permute-start | bytes 786440 | tf_op jit(solution)/shard_map/ppermute | solution.py:395
  36.9 28.1 %collective-permute-start.6 = (bf16[256,512]{1,0:T(8,128)(2,1)S(1)}, bf16[256,512]{1,0:T(8,128)(2,1)S(1)}, u32[]{:S(2)}, u32[]{:S(2)}) collective-permute-start(bf16[256,512]{1,0:T(8,128)(2,1)S(1)} %get-tuple-element.128), channel_id=1, source_target_pairs={{0,24},{2,26},{4,28},{6,30},{8,16},{10,18},{12,20},{14,22},{16,8},... | collective-permute-start | bytes 786440 | tf_op jit(solution)/shard_map/ppermute | solution.py:395
  70.3 25.9 %collective-permute-start.13 = (bf16[1024,256]{1,0:T(8,128)(2,1)S(1)}, bf16[1024,256]{1,0:T(8,128)(2,1)S(1)}, u32[]{:S(2)}, u32[]{:S(2)}) collective-permute-start(bf16[1024,256]{1,0:T(8,128)(2,1)S(1)} %get-tuple-element.139), channel_id=1, source_target_pairs={{0,2},{2,0},{4,6},{6,4},{8,10},{10,8},{12,14},{14,12},{16,18},{18,... | collective-permute-start | bytes 1572872 | tf_op jit(solution)/shard_map/ppermute | solution.py:399
  72.1 24.1 %collective-permute-start.14 = (bf16[1024,256]{1,0:T(8,128)(2,1)S(1)}, bf16[1024,256]{1,0:T(8,128)(2,1)S(1)}, u32[]{:S(2)}, u32[]{:S(2)}) collective-permute-start(bf16[1024,256]{1,0:T(8,128)(2,1)S(1)} %get-tuple-element.140), channel_id=1, source_target_pairs={{0,4},{2,6},{4,0},{6,2},{8,12},{10,14},{12,8},{14,10},{16,20},{18,... | collective-permute-start | bytes 1572872 | tf_op jit(solution)/shard_map/ppermute | solution.py:399
  73.9 22.2 %collective-permute-start.8 = (bf16[256,512]{1,0:T(8,128)(2,1)S(1)}, bf16[256,512]{1,0:T(8,128)(2,1)S(1)}, u32[]{:S(2)}, u32[]{:S(2)}) collective-permute-start(bf16[256,512]{1,0:T(8,128)(2,1)S(1)} %get-tuple-element.130), channel_id=1, source_target_pairs={{0,16},{2,18},{4,20},{6,22},{8,24},{10,26},{12,28},{14,30},{16,0},... | collective-permute-start | bytes 786440 | tf_op jit(solution)/shard_map/ppermute | solution.py:395
  122.3 22.2 %collective-permute-start.31 = (bf16[2048,128]{1,0:T(8,128)(2,1)S(1)}, bf16[2048,128]{1,0:T(8,128)(2,1)S(1)}, u32[]{:S(2)}, u32[]{:S(2)}) collective-permute-start(bf16[2048,128]{1,0:T(8,128)(2,1)S(1)} %maximum_convert_fusion.refs_0_), channel_id=1, source_target_pairs={{0,2},{2,0},{4,6},{6,4},{8,10},{10,8},{12,14},{14,12},{16,18},{18,... | collective-permute-start | bytes 1572872 | tf_op jit(solution)/shard_map/ppermute | solution.py:399
  124.2 20.2 %collective-permute-start.30 = (bf16[2048,128]{1,0:T(8,128)(2,1)S(1)}, bf16[2048,128]{1,0:T(8,128)(2,1)S(1)}, u32[]{:S(2)}, u32[]{:S(2)}) collective-permute-start(bf16[2048,128]{1,0:T(8,128)(2,1)S(1)} %maximum_convert_fusion.refs_0_), channel_id=1, source_target_pairs={{0,8},{2,10},{4,12},{6,14},{8,16},{10,18},{12,20},{14,22},{16,24},... | collective-permute-start | bytes 1572872 | tf_op jit(solution)/shard_map/ppermute | solution.py:474
  129.5 19.6 %collective-permute-start.26 = (bf16[2048,128]{1,0:T(8,128)(2,1)S(1)}, bf16[2048,128]{1,0:T(8,128)(2,1)S(1)}, u32[]{:S(2)}, u32[]{:S(2)}) collective-permute-start(bf16[2048,128]{1,0:T(8,128)(2,1)S(1)} %maximum_convert_fusion.1.refs_1_), channel_id=1, source_target_pairs={{0,4},{2,6},{4,0},{6,2},{8,12},{10,14},{12,8},{14,10},{16,20},{18,... | collective-permute-start | bytes 1572872 | tf_op jit(solution)/shard_map/ppermute | solution.py:399
  131.6 24.9 %collective-permute-start.25 = (bf16[2048,128]{1,0:T(8,128)(2,1)S(1)}, bf16[2048,128]{1,0:T(8,128)(2,1)S(1)}, u32[]{:S(2)}, u32[]{:S(2)}) collective-permute-start(bf16[2048,128]{1,0:T(8,128)(2,1)S(1)} %maximum_convert_fusion.1.refs_1_), channel_id=1, source_target_pairs={{0,2},{2,0},{4,6},{6,4},{8,10},{10,8},{12,14},{14,12},{16,18},{18,... | collective-permute-start | bytes 1572872 | tf_op jit(solution)/shard_map/ppermute | solution.py:399
  145.9 21.0 %collective-permute-start.37 = (bf16[2048,128]{1,0:T(8,128)(2,1)S(1)}, bf16[2048,128]{1,0:T(8,128)(2,1)S(1)}, u32[]{:S(2)}, u32[]{:S(2)}) collective-permute-start(bf16[2048,128]{1,0:T(8,128)(2,1)S(1)} %collective-permute-done.30.refs_0_.refs_2_), channel_id=1, source_target_pairs={{0,2},{2,0},{4,6},{6,4},{8,10},{10,8},{12,14},{14,12},{16,18},{18,... | collective-permute-start | bytes 1572872 | tf_op jit(solution)/shard_map/ppermute | solution.py:399
  158.1 21.4 %collective-permute-start.28 = (bf16[2048,128]{1,0:T(8,128)(2,1)S(1)}, bf16[2048,128]{1,0:T(8,128)(2,1)S(1)}, u32[]{:S(2)}, u32[]{:S(2)}) collective-permute-start(bf16[2048,128]{1,0:T(8,128)(2,1)S(1)} %collective-permute-done.24.refs_1_.refs_3_), channel_id=1, source_target_pairs={{0,2},{2,0},{4,6},{6,4},{8,10},{10,8},{12,14},{14,12},{16,18},{18,... | collective-permute-start | bytes 1572872 | tf_op jit(solution)/shard_map/ppermute | solution.py:399
  160.2 19.3 %collective-permute-start.27 = (bf16[2048,128]{1,0:T(8,128)(2,1)S(1)}, bf16[2048,128]{1,0:T(8,128)(2,1)S(1)}, u32[]{:S(2)}, u32[]{:S(2)}) collective-permute-start(bf16[2048,128]{1,0:T(8,128)(2,1)S(1)} %collective-permute-done.24.refs_1_.refs_3_), channel_id=1, source_target_pairs={{0,8},{2,10},{4,12},{6,14},{8,16},{10,18},{12,20},{14,22},{16,24},... | collective-permute-start | bytes 1572872 | tf_op jit(solution)/shard_map/ppermute | solution.py:474
  168.4 21.0 %collective-permute-start.43 = (bf16[2048,128]{1,0:T(8,128)(2,1)S(1)}, bf16[2048,128]{1,0:T(8,128)(2,1)S(1)}, u32[]{:S(2)}, u32[]{:S(2)}) collective-permute-start(bf16[2048,128]{1,0:T(8,128)(2,1)S(1)} %collective-permute-done.36.refs_0_.refs_8_), channel_id=1, source_target_pairs={{0,2},{2,0},{4,6},{6,4},{8,10},{10,8},{12,14},{14,12},{16,18},{18,... | collective-permute-start | bytes 1572872 | tf_op jit(solution)/shard_map/ppermute | solution.py:399
  181.1 19.5 %collective-permute-start.34 = (bf16[2048,128]{1,0:T(8,128)(2,1)S(1)}, bf16[2048,128]{1,0:T(8,128)(2,1)S(1)}, u32[]{:S(2)}, u32[]{:S(2)}) collective-permute-start(bf16[2048,128]{1,0:T(8,128)(2,1)S(1)} %collective-permute-done.27.refs_1_.refs_9_), channel_id=1, source_target_pairs={{0,2},{2,0},{4,6},{6,4},{8,10},{10,8},{12,14},{14,12},{16,18},{18,... | collective-permute-start | bytes 1572872 | tf_op jit(solution)/shard_map/ppermute | solution.py:399
  182.7 19.8 %collective-permute-start.33 = (bf16[2048,128]{1,0:T(8,128)(2,1)S(1)}, bf16[2048,128]{1,0:T(8,128)(2,1)S(1)}, u32[]{:S(2)}, u32[]{:S(2)}) collective-permute-start(bf16[2048,128]{1,0:T(8,128)(2,1)S(1)} %collective-permute-done.27.refs_1_.refs_9_), channel_id=1, source_target_pairs={{0,8},{2,10},{4,12},{6,14},{8,16},{10,18},{12,20},{14,22},{16,24},... | collective-permute-start | bytes 1572872 | tf_op jit(solution)/shard_map/ppermute | solution.py:474
  189.9 23.7 %collective-permute-start.49 = (bf16[2048,128]{1,0:T(8,128)(2,1)S(1)}, bf16[2048,128]{1,0:T(8,128)(2,1)S(1)}, u32[]{:S(2)}, u32[]{:S(2)}) collective-permute-start(bf16[2048,128]{1,0:T(8,128)(2,1)S(1)} %collective-permute-done.42.refs_0_.refs_14_), channel_id=1, source_target_pairs={{0,4},{2,6},{4,0},{6,2},{8,12},{10,14},{12,8},{14,10},{16,20},{18,... | collective-permute-start | bytes 1572872 | tf_op jit(solution)/shard_map/ppermute | solution.py:399
  194.5 20.1 %collective-permute-start.48 = (bf16[2048,128]{1,0:T(8,128)(2,1)S(1)}, bf16[2048,128]{1,0:T(8,128)(2,1)S(1)}, u32[]{:S(2)}, u32[]{:S(2)}) collective-permute-start(bf16[2048,128]{1,0:T(8,128)(2,1)S(1)} %collective-permute-done.43.refs_2_.refs_16_.refs_0_), channel_id=1, source_target_pairs={{0,8},{2,10},{4,12},{6,14},{8,16},{10,18},{12,20},{14,22},{16,24},... | collective-permute-start | bytes 1572872 | tf_op jit(solution)/shard_map/ppermute | solution.py:474
  202.5 23.7 %collective-permute-start.40 = (bf16[2048,128]{1,0:T(8,128)(2,1)S(1)}, bf16[2048,128]{1,0:T(8,128)(2,1)S(1)}, u32[]{:S(2)}, u32[]{:S(2)}) collective-permute-start(bf16[2048,128]{1,0:T(8,128)(2,1)S(1)} %collective-permute-done.33.refs_1_.refs_15_), channel_id=1, source_target_pairs={{0,4},{2,6},{4,0},{6,2},{8,12},{10,14},{12,8},{14,10},{16,20},{18,... | collective-permute-start | bytes 1572872 | tf_op jit(solution)/shard_map/ppermute | solution.py:399
  206.6 20.7 %collective-permute-start.39 = (bf16[2048,128]{1,0:T(8,128)(2,1)S(1)}, bf16[2048,128]{1,0:T(8,128)(2,1)S(1)}, u32[]{:S(2)}, u32[]{:S(2)}) collective-permute-start(bf16[2048,128]{1,0:T(8,128)(2,1)S(1)} %collective-permute-done.34.refs_3_.refs_17_.refs_1_), channel_id=1, source_target_pairs={{0,8},{2,10},{4,12},{6,14},{8,16},{10,18},{12,20},{14,22},{16,24},... | collective-permute-start | bytes 1572872 | tf_op jit(solution)/shard_map/ppermute | solution.py:474
  217.8 19.3 %collective-permute-start.51 = (bf16[2048,128]{1,0:T(8,128)(2,1)S(1)}, bf16[2048,128]{1,0:T(8,128)(2,1)S(1)}, u32[]{:S(2)}, u32[]{:S(2)}) collective-permute-start(bf16[2048,128]{1,0:T(8,128)(2,1)S(1)} %collective-permute-done.50.refs_4_.refs_24_.refs_8_), channel_id=1, source_target_pairs={{0,8},{2,10},{4,12},{6,14},{8,16},{10,18},{12,20},{14,22},{16,24},... | collective-permute-start | bytes 1572872 | tf_op jit(solution)/shard_map/ppermute | solution.py:474
  (46 other events, 424.2 us)
